TPU v7x, 32 devices: a whole 2x2x4 slice. The times are simulated.
32 devices in a mesh: dp: 16 (over z, x, core), fsdp: 2 (over y).
Axes of the slice: x: 2, y: 2, z: 4, core: 2. Of those that a mesh axis runs over, the one named last changes fastest.
Arguments:
- tokens: bfloat16 [32768, 1024], P(('dp', 'fsdp')), may hold values from -6 to 6
- incoming: bfloat16 [32, 512, 1024], P(('dp', 'fsdp')), may hold values from -6 to 6
- document_lengths: int32 [8], replicated, may hold values from 1 to 17408, as said below
- output_grad: bfloat16 [32768, 1024], P(('dp', 'fsdp')), may hold values from -12 to 12
- token_proj: bfloat16 [1024, 4096], P('dp', 'fsdp'), may hold values from -0.1875 to 0.1875
- state_proj: bfloat16 [1024, 4096], P('dp', 'fsdp'), may hold values from -0.1875 to 0.1875
- token_out: bfloat16 [2048, 1024], P('dp', 'fsdp'), may hold values from -1 to 1
- state_out: bfloat16 [2048, 1024], P('dp', 'fsdp'), may hold values from -1 to 1
- gate_weight: bfloat16 [1024, 1024], P('dp', 'fsdp'), may hold values from -0.1875 to 0.1875
- init_state: bfloat16 [512, 1024], P('dp', 'fsdp'), may hold values from -6 to 6
- hidden_in: bfloat16 [1024, 4096], P('dp', 'fsdp'), may hold values from -0.1875 to 0.1875
- hidden_out: bfloat16 [4096, 1024], P('dp', 'fsdp'), may hold values from -0.09375 to 0.09375
- token_gain: bfloat16 [1024], P('fsdp'), may hold values from 0.5 to 1.5
- state_gain: bfloat16 [1024], P('fsdp'), may hold values from 0.5 to 1.5
- hidden_gain: bfloat16 [1024], P('fsdp'), may hold values from 0.5 to 1.5
- gate_bias: bfloat16 [1024], P('fsdp'), may hold values from -4 to 4
Outputs:
- result: bfloat16 [32768, 1024], P(('dp', 'fsdp'))
- final_states: bfloat16 [32, 512, 1024], P(('dp', 'fsdp'))
- tokens_grad: bfloat16 [32768, 1024], P(('dp', 'fsdp'))
- token_proj_grad: float32 [1024, 4096], P('dp', 'fsdp')
- state_proj_grad: float32 [1024, 4096], P('dp', 'fsdp')
- token_out_grad: float32 [2048, 1024], P('dp', 'fsdp')
- state_out_grad: float32 [2048, 1024], P('dp', 'fsdp')
- gate_weight_grad: float32 [1024, 1024], P('dp', 'fsdp')
- init_state_grad: float32 [512, 1024], P('dp', 'fsdp')
- hidden_in_grad: float32 [1024, 4096], P('dp', 'fsdp')
- hidden_out_grad: float32 [4096, 1024], P('dp', 'fsdp')
- token_gain_grad: float32 [1024], P('fsdp')
- state_gain_grad: float32 [1024], P('fsdp')
- hidden_gain_grad: float32 [1024], P('fsdp')
- gate_bias_grad: float32 [1024], P('fsdp')
Inputs may be any that keep to these rules, and one draw needn't show every extreme that they name: `document_lengths`: the documents fill exactly 32 segments: the sum over documents of ceil(length / 1024) is 32. Exactly one document has the largest length; every other one has at most (9) * 1024 tokens.
All inputs are finite; a program needn't handle non-finite values.
Results may differ from a plain program's by a relative error of at most 0.019.
Values may be sent and summed in bfloat16 or wider, within the bound.
No kernel may reach another device: no remote copies, remote signals or barrier semaphores. Data moves between devices by JAX's collectives and lax.ppermute only.
A program may use at most 448 MiB of HBM per device.

v0:
```python
from functools import partial
import math

import jax
import jax.numpy as jnp
from jax import lax
from jax.sharding import PartitionSpec as P

HD = 128
WINDOW = 512


norm_eps = 1e-06
masked_score = -1e30


def layer_norm(values, gain):
    centered = values - jnp.mean(values, axis=-1, keepdims=True)
    inverse = lax.rsqrt(jnp.mean(centered * centered, axis=-1, keepdims=True) + norm_eps)
    return centered * inverse * gain


def norm_back(values, gain, grad_out):
    _, pullback = jax.vjp(layer_norm, values, gain)
    return pullback(grad_out)


def narrow(values):
    return values.astype(jnp.bfloat16)


def matmul(left, right):
    return jnp.dot(left, right, preferred_element_type=jnp.float32)


def matmul_left_t(left, right):
    return lax.dot_general(
        left, right, (((0,), (0,)), ((), ())), preferred_element_type=jnp.float32
    )


def matmul_right_t(left, right):
    return lax.dot_general(
        left, right, (((1,), (1,)), ((), ())), preferred_element_type=jnp.float32
    )


def split_heads(values):
    return values.reshape(values.shape[0], values.shape[1] // HD, HD)


def masked_scores(query, keys, allowed):
    raw = jnp.einsum(
        "rhd,khd->hrk", split_heads(query), split_heads(keys), preferred_element_type=jnp.float32
    )
    scores = raw * (1.0 / math.sqrt(HD))
    if allowed is None:
        return scores
    return jnp.where(allowed[None], scores, masked_score)


def attend(query, keys, values, allowed):
    scores = masked_scores(query, keys, allowed)
    top = jnp.max(scores, axis=-1, keepdims=True)
    weights = jnp.exp(scores - top)
    total = jnp.sum(weights, axis=-1, keepdims=True)
    probs = weights / total
    mixed = jnp.einsum(
        "hrk,khd->rhd", narrow(probs), split_heads(values), preferred_element_type=jnp.float32
    )
    return (narrow(mixed.reshape(query.shape[0], query.shape[1])), top + jnp.log(total))


def attend_back(query, keys, values, allowed, log_total, grad_mixed):
    probs = jnp.exp(masked_scores(query, keys, allowed) - log_total)
    grad_heads = split_heads(grad_mixed)
    grad_probs = jnp.einsum(
        "rhd,khd->hrk", grad_heads, split_heads(values), preferred_element_type=jnp.float32
    )
    grad_values = jnp.einsum(
        "hrk,rhd->khd", narrow(probs), grad_heads, preferred_element_type=jnp.float32
    )
    centered = grad_probs - jnp.sum(grad_probs * probs, axis=-1, keepdims=True)
    grad_raw = narrow(probs * centered * (1.0 / math.sqrt(HD)))
    grad_query = jnp.einsum(
        "hrk,khd->rhd", grad_raw, split_heads(keys), preferred_element_type=jnp.float32
    )
    grad_keys = jnp.einsum(
        "hrk,rhd->khd", grad_raw, split_heads(query), preferred_element_type=jnp.float32
    )
    return (
        grad_query.reshape(query.shape),
        grad_keys.reshape(keys.shape),
        grad_values.reshape(values.shape),
    )


def window_allowed(start, window):
    query_pos = start + jnp.arange(window)
    key_pos = start - window + jnp.arange(2 * window)
    later = key_pos[None, :] <= query_pos[:, None]
    near = key_pos[None, :] > query_pos[:, None] - window
    return later & near & (key_pos[None, :] >= 0)


def shards(
    tokens,
    incoming,
    document_lengths,
    output_grad,
    token_proj,
    state_proj,
    token_out,
    state_out,
    gate_weight,
    init_state,
    hidden_in,
    hidden_out,
    token_gain,
    state_gain,
    hidden_gain,
    gate_bias,
):
    columns = (
        lax.all_gather(token_proj, "fsdp", axis=1, tiled=True),
        lax.all_gather(state_proj, "fsdp", axis=1, tiled=True),
        lax.all_gather(token_out, "fsdp", axis=1, tiled=True),
        lax.all_gather(state_out, "fsdp", axis=1, tiled=True),
        lax.all_gather(gate_weight, "fsdp", axis=1, tiled=True),
        lax.all_gather(init_state, "fsdp", axis=1, tiled=True),
        lax.all_gather(hidden_in, "fsdp", axis=1, tiled=True),
        lax.all_gather(hidden_out, "fsdp", axis=1, tiled=True),
        lax.all_gather(token_gain, "fsdp", axis=0, tiled=True),
        lax.all_gather(state_gain, "fsdp", axis=0, tiled=True),
        lax.all_gather(hidden_gain, "fsdp", axis=0, tiled=True),
        lax.all_gather(gate_bias, "fsdp", axis=0, tiled=True),
    )
    weights = (
        lax.all_gather(columns[0], "dp", axis=0, tiled=True),
        lax.all_gather(columns[1], "dp", axis=0, tiled=True),
        lax.all_gather(columns[2], "dp", axis=0, tiled=True),
        lax.all_gather(columns[3], "dp", axis=0, tiled=True),
        lax.all_gather(columns[4], "dp", axis=0, tiled=True),
        lax.all_gather(columns[5], "dp", axis=0, tiled=True),
        lax.all_gather(columns[6], "dp", axis=0, tiled=True),
        lax.all_gather(columns[7], "dp", axis=0, tiled=True),
    )
    (
        full_token_proj,
        full_state_proj,
        full_token_out,
        full_state_out,
        full_gate_weight,
        full_init,
        full_hidden_in,
        full_hidden_out,
    ) = weights
    token_gain_f = columns[8].astype(jnp.float32)
    state_gain_f = columns[9].astype(jnp.float32)
    hidden_gain_f = columns[10].astype(jnp.float32)
    gate_bias_f = columns[11].astype(jnp.float32)
    seg_len, width = tokens.shape
    window = WINDOW
    blocks = seg_len // window
    segment_id = lax.axis_index(("dp", "fsdp"))
    counts = (document_lengths + seg_len - 1) // seg_len
    ends = jnp.cumsum(counts)
    starts = ends - counts
    inside = (segment_id >= starts) & (segment_id < ends)
    valid_len = jnp.sum(
        jnp.where(
            inside, jnp.minimum(seg_len, document_lengths - (segment_id - starts) * seg_len), 0
        )
    )
    first = jnp.any(segment_id == starts)
    piece = tokens.astype(jnp.float32)
    normed_low = narrow(layer_norm(piece, token_gain_f))
    projected = narrow(matmul(normed_low, full_token_proj))
    self_query = projected[:, :width]
    cross_query = projected[:, width : 2 * width]
    token_keys = projected[:, 2 * width : 3 * width]
    token_values = projected[:, 3 * width :]
    padding = jnp.zeros((window, width), jnp.bfloat16)
    padded_keys = jnp.concatenate([padding, token_keys], axis=0)
    padded_values = jnp.concatenate([padding, token_values], axis=0)
    state = jnp.where(first, full_init.astype(jnp.float32), incoming[0].astype(jnp.float32))
    state_inputs, normed_states, sides, inner_cats, mixed_states, gates, lives, key_masks = (
        [],
        [],
        [],
        [],
        [],
        [],
        [],
        [],
    )
    self_logs, cross_logs, inner_self_logs, inner_cross_logs, attended_parts = ([], [], [], [], [])
    for block_idx in range(blocks):
        start = block_idx * window
        state_normed = narrow(layer_norm(state, state_gain_f))
        state_side = narrow(matmul(state_normed, full_state_proj))
        state_keys = state_side[:, 2 * width : 3 * width]
        state_values = state_side[:, 3 * width :]
        self_part, self_log = attend(
            self_query[start : start + window],
            padded_keys[start : start + 2 * window],
            padded_values[start : start + 2 * window],
            window_allowed(start, window),
        )
        cross_part, cross_log = attend(
            cross_query[start : start + window], state_keys, state_values, None
        )
        attended_parts.append(jnp.concatenate([self_part, cross_part], axis=1))
        live_keys = start + jnp.arange(window) < valid_len
        key_allowed = jnp.broadcast_to(live_keys[None, :], (state.shape[0], window))
        inner_self, inner_self_log = attend(state_side[:, :width], state_keys, state_values, None)
        inner_cross, inner_cross_log = attend(
            state_side[:, width : 2 * width],
            token_keys[start : start + window],
            token_values[start : start + window],
            key_allowed,
        )
        inner_cat = jnp.concatenate([inner_self, inner_cross], axis=1)
        mixed_state = narrow(matmul(inner_cat, full_state_out))
        gate = jax.nn.sigmoid(matmul(mixed_state, full_gate_weight) + gate_bias_f)
        updated = gate * state + (1.0 - gate) * jnp.tanh(mixed_state.astype(jnp.float32))
        live = jnp.where(start < valid_len, 1.0, 0.0).astype(jnp.float32)
        state_inputs.append(state)
        normed_states.append(state_normed)
        sides.append(state_side)
        inner_cats.append(inner_cat)
        mixed_states.append(mixed_state)
        gates.append(gate)
        lives.append(live)
        key_masks.append(key_allowed)
        self_logs.append(self_log)
        cross_logs.append(cross_log)
        inner_self_logs.append(inner_self_log)
        inner_cross_logs.append(inner_cross_log)
        state = state + live * (updated - state)
    attended = jnp.concatenate(attended_parts, axis=0)
    middle = piece + matmul(attended, full_token_out)
    hidden_normed = narrow(layer_norm(middle, hidden_gain_f))
    hidden_pre = matmul(hidden_normed, full_hidden_in)
    activated = narrow(jax.nn.gelu(hidden_pre, approximate=True))
    result = middle + matmul(activated, full_hidden_out)
    columns_back = (
        lax.all_gather(token_proj, "fsdp", axis=1, tiled=True),
        lax.all_gather(state_proj, "fsdp", axis=1, tiled=True),
        lax.all_gather(token_out, "fsdp", axis=1, tiled=True),
        lax.all_gather(state_out, "fsdp", axis=1, tiled=True),
        lax.all_gather(gate_weight, "fsdp", axis=1, tiled=True),
        lax.all_gather(init_state, "fsdp", axis=1, tiled=True),
        lax.all_gather(hidden_in, "fsdp", axis=1, tiled=True),
        lax.all_gather(hidden_out, "fsdp", axis=1, tiled=True),
    )
    weights_back = (
        lax.all_gather(columns_back[0], "dp", axis=0, tiled=True),
        lax.all_gather(columns_back[1], "dp", axis=0, tiled=True),
        lax.all_gather(columns_back[2], "dp", axis=0, tiled=True),
        lax.all_gather(columns_back[3], "dp", axis=0, tiled=True),
        lax.all_gather(columns_back[4], "dp", axis=0, tiled=True),
        lax.all_gather(columns_back[5], "dp", axis=0, tiled=True),
        lax.all_gather(columns_back[6], "dp", axis=0, tiled=True),
        lax.all_gather(columns_back[7], "dp", axis=0, tiled=True),
    )
    (
        back_token_proj,
        back_state_proj,
        back_token_out,
        back_state_out,
        back_gate_weight,
        back_init,
        back_hidden_in,
        back_hidden_out,
    ) = weights_back
    grad_result = output_grad.astype(jnp.float32)
    grad_hidden_out = matmul_left_t(activated, output_grad)
    grad_activated = matmul_right_t(output_grad, back_hidden_out)
    _, gelu_pull = jax.vjp(partial(jax.nn.gelu, approximate=True), hidden_pre)
    grad_pre = narrow(gelu_pull(grad_activated)[0])
    grad_hidden_in = matmul_left_t(hidden_normed, grad_pre)
    grad_middle_part, grad_hidden_gain = norm_back(
        middle, hidden_gain_f, matmul_right_t(grad_pre, back_hidden_in)
    )
    grad_middle = grad_result + grad_middle_part
    grad_branch = narrow(grad_middle)
    grad_token_out = matmul_left_t(attended, grad_branch)
    grad_attended = narrow(matmul_right_t(grad_branch, back_token_out))
    grad_padded_keys = jnp.zeros((seg_len + window, width), jnp.float32)
    grad_padded_values = jnp.zeros((seg_len + window, width), jnp.float32)
    grad_self_parts, grad_cross_parts, side_key_grads, side_value_grads = ([], [], [], [])
    for block_idx in range(blocks):
        start = block_idx * window
        state_side = sides[block_idx]
        self_grad_query, self_grad_keys, self_grad_values = attend_back(
            self_query[start : start + window],
            padded_keys[start : start + 2 * window],
            padded_values[start : start + 2 * window],
            window_allowed(start, window),
            self_logs[block_idx],
            grad_attended[start : start + window, :width],
        )
        grad_padded_keys = grad_padded_keys.at[start : start + 2 * window].add(self_grad_keys)
        grad_padded_values = grad_padded_values.at[start : start + 2 * window].add(self_grad_values)
        cross_grad_query, cross_grad_keys, cross_grad_values = attend_back(
            cross_query[start : start + window],
            state_side[:, 2 * width : 3 * width],
            state_side[:, 3 * width :],
            None,
            cross_logs[block_idx],
            grad_attended[start : start + window, width:],
        )
        grad_self_parts.append(self_grad_query)
        grad_cross_parts.append(cross_grad_query)
        side_key_grads.append(cross_grad_keys)
        side_value_grads.append(cross_grad_values)
    grad_token_keys = grad_padded_keys[window:]
    grad_token_values = grad_padded_values[window:]
    grad_state = jnp.zeros_like(state)
    grad_state_proj = jnp.zeros((width, 4 * width), jnp.float32)
    grad_state_out = jnp.zeros((2 * width, width), jnp.float32)
    grad_gate_weight = jnp.zeros((width, width), jnp.float32)
    grad_gate_bias = jnp.zeros((width,), jnp.float32)
    grad_state_gain = jnp.zeros((width,), jnp.float32)
    for block_idx in reversed(range(blocks)):
        start = block_idx * window
        state_side = sides[block_idx]
        gate = gates[block_idx]
        live = lives[block_idx]
        state_in = state_inputs[block_idx]
        tanh_mixed = jnp.tanh(mixed_states[block_idx].astype(jnp.float32))
        grad_updated = live * grad_state
        grad_direct = (1.0 - live) * grad_state + grad_updated * gate
        grad_gate_pre = gate * (1.0 - gate) * grad_updated * (state_in - tanh_mixed)
        grad_gate_bias = grad_gate_bias + jnp.sum(grad_gate_pre, axis=0)
        grad_gate_low = narrow(grad_gate_pre)
        grad_gate_weight = grad_gate_weight + matmul_left_t(mixed_states[block_idx], grad_gate_low)
        grad_mixed = narrow(
            matmul_right_t(grad_gate_low, back_gate_weight)
            + grad_updated * (1.0 - gate) * (1.0 - tanh_mixed * tanh_mixed)
        )
        grad_state_out = grad_state_out + matmul_left_t(inner_cats[block_idx], grad_mixed)
        grad_inner = narrow(matmul_right_t(grad_mixed, back_state_out))
        self_query_grad, self_key_grad, self_value_grad = attend_back(
            state_side[:, :width],
            state_side[:, 2 * width : 3 * width],
            state_side[:, 3 * width :],
            None,
            inner_self_logs[block_idx],
            grad_inner[:, :width],
        )
        cross_query_grad, token_key_grad, token_value_grad = attend_back(
            state_side[:, width : 2 * width],
            token_keys[start : start + window],
            token_values[start : start + window],
            key_masks[block_idx],
            inner_cross_logs[block_idx],
            grad_inner[:, width:],
        )
        grad_token_keys = grad_token_keys.at[start : start + window].add(token_key_grad)
        grad_token_values = grad_token_values.at[start : start + window].add(token_value_grad)
        grad_side = narrow(
            jnp.concatenate(
                [
                    self_query_grad,
                    cross_query_grad,
                    self_key_grad + side_key_grads[block_idx],
                    self_value_grad + side_value_grads[block_idx],
                ],
                axis=1,
            )
        )
        grad_state_proj = grad_state_proj + matmul_left_t(normed_states[block_idx], grad_side)
        grad_state_norm, grad_gain_part = norm_back(
            state_in, state_gain_f, matmul_right_t(grad_side, back_state_proj)
        )
        grad_state_gain = grad_state_gain + grad_gain_part
        grad_state = grad_direct + grad_state_norm
    grad_init = jnp.where(first, grad_state, 0.0)
    grad_projected = narrow(
        jnp.concatenate(
            [
                jnp.concatenate(grad_self_parts, axis=0),
                jnp.concatenate(grad_cross_parts, axis=0),
                grad_token_keys,
                grad_token_values,
            ],
            axis=1,
        )
    )
    grad_token_proj = matmul_left_t(normed_low, grad_projected)
    grad_piece, grad_token_gain = norm_back(
        piece, token_gain_f, matmul_right_t(grad_projected, back_token_proj)
    )
    tokens_grad = narrow(grad_middle + grad_piece)
    row_parts = (
        lax.psum_scatter(
            grad_token_proj.astype(jnp.bfloat16), "dp", scatter_dimension=0, tiled=True
        ).astype(jnp.float32),
        lax.psum_scatter(
            grad_state_proj.astype(jnp.bfloat16), "dp", scatter_dimension=0, tiled=True
        ).astype(jnp.float32),
        lax.psum_scatter(
            grad_token_out.astype(jnp.bfloat16), "dp", scatter_dimension=0, tiled=True
        ).astype(jnp.float32),
        lax.psum_scatter(
            grad_state_out.astype(jnp.bfloat16), "dp", scatter_dimension=0, tiled=True
        ).astype(jnp.float32),
        lax.psum_scatter(
            grad_gate_weight.astype(jnp.bfloat16), "dp", scatter_dimension=0, tiled=True
        ).astype(jnp.float32),
        lax.psum_scatter(
            grad_init.astype(jnp.bfloat16), "dp", scatter_dimension=0, tiled=True
        ).astype(jnp.float32),
        lax.psum_scatter(
            grad_hidden_in.astype(jnp.bfloat16), "dp", scatter_dimension=0, tiled=True
        ).astype(jnp.float32),
        lax.psum_scatter(
            grad_hidden_out.astype(jnp.bfloat16), "dp", scatter_dimension=0, tiled=True
        ).astype(jnp.float32),
    )
    summed = (
        lax.psum_scatter(
            row_parts[0].astype(jnp.bfloat16), "fsdp", scatter_dimension=1, tiled=True
        ).astype(jnp.float32),
        lax.psum_scatter(
            row_parts[1].astype(jnp.bfloat16), "fsdp", scatter_dimension=1, tiled=True
        ).astype(jnp.float32),
        lax.psum_scatter(
            row_parts[2].astype(jnp.bfloat16), "fsdp", scatter_dimension=1, tiled=True
        ).astype(jnp.float32),
        lax.psum_scatter(
            row_parts[3].astype(jnp.bfloat16), "fsdp", scatter_dimension=1, tiled=True
        ).astype(jnp.float32),
        lax.psum_scatter(
            row_parts[4].astype(jnp.bfloat16), "fsdp", scatter_dimension=1, tiled=True
        ).astype(jnp.float32),
        lax.psum_scatter(
            row_parts[5].astype(jnp.bfloat16), "fsdp", scatter_dimension=1, tiled=True
        ).astype(jnp.float32),
        lax.psum_scatter(
            row_parts[6].astype(jnp.bfloat16), "fsdp", scatter_dimension=1, tiled=True
        ).astype(jnp.float32),
        lax.psum_scatter(
            row_parts[7].astype(jnp.bfloat16), "fsdp", scatter_dimension=1, tiled=True
        ).astype(jnp.float32),
        lax.psum_scatter(
            grad_token_gain.astype(jnp.bfloat16), "fsdp", scatter_dimension=0, tiled=True
        ).astype(jnp.float32),
        lax.psum_scatter(
            grad_state_gain.astype(jnp.bfloat16), "fsdp", scatter_dimension=0, tiled=True
        ).astype(jnp.float32),
        lax.psum_scatter(
            grad_hidden_gain.astype(jnp.bfloat16), "fsdp", scatter_dimension=0, tiled=True
        ).astype(jnp.float32),
        lax.psum_scatter(
            grad_gate_bias.astype(jnp.bfloat16), "fsdp", scatter_dimension=0, tiled=True
        ).astype(jnp.float32),
    )
    matrix_grads = summed[:8]
    vector_parts = summed[8:]
    vector_grads = lax.psum(
        (vector_parts[0], vector_parts[1], vector_parts[2], vector_parts[3]), "dp"
    )
    return (
        narrow(result),
        narrow(state)[None],
        tokens_grad,
        matrix_grads[0],
        matrix_grads[1],
        matrix_grads[2],
        matrix_grads[3],
        matrix_grads[4],
        matrix_grads[5],
        matrix_grads[6],
        matrix_grads[7],
        vector_grads[0],
        vector_grads[1],
        vector_grads[2],
        vector_grads[3],
    )


def solution(mesh):
    return jax.shard_map(
        shards,
        mesh=mesh,
        in_specs=(
            P(("dp", "fsdp"), None),
            P(("dp", "fsdp"), None, None),
            P(),
            P(("dp", "fsdp"), None),
            P("dp", "fsdp"),
            P("dp", "fsdp"),
            P("dp", "fsdp"),
            P("dp", "fsdp"),
            P("dp", "fsdp"),
            P("dp", "fsdp"),
            P("dp", "fsdp"),
            P("dp", "fsdp"),
            P("fsdp"),
            P("fsdp"),
            P("fsdp"),
            P("fsdp"),
        ),
        out_specs=(
            P(("dp", "fsdp"), None),
            P(("dp", "fsdp"), None, None),
            P(("dp", "fsdp"), None),
            P("dp", "fsdp"),
            P("dp", "fsdp"),
            P("dp", "fsdp"),
            P("dp", "fsdp"),
            P("dp", "fsdp"),
            P("dp", "fsdp"),
            P("dp", "fsdp"),
            P("dp", "fsdp"),
            P("fsdp"),
            P("fsdp"),
            P("fsdp"),
            P("fsdp"),
        ),
        check_vma=False,
    )
```

profile of v0, /device:TPU:0, one launch (start us, length us, event | category | flops | bytes accessed | tf_op | source)
XLA Modules:
  0.0 1575.3 jit_solution(9728071402252284468)
XLA Ops:
  23.0 9.1 all_gather.80
  50.9 11.1 all_gather.92
  111.5 17.5 %all-gather.13.cloned.1.call-done = bf16[1024,4096]{1,0:T(8,128)(2,1)} async-done(((bf16[64,4096]{1,0:T(8,128)(2,1)}), bf16[1024,4096]{1,0:T(8,128)(2,1)}) %all-gather.13.cloned.1.call-update) | async-done | bytes 8388624 | tf_op jit(solution)/shard_map/all_gather | solution.py:139
  129.0 11.8 convolution_convert_fusion.3
  152.3 52.0 %all-gather.17.cloned.1.call-done = bf16[1024,4096]{1,0:T(8,128)(2,1)} async-done(((bf16[64,4096]{1,0:T(8,128)(2,1)}), bf16[1024,4096]{1,0:T(8,128)(2,1)}) %all-gather.17.cloned.1.call-update) | async-done | bytes 8388624 | tf_op jit(solution)/shard_map/all_gather | solution.py:140
  204.3 9.1 convolution_convert_fusion.5
  264.2 32.9 %all-gather.21.cloned.1.call-done = bf16[1024,1024]{1,0:T(8,128)(2,1)} async-done(((bf16[64,1024]{1,0:T(8,128)(2,1)}), bf16[1024,1024]{1,0:T(8,128)(2,1)}) %all-gather.21.cloned.1.call-update) | async-done | bytes 2097168 | tf_op jit(solution)/shard_map/all_gather | solution.py:143
  400.6 9.5 fusion.277
  410.1 9.3 fusion.458
  428.5 14.7 fusion.304
  454.2 14.6 fusion.459
  468.8 30.9 %all-gather.25.cloned.1.call-done = bf16[1024,4096]{1,0:T(8,128)(2,1)} async-done(((bf16[64,4096]{1,0:T(8,128)(2,1)}), bf16[1024,4096]{1,0:T(8,128)(2,1)}) %all-gather.25.cloned.1.call-update) | async-done | bytes 8388624 | tf_op jit(solution)/shard_map/all_gather | solution.py:145
  499.7 29.9 %fusion.14 = (bf16[1024,4096]{1,0:T(8,128)(2,1)}, f32[1024,4096]{1,0:T(8,128)}) fusion(f32[1024,4096]{1,0:T(8,128)} %fusion.459, bf16[1024,4096]{1,0:T(8,128)(2,1)} %all-gather.25.cloned.1.call-done, f32[1024,1024]{0,1:T(8,128)} %copy-done.16, f32[1024]{0:T(1024)S(1)} %bitcast.366, f32[1024]{0:T(1024)S(1)} %fusion.357, f32[1024]{0:T(1024)S(1)} %broadcast_multiply_fusion), kind=kOutput, calls=%fused_computation.16 | convolution fusion | flops 8678014976 | bytes 54538240 | tf_op jit(solution)/shard_map/dot_general | solution.py:33
  529.6 16.3 %multiply_reduce_fusion.12 = (bf16[1024]{0:T(1024)(128)(2,1)}, f32[1024]{0:T(1024)S(1)}, f32[1024,1024]{0,1:T(8,128)S(1)}) fusion(f32[1024,1024]{0,1:T(8,128)} %copy-done.16, f32[1024]{0:T(1024)S(1)} %fusion.357, f32[1024]{0:T(1024)S(1)} %broadcast_multiply_fusion, f32[1024]{0:T(1024)S(1)} %bitcast.367, bf16[1024,4096]{1,0:T(8,128)(2,1)} %get-tuple-element.216, ...), kind=kOutput, calls=%fused_computation.157 | convolution fusion | flops 8597272576 | bytes 25184256 | tf_op jit(solution)/shard_map/dot_general | solution.py:43
  568.9 14.5 fusion.82
  583.3 15.3 add_convert_fusion.8
  598.6 14.4 fusion.298
  663.2 16.7 %fusion.73 = f32[8,128,512]{2,1,0:T(8,128)} fusion(bf16[512,8,128]{0,2,1:T(8,128)(2,1)} %bitcast.330, f32[8,512,512]{1,2,0:T(8,128)} %fusion.329, f32[8,512,512]{1,2,0:T(8,128)} %get-tuple-element.207, f32[8,512]{1,0:T(8,128)S(1)} %copy-done.91), kind=kOutput, calls=%fused_computation.123 | convolution fusion | flops 555749888 | bytes 19939328 | tf_op jit(solution)/shard_map/hrk,rhd->khd/dot_general | solution.py:88
  679.9 14.5 fusion.301
  694.4 17.5 %add_convert_fusion.6 = bf16[8,128,512]{2,1,0:T(8,128)(2,1)} fusion(f32[8,128,512]{2,1,0:T(8,128)} %fusion.73, bf16[512,8,128]{0,2,1:T(8,128)(2,1)} %bitcast.327, f32[8,512,512]{1,2,0:T(8,128)} %fusion.331, f32[8,512,512]{1,2,0:T(8,128)} %copy-done.2, f32[8,512]{1,0:T(8,128)S(1)} %copy-done.95), kind=kOutput, calls=%fused_computation.276 | convolution fusion | flops 556798464 | bytes 20987904 | tf_op jit(solution)/shard_map/hrk,rhd->khd/dot_general | solution.py:88
  711.9 14.6 fusion.295
  726.5 11.7 multiply_reduce_fusion.15
  748.8 9.6 convolution_convert_fusion.6
  767.7 15.4 convolution_convert_fusion.1
  783.6 18.0 %convolution_convert_fusion = bf16[4096,1024]{1,0:T(8,128)(2,1)} fusion(bf16[1024,1024]{1,0:T(8,128)(2,1)} %param.35, f32[1024,4096]{1,0:T(8,128)} %get-tuple-element.217), kind=kOutput, calls=%fused_computation.93 | convolution fusion | flops 8631877632 | bytes 27262976 | tf_op jit(solution)/shard_map/dot_general | solution.py:37
  806.5 13.2 fusion.338
  819.7 13.7 add_convert_fusion
  858.8 15.0 fusion.116
  873.8 17.6 %fusion.123 = f32[8,128,512]{2,1,0:T(8,128)} fusion(bf16[512,8,128]{0,2,1:T(8,128)(2,1)S(1)} %bitcast.338, f32[8,512,512]{1,2,0:T(8,128)} %fusion.325, f32[8,512,512]{1,2,0:T(8,128)} %copy-done.8, f32[8,512]{1,0:T(8,128)S(1)} %copy-done.130, pred[512]{0:T(512)(128)(4,1)S(1)} %copy-done.138), kind=kOutput, calls=%fused_computation.141 | convolution fusion | flops 559944192 | bytes 19939840 | tf_op jit(solution)/shard_map/hrk,rhd->khd/dot_general | solution.py:88
  891.4 9.7 fusion.251
  901.1 31.7 %fusion.38 = f32[8,128,1024]{2,1,0:T(8,128)} fusion(bf16[512,8,128]{0,2,1:T(8,128)(2,1)} %bitcast.323, f32[8,512,1024]{2,1,0:T(8,128)} %fusion.251, f32[8,512,1024]{2,1,0:T(8,128)} %get-tuple-element.205, f32[8,512]{1,0:T(8,128)S(1)} %log_add_fusion.6), kind=kOutput, calls=%fused_computation.67 | convolution fusion | flops 1103107072 | bytes 38813696 | tf_op jit(solution)/shard_map/hrk,rhd->khd/dot_general | solution.py:88
  941.0 32.5 %fusion.46 = f32[8,128,1024]{2,1,0:T(8,128)} fusion(bf16[512,8,128]{0,2,1:T(8,128)(2,1)} %bitcast.321, f32[8,512,1024]{2,1,0:T(8,128)} %fusion.254, f32[8,512,1024]{2,1,0:T(8,128)} %copy-done, f32[8,512]{1,0:T(8,128)S(1)} %log_add_fusion.7), kind=kOutput, calls=%fused_computation.71 | convolution fusion | flops 1103107072 | bytes 38813696 | tf_op jit(solution)/shard_map/hrk,rhd->khd/dot_general | solution.py:88
  980.2 14.1 fusion.307
  994.3 14.2 fusion.310
  1008.5 37.3 %fusion.286 = bf16[8,128,512]{2,1,0:T(8,128)(2,1)} fusion(bf16[1024,8,128]{0,2,1:T(8,128)(2,1)S(1)} %bitcast.317, f32[8,512,1024]{2,1,0:T(8,128)} %fusion.251, f32[8,512,1024]{2,1,0:T(8,128)} %get-tuple-element.205, f32[8,512]{1,0:T(8,128)S(1)} %log_add_fusion.6), kind=kOutput, calls=%fused_computation.304 | convolution fusion | flops 1103631360 | bytes 36716544 | tf_op jit(solution)/shard_map/hrk,khd->rhd/dot_general | solution.py:85
  1045.8 31.7 %fusion.283 = bf16[8,128,512]{2,1,0:T(8,128)(2,1)} fusion(bf16[1024,8,128]{0,2,1:T(8,128)(2,1)} %bitcast.318, f32[8,512,1024]{2,1,0:T(8,128)} %fusion.254, f32[8,512,1024]{2,1,0:T(8,128)} %copy-done, f32[8,512]{1,0:T(8,128)S(1)} %log_add_fusion.7), kind=kOutput, calls=%fused_computation.303 | convolution fusion | flops 1103631360 | bytes 36716544 | tf_op jit(solution)/shard_map/hrk,khd->rhd/dot_general | solution.py:85
  1077.6 18.9 %convolution_convert_fusion.2 = bf16[1024,4096]{1,0:T(8,128)(2,1)} fusion(bf16[1024,1024]{0,1:T(8,128)(2,1)S(1)} %copy-done.6, f32[1024]{0:T(1024)S(1)} %bitcast.362, f32[1024]{0:T(1024)S(1)} %copy-done.111, f32[1024]{0:T(1024)S(1)} %copy-done.105, bf16[1024,1024]{0,1:T(8,128)(2,1)} %convert.78, bf16[1024,1024]{0,1:T(8,128)(2,1)} %convert.77, ...), kind=kOutput, calls=%fused_computation.95 | convolution fusion | flops 8649703424 | bytes 18886656 | tf_op jit(solution)/shard_map/dot_general | solution.py:37
  1099.0 22.9 %reduce-scatter.41.cloned.1.call-done = bf16[64,4096]{1,0:T(8,128)(2,1)} async-done(((bf16[1024,4096]{1,0:T(8,128)(2,1)}), bf16[64,4096]{1,0:T(8,128)(2,1)}) %reduce-scatter.41.cloned.1.call-update) | async-done | bytes 524304 | tf_op jit(solution)/shard_map/reduce_scatter | solution.py:416
  1123.2 107.0 %reduce-scatter.45.cloned.1.call-done = bf16[256,1024]{1,0:T(8,128)(2,1)} async-done(((bf16[4096,1024]{1,0:T(8,128)(2,1)}), bf16[256,1024]{1,0:T(8,128)(2,1)}) %reduce-scatter.45.cloned.1.call-update) | async-done | bytes 524304 | tf_op jit(solution)/shard_map/reduce_scatter | solution.py:419
  1230.3 15.7 fusion.140
  1246.0 92.6 %reduce-scatter.21.cloned.1.call-done = bf16[64,4096]{1,0:T(8,128)(2,1)} async-done(((bf16[1024,4096]{1,0:T(8,128)(2,1)}), bf16[64,4096]{1,0:T(8,128)(2,1)}) %reduce-scatter.21.cloned.1.call-update) | async-done | bytes 524304 | tf_op jit(solution)/shard_map/reduce_scatter | solution.py:401
  1338.7 16.6 %add_convert_fusion.4 = bf16[1024,1024]{0,1:T(8,128)(2,1)} fusion(f32[1024,1024]{0,1:T(8,128)} %copy-done.16, bf16[4096,1024]{1,0:T(8,128)(2,1)} %all-gather.27.cloned.1.call-done, f32[1024,4096]{1,0:T(8,128)} %get-tuple-element.217), kind=kOutput, calls=%fused_computation.180 | convolution fusion | flops 8629780480 | bytes 31457280 | tf_op jit(solution)/shard_map/dot_general | solution.py:33
  1359.2 87.8 %reduce-scatter.17.cloned.1.call-done = bf16[64,4096]{1,0:T(8,128)(2,1)} async-done(((bf16[1024,4096]{1,0:T(8,128)(2,1)}), bf16[64,4096]{1,0:T(8,128)(2,1)}) %reduce-scatter.17.cloned.1.call-update) | async-done | bytes 524304 | tf_op jit(solution)/shard_map/reduce_scatter | solution.py:398
  1466.5 32.2 %all-reduce.8 = (f32[512]{0:T(512)}, f32[512]{0:T(512)}, f32[512]{0:T(512)}, f32[512]{0:T(512)}) all-reduce(f32[512]{0:T(512)S(1)} %dynamic-slice_convert_fusion.3, f32[512]{0:T(512)S(1)} %dynamic-slice_convert_fusion.2, f32[512]{0:T(512)S(1)} %dynamic-slice_convert_fusion.1, ...), channel_id=1, replica_groups=mesh['dp'=16,'fsdp'=2] {'dp'}, use_global_device_ids=true, to_apply=%region_61.62 | all-reduce | flops 2048 | bytes 16384 | tf_op jit(solution)/shard_map/psum | solution.py:463
  1504.8 10.9 reduce-scatter.43.cloned.1.call-done
  1517.5 15.2 reduce-scatter.47.cloned.1.call-done
  1534.4 15.0 reduce-scatter.23.cloned.1.call-done
  1551.3 15.0 reduce-scatter.19.cloned.1.call-done
  (587 shorter events, 445.0 us)
Async XLA Ops:
  7.2 99.1 %all-gather.15.cloned.1.call-start = ((), (), s32[]{:S(2)}) async-start(), calls=%async_computation.17 | async-start | bytes 1114112 | tf_op jit(solution)/shard_map/all_gather | solution.py:144
  14.5 114.5 %all-gather.13.cloned.1.call-start = ((), (), s32[]{:S(2)}) async-start(), calls=%async_computation.16 | async-start | bytes 8912896 | tf_op jit(solution)/shard_map/all_gather | solution.py:139
  23.0 181.3 %all-gather.17.cloned.1.call-start = ((), (), s32[]{:S(2)}) async-start(), calls=%async_computation.18 | async-start | bytes 8912896 | tf_op jit(solution)/shard_map/all_gather | solution.py:140
  32.2 226.2 %all-gather.19.cloned.1.call-start = ((), (), s32[]{:S(2)}) async-start(), calls=%async_computation.19 | async-start | bytes 4456448 | tf_op jit(solution)/shard_map/all_gather | solution.py:142
  38.2 258.9 %all-gather.21.cloned.1.call-start = ((), (), s32[]{:S(2)}) async-start(), calls=%async_computation.20 | async-start | bytes 2228224 | tf_op jit(solution)/shard_map/all_gather | solution.py:143
  44.9 365.2 %all-gather.23.cloned.1.call-start = ((), (), s32[]{:S(2)}) async-start(), calls=%async_computation.21 | async-start | bytes 4456448 | tf_op jit(solution)/shard_map/all_gather | solution.py:141
  50.9 55.4 %copy-start.18 = (bf16[1,512,1024]{2,1,0:T(8,128)(2,1)S(1)}, bf16[1,512,1024]{2,1,0:T(8,128)(2,1)}, u32[]{:S(2)}) copy-start(bf16[1,512,1024]{2,1,0:T(8,128)(2,1)} %param.33) | copy-start | bytes 3145732
  50.9 403.3 %all-gather.27.cloned.1.call-start = ((), (), s32[]{:S(2)}) async-start(), calls=%async_computation.23 | async-start | bytes 8912896 | tf_op jit(solution)/shard_map/all_gather | solution.py:146
  62.1 437.6 %all-gather.25.cloned.1.call-start = ((), (), s32[]{:S(2)}) async-start(), calls=%async_computation.22 | async-start | bytes 8912896 | tf_op jit(solution)/shard_map/all_gather | solution.py:145
  69.5 1027.0 %reduce-scatter.37.cloned.1.call-start = ((), (), s32[]{:S(2)}) async-start(), calls=%async_computation.34 | async-start | bytes 1114112 | tf_op jit(solution)/shard_map/reduce_scatter | solution.py:413
  75.1 176.0 %copy-start.137 = (pred[512]{0:T(512)(128)(4,1)}, pred[512]{0:T(512)(128)(4,1)S(1)}, u32[]{:S(2)}) copy-start(pred[512]{0:T(512)(128)(4,1)S(1)} %get-tuple-element.222) | copy-start | bytes 1540
  75.1 265.8 %copy-start.139 = (pred[512]{0:T(512)(128)(4,1)}, pred[512]{0:T(512)(128)(4,1)S(1)}, u32[]{:S(2)}) copy-start(pred[512]{0:T(512)(128)(4,1)S(1)} %get-tuple-element.223) | copy-start | bytes 1540
  80.2 48.8 %copy-start.108 = (f32[2,1,512]{2,1,0:T(1,128)}, f32[2,1,512]{2,1,0:T(1,128)S(1)}, u32[]{:S(2)}) copy-start(f32[2,1,512]{2,1,0:T(1,128)S(1)} %convert_element_type.442) | copy-start | bytes 12292
  85.2 218.7 %copy-start.89 = (f32[2,1,512]{2,1,0:T(1,128)}, f32[2,1,512]{2,1,0:T(1,128)S(1)}, u32[]{:S(2)}) copy-start(f32[2,1,512]{2,1,0:T(1,128)S(1)} %convert_element_type.443) | copy-start | bytes 12292
  99.9 40.9 %copy-start.4 = (bf16[1024,1024]{0,1:T(8,128)(2,1)}, bf16[1024,1024]{0,1:T(8,128)(2,1)S(1)}, u32[]{:S(2)}) copy-start(bf16[1024,1024]{0,1:T(8,128)(2,1)S(1)} %copy.124) | copy-start | bytes 6291460
  100.3 40.5 %copy-start.104 = (f32[1024]{0:T(1024)}, f32[1024]{0:T(1024)S(1)}, u32[]{:S(2)}) copy-start(f32[1024]{0:T(1024)S(1)} %broadcast_multiply_fusion.1) | copy-start | bytes 12292
  100.9 39.9 %copy-start.106 = (f32[1024]{0:T(1024)}, f32[1024]{0:T(1024)S(1)}, u32[]{:S(2)}) copy-start(f32[1024]{0:T(1024)S(1)} %fusion.139) | copy-start | bytes 12292
  100.9 39.9 %copy-start.110 = (f32[1024]{0:T(1024)}, f32[1024]{0:T(1024)S(1)}, u32[]{:S(2)}) copy-start(f32[1024]{0:T(1024)S(1)} %fusion.356) | copy-start | bytes 12292
  108.5 95.8 %copy-start.117 = (f32[512]{0:T(512)}, f32[512]{0:T(512)S(1)}, u32[]{:S(2)}) copy-start(f32[512]{0:T(512)S(1)} %broadcast_multiply_fusion.3) | copy-start | bytes 6148
  111.5 92.8 %copy-start.133 = (f32[512]{0:T(512)}, f32[512]{0:T(512)S(1)}, u32[]{:S(2)}) copy-start(f32[512]{0:T(512)S(1)} %fusion.374) | copy-start | bytes 6148
  215.3 39.6 %copy-start.29 = (bf16[64,8,8,128]{3,2,1,0:T(8,128)(2,1)}, bf16[64,8,8,128]{3,2,1,0:T(8,128)(2,1)S(1)}, u32[]{:S(2)}) copy-start(bf16[64,8,8,128]{3,2,1,0:T(8,128)(2,1)S(1)} %get-tuple-element.189) | copy-start | bytes 3145732
  303.6 63.4 %copy-start.10 = (f32[512,1024]{1,0:T(8,128)}, f32[512,1024]{1,0:T(8,128)S(1)}, u32[]{:S(2)}) copy-start(f32[512,1024]{1,0:T(8,128)S(1)} %get-tuple-element.168) | copy-start | bytes 6291460
  320.9 107.5 %copy-start.24 = (bf16[512,1024]{0,1:T(8,128)(2,1)}, bf16[512,1024]{0,1:T(8,128)(2,1)S(1)}, u32[]{:S(2)}) copy-start(bf16[512,1024]{0,1:T(8,128)(2,1)S(1)} %copy.252) | copy-start | bytes 3145732
  347.9 45.0 %copy-start.85 = (f32[8,512]{1,0:T(8,128)}, f32[8,512]{1,0:T(8,128)S(1)}, u32[]{:S(2)}) copy-start(f32[8,512]{1,0:T(8,128)S(1)} %get-tuple-element.208) | copy-start | bytes 49156
  354.8 38.1 %copy-start.100 = (f32[8,512]{1,0:T(8,128)}, f32[8,512]{1,0:T(8,128)S(1)}, u32[]{:S(2)}) copy-start(f32[8,512]{1,0:T(8,128)S(1)} %fusion.21) | copy-start | bytes 49156
  363.0 37.6 %copy-start.87 = (f32[8,512]{1,0:T(8,128)}, f32[8,512]{1,0:T(8,128)S(1)}, u32[]{:S(2)}) copy-start(f32[8,512]{1,0:T(8,128)S(1)} %get-tuple-element.204) | copy-start | bytes 49156
  423.8 145.0 %copy-start.93 = (f32[8,512]{1,0:T(8,128)}, f32[8,512]{1,0:T(8,128)S(1)}, u32[]{:S(2)}) copy-start(f32[8,512]{1,0:T(8,128)S(1)} %log_add_fusion.4) | copy-start | bytes 49156
  423.9 174.7 %copy-start.131 = (f32[8,512]{1,0:T(8,128)}, f32[8,512]{1,0:T(8,128)S(1)}, u32[]{:S(2)}) copy-start(f32[8,512]{1,0:T(8,128)S(1)} %log_add_fusion.3) | copy-start | bytes 49156
  454.2 45.5 %copy-start.129 = (f32[2,1,512]{2,1,0:T(1,128)S(1)}, f32[2,1,512]{2,1,0:T(1,128)}, u32[]{:S(2)}) copy-start(f32[2,1,512]{2,1,0:T(1,128)} %convert_element_type.445) | copy-start | bytes 12292
  568.8 44.3 %copy-start.80 = (bf16[8,128,512]{2,1,0:T(8,128)(2,1)}, bf16[8,128,512]{2,1,0:T(8,128)(2,1)S(1)}, u32[]{:S(2)}) copy-start(bf16[8,128,512]{2,1,0:T(8,128)(2,1)S(1)} %add_convert_fusion.7) | copy-start | bytes 3145732
  742.1 355.0 %reduce-scatter.33.cloned.1.call-start = ((), (), s32[]{:S(2)}) async-start(), calls=%async_computation.32 | async-start | bytes 2228224 | tf_op jit(solution)/shard_map/reduce_scatter | solution.py:410
  748.7 349.0 %reduce-scatter.25.cloned.1.call-start = ((), (), s32[]{:S(2)}) async-start(), calls=%async_computation.28 | async-start | bytes 4456448 | tf_op jit(solution)/shard_map/reduce_scatter | solution.py:404
  758.4 340.0 %reduce-scatter.29.cloned.1.call-start = ((), (), s32[]{:S(2)}) async-start(), calls=%async_computation.30 | async-start | bytes 4456448 | tf_op jit(solution)/shard_map/reduce_scatter | solution.py:407
  767.7 354.2 %reduce-scatter.41.cloned.1.call-start = ((), (), s32[]{:S(2)}) async-start(), calls=%async_computation.36 | async-start | bytes 8912896 | tf_op jit(solution)/shard_map/reduce_scatter | solution.py:416
  783.1 447.1 %reduce-scatter.45.cloned.1.call-start = ((), (), s32[]{:S(2)}) async-start(), calls=%async_computation.38 | async-start | bytes 8912896 | tf_op jit(solution)/shard_map/reduce_scatter | solution.py:419
  801.7 537.0 %reduce-scatter.21.cloned.1.call-start = ((), (), s32[]{:S(2)}) async-start(), calls=%async_computation.26 | async-start | bytes 8912896 | tf_op jit(solution)/shard_map/reduce_scatter | solution.py:401
  833.5 613.6 %reduce-scatter.17.cloned.1.call-start = ((), (), s32[]{:S(2)}) async-start(), calls=%async_computation.24 | async-start | bytes 8912896 | tf_op jit(solution)/shard_map/reduce_scatter | solution.py:398
  1045.8 31.7 %copy-start.111 = (f32[1024]{0:T(1024)S(1)}, f32[1024]{0:T(1024)}, u32[]{:S(2)}) copy-start(f32[1024]{0:T(1024)} %copy-done.110) | copy-start | bytes 12292
  1045.8 31.7 %copy-start.152 = (bf16[8,128,512]{2,1,0:T(8,128)(2,1)S(1)}, bf16[8,128,512]{2,1,0:T(8,128)(2,1)}, u32[]{:S(2)}) copy-start(bf16[8,128,512]{2,1,0:T(8,128)(2,1)} %fusion.307) | copy-start | bytes 3145732
  1096.5 402.2 %reduce-scatter.39.cloned.1.call-start = ((), (), s32[]{:S(2)}) async-start(), calls=%async_computation.35 | async-start | bytes 98304 | tf_op jit(solution)/shard_map/reduce_scatter | solution.py:439
  1097.1 403.0 %reduce-scatter.35.cloned.1.call-start = ((), (), s32[]{:S(2)}) async-start(), calls=%async_computation.33 | async-start | bytes 196608 | tf_op jit(solution)/shard_map/reduce_scatter | solution.py:436
  1097.7 403.9 %reduce-scatter.27.cloned.1.call-start = ((), (), s32[]{:S(2)}) async-start(), calls=%async_computation.29 | async-start | bytes 393216 | tf_op jit(solution)/shard_map/reduce_scatter | solution.py:430
  1098.4 404.8 %reduce-scatter.31.cloned.1.call-start = ((), (), s32[]{:S(2)}) async-start(), calls=%async_computation.31 | async-start | bytes 393216 | tf_op jit(solution)/shard_map/reduce_scatter | solution.py:433
  1099.0 416.7 %reduce-scatter.43.cloned.1.call-start = ((), (), s32[]{:S(2)}) async-start(), calls=%async_computation.37 | async-start | bytes 786432 | tf_op jit(solution)/shard_map/reduce_scatter | solution.py:442
  1121.9 410.7 %reduce-scatter.47.cloned.1.call-start = ((), (), s32[]{:S(2)}) async-start(), calls=%async_computation.39 | async-start | bytes 786432 | tf_op jit(solution)/shard_map/reduce_scatter | solution.py:445
  1230.2 319.3 %reduce-scatter.23.cloned.1.call-start = ((), (), s32[]{:S(2)}) async-start(), calls=%async_computation.27 | async-start | bytes 786432 | tf_op jit(solution)/shard_map/reduce_scatter | solution.py:427
  1338.7 108.4 %copy-start.113 = (f32[1024]{0:T(1024)S(1)}, f32[1024]{0:T(1024)}, u32[]{:S(2)}) copy-start(f32[1024]{0:T(1024)} %copy-done.112) | copy-start | bytes 12292
  1338.7 227.6 %reduce-scatter.19.cloned.1.call-start = ((), (), s32[]{:S(2)}) async-start(), calls=%async_computation.25 | async-start | bytes 786432 | tf_op jit(solution)/shard_map/reduce_scatter | solution.py:424
  (147 other events, 1205.4 us)
Sparse Core Ops, SparseCore 0:
  14.6 38.3 all-gather.14
  55.1 73.8 all-gather.12
  131.1 73.1 all-gather.16
  206.3 48.7 all-gather.18
  257.2 39.8 all-gather.20
  299.1 49.4 all-gather.22
  350.8 73.3 all-gather.26
  426.4 73.1 all-gather.24
  742.2 55.5 reduce-scatter.36
  801.9 60.6 reduce-scatter.32
  866.4 71.8 reduce-scatter.24
  942.5 71.3 reduce-scatter.28
  1018.0 103.8 reduce-scatter.40
  1125.8 104.3 reduce-scatter.44
  1234.1 104.4 reduce-scatter.20
  1342.5 104.4 reduce-scatter.16
  1449.0 9.6 reduce-scatter.38
  1460.8 10.2 reduce-scatter.34
  1473.3 11.6 reduce-scatter.26
  1487.2 11.6 reduce-scatter.30
  1501.1 14.5 reduce-scatter.42
  1518.0 14.5 reduce-scatter.46
  1534.9 14.5 reduce-scatter.22
  1551.7 14.5 reduce-scatter.18
where the time goes:
time: 1590 us; the launch traced here: 1580 us
  matrix products  752 us (47%)
  waiting for transfers between devices  502 us (32%)
  blocking collectives  116 us (7%)
  local copies, waits for them, and re-layouts  99.2 us (6%)
  other arithmetic  84.5 us (5%)
  between operations  19.1 us (1%)
    dot_general x8, matrix products, attend_back(): jnp.einsum('hrk,rhd->khd', grad_raw, split_heads(query), preferred_elemen...  161 us
    dot_general x8, matrix products, attend_back(): jnp.einsum('hrk,khd->rhd', grad_raw, split_heads(keys), preferred_element...  156 us
    reduce_scatter x1, waiting for transfers between devices, shards(): lax.psum_scatter(grad_hidden_out.astype(jnp.bfloat16), 'dp', scatter_dime...  107 us
    dot_general x10, matrix products, matmul_left_t(): lax.dot_general(left, right, (((0,), (0,)), ((), ())), preferred_element_...  104 us
    dot_general x10, matrix products, matmul(): return jnp.dot(left, right, preferred_element_type=jnp.float32)  101 us
    reduce_scatter x1, waiting for transfers between devices, shards(): lax.psum_scatter(grad_state_proj.astype(jnp.bfloat16), 'dp', scatter_dime...  92.6 us
    reduce_scatter x1, waiting for transfers between devices, shards(): lax.psum_scatter(grad_token_proj.astype(jnp.bfloat16), 'dp', scatter_dime...  87.8 us
    dot_general x10, matrix products, matmul_right_t(): lax.dot_general(left, right, (((1,), (1,)), ((), ())), preferred_element_...  80 us
  transfers between devices with their start and end apart: 24, of which 12 were waited for; matrix products, arithmetic and copies ran while one was open for 43% of the time, Pallas kernels for 0%

commit v1 on v0

--- a/solution.py
+++ b/solution.py
@@ -4,6 +4,8 @@
 import jax
 import jax.numpy as jnp
 from jax import lax
+from jax.experimental import pallas as pl
+from jax.experimental.pallas import tpu as pltpu
 from jax.sharding import PartitionSpec as P
 
 HD = 128
@@ -45,62 +47,262 @@
     )
 
 
-def split_heads(values):
-    return values.reshape(values.shape[0], values.shape[1] // HD, HD)
-
-
-def masked_scores(query, keys, allowed):
-    raw = jnp.einsum(
-        "rhd,khd->hrk", split_heads(query), split_heads(keys), preferred_element_type=jnp.float32
-    )
-    scores = raw * (1.0 / math.sqrt(HD))
-    if allowed is None:
-        return scores
-    return jnp.where(allowed[None], scores, masked_score)
-
-
-def attend(query, keys, values, allowed):
-    scores = masked_scores(query, keys, allowed)
-    top = jnp.max(scores, axis=-1, keepdims=True)
-    weights = jnp.exp(scores - top)
-    total = jnp.sum(weights, axis=-1, keepdims=True)
-    probs = weights / total
-    mixed = jnp.einsum(
-        "hrk,khd->rhd", narrow(probs), split_heads(values), preferred_element_type=jnp.float32
-    )
-    return (narrow(mixed.reshape(query.shape[0], query.shape[1])), top + jnp.log(total))
-
-
-def attend_back(query, keys, values, allowed, log_total, grad_mixed):
-    probs = jnp.exp(masked_scores(query, keys, allowed) - log_total)
-    grad_heads = split_heads(grad_mixed)
-    grad_probs = jnp.einsum(
-        "rhd,khd->hrk", grad_heads, split_heads(values), preferred_element_type=jnp.float32
-    )
-    grad_values = jnp.einsum(
-        "hrk,rhd->khd", narrow(probs), grad_heads, preferred_element_type=jnp.float32
-    )
-    centered = grad_probs - jnp.sum(grad_probs * probs, axis=-1, keepdims=True)
-    grad_raw = narrow(probs * centered * (1.0 / math.sqrt(HD)))
-    grad_query = jnp.einsum(
-        "hrk,khd->rhd", grad_raw, split_heads(keys), preferred_element_type=jnp.float32
-    )
-    grad_keys = jnp.einsum(
-        "hrk,rhd->khd", grad_raw, split_heads(query), preferred_element_type=jnp.float32
-    )
-    return (
-        grad_query.reshape(query.shape),
-        grad_keys.reshape(keys.shape),
-        grad_values.reshape(values.shape),
-    )
-
-
-def window_allowed(start, window):
-    query_pos = start + jnp.arange(window)
-    key_pos = start - window + jnp.arange(2 * window)
-    later = key_pos[None, :] <= query_pos[:, None]
-    near = key_pos[None, :] > query_pos[:, None] - window
-    return later & near & (key_pos[None, :] >= 0)
+EXP_SCALE = math.log2(math.e) / math.sqrt(HD)
+RAW_SCALE = 1.0 / math.sqrt(HD)
+NT = (((1,), (1,)), ((), ()))
+TN = (((0,), (0,)), ((), ()))
+NN = (((1,), (0,)), ((), ()))
+MIB = 1 << 20
+
+
+def dot(a, b, dims):
+    return lax.dot_general(a, b, dims, preferred_element_type=jnp.float32)
+
+
+def attend_tile(q, k, v, mask):
+    scores = dot(k, q, NT)
+    if mask is not None:
+        scores = jnp.where(mask, scores, masked_score)
+    top = jnp.max(scores, axis=0, keepdims=True)
+    weights = jnp.exp2((scores - top) * EXP_SCALE)
+    total = jnp.sum(weights, axis=0, keepdims=True)
+    mixed = dot(v, weights.astype(jnp.bfloat16), TN) / total
+    return mixed.T.astype(jnp.bfloat16), top * EXP_SCALE + jnp.log2(total)
+
+
+def attend_back_tile(q, k, v, mask, log_total, grad_out, delta):
+    probs = jnp.exp2(dot(k, q, NT) * EXP_SCALE - log_total)
+    if mask is not None:
+        probs = jnp.where(mask, probs, 0.0)
+    grad_probs = dot(v, grad_out, NT)
+    grad_raw = (probs * (grad_probs - delta)).astype(jnp.bfloat16)
+    grad_v = dot(probs.astype(jnp.bfloat16), grad_out, NN)
+    grad_k = dot(grad_raw, q, NN)
+    grad_q = dot(k, grad_raw, TN)
+    return grad_q, grad_k, grad_v
+
+
+def row_delta(out, grad_out):
+    both = out.astype(jnp.float32) * grad_out.astype(jnp.float32)
+    return jnp.sum(both.T, axis=0, keepdims=True)
+
+
+def band_mask(rows, cols, key_start, query_start, window):
+    key = lax.broadcasted_iota(jnp.int32, (rows, cols), 0) + key_start
+    query = lax.broadcasted_iota(jnp.int32, (rows, cols), 1) + query_start
+    return (key <= query) & (key > query - window)
+
+
+TILE = 256
+
+
+def self_kernel(window, q_ref, k_ref, v_ref, out_ref, log_ref):
+    rows = q_ref.shape[0]
+    for start in range(0, rows, TILE):
+        low = max(0, start - window)
+        size = start + TILE - low
+        mask = band_mask(size, TILE, low, start, window)
+        out, log = attend_tile(
+            q_ref[start : start + TILE, :], k_ref[low : low + size, :], v_ref[low : low + size, :], mask
+        )
+        out_ref[start : start + TILE, :] = out
+        log_ref[0, :, start : start + TILE] = log
+
+
+def column(rows, offset):
+    return pl.BlockSpec((rows, HD), lambda h: (0, h + offset))
+
+
+def stat(rows):
+    return pl.BlockSpec((1, 1, rows), lambda h: (h, 0, 0))
+
+
+def self_attention(projected, window):
+    rows, width = projected.shape
+    heads = width // 4 // HD
+    return pl.pallas_call(
+        partial(self_kernel, window),
+        grid=(heads,),
+        in_specs=[column(rows, 0), column(rows, 2 * heads), column(rows, 3 * heads)],
+        out_specs=[column(rows, 0), stat(rows)],
+        out_shape=[
+            jax.ShapeDtypeStruct((rows, width // 4), jnp.bfloat16),
+            jax.ShapeDtypeStruct((heads, 1, rows), jnp.float32),
+        ],
+        compiler_params=pltpu.CompilerParams(vmem_limit_bytes=40 * MIB),
+        cost_estimate=pl.CostEstimate(
+            flops=heads * 4 * 2304 * 256 * HD, bytes_accessed=8 * MIB, transcendentals=heads * 2304 * 256
+        ),
+        name="self_attention",
+    )(projected, projected, projected)
+
+
+def state_kernel(live_ref, cq_ref, sq_ref, scq_ref, sk_ref, sv_ref, tk_ref, tv_ref,
+                 cross_ref, inner_self_ref, inner_cross_ref, cross_log, self_log, inner_log):
+    rows = cq_ref.shape[0]
+    for start in range(0, rows, TILE):
+        at = slice(start, start + TILE)
+        cross_ref[at, :], cross_log[0, :, at] = attend_tile(cq_ref[at, :], sk_ref[...], sv_ref[...], None)
+        inner_self_ref[at, :], self_log[0, :, at] = attend_tile(sq_ref[at, :], sk_ref[...], sv_ref[...], None)
+        key = lax.broadcasted_iota(jnp.int32, (rows, TILE), 0)
+        inner_cross_ref[at, :], inner_log[0, :, at] = attend_tile(
+            scq_ref[at, :], tk_ref[...], tv_ref[...], key < live_ref[0]
+        )
+
+
+def state_attention(projected, state_side, live_keys, block):
+    rows, width = state_side.shape
+    heads = width // 4 // HD
+    def piece(offset):
+        return pl.BlockSpec((rows, HD), lambda h: (block, h + offset))
+    out = jax.ShapeDtypeStruct((rows, width // 4), jnp.bfloat16)
+    log = jax.ShapeDtypeStruct((heads, 1, rows), jnp.float32)
+    return pl.pallas_call(
+        state_kernel,
+        grid=(heads,),
+        in_specs=[pl.BlockSpec(memory_space=pltpu.SMEM),
+                  piece(heads), column(rows, 0), column(rows, heads), column(rows, 2 * heads), column(rows, 3 * heads),
+                  piece(2 * heads), piece(3 * heads)],
+        out_specs=[column(rows, 0)] * 3 + [stat(rows)] * 3,
+        out_shape=[out] * 3 + [log] * 3,
+        compiler_params=pltpu.CompilerParams(vmem_limit_bytes=40 * MIB),
+        cost_estimate=pl.CostEstimate(
+            flops=heads * 3 * 4 * rows * rows * HD, bytes_accessed=8 * MIB, transcendentals=heads * 3 * rows * rows
+        ),
+        name="state_attention",
+    )(live_keys, projected, state_side, state_side, state_side, state_side, projected, projected)
+
+
+def self_back_kernel(window, q_ref, k_ref, v_ref, out_ref, log_ref, grad_ref, ek_ref, ev_ref, gq_ref, gk_ref, gv_ref, sk_ref, sv_ref):
+    rows = q_ref.shape[0]
+    extra = ek_ref.shape[0]
+    sk_ref[...] = jnp.zeros_like(sk_ref)
+    sv_ref[:extra, :] = ev_ref[...]
+    sv_ref[extra:, :] = jnp.zeros((rows - extra, HD), jnp.float32)
+    for start in range(0, rows, TILE):
+        at = slice(start, start + TILE)
+        low = max(0, start - window)
+        size = start + TILE - low
+        keys = slice(low, low + size)
+        mask = band_mask(size, TILE, low, start, window)
+        grad_out = grad_ref[at, :]
+        grad_q, grad_k, grad_v = attend_back_tile(
+            q_ref[at, :], k_ref[keys, :], v_ref[keys, :], mask, log_ref[0, :, at], grad_out,
+            row_delta(out_ref[at, :], grad_out))
+        gq_ref[at, :] = (grad_q * RAW_SCALE).T.astype(jnp.bfloat16)
+        sk_ref[keys, :] += grad_k
+        sv_ref[keys, :] += grad_v
+    gk_ref[:extra, :] = (sk_ref[:extra, :] * RAW_SCALE + ek_ref[...]).astype(jnp.bfloat16)
+    gk_ref[extra:, :] = (sk_ref[extra:, :] * RAW_SCALE).astype(jnp.bfloat16)
+    gv_ref[...] = sv_ref[...].astype(jnp.bfloat16)
+
+
+def self_attention_back(projected, out, log, grad_attended, extra_k, extra_v, window):
+    rows, width = projected.shape
+    heads = width // 4 // HD
+    extra = extra_k.shape[0]
+    grad = jax.ShapeDtypeStruct((rows, width // 4), jnp.bfloat16)
+    return pl.pallas_call(
+        partial(self_back_kernel, window),
+        grid=(heads,),
+        in_specs=[column(rows, 0), column(rows, 2 * heads), column(rows, 3 * heads), column(rows, 0), stat(rows),
+                  column(rows, 0), column(extra, 0), column(extra, 0)],
+        out_specs=[column(rows, 0)] * 3,
+        out_shape=[grad] * 3,
+        scratch_shapes=[pltpu.VMEM((rows, HD), jnp.float32)] * 2,
+        compiler_params=pltpu.CompilerParams(vmem_limit_bytes=40 * MIB),
+        cost_estimate=pl.CostEstimate(
+            flops=heads * 10 * 2304 * 256 * HD, bytes_accessed=16 * MIB, transcendentals=heads * 2304 * 256
+        ),
+        name="self_attention_back",
+    )(projected, projected, projected, out, log, grad_attended, extra_k, extra_v)
+
+
+def cross_back_kernel(cq_ref, sk_ref, sv_ref, out_ref, log_ref, grad_ref, gq_ref, gk_ref, gv_ref):
+    rows = cq_ref.shape[0]
+    total_k = total_v = 0.0
+    for start in range(0, rows, TILE):
+        at = slice(start, start + TILE)
+        grad_out = grad_ref[at, :]
+        grad_q, grad_k, grad_v = attend_back_tile(
+            cq_ref[at, :], sk_ref[...], sv_ref[...], None, log_ref[0, :, at], grad_out,
+            row_delta(out_ref[at, :], grad_out))
+        gq_ref[at, :] = (grad_q * RAW_SCALE).T.astype(jnp.bfloat16)
+        total_k = total_k + grad_k
+        total_v = total_v + grad_v
+    gk_ref[...] = (total_k * RAW_SCALE).astype(jnp.bfloat16)
+    gv_ref[...] = total_v.astype(jnp.bfloat16)
+
+
+def cross_attention_back(projected, state_side, out, log, grad_attended, block):
+    rows, width = state_side.shape
+    heads = width // 4 // HD
+    grad = jax.ShapeDtypeStruct((rows, width // 4), jnp.bfloat16)
+    def piece(offset):
+        return pl.BlockSpec((rows, HD), lambda h: (block, h + offset))
+    return pl.pallas_call(
+        cross_back_kernel,
+        grid=(heads,),
+        in_specs=[piece(heads), column(rows, 2 * heads), column(rows, 3 * heads), column(rows, 0), stat(rows), piece(heads)],
+        out_specs=[column(rows, 0)] * 3,
+        out_shape=[grad] * 3,
+        compiler_params=pltpu.CompilerParams(vmem_limit_bytes=40 * MIB),
+        cost_estimate=pl.CostEstimate(
+            flops=heads * 10 * rows * rows * HD, bytes_accessed=8 * MIB, transcendentals=heads * rows * rows
+        ),
+        name="cross_attention_back",
+    )(projected, state_side, state_side, out, log, grad_attended)
+
+
+def state_back_kernel(live_ref, cq_ref, sq_ref, scq_ref, sk_ref, sv_ref, tk_ref, tv_ref,
+                      co_ref, so_ref, io_ref, cl_ref, sl_ref, il_ref, cg_ref, sg_ref, ig_ref,
+                      gcq_ref, gsq_ref, gscq_ref, gsk_ref, gsv_ref, gtk_ref, gtv_ref):
+    rows = cq_ref.shape[0]
+    sums = [0.0] * 4
+    for start in range(0, rows, TILE):
+        at = slice(start, start + TILE)
+        key = lax.broadcasted_iota(jnp.int32, (rows, TILE), 0)
+        for q_ref, k_ref, v_ref, o_ref, l_ref, g_ref, gq_ref, mask, slot in (
+            (cq_ref, sk_ref, sv_ref, co_ref, cl_ref, cg_ref, gcq_ref, None, 0),
+            (sq_ref, sk_ref, sv_ref, so_ref, sl_ref, sg_ref, gsq_ref, None, 0),
+            (scq_ref, tk_ref, tv_ref, io_ref, il_ref, ig_ref, gscq_ref, key < live_ref[0], 2),
+        ):
+            grad_out = g_ref[at, :]
+            grad_q, grad_k, grad_v = attend_back_tile(
+                q_ref[at, :], k_ref[...], v_ref[...], mask, l_ref[0, :, at], grad_out,
+                row_delta(o_ref[at, :], grad_out))
+            gq_ref[at, :] = (grad_q * RAW_SCALE).T.astype(jnp.bfloat16)
+            sums[slot] = sums[slot] + grad_k
+            sums[slot + 1] = sums[slot + 1] + grad_v
+    gsk_ref[...] = (sums[0] * RAW_SCALE).astype(jnp.bfloat16)
+    gsv_ref[...] = sums[1].astype(jnp.bfloat16)
+    gtk_ref[...] = sums[2] * RAW_SCALE
+    gtv_ref[...] = sums[3]
+
+
+def state_attention_back(projected, state_side, live_keys, outs, logs, grad_attended, grad_inner, block):
+    rows, width = state_side.shape
+    heads = width // 4 // HD
+    def piece(offset):
+        return pl.BlockSpec((rows, HD), lambda h: (block, h + offset))
+    grad = jax.ShapeDtypeStruct((rows, width // 4), jnp.bfloat16)
+    wide = jax.ShapeDtypeStruct((rows, width // 4), jnp.float32)
+    return pl.pallas_call(
+        state_back_kernel,
+        grid=(heads,),
+        in_specs=[pl.BlockSpec(memory_space=pltpu.SMEM),
+                  piece(heads), column(rows, 0), column(rows, heads), column(rows, 2 * heads), column(rows, 3 * heads),
+                  piece(2 * heads), piece(3 * heads)] + [column(rows, 0)] * 3 + [stat(rows)] * 3
+                 + [piece(heads), column(rows, 0), column(rows, heads)],
+        out_specs=[column(rows, 0)] * 7,
+        out_shape=[grad] * 5 + [wide] * 2,
+        compiler_params=pltpu.CompilerParams(vmem_limit_bytes=40 * MIB),
+        cost_estimate=pl.CostEstimate(
+            flops=heads * 30 * rows * rows * HD, bytes_accessed=16 * MIB, transcendentals=3 * heads * rows * rows
+        ),
+        name="state_attention_back",
+    )(live_keys, projected, state_side, state_side, state_side, state_side, projected, projected,
+      *outs, *logs, grad_attended, grad_inner, grad_inner)
 
 
 def shards(
@@ -176,51 +378,26 @@
     piece = tokens.astype(jnp.float32)
     normed_low = narrow(layer_norm(piece, token_gain_f))
     projected = narrow(matmul(normed_low, full_token_proj))
-    self_query = projected[:, :width]
-    cross_query = projected[:, width : 2 * width]
-    token_keys = projected[:, 2 * width : 3 * width]
-    token_values = projected[:, 3 * width :]
-    padding = jnp.zeros((window, width), jnp.bfloat16)
-    padded_keys = jnp.concatenate([padding, token_keys], axis=0)
-    padded_values = jnp.concatenate([padding, token_values], axis=0)
+    self_out, self_log = self_attention(projected, window)
     state = jnp.where(first, full_init.astype(jnp.float32), incoming[0].astype(jnp.float32))
-    state_inputs, normed_states, sides, inner_cats, mixed_states, gates, lives, key_masks = (
-        [],
-        [],
-        [],
-        [],
-        [],
-        [],
-        [],
-        [],
-    )
-    self_logs, cross_logs, inner_self_logs, inner_cross_logs, attended_parts = ([], [], [], [], [])
+    state_inputs, normed_states, sides, inner_cats, mixed_states, gates, lives, key_counts = (
+        [],
+        [],
+        [],
+        [],
+        [],
+        [],
+        [],
+        [],
+    )
+    state_outs, state_logs = ([], [])
     for block_idx in range(blocks):
         start = block_idx * window
         state_normed = narrow(layer_norm(state, state_gain_f))
         state_side = narrow(matmul(state_normed, full_state_proj))
-        state_keys = state_side[:, 2 * width : 3 * width]
-        state_values = state_side[:, 3 * width :]
-        self_part, self_log = attend(
-            self_query[start : start + window],
-            padded_keys[start : start + 2 * window],
-            padded_values[start : start + 2 * window],
-            window_allowed(start, window),
-        )
-        cross_part, cross_log = attend(
-            cross_query[start : start + window], state_keys, state_values, None
-        )
-        attended_parts.append(jnp.concatenate([self_part, cross_part], axis=1))
-        live_keys = start + jnp.arange(window) < valid_len
-        key_allowed = jnp.broadcast_to(live_keys[None, :], (state.shape[0], window))
-        inner_self, inner_self_log = attend(state_side[:, :width], state_keys, state_values, None)
-        inner_cross, inner_cross_log = attend(
-            state_side[:, width : 2 * width],
-            token_keys[start : start + window],
-            token_values[start : start + window],
-            key_allowed,
-        )
-        inner_cat = jnp.concatenate([inner_self, inner_cross], axis=1)
+        live_keys = jnp.clip(valid_len - start, 0, window).astype(jnp.int32).reshape(1)
+        outs = state_attention(projected, state_side, live_keys, block_idx)
+        inner_cat = jnp.concatenate([outs[1], outs[2]], axis=1)
         mixed_state = narrow(matmul(inner_cat, full_state_out))
         gate = jax.nn.sigmoid(matmul(mixed_state, full_gate_weight) + gate_bias_f)
         updated = gate * state + (1.0 - gate) * jnp.tanh(mixed_state.astype(jnp.float32))
@@ -232,13 +409,12 @@
         mixed_states.append(mixed_state)
         gates.append(gate)
         lives.append(live)
-        key_masks.append(key_allowed)
-        self_logs.append(self_log)
-        cross_logs.append(cross_log)
-        inner_self_logs.append(inner_self_log)
-        inner_cross_logs.append(inner_cross_log)
+        key_counts.append(live_keys)
+        state_outs.append(outs[:3])
+        state_logs.append(outs[3:])
         state = state + live * (updated - state)
-    attended = jnp.concatenate(attended_parts, axis=0)
+    cross_out = jnp.concatenate([outs[0] for outs in state_outs], axis=0)
+    attended = jnp.concatenate([self_out, cross_out], axis=1)
     middle = piece + matmul(attended, full_token_out)
     hidden_normed = narrow(layer_norm(middle, hidden_gain_f))
     hidden_pre = matmul(hidden_normed, full_hidden_in)
@@ -287,44 +463,33 @@
     grad_branch = narrow(grad_middle)
     grad_token_out = matmul_left_t(attended, grad_branch)
     grad_attended = narrow(matmul_right_t(grad_branch, back_token_out))
-    grad_padded_keys = jnp.zeros((seg_len + window, width), jnp.float32)
-    grad_padded_values = jnp.zeros((seg_len + window, width), jnp.float32)
-    grad_self_parts, grad_cross_parts, side_key_grads, side_value_grads = ([], [], [], [])
-    for block_idx in range(blocks):
-        start = block_idx * window
-        state_side = sides[block_idx]
-        self_grad_query, self_grad_keys, self_grad_values = attend_back(
-            self_query[start : start + window],
-            padded_keys[start : start + 2 * window],
-            padded_values[start : start + 2 * window],
-            window_allowed(start, window),
-            self_logs[block_idx],
-            grad_attended[start : start + window, :width],
-        )
-        grad_padded_keys = grad_padded_keys.at[start : start + 2 * window].add(self_grad_keys)
-        grad_padded_values = grad_padded_values.at[start : start + 2 * window].add(self_grad_values)
-        cross_grad_query, cross_grad_keys, cross_grad_values = attend_back(
-            cross_query[start : start + window],
-            state_side[:, 2 * width : 3 * width],
-            state_side[:, 3 * width :],
-            None,
-            cross_logs[block_idx],
-            grad_attended[start : start + window, width:],
-        )
-        grad_self_parts.append(self_grad_query)
-        grad_cross_parts.append(cross_grad_query)
-        side_key_grads.append(cross_grad_keys)
-        side_value_grads.append(cross_grad_values)
-    grad_token_keys = grad_padded_keys[window:]
-    grad_token_values = grad_padded_values[window:]
-    grad_state = jnp.zeros_like(state)
-    grad_state_proj = jnp.zeros((width, 4 * width), jnp.float32)
+    last = blocks - 1
+    last_start = last * window
+    cross_grad, last_keys_grad, last_values_grad = cross_attention_back(
+        projected,
+        sides[last],
+        state_outs[last][0],
+        state_logs[last][0],
+        grad_attended,
+        last,
+    )
+    cross_grads = [cross_grad]
+    grad_side = jnp.concatenate([last_keys_grad, last_values_grad], axis=1)
+    grad_state_proj = jnp.concatenate(
+        [
+            jnp.zeros((width, 2 * width), jnp.float32),
+            matmul_left_t(normed_states[last], grad_side),
+        ],
+        axis=1,
+    )
+    grad_state, grad_state_gain = norm_back(
+        state_inputs[last], state_gain_f, matmul_right_t(grad_side, back_state_proj[:, 2 * width :])
+    )
     grad_state_out = jnp.zeros((2 * width, width), jnp.float32)
     grad_gate_weight = jnp.zeros((width, width), jnp.float32)
     grad_gate_bias = jnp.zeros((width,), jnp.float32)
-    grad_state_gain = jnp.zeros((width,), jnp.float32)
-    for block_idx in reversed(range(blocks)):
-        start = block_idx * window
+    extra_keys, extra_values = ([], [])
+    for block_idx in reversed(range(last)):
         state_side = sides[block_idx]
         gate = gates[block_idx]
         live = lives[block_idx]
@@ -342,52 +507,38 @@
         )
         grad_state_out = grad_state_out + matmul_left_t(inner_cats[block_idx], grad_mixed)
         grad_inner = narrow(matmul_right_t(grad_mixed, back_state_out))
-        self_query_grad, self_key_grad, self_value_grad = attend_back(
-            state_side[:, :width],
-            state_side[:, 2 * width : 3 * width],
-            state_side[:, 3 * width :],
-            None,
-            inner_self_logs[block_idx],
-            grad_inner[:, :width],
+        parts = state_attention_back(
+            projected,
+            state_side,
+            key_counts[block_idx],
+            state_outs[block_idx],
+            state_logs[block_idx],
+            grad_attended,
+            grad_inner,
+            block_idx,
         )
-        cross_query_grad, token_key_grad, token_value_grad = attend_back(
-            state_side[:, width : 2 * width],
-            token_keys[start : start + window],
-            token_values[start : start + window],
-            key_masks[block_idx],
-            inner_cross_logs[block_idx],
-            grad_inner[:, width:],
-        )
-        grad_token_keys = grad_token_keys.at[start : start + window].add(token_key_grad)
-        grad_token_values = grad_token_values.at[start : start + window].add(token_value_grad)
-        grad_side = narrow(
-            jnp.concatenate(
-                [
-                    self_query_grad,
-                    cross_query_grad,
-                    self_key_grad + side_key_grads[block_idx],
-                    self_value_grad + side_value_grads[block_idx],
-                ],
-                axis=1,
-            )
-        )
+        cross_grads.insert(0, parts[0])
+        grad_side = jnp.concatenate(parts[1:5], axis=1)
+        extra_keys.insert(0, parts[5])
+        extra_values.insert(0, parts[6])
         grad_state_proj = grad_state_proj + matmul_left_t(normed_states[block_idx], grad_side)
         grad_state_norm, grad_gain_part = norm_back(
             state_in, state_gain_f, matmul_right_t(grad_side, back_state_proj)
         )
         grad_state_gain = grad_state_gain + grad_gain_part
         grad_state = grad_direct + grad_state_norm
+    self_grad, keys_grad, values_grad = self_attention_back(
+        projected,
+        self_out,
+        self_log,
+        grad_attended,
+        jnp.concatenate(extra_keys, axis=0),
+        jnp.concatenate(extra_values, axis=0),
+        window,
+    )
     grad_init = jnp.where(first, grad_state, 0.0)
-    grad_projected = narrow(
-        jnp.concatenate(
-            [
-                jnp.concatenate(grad_self_parts, axis=0),
-                jnp.concatenate(grad_cross_parts, axis=0),
-                grad_token_keys,
-                grad_token_values,
-            ],
-            axis=1,
-        )
+    grad_projected = jnp.concatenate(
+        [self_grad, jnp.concatenate(cross_grads, axis=0), keys_grad, values_grad], axis=1
     )
     grad_token_proj = matmul_left_t(normed_low, grad_projected)
     grad_piece, grad_token_gain = norm_back(

time: 1590 us -> 1470 us (0.925)
  matrix products: 752 us -> 275 us
  waiting for transfers between devices: 502 us -> 837 us
  Pallas kernels: 0 us -> 120 us
  local copies, waits for them, and re-layouts: 99.2 us -> 49.5 us
  other arithmetic: 84.5 us -> 40.4 us
    dot_general x48 -> x0, matrix products: 466 us -> none  [the longest x8 161 us: attend_back(): jnp.einsum('hrk,rhd->khd', grad_raw, split_heads(query), preferred_elemen...]
    pallas_call x0 -> x6, Pallas kernels: none -> 120 us  [the longest x2 51 us: state_attention(): pl.pallas_call(state_kernel, grid=(heads,), in_specs=[pl.BlockSpec(memory...]
    reduce_scatter x1, waiting for transfers between devices: 0.02 us -> 75.6 us  [shards(): lax.psum_scatter(grad_state_out.astype(jnp.bfloat16), 'dp', scatter_dimen...]
    reduce_scatter x1, waiting for transfers between devices: 0.02 us -> 74.6 us  [shards(): lax.psum_scatter(grad_token_out.astype(jnp.bfloat16), 'dp', scatter_dimen...]
    reduce_scatter x1, waiting for transfers between devices: 22.9 us -> 79.9 us  [shards(): lax.psum_scatter(grad_hidden_in.astype(jnp.bfloat16), 'dp', scatter_dimen...]
    all_gather x1, waiting for transfers between devices: 0.01 us -> 56.1 us  [shards(): lax.all_gather(columns[7], 'dp', axis=0, tiled=True)]
    reduce_scatter x1, waiting for transfers between devices: 107 us -> 59.9 us  [shards(): lax.psum_scatter(grad_hidden_out.astype(jnp.bfloat16), 'dp', scatter_dime...]
    all_gather x1, waiting for transfers between devices: 17.5 us -> 64.2 us  [shards(): lax.all_gather(columns[0], 'dp', axis=0, tiled=True)]
  transfers between devices with their start and end apart: 24 -> 24, of which waited for: 12 -> 20; matrix products, arithmetic and copies ran while one was open for 43% -> 17% of each run, Pallas kernels for 0% -> 6%
where the time goes in v1:
time: 1470 us; the launch traced here: 1460 us
  waiting for transfers between devices  837 us (57%)
  matrix products  275 us (19%)
  Pallas kernels  120 us (8%)
  blocking collectives  117 us (8%)
  local copies, waits for them, and re-layouts  49.5 us (3%)
  other arithmetic  40.4 us (3%)
  between operations  18.9 us (1%)
    dot_general x10, matrix products, matmul(): return jnp.dot(left, right, preferred_element_type=jnp.float32)  106 us
    reduce_scatter x1, waiting for transfers between devices, shards(): lax.psum_scatter(grad_token_proj.astype(jnp.bfloat16), 'dp', scatter_dime...  106 us
    reduce_scatter x1, waiting for transfers between devices, shards(): lax.psum_scatter(grad_state_proj.astype(jnp.bfloat16), 'dp', scatter_dime...  91.4 us
    dot_general x8, matrix products, matmul_left_t(): lax.dot_general(left, right, (((0,), (0,)), ((), ())), preferred_element_...  90.8 us
    reduce_scatter x1, waiting for transfers between devices, shards(): lax.psum_scatter(grad_hidden_in.astype(jnp.bfloat16), 'dp', scatter_dimen...  79.9 us
    dot_general x8, matrix products, matmul_right_t(): lax.dot_general(left, right, (((1,), (1,)), ((), ())), preferred_element_...  77.7 us
    reduce_scatter x1, waiting for transfers between devices, shards(): lax.psum_scatter(grad_state_out.astype(jnp.bfloat16), 'dp', scatter_dimen...  75.6 us
    reduce_scatter x1, waiting for transfers between devices, shards(): lax.psum_scatter(grad_token_out.astype(jnp.bfloat16), 'dp', scatter_dimen...  74.6 us
  transfers between devices with their start and end apart: 24, of which 20 were waited for; matrix products, arithmetic and copies ran while one was open for 17% of the time, Pallas kernels for 6%

profile of v1, /device:TPU:0, one launch (start us, length us, event | category | flops | bytes accessed | tf_op | source)
XLA Modules:
  0.0 1459.6 jit_solution(1696466591117339560)
XLA Ops:
  7.3 7.3 all_gather.77
  14.7 8.5 all_gather.80
  23.2 9.1 all_gather.75
  38.4 6.6 all_gather.84
  45.1 7.4 all_gather.87
  52.6 9.8 all_gather.92
  62.4 7.2 all_gather.90
  103.7 25.4 %all-gather.17.cloned.1.call-done = bf16[1024,4096]{1,0:T(8,128)(2,1)} async-done(((bf16[64,4096]{1,0:T(8,128)(2,1)}), bf16[1024,4096]{1,0:T(8,128)(2,1)}) %all-gather.17.cloned.1.call-update) | async-done | bytes 8388624 | tf_op jit(solution)/shard_map/all_gather | solution.py:342
  129.1 11.1 convolution_convert_fusion.5.sq_ref.scq_ref.sk_ref.sv_ref
  140.3 64.2 %all-gather.13.cloned.1.call-done = bf16[1024,4096]{1,0:T(8,128)(2,1)} async-done(((bf16[64,4096]{1,0:T(8,128)(2,1)}), bf16[1024,4096]{1,0:T(8,128)(2,1)}) %all-gather.13.cloned.1.call-update) | async-done | bytes 8388624 | tf_op jit(solution)/shard_map/all_gather | solution.py:341
  204.5 15.0 %convolution_convert_fusion.3.q_ref.k_ref.v_ref.cq_ref.tk_ref.tv_ref = bf16[1024,4096]{1,0:T(8,128)(2,1)} fusion(bf16[1024,4096]{1,0:T(8,128)(2,1)} %all-gather.13.cloned.1.call-done, bf16[1024,1024]{0,1:T(8,128)(2,1)S(1)} %copy.36, f32[1024]{0:T(1024)S(1)} %bitcast.81, f32[1024]{0:T(1024)S(1)} %fusion.44, f32[1024]{0:T(1024)S(1)} %broadcast_multiply_fusion.1), kind=kOutput, calls=%fused_computation.15 | convolution fusion | flops 8599371776 | bytes 18886656 | tf_op jit(solution)/shard_map/dot_general | solution.py:35
  219.5 25.0 %state_attention.2 = (bf16[512,1024]{1,0:T(8,128)(2,1)S(1)}, bf16[512,1024]{1,0:T(8,128)(2,1)S(1)}, bf16[512,1024]{1,0:T(8,128)(2,1)S(1)}, f32[8,1,512]{2,1,0:T(...) custom-call(s32[1]{0:T(128)} %bitcast.3.live_ref, ...), custom_call_target="tpu_custom_call" | custom-call | flops 3221225472 | bytes 8388608 | tf_op jit(solution)/shard_map/state_attention/pallas_call | solution.py:160
  247.7 7.2 all-gather.19.cloned.1.call-done
  261.0 36.3 %all-gather.21.cloned.1.call-done = bf16[1024,1024]{1,0:T(8,128)(2,1)} async-done(((bf16[64,1024]{1,0:T(8,128)(2,1)}), bf16[1024,1024]{1,0:T(8,128)(2,1)}) %all-gather.21.cloned.1.call-update) | async-done | bytes 2097168 | tf_op jit(solution)/shard_map/all_gather | solution.py:345
  304.3 17.5 %self_attention.1 = (bf16[1024,1024]{1,0:T(8,128)(2,1)S(1)}, f32[8,1,1024]{2,1,0:T(1,128)S(1)}) custom-call(bf16[1024,4096]{1,0:T(8,128)(2,1)S(1)} %bitcast.72, bf16[1024,4096]{1,0:T(8,128)(2,1)S(1)} %bitcast.72, bf16[1024,4096]{1,0:T(8,128)(2,1)S(1)} %bitcast.72), custom_call_target="tpu_custom_call" | custom-call | flops 2415919104 | bytes 8388608 | tf_op jit(solution)/shard_map/self_attention/pallas_call | solution.py:123
  326.8 25.9 %state_attention.3 = (bf16[512,1024]{1,0:T(8,128)(2,1)S(1)}, bf16[512,1024]{1,0:T(8,128)(2,1)S(1)}, bf16[512,1024]{1,0:T(8,128)(2,1)S(1)}, f32[8,1,512]{2,1,0:T(...) custom-call(s32[1]{0:T(128)} %bitcast.6.live_ref, ...), custom_call_target="tpu_custom_call" | custom-call | flops 3221225472 | bytes 8388608 | tf_op jit(solution)/shard_map/state_attention/pallas_call | solution.py:160
  357.6 8.3 fusion.62
  368.4 56.1 %all-gather.27.cloned.1.call-done = bf16[4096,1024]{1,0:T(8,128)(2,1)} async-done(((bf16[256,1024]{1,0:T(8,128)(2,1)}), bf16[4096,1024]{1,0:T(8,128)(2,1)}) %all-gather.27.cloned.1.call-update) | async-done | bytes 8388624 | tf_op jit(solution)/shard_map/all_gather | solution.py:348
  424.4 16.0 %fusion.63 = f32[1024,4096]{1,0:T(8,128)} fusion(bf16[1024,1024]{1,0:T(8,128)(2,1)} %param.19, bf16[4096,1024]{1,0:T(8,128)(2,1)} %all-gather.27.cloned.1.call-done), kind=kOutput, calls=%fused_computation.142 | convolution fusion | flops 8589934592 | bytes 27262976 | tf_op jit(solution)/shard_map/dot_general | solution.py:45
  440.4 59.3 %all-gather.25.cloned.1.call-done = bf16[1024,4096]{1,0:T(8,128)(2,1)} async-done(((bf16[64,4096]{1,0:T(8,128)(2,1)}), bf16[1024,4096]{1,0:T(8,128)(2,1)}) %all-gather.25.cloned.1.call-update) | async-done | bytes 8388624 | tf_op jit(solution)/shard_map/all_gather | solution.py:347
  499.8 29.8 %fusion.6 = (bf16[1024,4096]{1,0:T(8,128)(2,1)}, f32[1024,4096]{1,0:T(8,128)}) fusion(f32[1024,4096]{1,0:T(8,128)} %fusion.63, bf16[1024,4096]{1,0:T(8,128)(2,1)} %all-gather.25.cloned.1.call-done, f32[1024,1024]{0,1:T(8,128)} %copy-done.29, f32[1024]{0:T(1024)S(1)} %bitcast.86, f32[1024]{0:T(1024)S(1)} %fusion.45, f32[1024]{0:T(1024)S(1)} %broadcast_multiply_fusion), kind=kOutput, calls=%fused_computation.8 | convolution fusion | flops 8678014976 | bytes 54538240 | tf_op jit(solution)/shard_map/dot_general | solution.py:35
  529.6 16.0 %multiply_reduce_fusion = (bf16[1024]{0:T(1024)(128)(2,1)}, f32[1024]{0:T(1024)S(1)}, f32[1024,1024]{0,1:T(8,128)S(1)}) fusion(f32[1024,1024]{0,1:T(8,128)} %copy-done.29, f32[1024]{0:T(1024)S(1)} %fusion.45, f32[1024]{0:T(1024)S(1)} %broadcast_multiply_fusion, f32[1024]{0:T(1024)S(1)} %bitcast.87, bf16[1024,4096]{1,0:T(8,128)(2,1)} %get-tuple-element.124, ...), kind=kOutput, calls=%fused_computation.36 | convolution fusion | flops 8597272576 | bytes 25184256 | tf_op jit(solution)/shard_map/dot_general | solution.py:45
  555.7 10.4 cross_attention_back.1
  585.7 22.7 %state_attention_back.1 = (bf16[512,1024]{1,0:T(8,128)(2,1)S(1)}, bf16[512,1024]{1,0:T(8,128)(2,1)S(1)}, bf16[512,1024]{1,0:T(8,128)(2,1)S(1)}, bf16[512,1024]{1...) custom-call(s32[1]{0:T(128)} %bitcast.3.live_ref, ...), custom_call_target="tpu_custom_call" | custom-call | flops 8053063680 | bytes 16777216 | tf_op jit(solution)/shard_map/state_attention_back/pallas_call | solution.py:290
  612.9 10.0 multiply_reduce_fusion.3
  631.1 8.5 convolution_convert_fusion.7
  650.3 18.2 %self_attention_back.1 = (bf16[1024,1024]{1,0:T(8,128)(2,1)S(1)}, bf16[1024,1024]{1,0:T(8,128)(2,1)S(1)}, bf16[1024,1024]{1,0:T(8,128)(2,1)S(1)}) custom-call(bf16[1024,4096]{1,0:T(8,128)(2,1)} %convolution_convert_fusion.3.q_ref.k_ref.v_ref.cq_ref.tk_ref.tv_ref, bf16[1024,4096]{1,0:T(8,128)(2,1)} %convolution_convert_fusion.3.q_ref.k_ref.v_ref.cq_ref.tk_ref.tv_ref, ...), custom_call_target="tpu_custom_call" | custom-call | flops 6039797760 | bytes 16777216 | tf_op jit(solution)/shard_map/self_attention_back/pallas_call | solution.py:205
  672.5 19.4 %convolution_convert_fusion.2 = bf16[1024,4096]{1,0:T(8,128)(2,1)} fusion(bf16[1024,1024]{0,1:T(8,128)(2,1)} %copy-done.25, f32[1024]{0:T(1024)S(1)} %bitcast.82, f32[1024]{0:T(1024)S(1)} %copy-done.56, f32[1024]{0:T(1024)S(1)} %copy-done.50, bf16[1024,1024]{1,0:T(8,128)(2,1)} %copy-done.17, bf16[1024,1024]{1,0:T(8,128)(2,1)} %copy-done.16, ...), kind=kOutput, calls=%fused_computation.14 | convolution fusion | flops 8641314816 | bytes 18886656 | tf_op jit(solution)/shard_map/dot_general | solution.py:39
  692.4 8.5 fusion.54
  700.8 11.4 add_convert_fusion
  712.3 15.6 %convolution_convert_fusion.1 = bf16[1024,4096]{1,0:T(8,128)(2,1)} fusion(bf16[1024,4096]{1,0:T(8,128)(2,1)} %get-tuple-element.124, f32[1024,1024]{0,1:T(8,128)} %copy-done.29, f32[1024]{0:T(1024)S(1)} %bitcast.89, f32[1024]{0:T(1024)S(1)} %fusion.45, f32[1024]{0:T(1024)S(1)} %broadcast_multiply_fusion), kind=kOutput, calls=%fused_computation.13 | convolution fusion | flops 8598323200 | bytes 20983808 | tf_op jit(solution)/shard_map/dot_general | solution.py:39
  729.5 17.3 %convolution_convert_fusion = bf16[4096,1024]{1,0:T(8,128)(2,1)} fusion(bf16[1024,1024]{1,0:T(8,128)(2,1)S(1)} %copy-done.42, f32[1024,4096]{1,0:T(8,128)} %get-tuple-element.125), kind=kOutput, calls=%fused_computation.12 | convolution fusion | flops 8631877632 | bytes 27262976 | tf_op jit(solution)/shard_map/dot_general | solution.py:39
  748.1 74.6 %reduce-scatter.25.cloned.1.call-done = bf16[128,1024]{1,0:T(8,128)(2,1)} async-done(((bf16[2048,1024]{1,0:T(8,128)(2,1)}), bf16[128,1024]{1,0:T(8,128)(2,1)}) %reduce-scatter.25.cloned.1.call-update) | async-done | bytes 262160 | tf_op jit(solution)/shard_map/reduce_scatter | solution.py:555
  822.7 75.6 %reduce-scatter.29.cloned.1.call-done = bf16[128,1024]{1,0:T(8,128)(2,1)} async-done(((bf16[2048,1024]{1,0:T(8,128)(2,1)}), bf16[128,1024]{1,0:T(8,128)(2,1)}) %reduce-scatter.29.cloned.1.call-update) | async-done | bytes 262160 | tf_op jit(solution)/shard_map/reduce_scatter | solution.py:558
  900.3 105.8 %reduce-scatter.17.cloned.1.call-done = bf16[64,4096]{1,0:T(8,128)(2,1)} async-done(((bf16[1024,4096]{1,0:T(8,128)(2,1)}), bf16[64,4096]{1,0:T(8,128)(2,1)}) %reduce-scatter.17.cloned.1.call-update) | async-done | bytes 524304 | tf_op jit(solution)/shard_map/reduce_scatter | solution.py:549
  1006.2 16.8 %add_convert_fusion.2 = bf16[1024,1024]{0,1:T(8,128)(2,1)} fusion(f32[1024,1024]{0,1:T(8,128)} %copy-done.29, bf16[4096,1024]{1,0:T(8,128)(2,1)} %all-gather.27.cloned.1.call-done, f32[1024,4096]{1,0:T(8,128)} %get-tuple-element.125), kind=kOutput, calls=%fused_computation.40 | convolution fusion | flops 8629780480 | bytes 31457280 | tf_op jit(solution)/shard_map/dot_general | solution.py:35
  1022.9 91.4 %reduce-scatter.21.cloned.1.call-done = bf16[64,4096]{1,0:T(8,128)(2,1)} async-done(((bf16[1024,4096]{1,0:T(8,128)(2,1)}), bf16[64,4096]{1,0:T(8,128)(2,1)}) %reduce-scatter.21.cloned.1.call-update) | async-done | bytes 524304 | tf_op jit(solution)/shard_map/reduce_scatter | solution.py:552
  1114.7 20.0 %fusion.16 = (f32[1024]{0:T(1024)S(1)}, f32[1024,1024]{0,1:T(8,128)}) fusion(bf16[1024,1024]{0,1:T(8,128)(2,1)} %copy-done.25, f32[1024]{0:T(1024)S(1)} %bitcast.83, f32[1024]{0:T(1024)S(1)} %copy-done.50, bf16[1024,4096]{1,0:T(8,128)(2,1)} %all-gather.13.cloned.1.call-done, bf16[1024,1024]{1,0:T(8,128)(2,1)} %copy-done.17, ...), kind=kOutput, calls=%fused_computation.32 | convolution fusion | flops 8637119488 | bytes 23080960 | tf_op jit(solution)/shard_map/dot_general | solution.py:45
  1142.8 79.9 %reduce-scatter.41.cloned.1.call-done = bf16[64,4096]{1,0:T(8,128)(2,1)} async-done(((bf16[1024,4096]{1,0:T(8,128)(2,1)}), bf16[64,4096]{1,0:T(8,128)(2,1)}) %reduce-scatter.41.cloned.1.call-update) | async-done | bytes 524304 | tf_op jit(solution)/shard_map/reduce_scatter | solution.py:567
  1238.3 33.1 %all-reduce.5 = (f32[512]{0:T(512)}, f32[512]{0:T(512)}, f32[512]{0:T(512)}, f32[512]{0:T(512)}) all-reduce(f32[512]{0:T(512)S(1)} %get-tuple-element.134, f32[512]{0:T(512)S(1)} %get-tuple-element.133, f32[512]{0:T(512)S(1)} %get-tuple-element.132, f32[512]{0:T(512)S(1)} %get-tuple-element.131), channel_id=1, replica_groups=mesh['dp'=16,'fsdp'=2] {'dp'}, use_global_device_ids=true, to_apply=%region_37.38 | all-reduce | flops 2048 | bytes 16384 | tf_op jit(solution)/shard_map/psum | solution.py:614
  1271.4 59.9 %reduce-scatter.45.cloned.1.call-done = bf16[256,1024]{1,0:T(8,128)(2,1)} async-done(((bf16[4096,1024]{1,0:T(8,128)(2,1)}), bf16[256,1024]{1,0:T(8,128)(2,1)}) %reduce-scatter.45.cloned.1.call-update) | async-done | bytes 524304 | tf_op jit(solution)/shard_map/reduce_scatter | solution.py:570
  1344.4 11.0 reduce-scatter.35.cloned.1.call-done
  1356.8 12.4 reduce-scatter.27.cloned.1.call-done
  1370.8 12.2 reduce-scatter.31.cloned.1.call-done
  1384.7 15.2 %reduce-scatter.19.cloned.1.call-done = bf16[64,2048]{1,0:T(8,128)(2,1)} async-done(((bf16[64,4096]{1,0:T(8,128)(2,1)}), bf16[64,2048]{1,0:T(8,128)(2,1)}) %reduce-scatter.19.cloned.1.call-update) | async-done | bytes 262160 | tf_op jit(solution)/shard_map/reduce_scatter | solution.py:575
  1401.7 15.1 %reduce-scatter.23.cloned.1.call-done = bf16[64,2048]{1,0:T(8,128)(2,1)} async-done(((bf16[64,4096]{1,0:T(8,128)(2,1)}), bf16[64,2048]{1,0:T(8,128)(2,1)}) %reduce-scatter.23.cloned.1.call-update) | async-done | bytes 262160 | tf_op jit(solution)/shard_map/reduce_scatter | solution.py:578
  1418.6 15.1 %reduce-scatter.43.cloned.1.call-done = bf16[64,2048]{1,0:T(8,128)(2,1)} async-done(((bf16[64,4096]{1,0:T(8,128)(2,1)}), bf16[64,2048]{1,0:T(8,128)(2,1)}) %reduce-scatter.43.cloned.1.call-update) | async-done | bytes 262160 | tf_op jit(solution)/shard_map/reduce_scatter | solution.py:593
  1435.5 15.0 %reduce-scatter.47.cloned.1.call-done = bf16[256,512]{1,0:T(8,128)(2,1)} async-done(((bf16[256,1024]{1,0:T(8,128)(2,1)}), bf16[256,512]{1,0:T(8,128)(2,1)}) %reduce-scatter.47.cloned.1.call-update) | async-done | bytes 262160 | tf_op jit(solution)/shard_map/reduce_scatter | solution.py:596
  (312 shorter events, 176.7 us)
Async XLA Ops:
  7.2 45.4 %copy-start.47 = (bf16[256,512]{1,0:T(8,128)(2,1)S(1)}, bf16[256,512]{1,0:T(8,128)(2,1)}, u32[]{:S(2)}) copy-start(bf16[256,512]{1,0:T(8,128)(2,1)} %param.27) | copy-start | bytes 786436
  7.2 55.2 %copy-start.48 = (bf16[64,2048]{1,0:T(8,128)(2,1)S(1)}, bf16[64,2048]{1,0:T(8,128)(2,1)}, u32[]{:S(2)}) copy-start(bf16[64,2048]{1,0:T(8,128)(2,1)} %param.26) | copy-start | bytes 786436
  7.2 62.5 %copy-start.71 = (s32[8]{0:T(128)S(1)}, s32[8]{0:T(128)}, u32[]{:S(2)}) copy-start(s32[8]{0:T(128)} %param.18) | copy-start | bytes 100
  7.2 91.9 %all-gather.15.cloned.1.call-start = ((), (), s32[]{:S(2)}) async-start(), calls=%async_computation.17 | async-start | bytes 1114112 | tf_op jit(solution)/shard_map/all_gather | solution.py:346
  14.6 114.5 %all-gather.17.cloned.1.call-start = ((), (), s32[]{:S(2)}) async-start(), calls=%async_computation.18 | async-start | bytes 8912896 | tf_op jit(solution)/shard_map/all_gather | solution.py:342
  23.1 181.3 %all-gather.13.cloned.1.call-start = ((), (), s32[]{:S(2)}) async-start(), calls=%async_computation.16 | async-start | bytes 8912896 | tf_op jit(solution)/shard_map/all_gather | solution.py:341
  32.3 43.0 %copy-start.72 = (bf16[512]{0:T(512)(128)(2,1)S(1)}, bf16[512]{0:T(512)(128)(2,1)}, u32[]{:S(2)}) copy-start(bf16[512]{0:T(512)(128)(2,1)} %param.28) | copy-start | bytes 3076
  32.3 47.4 %copy-start.73 = (bf16[512]{0:T(512)(128)(2,1)S(1)}, bf16[512]{0:T(512)(128)(2,1)}, u32[]{:S(2)}) copy-start(bf16[512]{0:T(512)(128)(2,1)} %param.29) | copy-start | bytes 3076
  32.3 51.7 %copy-start.74 = (bf16[512]{0:T(512)(128)(2,1)S(1)}, bf16[512]{0:T(512)(128)(2,1)}, u32[]{:S(2)}) copy-start(bf16[512]{0:T(512)(128)(2,1)} %param.31) | copy-start | bytes 3076
  32.3 56.1 %copy-start.75 = (bf16[512]{0:T(512)(128)(2,1)S(1)}, bf16[512]{0:T(512)(128)(2,1)}, u32[]{:S(2)}) copy-start(bf16[512]{0:T(512)(128)(2,1)} %param.30) | copy-start | bytes 3076
  32.3 222.5 %all-gather.19.cloned.1.call-start = ((), (), s32[]{:S(2)}) async-start(), calls=%async_computation.19 | async-start | bytes 4456448 | tf_op jit(solution)/shard_map/all_gather | solution.py:344
  38.4 258.9 %all-gather.21.cloned.1.call-start = ((), (), s32[]{:S(2)}) async-start(), calls=%async_computation.20 | async-start | bytes 2228224 | tf_op jit(solution)/shard_map/all_gather | solution.py:345
  45.1 312.6 %all-gather.23.cloned.1.call-start = ((), (), s32[]{:S(2)}) async-start(), calls=%async_computation.21 | async-start | bytes 4456448 | tf_op jit(solution)/shard_map/all_gather | solution.py:343
  52.5 371.9 %all-gather.27.cloned.1.call-start = ((), (), s32[]{:S(2)}) async-start(), calls=%async_computation.23 | async-start | bytes 8912896 | tf_op jit(solution)/shard_map/all_gather | solution.py:348
  62.4 437.4 %all-gather.25.cloned.1.call-start = ((), (), s32[]{:S(2)}) async-start(), calls=%async_computation.22 | async-start | bytes 8912896 | tf_op jit(solution)/shard_map/all_gather | solution.py:347
  69.6 677.3 %reduce-scatter.37.cloned.1.call-start = ((), (), s32[]{:S(2)}) async-start(), calls=%async_computation.34 | async-start | bytes 1114112 | tf_op jit(solution)/shard_map/reduce_scatter | solution.py:564
  75.3 129.2 %copy-start.25 = (bf16[1024,1024]{0,1:T(8,128)(2,1)}, bf16[1024,1024]{0,1:T(8,128)(2,1)S(1)}, u32[]{:S(2)}) copy-start(bf16[1024,1024]{0,1:T(8,128)(2,1)S(1)} %copy.36) | copy-start | bytes 6291460
  79.7 124.8 %copy-start.53 = (f32[2,1,512]{2,1,0:T(1,128)}, f32[2,1,512]{2,1,0:T(1,128)S(1)}, u32[]{:S(2)}) copy-start(f32[2,1,512]{2,1,0:T(1,128)S(1)} %convert_element_type.234) | copy-start | bytes 12292
  88.4 208.9 %copy-start.66 = (f32[2,1,512]{2,1,0:T(1,128)}, f32[2,1,512]{2,1,0:T(1,128)S(1)}, u32[]{:S(2)}) copy-start(f32[2,1,512]{2,1,0:T(1,128)S(1)} %convert_element_type.236) | copy-start | bytes 12292
  97.9 106.6 %copy-start.49 = (f32[1024]{0:T(1024)}, f32[1024]{0:T(1024)S(1)}, u32[]{:S(2)}) copy-start(f32[1024]{0:T(1024)S(1)} %broadcast_multiply_fusion.1) | copy-start | bytes 12292
  99.1 105.4 %copy-start.55 = (f32[1024]{0:T(1024)}, f32[1024]{0:T(1024)S(1)}, u32[]{:S(2)}) copy-start(f32[1024]{0:T(1024)S(1)} %fusion.44) | copy-start | bytes 12292
  101.3 38.9 %copy-start.59 = (f32[512]{0:T(512)}, f32[512]{0:T(512)S(1)}, u32[]{:S(2)}) copy-start(f32[512]{0:T(512)S(1)} %broadcast_multiply_fusion.3) | copy-start | bytes 6148
  103.7 36.5 %copy-start.61 = (f32[512]{0:T(512)}, f32[512]{0:T(512)S(1)}, u32[]{:S(2)}) copy-start(f32[512]{0:T(512)S(1)} %multiply_reduce_fusion.8) | copy-start | bytes 6148
  103.7 36.5 %copy-start.63 = (f32[512]{0:T(512)}, f32[512]{0:T(512)S(1)}, u32[]{:S(2)}) copy-start(f32[512]{0:T(512)S(1)} %fusion.46) | copy-start | bytes 6148
  247.7 49.6 %copy-start.32 = (bf16[1,512,1024]{2,1,0:T(8,128)(2,1)S(1)}, bf16[1,512,1024]{2,1,0:T(8,128)(2,1)}, u32[]{:S(2)}) copy-start(bf16[1,512,1024]{2,1,0:T(8,128)(2,1)} %param.17) | copy-start | bytes 3145732
  247.7 49.6 %copy-start.35 = (bf16[512,1024]{1,0:T(8,128)(2,1)S(1)}, bf16[512,1024]{1,0:T(8,128)(2,1)}, u32[]{:S(2)}) copy-start(bf16[512,1024]{1,0:T(8,128)(2,1)} %all-gather.15.cloned.1.call-done) | copy-start | bytes 3145732
  626.8 120.7 %reduce-scatter.33.cloned.1.call-start = ((), (), s32[]{:S(2)}) async-start(), calls=%async_computation.32 | async-start | bytes 2228224 | tf_op jit(solution)/shard_map/reduce_scatter | solution.py:561
  631.1 191.6 %reduce-scatter.25.cloned.1.call-start = ((), (), s32[]{:S(2)}) async-start(), calls=%async_computation.28 | async-start | bytes 4456448 | tf_op jit(solution)/shard_map/reduce_scatter | solution.py:555
  639.6 258.7 %reduce-scatter.29.cloned.1.call-start = ((), (), s32[]{:S(2)}) async-start(), calls=%async_computation.30 | async-start | bytes 4456448 | tf_op jit(solution)/shard_map/reduce_scatter | solution.py:558
  646.8 359.2 %reduce-scatter.17.cloned.1.call-start = ((), (), s32[]{:S(2)}) async-start(), calls=%async_computation.24 | async-start | bytes 8912896 | tf_op jit(solution)/shard_map/reduce_scatter | solution.py:549
  650.3 22.2 %copy-start.54 = (f32[2,1,512]{2,1,0:T(1,128)S(1)}, f32[2,1,512]{2,1,0:T(1,128)}, u32[]{:S(2)}) copy-start(f32[2,1,512]{2,1,0:T(1,128)} %copy-done.53) | copy-start | bytes 12292
  650.3 22.2 %copy-start.56 = (f32[1024]{0:T(1024)S(1)}, f32[1024]{0:T(1024)}, u32[]{:S(2)}) copy-start(f32[1024]{0:T(1024)} %copy-done.55) | copy-start | bytes 12292
  691.9 422.5 %reduce-scatter.21.cloned.1.call-start = ((), (), s32[]{:S(2)}) async-start(), calls=%async_computation.26 | async-start | bytes 8912896 | tf_op jit(solution)/shard_map/reduce_scatter | solution.py:552
  712.2 510.5 %reduce-scatter.41.cloned.1.call-start = ((), (), s32[]{:S(2)}) async-start(), calls=%async_computation.36 | async-start | bytes 8912896 | tf_op jit(solution)/shard_map/reduce_scatter | solution.py:567
  727.9 603.3 %reduce-scatter.45.cloned.1.call-start = ((), (), s32[]{:S(2)}) async-start(), calls=%async_computation.38 | async-start | bytes 8912896 | tf_op jit(solution)/shard_map/reduce_scatter | solution.py:570
  746.8 152.2 %copy-start.80 = (u32[32]{0:T(128)S(1)}, u32[32]{0:T(128)}, u32[]{:S(2)}) copy-start(u32[32]{0:T(128)} %constant.88) | copy-start | bytes 388
  746.9 596.1 %reduce-scatter.39.cloned.1.call-start = ((), (), s32[]{:S(2)}) async-start(), calls=%async_computation.35 | async-start | bytes 98304 | tf_op jit(solution)/shard_map/reduce_scatter | solution.py:590
  747.4 607.9 %reduce-scatter.35.cloned.1.call-start = ((), (), s32[]{:S(2)}) async-start(), calls=%async_computation.33 | async-start | bytes 196608 | tf_op jit(solution)/shard_map/reduce_scatter | solution.py:587
  748.0 621.2 %reduce-scatter.27.cloned.1.call-start = ((), (), s32[]{:S(2)}) async-start(), calls=%async_computation.29 | async-start | bytes 393216 | tf_op jit(solution)/shard_map/reduce_scatter | solution.py:581
  822.7 560.4 %reduce-scatter.31.cloned.1.call-start = ((), (), s32[]{:S(2)}) async-start(), calls=%async_computation.31 | async-start | bytes 393216 | tf_op jit(solution)/shard_map/reduce_scatter | solution.py:584
  898.4 501.6 %reduce-scatter.19.cloned.1.call-start = ((), (), s32[]{:S(2)}) async-start(), calls=%async_computation.25 | async-start | bytes 786432 | tf_op jit(solution)/shard_map/reduce_scatter | solution.py:575
  1006.1 108.6 %copy-start.15 = (bf16[1024,1024]{1,0:T(8,128)(2,1)S(1)}, bf16[1024,1024]{1,0:T(8,128)(2,1)}, u32[]{:S(2)}) copy-start(bf16[1024,1024]{1,0:T(8,128)(2,1)} %copy-done.14) | copy-start | bytes 6291460
  1006.1 410.7 %reduce-scatter.23.cloned.1.call-start = ((), (), s32[]{:S(2)}) async-start(), calls=%async_computation.27 | async-start | bytes 786432 | tf_op jit(solution)/shard_map/reduce_scatter | solution.py:578
  1114.4 319.3 %reduce-scatter.43.cloned.1.call-start = ((), (), s32[]{:S(2)}) async-start(), calls=%async_computation.37 | async-start | bytes 786432 | tf_op jit(solution)/shard_map/reduce_scatter | solution.py:593
  1138.9 83.8 %copy-start.58 = (f32[1024]{0:T(1024)S(1)}, f32[1024]{0:T(1024)}, u32[]{:S(2)}) copy-start(f32[1024]{0:T(1024)} %copy-done.57) | copy-start | bytes 12292
  1222.7 227.8 %reduce-scatter.47.cloned.1.call-start = ((), (), s32[]{:S(2)}) async-start(), calls=%async_computation.39 | async-start | bytes 786432 | tf_op jit(solution)/shard_map/reduce_scatter | solution.py:596
  1229.0 102.3 %copy-start.19 = (bf16[512,1024]{1,0:T(8,128)(2,1)S(1)}, bf16[512,1024]{1,0:T(8,128)(2,1)}, u32[]{:S(2)}) copy-start(bf16[512,1024]{1,0:T(8,128)(2,1)} %copy-done.18) | copy-start | bytes 3145732
  1229.0 102.3 %copy-start.21 = (bf16[512,1024]{1,0:T(8,128)(2,1)S(1)}, bf16[512,1024]{1,0:T(8,128)(2,1)}, u32[]{:S(2)}) copy-start(bf16[512,1024]{1,0:T(8,128)(2,1)} %copy-done.20) | copy-start | bytes 3145732
  (63 other events, 332.0 us)
Sparse Core Ops, SparseCore 0:
  14.7 38.3 all-gather.14
  55.3 73.7 all-gather.16
  131.3 73.1 all-gather.12
  206.5 48.3 all-gather.18
  256.9 40.3 all-gather.20
  299.3 49.4 all-gather.22
  351.0 73.3 all-gather.26
  426.6 73.1 all-gather.24
  626.9 55.5 reduce-scatter.36
  686.6 60.6 reduce-scatter.32
  751.1 71.4 reduce-scatter.24
  826.8 71.4 reduce-scatter.28
  902.4 103.6 reduce-scatter.16
  1010.0 104.3 reduce-scatter.20
  1118.3 104.3 reduce-scatter.40
  1226.6 104.5 reduce-scatter.44
  1333.3 9.6 reduce-scatter.38
  1345.0 10.2 reduce-scatter.34
  1357.5 11.6 reduce-scatter.26
  1371.4 11.6 reduce-scatter.30
  1385.3 14.5 reduce-scatter.18
  1402.3 14.5 reduce-scatter.22
  1419.1 14.5 reduce-scatter.42
  1435.9 14.5 reduce-scatter.46

commit v2 on v1

--- a/solution.py
+++ b/solution.py
@@ -305,6 +305,239 @@
       *outs, *logs, grad_attended, grad_inner, grad_inner)
 
 
+def lines_along_z(dp):
+    return [[line + 4 * z for z in range(dp // 4)] for line in range(4)]
+
+
+def swap(values, axis):
+    if axis == "y":
+        return lax.ppermute(values, "fsdp", [(0, 1), (1, 0)])
+    bit = {"x": 2, "core": 1}[axis]
+    return lax.ppermute(values, "dp", [(d, d ^ bit) for d in range(16)])
+
+
+def place():
+    dp = lax.axis_index("dp")
+    return jnp.stack([(dp // 2) % 2, dp % 2, lax.axis_index("fsdp")]).astype(jnp.int32)
+
+
+def assemble_kernel(sizes, place_ref, *refs):
+    x, core, y = place_ref[0], place_ref[1], place_ref[2]
+    pieces, outs = refs[:8], refs[8:]
+    half = pieces[0].shape[-1]
+    for which, piece in enumerate(pieces):
+        order, far, other = which // 4, (which // 2) % 2, which % 2
+        for near in range(2):
+            dx, dy = (near, far) if order == 0 else (far, near)
+            line = (x ^ dx) * 2 + (core ^ other)
+            at = pl.multiple_of((y ^ dy) * (2 * half) + order * half, 128)
+            row = 0
+            for size, out in zip(sizes, outs):
+                out[0, line, :, pl.ds(at, half)] = piece[near, 0, row : row + size, :]
+                row += size
+
+
+def assemble(pieces, sizes, where):
+    _, depth, rows, half = pieces[0].shape
+    outs = pl.pallas_call(
+        partial(assemble_kernel, sizes),
+        grid_spec=pltpu.PrefetchScalarGridSpec(
+            num_scalar_prefetch=1,
+            grid=(depth,),
+            in_specs=[pl.BlockSpec((2, 1, rows, half), lambda z, p: (0, z, 0, 0))] * 8,
+            out_specs=[
+                pl.BlockSpec((1, 4, size, 4 * half), lambda z, p: (z, 0, 0, 0)) for size in sizes
+            ],
+        ),
+        out_shape=[
+            jax.ShapeDtypeStruct((depth, 4, size, 4 * half), jnp.bfloat16) for size in sizes
+        ],
+        compiler_params=pltpu.CompilerParams(vmem_limit_bytes=40 * MIB),
+        cost_estimate=pl.CostEstimate(
+            flops=0, bytes_accessed=64 * depth * half * rows, transcendentals=0
+        ),
+        name="assemble",
+    )(where, *pieces)
+    return [out.reshape(-1, 4 * half) for out in outs]
+
+
+def gather_group(blocks, where):
+    packed = blocks[0] if len(blocks) == 1 else jnp.concatenate(blocks, axis=0)
+    lanes = lax.all_gather(packed, "dp", axis=0, axis_index_groups=lines_along_z(16))
+    half = packed.shape[1] // 2
+    first, second = lanes[:, :, :half], lanes[:, :, half:]
+    first = jnp.stack([first, swap(first, "x")])
+    second = jnp.stack([second, swap(second, "y")])
+    pieces = [first, swap(first, "core")]
+    far = swap(first, "y")
+    pieces += [far, swap(far, "core"), second, swap(second, "core")]
+    far = swap(second, "x")
+    pieces += [far, swap(far, "core")]
+    return assemble(pieces, [block.shape[0] for block in blocks], where)
+
+
+def add(left, right):
+    return left.astype(jnp.float32) + right.astype(jnp.float32)
+
+
+def fold_core_kernel(place_ref, keep_ref, come_ref, kx_ref, sx_ref, ky_ref, sy_ref):
+    half = come_ref.shape[-1] // 4
+    y = place_ref[2]
+
+    def along_x(out):
+        for z in range(out.shape[0]):
+            for part in range(2):
+                at = slice(2 * part * half, (2 * part + 1) * half)
+                out[z, :, part * half : (part + 1) * half] = narrow(
+                    add(keep_ref[z, 0, 0, :, at], come_ref[z, 0, :, at])
+                )
+
+    def along_y(out, side):
+        at = pl.ds(pl.multiple_of(side * 2 * half + half, 128), half)
+        for z in range(out.shape[0]):
+            out[z, 0] = narrow(add(keep_ref[z, 0, 0, :, at], come_ref[z, 0, :, at]))
+
+    @pl.when(pl.program_id(0) == 0)
+    def _():
+        along_x(kx_ref)
+
+    @pl.when(pl.program_id(0) == 1)
+    def _():
+        along_x(sx_ref)
+
+    along_y(ky_ref, y)
+    along_y(sy_ref, 1 - y)
+
+
+def fold_core(grad, come, where):
+    depth, _, _, rows, cols = grad.shape
+    half = cols // 4
+    across_x = jax.ShapeDtypeStruct((depth, rows, 2 * half), jnp.bfloat16)
+    across_y = jax.ShapeDtypeStruct((depth, 2, rows, half), jnp.bfloat16)
+    whole = pl.BlockSpec((depth, rows, 2 * half), lambda d, p: (0, 0, 0))
+    part = pl.BlockSpec((depth, 1, rows, half), lambda d, p: (0, p[0] ^ d, 0, 0))
+    return pl.pallas_call(
+        fold_core_kernel,
+        grid_spec=pltpu.PrefetchScalarGridSpec(
+            num_scalar_prefetch=1,
+            grid=(2,),
+            in_specs=[
+                pl.BlockSpec((depth, 1, 1, rows, cols), lambda d, p: (0, p[0] ^ d, p[1], 0, 0)),
+                pl.BlockSpec((depth, 1, rows, cols), lambda d, p: (0, p[0] ^ d, 0, 0)),
+            ],
+            out_specs=[whole, whole, part, part],
+        ),
+        out_shape=[across_x, across_x, across_y, across_y],
+        compiler_params=pltpu.CompilerParams(vmem_limit_bytes=40 * MIB),
+        cost_estimate=pl.CostEstimate(
+            flops=grad.size // 2, bytes_accessed=3 * grad.size, transcendentals=0
+        ),
+        name="fold_core",
+    )(where, grad, come)
+
+
+def fold_far_kernel(place_ref, kx_ref, rx_ref, ky_ref, ry_ref, kxy_ref, sxy_ref, kyx_ref, syx_ref):
+    half = kxy_ref.shape[-1]
+    x, y = place_ref[0], place_ref[2]
+    for z in range(kx_ref.shape[0]):
+        for side, out in ((y, kxy_ref), (1 - y, sxy_ref)):
+            at = pl.ds(pl.multiple_of(side * half, 128), half)
+            out[z] = narrow(add(kx_ref[z, :, at], rx_ref[z, :, at]))
+        for side, out in ((x, kyx_ref), (1 - x, syx_ref)):
+            out[z] = narrow(add(ky_ref[z, side], ry_ref[z, side]))
+
+
+def fold_far(kx, rx, ky, ry, where):
+    depth, _, rows, half = ky.shape
+    step = depth // 2
+    out = jax.ShapeDtypeStruct((depth, rows, half), jnp.bfloat16)
+    whole = pl.BlockSpec((step, rows, 2 * half), lambda z, p: (z, 0, 0))
+    pair = pl.BlockSpec((step, 2, rows, half), lambda z, p: (z, 0, 0, 0))
+    return pl.pallas_call(
+        fold_far_kernel,
+        grid_spec=pltpu.PrefetchScalarGridSpec(
+            num_scalar_prefetch=1,
+            grid=(2,),
+            in_specs=[whole, whole, pair, pair],
+            out_specs=[pl.BlockSpec((step, rows, half), lambda z, p: (z, 0, 0))] * 4,
+        ),
+        out_shape=[out] * 4,
+        compiler_params=pltpu.CompilerParams(vmem_limit_bytes=40 * MIB),
+        cost_estimate=pl.CostEstimate(
+            flops=2 * kx.size, bytes_accessed=12 * kx.size, transcendentals=0
+        ),
+        name="fold_far",
+    )(where, kx, rx, ky, ry)
+
+
+def fold_last_kernel(kxy_ref, rxy_ref, kyx_ref, ryx_ref, out_ref):
+    half = kxy_ref.shape[-1]
+    out_ref[:, :, :half] = narrow(add(kxy_ref[...], rxy_ref[...]))
+    out_ref[:, :, half:] = narrow(add(kyx_ref[...], ryx_ref[...]))
+
+
+def fold_last(kxy, rxy, kyx, ryx):
+    depth, rows, half = kxy.shape
+    step = depth // 2
+    return pl.pallas_call(
+        fold_last_kernel,
+        grid=(2,),
+        in_specs=[pl.BlockSpec((step, rows, half), lambda z: (z, 0, 0))] * 4,
+        out_specs=pl.BlockSpec((step, rows, 2 * half), lambda z: (z, 0, 0)),
+        out_shape=jax.ShapeDtypeStruct((depth, rows, 2 * half), jnp.bfloat16),
+        compiler_params=pltpu.CompilerParams(vmem_limit_bytes=40 * MIB),
+        cost_estimate=pl.CostEstimate(
+            flops=2 * kxy.size, bytes_accessed=12 * kxy.size, transcendentals=0
+        ),
+        name="fold_last",
+    )(kxy, rxy, kyx, ryx)
+
+
+def scatter_group(grad, where):
+    rows, cols = grad.shape[0] // 16, grad.shape[1]
+    grad = grad.reshape(4, 2, 2, rows, cols)
+    come = swap(lax.dynamic_index_in_dim(grad, 1 - where[1], 2, keepdims=False), "core")
+    kx, sx, ky, sy = fold_core(grad, come, where)
+    kxy, sxy, kyx, syx = fold_far(kx, swap(sx, "x"), ky, swap(sy, "y"), where)
+    line = fold_last(kxy, swap(sxy, "y"), kyx, swap(syx, "x"))
+    return lax.psum_scatter(
+        line.reshape(4 * rows, cols // 2),
+        "dp",
+        scatter_dimension=0,
+        axis_index_groups=lines_along_z(16),
+        tiled=True,
+    )
+
+
+def paired():
+    return lax.axis_size("dp") == 16 and lax.axis_size("fsdp") == 2
+
+
+def gather(blocks, where):
+    if paired():
+        return gather_group(blocks, where)
+    rows = [lax.all_gather(block, "fsdp", axis=1, tiled=True) for block in blocks]
+    return [lax.all_gather(block, "dp", axis=0, tiled=True) for block in rows]
+
+
+def scatter(grad, where):
+    if paired():
+        return scatter_group(grad, where)
+    rows = lax.psum_scatter(grad, "dp", scatter_dimension=0, tiled=True)
+    return lax.psum_scatter(rows, "fsdp", scatter_dimension=1, tiled=True)
+
+
+def gather_vectors(vectors):
+    return lax.all_gather(vectors, "fsdp", axis=1, tiled=True).astype(jnp.float32)
+
+
+def scatter_vectors(vectors):
+    every = lax.all_gather(vectors, ("dp", "fsdp"), axis=0)
+    part = vectors.shape[1] // lax.axis_size("fsdp")
+    total = jnp.sum(every, axis=0)
+    return lax.dynamic_slice_in_dim(total, lax.axis_index("fsdp") * part, part, axis=1)
+
+
 def shards(
     tokens,
     incoming,
@@ -323,44 +556,16 @@
     hidden_gain,
     gate_bias,
 ):
-    columns = (
-        lax.all_gather(token_proj, "fsdp", axis=1, tiled=True),
-        lax.all_gather(state_proj, "fsdp", axis=1, tiled=True),
-        lax.all_gather(token_out, "fsdp", axis=1, tiled=True),
-        lax.all_gather(state_out, "fsdp", axis=1, tiled=True),
-        lax.all_gather(gate_weight, "fsdp", axis=1, tiled=True),
-        lax.all_gather(init_state, "fsdp", axis=1, tiled=True),
-        lax.all_gather(hidden_in, "fsdp", axis=1, tiled=True),
-        lax.all_gather(hidden_out, "fsdp", axis=1, tiled=True),
-        lax.all_gather(token_gain, "fsdp", axis=0, tiled=True),
-        lax.all_gather(state_gain, "fsdp", axis=0, tiled=True),
-        lax.all_gather(hidden_gain, "fsdp", axis=0, tiled=True),
-        lax.all_gather(gate_bias, "fsdp", axis=0, tiled=True),
-    )
-    weights = (
-        lax.all_gather(columns[0], "dp", axis=0, tiled=True),
-        lax.all_gather(columns[1], "dp", axis=0, tiled=True),
-        lax.all_gather(columns[2], "dp", axis=0, tiled=True),
-        lax.all_gather(columns[3], "dp", axis=0, tiled=True),
-        lax.all_gather(columns[4], "dp", axis=0, tiled=True),
-        lax.all_gather(columns[5], "dp", axis=0, tiled=True),
-        lax.all_gather(columns[6], "dp", axis=0, tiled=True),
-        lax.all_gather(columns[7], "dp", axis=0, tiled=True),
-    )
-    (
-        full_token_proj,
-        full_state_proj,
-        full_token_out,
-        full_state_out,
-        full_gate_weight,
-        full_init,
-        full_hidden_in,
-        full_hidden_out,
-    ) = weights
-    token_gain_f = columns[8].astype(jnp.float32)
-    state_gain_f = columns[9].astype(jnp.float32)
-    hidden_gain_f = columns[10].astype(jnp.float32)
-    gate_bias_f = columns[11].astype(jnp.float32)
+    where = place()
+    gains = gather_vectors(jnp.stack([token_gain, state_gain, hidden_gain, gate_bias]))
+    token_gain_f, state_gain_f, hidden_gain_f, gate_bias_f = gains
+    (full_token_proj,) = gather([token_proj], where)
+    (full_state_proj,) = gather([state_proj], where)
+    full_state_out, full_gate_weight, full_token_out, full_init = gather(
+        [state_out, gate_weight, token_out, init_state], where
+    )
+    (full_hidden_in,) = gather([hidden_in], where)
+    (full_hidden_out,) = gather([hidden_out], where)
     seg_len, width = tokens.shape
     window = WINDOW
     blocks = seg_len // window
@@ -420,49 +625,19 @@
     hidden_pre = matmul(hidden_normed, full_hidden_in)
     activated = narrow(jax.nn.gelu(hidden_pre, approximate=True))
     result = middle + matmul(activated, full_hidden_out)
-    columns_back = (
-        lax.all_gather(token_proj, "fsdp", axis=1, tiled=True),
-        lax.all_gather(state_proj, "fsdp", axis=1, tiled=True),
-        lax.all_gather(token_out, "fsdp", axis=1, tiled=True),
-        lax.all_gather(state_out, "fsdp", axis=1, tiled=True),
-        lax.all_gather(gate_weight, "fsdp", axis=1, tiled=True),
-        lax.all_gather(init_state, "fsdp", axis=1, tiled=True),
-        lax.all_gather(hidden_in, "fsdp", axis=1, tiled=True),
-        lax.all_gather(hidden_out, "fsdp", axis=1, tiled=True),
-    )
-    weights_back = (
-        lax.all_gather(columns_back[0], "dp", axis=0, tiled=True),
-        lax.all_gather(columns_back[1], "dp", axis=0, tiled=True),
-        lax.all_gather(columns_back[2], "dp", axis=0, tiled=True),
-        lax.all_gather(columns_back[3], "dp", axis=0, tiled=True),
-        lax.all_gather(columns_back[4], "dp", axis=0, tiled=True),
-        lax.all_gather(columns_back[5], "dp", axis=0, tiled=True),
-        lax.all_gather(columns_back[6], "dp", axis=0, tiled=True),
-        lax.all_gather(columns_back[7], "dp", axis=0, tiled=True),
-    )
-    (
-        back_token_proj,
-        back_state_proj,
-        back_token_out,
-        back_state_out,
-        back_gate_weight,
-        back_init,
-        back_hidden_in,
-        back_hidden_out,
-    ) = weights_back
     grad_result = output_grad.astype(jnp.float32)
     grad_hidden_out = matmul_left_t(activated, output_grad)
-    grad_activated = matmul_right_t(output_grad, back_hidden_out)
+    grad_activated = matmul_right_t(output_grad, full_hidden_out)
     _, gelu_pull = jax.vjp(partial(jax.nn.gelu, approximate=True), hidden_pre)
     grad_pre = narrow(gelu_pull(grad_activated)[0])
     grad_hidden_in = matmul_left_t(hidden_normed, grad_pre)
     grad_middle_part, grad_hidden_gain = norm_back(
-        middle, hidden_gain_f, matmul_right_t(grad_pre, back_hidden_in)
+        middle, hidden_gain_f, matmul_right_t(grad_pre, full_hidden_in)
     )
     grad_middle = grad_result + grad_middle_part
     grad_branch = narrow(grad_middle)
     grad_token_out = matmul_left_t(attended, grad_branch)
-    grad_attended = narrow(matmul_right_t(grad_branch, back_token_out))
+    grad_attended = narrow(matmul_right_t(grad_branch, full_token_out))
     last = blocks - 1
     last_start = last * window
     cross_grad, last_keys_grad, last_values_grad = cross_attention_back(
@@ -483,7 +658,7 @@
         axis=1,
     )
     grad_state, grad_state_gain = norm_back(
-        state_inputs[last], state_gain_f, matmul_right_t(grad_side, back_state_proj[:, 2 * width :])
+        state_inputs[last], state_gain_f, matmul_right_t(grad_side, full_state_proj[:, 2 * width :])
     )
     grad_state_out = jnp.zeros((2 * width, width), jnp.float32)
     grad_gate_weight = jnp.zeros((width, width), jnp.float32)
@@ -502,11 +677,11 @@
         grad_gate_low = narrow(grad_gate_pre)
         grad_gate_weight = grad_gate_weight + matmul_left_t(mixed_states[block_idx], grad_gate_low)
         grad_mixed = narrow(
-            matmul_right_t(grad_gate_low, back_gate_weight)
+            matmul_right_t(grad_gate_low, full_gate_weight)
             + grad_updated * (1.0 - gate) * (1.0 - tanh_mixed * tanh_mixed)
         )
         grad_state_out = grad_state_out + matmul_left_t(inner_cats[block_idx], grad_mixed)
-        grad_inner = narrow(matmul_right_t(grad_mixed, back_state_out))
+        grad_inner = narrow(matmul_right_t(grad_mixed, full_state_out))
         parts = state_attention_back(
             projected,
             state_side,
@@ -523,7 +698,7 @@
         extra_values.insert(0, parts[6])
         grad_state_proj = grad_state_proj + matmul_left_t(normed_states[block_idx], grad_side)
         grad_state_norm, grad_gain_part = norm_back(
-            state_in, state_gain_f, matmul_right_t(grad_side, back_state_proj)
+            state_in, state_gain_f, matmul_right_t(grad_side, full_state_proj)
         )
         grad_state_gain = grad_state_gain + grad_gain_part
         grad_state = grad_direct + grad_state_norm
@@ -542,78 +717,24 @@
     )
     grad_token_proj = matmul_left_t(normed_low, grad_projected)
     grad_piece, grad_token_gain = norm_back(
-        piece, token_gain_f, matmul_right_t(grad_projected, back_token_proj)
+        piece, token_gain_f, matmul_right_t(grad_projected, full_token_proj)
     )
     tokens_grad = narrow(grad_middle + grad_piece)
-    row_parts = (
-        lax.psum_scatter(
-            grad_token_proj.astype(jnp.bfloat16), "dp", scatter_dimension=0, tiled=True
-        ).astype(jnp.float32),
-        lax.psum_scatter(
-            grad_state_proj.astype(jnp.bfloat16), "dp", scatter_dimension=0, tiled=True
-        ).astype(jnp.float32),
-        lax.psum_scatter(
-            grad_token_out.astype(jnp.bfloat16), "dp", scatter_dimension=0, tiled=True
-        ).astype(jnp.float32),
-        lax.psum_scatter(
-            grad_state_out.astype(jnp.bfloat16), "dp", scatter_dimension=0, tiled=True
-        ).astype(jnp.float32),
-        lax.psum_scatter(
-            grad_gate_weight.astype(jnp.bfloat16), "dp", scatter_dimension=0, tiled=True
-        ).astype(jnp.float32),
-        lax.psum_scatter(
-            grad_init.astype(jnp.bfloat16), "dp", scatter_dimension=0, tiled=True
-        ).astype(jnp.float32),
-        lax.psum_scatter(
-            grad_hidden_in.astype(jnp.bfloat16), "dp", scatter_dimension=0, tiled=True
-        ).astype(jnp.float32),
-        lax.psum_scatter(
-            grad_hidden_out.astype(jnp.bfloat16), "dp", scatter_dimension=0, tiled=True
-        ).astype(jnp.float32),
-    )
-    summed = (
-        lax.psum_scatter(
-            row_parts[0].astype(jnp.bfloat16), "fsdp", scatter_dimension=1, tiled=True
-        ).astype(jnp.float32),
-        lax.psum_scatter(
-            row_parts[1].astype(jnp.bfloat16), "fsdp", scatter_dimension=1, tiled=True
-        ).astype(jnp.float32),
-        lax.psum_scatter(
-            row_parts[2].astype(jnp.bfloat16), "fsdp", scatter_dimension=1, tiled=True
-        ).astype(jnp.float32),
-        lax.psum_scatter(
-            row_parts[3].astype(jnp.bfloat16), "fsdp", scatter_dimension=1, tiled=True
-        ).astype(jnp.float32),
-        lax.psum_scatter(
-            row_parts[4].astype(jnp.bfloat16), "fsdp", scatter_dimension=1, tiled=True
-        ).astype(jnp.float32),
-        lax.psum_scatter(
-            row_parts[5].astype(jnp.bfloat16), "fsdp", scatter_dimension=1, tiled=True
-        ).astype(jnp.float32),
-        lax.psum_scatter(
-            row_parts[6].astype(jnp.bfloat16), "fsdp", scatter_dimension=1, tiled=True
-        ).astype(jnp.float32),
-        lax.psum_scatter(
-            row_parts[7].astype(jnp.bfloat16), "fsdp", scatter_dimension=1, tiled=True
-        ).astype(jnp.float32),
-        lax.psum_scatter(
-            grad_token_gain.astype(jnp.bfloat16), "fsdp", scatter_dimension=0, tiled=True
-        ).astype(jnp.float32),
-        lax.psum_scatter(
-            grad_state_gain.astype(jnp.bfloat16), "fsdp", scatter_dimension=0, tiled=True
-        ).astype(jnp.float32),
-        lax.psum_scatter(
-            grad_hidden_gain.astype(jnp.bfloat16), "fsdp", scatter_dimension=0, tiled=True
-        ).astype(jnp.float32),
-        lax.psum_scatter(
-            grad_gate_bias.astype(jnp.bfloat16), "fsdp", scatter_dimension=0, tiled=True
-        ).astype(jnp.float32),
-    )
-    matrix_grads = summed[:8]
-    vector_parts = summed[8:]
-    vector_grads = lax.psum(
-        (vector_parts[0], vector_parts[1], vector_parts[2], vector_parts[3]), "dp"
-    )
+    vectors = jnp.stack([grad_token_gain, grad_state_gain, grad_hidden_gain, grad_gate_bias])
+    vector_grads = scatter_vectors(vectors)
+    matrix_grads = [
+        scatter(narrow(grad), where).astype(jnp.float32)
+        for grad in (
+            grad_token_proj,
+            grad_state_proj,
+            grad_token_out,
+            grad_state_out,
+            grad_gate_weight,
+            grad_init,
+            grad_hidden_in,
+            grad_hidden_out,
+        )
+    ]
     return (
         narrow(result),
         narrow(state)[None],

time: 1470 us -> 1090 us (0.74)
  waiting for transfers between devices: 837 us -> 301 us
  Pallas kernels: 120 us -> 208 us
  starting transfers between devices: 1.98 us -> 63.4 us
  local copies, waits for them, and re-layouts: 49.5 us -> 93.7 us
  matrix products: 275 us -> 249 us
  blocking collectives: 117 us -> 100 us
    reduce_scatter x16 -> x8, waiting for transfers between devices: 587 us -> 0.01 us  [scatter_group(): lax.psum_scatter(line.reshape(4 * rows, cols // 2), 'dp', scatter_dimensi...]
    ppermute x0 -> x80, waiting for transfers between devices: none -> 171 us  [the longest x26 96 us: swap(): return lax.ppermute(values, 'fsdp', [(0, 1), (1, 0)])]
    all_gather x8 -> x5, waiting for transfers between devices: 248 us -> 127 us  [gather_group(): lax.all_gather(packed, 'dp', axis=0, axis_index_groups=lines_along_z(16))]
    pallas_call x0 -> x29, Pallas kernels: none -> 88.8 us  [the longest x5 32.9 us: assemble(): pl.pallas_call(partial(assemble_kernel, sizes), grid_spec=pltpu.PrefetchS...]
    ppermute x0 -> x80, starting transfers between devices: none -> 62 us  [the longest x54 33.7 us: swap(): return lax.ppermute(values, 'dp', [(d, d ^ bit) for d in range(16)])]
    psum x1 -> x0, blocking collectives: 33.1 us -> none  [shards(): lax.psum((vector_parts[0], vector_parts[1], vector_parts[2], vector_parts...]
    dot_general x10, matrix products: 106 us -> 83.7 us  [matmul(): return jnp.dot(left, right, preferred_element_type=jnp.float32)]
    all_gather x12 -> x2, blocking collectives: 79.1 us -> 100 us  [the longest x1 68.9 us: scatter_vectors(): every = lax.all_gather(vectors, ('dp', 'fsdp'), axis=0)]
  transfers between devices with their start and end apart: 24 -> 93, of which waited for: 20 -> 29; matrix products, arithmetic and copies ran while one was open for 17% -> 20% of each run, Pallas kernels for 6% -> 11%
where the time goes in v2:
time: 1090 us
  waiting for transfers between devices  301 us (28%)
  matrix products  249 us (23%)
  Pallas kernels  208 us (19%)
  blocking collectives  100 us (9%)
  local copies, waits for them, and re-layouts  93.7 us (9%)
  starting transfers between devices  63.4 us (6%)
  other arithmetic  50.6 us (5%)
  between operations  19 us (2%)
    all_gather x5, waiting for transfers between devices, gather_group(): lax.all_gather(packed, 'dp', axis=0, axis_index_groups=lines_along_z(16))  127 us
    ppermute x26, waiting for transfers between devices, swap(): return lax.ppermute(values, 'fsdp', [(0, 1), (1, 0)])  96 us
    dot_general x8, matrix products, matmul_left_t(): lax.dot_general(left, right, (((0,), (0,)), ((), ())), preferred_element_...  84.3 us
    dot_general x10, matrix products, matmul(): return jnp.dot(left, right, preferred_element_type=jnp.float32)  83.7 us
    dot_general x8, matrix products, matmul_right_t(): lax.dot_general(left, right, (((1,), (1,)), ((), ())), preferred_element_...  80.7 us
    ppermute x54, waiting for transfers between devices, swap(): return lax.ppermute(values, 'dp', [(d, d ^ bit) for d in range(16)])  75.1 us
    all_gather x1, blocking collectives, scatter_vectors(): every = lax.all_gather(vectors, ('dp', 'fsdp'), axis=0)  68.9 us
    unnamed x321, local copies, waits for them, and re-layouts  57.8 us
  transfers between devices with their start and end apart: 93, of which 29 were waited for; matrix products, arithmetic and copies ran while one was open for 20% of the time, Pallas kernels for 11%

profile of v2, /device:TPU:0, one launch (start us, length us, event | category | flops | bytes accessed | tf_op | source)
XLA Modules:
  0.0 1085.4 jit_solution(13023966295824506862)
XLA Ops:
  11.9 28.4 %all-gather.13.cloned.1.call-done = bf16[256,2048]{1,0:T(8,128)(2,1)} async-done(((bf16[64,2048]{1,0:T(8,128)(2,1)}), bf16[256,2048]{1,0:T(8,128)(2,1)}) %all-gather.13.cloned.1.call-update) | async-done | bytes 1048592 | tf_op jit(solution)/shard_map/all_gather | solution.py:366
  45.5 23.8 %all-gather.17.cloned.1.call-done = bf16[256,2048]{1,0:T(8,128)(2,1)} async-done(((bf16[64,2048]{1,0:T(8,128)(2,1)}), bf16[256,2048]{1,0:T(8,128)(2,1)}) %all-gather.17.cloned.1.call-update) | async-done | bytes 1048592 | tf_op jit(solution)/shard_map/all_gather | solution.py:366
  74.9 23.4 %all-gather.21.cloned.1.call-done = bf16[1024,512]{1,0:T(8,128)(2,1)} async-done(((bf16[256,512]{1,0:T(8,128)(2,1)}), bf16[1024,512]{1,0:T(8,128)(2,1)}) %all-gather.21.cloned.1.call-update) | async-done | bytes 1048592 | tf_op jit(solution)/shard_map/all_gather | solution.py:366
  105.1 22.1 %all-gather.19.cloned.1.call-done = bf16[256,2048]{1,0:T(8,128)(2,1)} async-done(((bf16[64,2048]{1,0:T(8,128)(2,1)}), bf16[256,2048]{1,0:T(8,128)(2,1)}) %all-gather.19.cloned.1.call-update) | async-done | bytes 1048592 | tf_op jit(solution)/shard_map/all_gather | solution.py:366
  133.6 29.4 %all-gather.15.cloned.1.call-done = bf16[1408,512]{1,0:T(8,128)(2,1)} async-done(((bf16[352,512]{1,0:T(8,128)(2,1)}), bf16[1408,512]{1,0:T(8,128)(2,1)}) %all-gather.15.cloned.1.call-update) | async-done | bytes 1441808 | tf_op jit(solution)/shard_map/all_gather | solution.py:366
  173.0 10.2 collective-permute-done.8
  188.3 20.9 %collective-permute-done.2.refs_2_ = bf16[2,4,64,1024]{3,2,1,0:T(8,128)(2,1)} collective-permute-done((bf16[2,4,64,1024]{3,2,1,0:T(8,128)(2,1)S(1)}, bf16[2,4,64,1024]{3,2,1,0:T(8,128)(2,1)}, u32[]{:S(2)}, u32[]{:S(2)}) %collective-permute-start.2) | collective-permute-done | bytes 1048608 | tf_op jit(solution)/shard_map/ppermute | solution.py:314
  214.1 17.5 %collective-permute-done.18.refs_2_ = bf16[2,4,64,1024]{3,2,1,0:T(8,128)(2,1)} collective-permute-done((bf16[2,4,64,1024]{3,2,1,0:T(8,128)(2,1)S(1)}, bf16[2,4,64,1024]{3,2,1,0:T(8,128)(2,1)}, u32[]{:S(2)}, u32[]{:S(2)}) %collective-permute-start.18) | collective-permute-done | bytes 1048608 | tf_op jit(solution)/shard_map/ppermute | solution.py:314
  239.4 14.5 %collective-permute-done.34.refs_2_ = bf16[2,4,256,256]{3,2,1,0:T(8,128)(2,1)S(1)} collective-permute-done((bf16[2,4,256,256]{3,2,1,0:T(8,128)(2,1)S(1)}, bf16[2,4,256,256]{3,2,1,0:T(8,128)(2,1)S(1)}, u32[]{:S(2)}, u32[]{:S(2)}) %collective-permute-start.34) | collective-permute-done | bytes 1048608 | tf_op jit(solution)/shard_map/ppermute | solution.py:314
  261.3 13.0 %collective-permute-done.26.refs_2_ = bf16[2,4,64,1024]{3,2,1,0:T(8,128)(2,1)} collective-permute-done((bf16[2,4,64,1024]{3,2,1,0:T(8,128)(2,1)}, bf16[2,4,64,1024]{3,2,1,0:T(8,128)(2,1)}, u32[]{:S(2)}, u32[]{:S(2)}) %collective-permute-start.26) | collective-permute-done | bytes 1048608 | tf_op jit(solution)/shard_map/ppermute | solution.py:314
  274.3 7.6 collective-permute-done.30.refs_6_
  298.7 31.6 %all_gather.39 = bf16[4,1024]{1,0:T(4,128)(2,1)S(1)} all-gather(bf16[4,512]{1,0:T(4,128)(2,1)S(1)} %pad_maximum_fusion.12), channel_id=1, replica_groups=mesh['dp'=16,'fsdp'=2] {'fsdp'}, dimensions={1}, use_global_device_ids=true | all-gather | bytes 12288 | tf_op jit(solution)/shard_map/all_gather | solution.py:531
  332.8 7.3 assemble.5
  340.2 6.6 assemble.7
  346.9 6.2 assemble.9
  353.6 7.0 assemble.8
  361.2 11.9 %convolution_convert_fusion.3.q_ref.k_ref.v_ref.cq_ref.tk_ref.tv_ref = bf16[1024,4096]{1,0:T(8,128)(2,1)S(1)} fusion(bf16[1024,4096]{1,0:T(8,128)(2,1)} %bitcast.181, bf16[1024,1024]{0,1:T(8,128)(2,1)S(1)} %copy-done.68, f32[1024]{0:T(1024)S(1)} %bitcast.211, f32[1024]{0:T(1024)S(1)} %fusion.49, f32[1024]{0:T(1024)S(1)} %broadcast_multiply_fusion.2), kind=kOutput, calls=%fused_computation.20 | convolution fusion | flops 8599371776 | bytes 18886656 | tf_op jit(solution)/shard_map/dot_general | solution.py:35
  373.1 17.5 %self_attention.1 = (bf16[1024,1024]{1,0:T(8,128)(2,1)S(1)}, f32[8,1,1024]{2,1,0:T(1,128)S(1)}) custom-call(bf16[1024,4096]{1,0:T(8,128)(2,1)S(1)} %convolution_convert_fusion.3.q_ref.k_ref.v_ref.cq_ref.tk_ref.tv_ref, bf16[1024,4096]{1,0:T(8,128)(2,1)S(1)} %convolution_convert_fusion.3.q_ref.k_ref.v_ref.cq_ref.tk_ref.tv_ref, ...), custom_call_target="tpu_custom_call" | custom-call | flops 2415919104 | bytes 8388608 | tf_op jit(solution)/shard_map/self_attention/pallas_call | solution.py:123
  404.9 8.1 convolution_convert_fusion.5.sq_ref.scq_ref.sk_ref.sv_ref
  413.0 25.7 %state_attention.2 = (bf16[512,1024]{1,0:T(8,128)(2,1)S(1)}, bf16[512,1024]{1,0:T(8,128)(2,1)S(1)}, bf16[512,1024]{1,0:T(8,128)(2,1)S(1)}, f32[8,1,512]{2,1,0:T(...) custom-call(s32[1]{0:T(128)} %bitcast.12.live_ref, bf16[1024,4096]{1,0:T(8,128)(2,1)} %copy-done, ...), custom_call_target="tpu_custom_call" | custom-call | flops 3221225472 | bytes 8388608 | tf_op jit(solution)/shard_map/state_attention/pallas_call | solution.py:160
  450.2 8.7 convolution_convert_fusion.4.sq_ref.scq_ref.sk_ref.sv_ref
  458.9 25.7 %state_attention.3 = (bf16[512,1024]{1,0:T(8,128)(2,1)S(1)}, bf16[512,1024]{1,0:T(8,128)(2,1)S(1)}, bf16[512,1024]{1,0:T(8,128)(2,1)S(1)}, f32[8,1,512]{2,1,0:T(...) custom-call(s32[1]{0:T(128)} %bitcast.27.live_ref, bf16[1024,4096]{1,0:T(8,128)(2,1)} %copy-done, ...), custom_call_target="tpu_custom_call" | custom-call | flops 3221225472 | bytes 8388608 | tf_op jit(solution)/shard_map/state_attention/pallas_call | solution.py:160
  484.7 7.6 fusion.69
  492.9 15.9 %fusion.58 = f32[1024,4096]{1,0:T(8,128)} fusion(bf16[1024,4096]{1,0:T(8,128)(2,1)} %bitcast.189, f32[1024,1024]{0,1:T(8,128)S(1)} %get-tuple-element.284, f32[1024]{0:T(1024)S(1)} %bitcast.217, f32[1024]{0:T(1024)S(1)} %fusion.50, f32[1024]{0:T(1024)S(1)} %broadcast_multiply_fusion.1), kind=kOutput, calls=%fused_computation.171 | convolution fusion | flops 8594128896 | bytes 29372416 | tf_op jit(solution)/shard_map/dot_general | solution.py:35
  508.7 23.8 %fusion.6 = bf16[1024,4096]{1,0:T(8,128)(2,1)} fusion(f32[1024,4096]{1,0:T(8,128)} %fusion.58, bf16[4096,1024]{1,0:T(8,128)(2,1)} %bitcast.183, bf16[1024,1024]{1,0:T(8,128)(2,1)S(1)} %copy-done.90), kind=kOutput, calls=%fused_computation.8 | convolution fusion | flops 8673820672 | bytes 35651584 | tf_op jit(solution)/shard_map/dot_general | solution.py:45
  532.6 15.8 %multiply_reduce_fusion = (f32[1024]{0:T(1024)}, f32[1024]{0:T(1024)S(1)}, f32[1024,1024]{0,1:T(8,128)S(1)}) fusion(f32[1024,1024]{0,1:T(8,128)} %copy-done.79, f32[1024]{0:T(1024)S(1)} %fusion.50, f32[1024]{0:T(1024)S(1)} %broadcast_multiply_fusion.1, f32[1024]{0:T(1024)S(1)} %bitcast.218, bf16[1024,4096]{1,0:T(8,128)(2,1)} %fusion.6, ...), kind=kOutput, calls=%fused_computation.41 | convolution fusion | flops 8597272576 | bytes 25186304 | tf_op jit(solution)/shard_map/dot_general | solution.py:45
  558.8 12.5 %convolution_convert_fusion.7 = bf16[2048,1024]{1,0:T(8,128)(2,1)} fusion(bf16[1024,1024]{0,1:T(8,128)(2,1)S(1)} %fusion.22, bf16[512,1024]{1,0:T(8,128)(2,1)S(1)} %get-tuple-element.115.out_ref, bf16[512,1024]{1,0:T(8,128)(2,1)S(1)} %copy-done.43, bf16[1024,1024]{1,0:T(8,128)(2,1)S(1)} %get-tuple-element.108.out_ref), kind=kOutput, calls=%fused_computation.53 | convolution fusion | flops 4309647360 | bytes 10485760 | tf_op jit(solution)/shard_map/dot_general | solution.py:39
  571.4 10.0 cross_attention_back.1
  583.3 6.4 multiply_reduce_fusion.4
  602.5 22.7 %state_attention_back.1 = (bf16[512,1024]{1,0:T(8,128)(2,1)S(1)}, bf16[512,1024]{1,0:T(8,128)(2,1)S(1)}, bf16[512,1024]{1,0:T(8,128)(2,1)S(1)}, bf16[512,1024]{1...) custom-call(s32[1]{0:T(128)} %bitcast.12.live_ref, ...), custom_call_target="tpu_custom_call" | custom-call | flops 8053063680 | bytes 16777216 | tf_op jit(solution)/shard_map/state_attention_back/pallas_call | solution.py:290
  637.0 9.5 multiply_reduce_fusion.3
  651.7 18.2 %self_attention_back.1 = (bf16[1024,1024]{1,0:T(8,128)(2,1)S(1)}, bf16[1024,1024]{1,0:T(8,128)(2,1)S(1)}, bf16[1024,1024]{1,0:T(8,128)(2,1)S(1)}) custom-call(bf16[1024,4096]{1,0:T(8,128)(2,1)} %copy-done, bf16[1024,4096]{1,0:T(8,128)(2,1)} %copy-done, bf16[1024,4096]{1,0:T(8,128)(2,1)} %copy-done, bf16[1024,1024]{1,0:T(8,128)(2,1)S(1)} %copy-done.17, ...), custom_call_target="tpu_custom_call" | custom-call | flops 6039797760 | bytes 16777216 | tf_op jit(solution)/shard_map/self_attention_back/pallas_call | solution.py:205
  673.8 16.2 %convolution_convert_fusion.2 = bf16[1024,4096]{1,0:T(8,128)(2,1)} fusion(bf16[1024,1024]{0,1:T(8,128)(2,1)} %copy.37, f32[1024]{0:T(1024)S(1)} %bitcast.212, f32[1024]{0:T(1024)S(1)} %copy-done.119, f32[1024]{0:T(1024)S(1)} %copy-done.115, bf16[1024,1024]{1,0:T(8,128)(2,1)} %copy-done.60, bf16[1024,1024]{1,0:T(8,128)(2,1)} %copy-done.59, ...), kind=kOutput, calls=%fused_computation.19 | convolution fusion | flops 8641314816 | bytes 18886656 | tf_op jit(solution)/shard_map/dot_general | solution.py:39
  728.1 14.7 %convolution_convert_fusion.1 = bf16[1024,4096]{1,0:T(8,128)(2,1)} fusion(bf16[1024,4096]{1,0:T(8,128)(2,1)} %fusion.6, f32[1024,1024]{0,1:T(8,128)S(1)} %copy-done.81, f32[1024]{0:T(1024)} %bitcast.220, f32[1024]{0:T(1024)} %copy-done.130, f32[1024]{0:T(1024)S(1)} %broadcast_multiply_fusion.1), kind=kOutput, calls=%fused_computation.18 | convolution fusion | flops 8598323200 | bytes 20983808 | tf_op jit(solution)/shard_map/dot_general | solution.py:39
  746.4 8.5 fusion.59
  761.2 13.2 %add_convert_fusion = bf16[1024,4096]{1,0:T(8,128)(2,1)} fusion(f32[1024,2048]{1,0:T(8,128)} %fusion.59, bf16[512,4096]{1,0:T(8,128)(2,1)} %copy-done.113, f32[512,1024]{1,0:T(8,128)} %get-tuple-element.249, f32[512]{0:T(512)S(1)} %copy-done.137, f32[512]{0:T(512)S(1)} %copy-done.134, f32[1024]{0:T(1024)S(1)} %bitcast.210), kind=kOutput, calls=%fused_computation.14 | convolution fusion | flops 4305453056 | bytes 23076864 | tf_op jit(solution)/shard_map/dot_general | solution.py:39
  776.5 6.3 fold_core.8
  793.9 11.6 %collective-permute-done.41.rx_ref = bf16[4,64,2048]{2,1,0:T(8,128)(2,1)S(1)} collective-permute-done((bf16[4,64,2048]{2,1,0:T(8,128)(2,1)}, bf16[4,64,2048]{2,1,0:T(8,128)(2,1)S(1)}, u32[]{:S(2)}, u32[]{:S(2)}) %collective-permute-start.41) | collective-permute-done | bytes 1048608 | tf_op jit(solution)/shard_map/ppermute | solution.py:316
  811.1 9.1 collective-permute-done.43.rxy_ref
  822.9 15.5 %convolution_convert_fusion = bf16[4096,1024]{1,0:T(8,128)(2,1)S(1)} fusion(bf16[1024,1024]{1,0:T(8,128)(2,1)S(1)} %copy-done.91, f32[1024,4096]{1,0:T(8,128)} %fusion.58), kind=kOutput, calls=%fused_computation.17 | convolution fusion | flops 8631877632 | bytes 27262976 | tf_op jit(solution)/shard_map/dot_general | solution.py:39
  857.3 16.3 %collective-permute-done.46.rx_ref = bf16[4,64,2048]{2,1,0:T(8,128)(2,1)S(1)} collective-permute-done((bf16[4,64,2048]{2,1,0:T(8,128)(2,1)S(1)}, bf16[4,64,2048]{2,1,0:T(8,128)(2,1)S(1)}, u32[]{:S(2)}, u32[]{:S(2)}) %collective-permute-start.46) | collective-permute-done | bytes 1048608 | tf_op jit(solution)/shard_map/ppermute | solution.py:316
  880.0 16.1 %collective-permute-done.71.rx_ref = bf16[4,64,2048]{2,1,0:T(8,128)(2,1)S(1)} collective-permute-done((bf16[4,64,2048]{2,1,0:T(8,128)(2,1)}, bf16[4,64,2048]{2,1,0:T(8,128)(2,1)S(1)}, u32[]{:S(2)}, u32[]{:S(2)}) %collective-permute-start.71) | collective-permute-done | bytes 1048608 | tf_op jit(solution)/shard_map/ppermute | solution.py:316
  901.3 6.5 collective-permute-done.48.rxy_ref
  910.4 16.9 %add_convert_fusion.2 = bf16[1024,1024]{0,1:T(8,128)(2,1)} fusion(f32[1024,1024]{0,1:T(8,128)} %copy-done.79, bf16[4096,1024]{1,0:T(8,128)(2,1)} %bitcast.184, f32[1024,4096]{1,0:T(8,128)} %fusion.58), kind=kOutput, calls=%fused_computation.49 | convolution fusion | flops 8629780480 | bytes 31457280 | tf_op jit(solution)/shard_map/dot_general | solution.py:35
  937.4 14.7 %fusion.19 = (f32[1024]{0:T(1024)S(1)}, f32[1024,1024]{0,1:T(8,128)S(1)}) fusion(bf16[1024,1024]{0,1:T(8,128)(2,1)} %copy.37, f32[1024]{0:T(1024)S(1)} %bitcast.213, f32[1024]{0:T(1024)S(1)} %copy-done.115, bf16[1024,4096]{1,0:T(8,128)(2,1)} %bitcast.182, bf16[1024,1024]{1,0:T(8,128)(2,1)} %copy-done.60, bf16[1024,1024]{1,0:T(8,128)(2,1)} %copy-done.59, ...), kind=kOutput, calls=%fused_computation.37 | convolution fusion | flops 8637119488 | bytes 23080960 | tf_op jit(solution)/shard_map/dot_general | solution.py:45
  963.7 8.2 collective-permute-done.78.rxy_ref
  973.1 6.3 add_convert_fusion.1
  987.5 68.9 %all-gather.6 = f32[32,4,1024]{2,1,0:T(4,128)S(1)} all-gather(f32[1,4,1024]{2,1,0:T(4,128)S(1)} %maximum_bitcast_fusion), channel_id=7, replica_groups=mesh['dp'=16,'fsdp'=2] {'dp','fsdp'}, dimensions={0}, use_global_device_ids=true | all-gather | bytes 540672 | tf_op jit(solution)/shard_map/all_gather | solution.py:535
  (619 shorter events, 308.0 us)
Async XLA Ops:
  7.2 33.1 %all-gather.13.cloned.1.call-start = ((), (), s32[]{:S(2)}) async-start(), calls=%async_computation.16 | async-start | bytes 1310720 | tf_op jit(solution)/shard_map/all_gather | solution.py:366
  7.9 61.4 %all-gather.17.cloned.1.call-start = ((), (), s32[]{:S(2)}) async-start(), calls=%async_computation.18 | async-start | bytes 1310720 | tf_op jit(solution)/shard_map/all_gather | solution.py:366
  8.7 89.6 %all-gather.21.cloned.1.call-start = ((), (), s32[]{:S(2)}) async-start(), calls=%async_computation.20 | async-start | bytes 1310720 | tf_op jit(solution)/shard_map/all_gather | solution.py:366
  9.4 117.8 %all-gather.19.cloned.1.call-start = ((), (), s32[]{:S(2)}) async-start(), calls=%async_computation.19 | async-start | bytes 1310720 | tf_op jit(solution)/shard_map/all_gather | solution.py:366
  10.0 153.1 %all-gather.15.cloned.1.call-start = ((), (), s32[]{:S(2)}) async-start(), calls=%async_computation.17 | async-start | bytes 1802240 | tf_op jit(solution)/shard_map/all_gather | solution.py:366
  11.8 1053.1 %reduce-scatter.19.cloned.1.call-start = ((), (), s32[]{:S(2)}) async-start(), calls=%async_computation.13 | async-start | bytes 163840 | tf_op jit(solution)/shard_map/reduce_scatter | solution.py:503
  42.5 59.9 %collective-permute-start = (bf16[4,64,1024]{2,1,0:T(8,128)(2,1)S(1)}, bf16[4,64,1024]{2,1,0:T(8,128)(2,1)S(1)}, u32[]{:S(2)}, u32[]{:S(2)}) collective-permute-start(bf16[4,64,1024]{2,1,0:T(8,128)(2,1)S(1)} %get-tuple-element.271), channel_id=1, source_target_pairs={{0,4},{2,6},{4,0},{6,2},{8,12},{10,14},{12,8},{14,10},{16,20},{18,... | collective-permute-start | bytes 1572872 | tf_op jit(solution)/shard_map/ppermute | solution.py:316
  44.0 61.0 %collective-permute-start.4 = (bf16[4,64,1024]{2,1,0:T(8,128)(2,1)}, bf16[4,64,1024]{2,1,0:T(8,128)(2,1)}, u32[]{:S(2)}, u32[]{:S(2)}) collective-permute-start(bf16[4,64,1024]{2,1,0:T(8,128)(2,1)} %get-tuple-element.270), channel_id=1, source_target_pairs={{0,1},{1,0},{2,3},{3,2},{4,5},{5,4},{6,7},{7,6},{8,9},{9,8},{10,11... | collective-permute-start | bytes 1572872 | tf_op jit(solution)/shard_map/ppermute | solution.py:314
  71.9 58.0 %collective-permute-start.16 = (bf16[4,64,1024]{2,1,0:T(8,128)(2,1)}, bf16[4,64,1024]{2,1,0:T(8,128)(2,1)}, u32[]{:S(2)}, u32[]{:S(2)}) collective-permute-start(bf16[4,64,1024]{2,1,0:T(8,128)(2,1)} %get-tuple-element.267), channel_id=1, source_target_pairs={{0,4},{2,6},{4,0},{6,2},{8,12},{10,14},{12,8},{14,10},{16,20},{18,... | collective-permute-start | bytes 1572872 | tf_op jit(solution)/shard_map/ppermute | solution.py:316
  73.4 58.0 %collective-permute-start.20 = (bf16[4,64,1024]{2,1,0:T(8,128)(2,1)}, bf16[4,64,1024]{2,1,0:T(8,128)(2,1)S(1)}, u32[]{:S(2)}, u32[]{:S(2)}) collective-permute-start(bf16[4,64,1024]{2,1,0:T(8,128)(2,1)} %get-tuple-element.266), channel_id=1, source_target_pairs={{0,1},{1,0},{2,3},{3,2},{4,5},{5,4},{6,7},{7,6},{8,9},{9,8},{10,11... | collective-permute-start | bytes 1572872 | tf_op jit(solution)/shard_map/ppermute | solution.py:314
  100.9 65.0 %collective-permute-start.32 = (bf16[4,256,256]{2,1,0:T(8,128)(2,1)}, bf16[4,256,256]{2,1,0:T(8,128)(2,1)S(1)}, u32[]{:S(2)}, u32[]{:S(2)}) collective-permute-start(bf16[4,256,256]{2,1,0:T(8,128)(2,1)} %get-tuple-element.263), channel_id=1, source_target_pairs={{0,4},{2,6},{4,0},{6,2},{8,12},{10,14},{12,8},{14,10},{16,20},{18,... | collective-permute-start | bytes 1572872 | tf_op jit(solution)/shard_map/ppermute | solution.py:316
  102.4 65.1 %collective-permute-start.36 = (bf16[4,256,256]{2,1,0:T(8,128)(2,1)}, bf16[4,256,256]{2,1,0:T(8,128)(2,1)}, u32[]{:S(2)}, u32[]{:S(2)}) collective-permute-start(bf16[4,256,256]{2,1,0:T(8,128)(2,1)} %get-tuple-element.262), channel_id=1, source_target_pairs={{0,1},{1,0},{2,3},{3,2},{4,5},{5,4},{6,7},{7,6},{8,9},{9,8},{10,11... | collective-permute-start | bytes 1572872 | tf_op jit(solution)/shard_map/ppermute | solution.py:314
  105.0 81.7 %collective-permute-start.1 = (bf16[2,4,64,1024]{3,2,1,0:T(8,128)(2,1)S(1)}, bf16[2,4,64,1024]{3,2,1,0:T(8,128)(2,1)}, u32[]{:S(2)}, u32[]{:S(2)}) collective-permute-start(bf16[2,4,64,1024]{3,2,1,0:T(8,128)(2,1)S(1)} %pad_maximum_fusion.3.refs_0_), channel_id=1, source_target_pairs={{0,2},{2,0},{4,6},{6,4},{8,10},{10,8},{12,14},{14,12},{16,18},{18,... | collective-permute-start | bytes 3145736 | tf_op jit(solution)/shard_map/ppermute | solution.py:316
  129.9 40.3 %collective-permute-start.24 = (bf16[4,64,1024]{2,1,0:T(8,128)(2,1)}, bf16[4,64,1024]{2,1,0:T(8,128)(2,1)}, u32[]{:S(2)}, u32[]{:S(2)}) collective-permute-start(bf16[4,64,1024]{2,1,0:T(8,128)(2,1)} %get-tuple-element.259), channel_id=1, source_target_pairs={{0,4},{2,6},{4,0},{6,2},{8,12},{10,14},{12,8},{14,10},{16,20},{18,... | collective-permute-start | bytes 1572872 | tf_op jit(solution)/shard_map/ppermute | solution.py:316
  132.2 38.7 %collective-permute-start.28 = (bf16[4,64,1024]{2,1,0:T(8,128)(2,1)}, bf16[4,64,1024]{2,1,0:T(8,128)(2,1)S(1)}, u32[]{:S(2)}, u32[]{:S(2)}) collective-permute-start(bf16[4,64,1024]{2,1,0:T(8,128)(2,1)} %get-tuple-element.258), channel_id=1, source_target_pairs={{0,1},{1,0},{2,3},{3,2},{4,5},{5,4},{6,7},{7,6},{8,9},{9,8},{10,11... | collective-permute-start | bytes 1572872 | tf_op jit(solution)/shard_map/ppermute | solution.py:314
  170.2 38.9 %collective-permute-start.2 = (bf16[2,4,64,1024]{3,2,1,0:T(8,128)(2,1)S(1)}, bf16[2,4,64,1024]{3,2,1,0:T(8,128)(2,1)}, u32[]{:S(2)}, u32[]{:S(2)}) collective-permute-start(bf16[2,4,64,1024]{3,2,1,0:T(8,128)(2,1)S(1)} %pad_maximum_fusion.3.refs_0_), channel_id=1, source_target_pairs={{0,1},{1,0},{2,3},{3,2},{4,5},{5,4},{6,7},{7,6},{8,9},{9,8},{10,11... | collective-permute-start | bytes 3145736 | tf_op jit(solution)/shard_map/ppermute | solution.py:314
  170.8 38.3 %collective-permute-start.5 = (bf16[2,4,64,1024]{3,2,1,0:T(8,128)(2,1)S(1)}, bf16[2,4,64,1024]{3,2,1,0:T(8,128)(2,1)S(1)}, u32[]{:S(2)}, u32[]{:S(2)}) collective-permute-start(bf16[2,4,64,1024]{3,2,1,0:T(8,128)(2,1)S(1)} %pad_maximum_fusion.4.refs_4_), channel_id=1, source_target_pairs={{0,2},{2,0},{4,6},{6,4},{8,10},{10,8},{12,14},{14,12},{16,18},{18,... | collective-permute-start | bytes 3145736 | tf_op jit(solution)/shard_map/ppermute | solution.py:316
  186.7 44.9 %collective-permute-start.18 = (bf16[2,4,64,1024]{3,2,1,0:T(8,128)(2,1)S(1)}, bf16[2,4,64,1024]{3,2,1,0:T(8,128)(2,1)}, u32[]{:S(2)}, u32[]{:S(2)}) collective-permute-start(bf16[2,4,64,1024]{3,2,1,0:T(8,128)(2,1)S(1)} %pad_maximum_fusion.5.refs_0_), channel_id=1, source_target_pairs={{0,1},{1,0},{2,3},{3,2},{4,5},{5,4},{6,7},{7,6},{8,9},{9,8},{10,11... | collective-permute-start | bytes 3145736 | tf_op jit(solution)/shard_map/ppermute | solution.py:314
  212.6 41.3 %collective-permute-start.34 = (bf16[2,4,256,256]{3,2,1,0:T(8,128)(2,1)S(1)}, bf16[2,4,256,256]{3,2,1,0:T(8,128)(2,1)S(1)}, u32[]{:S(2)}, u32[]{:S(2)}) collective-permute-start(bf16[2,4,256,256]{3,2,1,0:T(8,128)(2,1)S(1)} %pad_maximum_fusion.9.refs_0_), channel_id=1, source_target_pairs={{0,1},{1,0},{2,3},{3,2},{4,5},{5,4},{6,7},{7,6},{8,9},{9,8},{10,11... | collective-permute-start | bytes 3145736 | tf_op jit(solution)/shard_map/ppermute | solution.py:314
  237.9 36.4 %collective-permute-start.26 = (bf16[2,4,64,1024]{3,2,1,0:T(8,128)(2,1)}, bf16[2,4,64,1024]{3,2,1,0:T(8,128)(2,1)}, u32[]{:S(2)}, u32[]{:S(2)}) collective-permute-start(bf16[2,4,64,1024]{3,2,1,0:T(8,128)(2,1)} %pad_maximum_fusion.7.refs_0_), channel_id=1, source_target_pairs={{0,1},{1,0},{2,3},{3,2},{4,5},{5,4},{6,7},{7,6},{8,9},{9,8},{10,11... | collective-permute-start | bytes 3145736 | tf_op jit(solution)/shard_map/ppermute | solution.py:314
  259.7 36.8 %collective-permute-start.7 = (bf16[2,4,64,1024]{3,2,1,0:T(8,128)(2,1)}, bf16[2,4,64,1024]{3,2,1,0:T(8,128)(2,1)}, u32[]{:S(2)}, u32[]{:S(2)}) collective-permute-start(bf16[2,4,64,1024]{3,2,1,0:T(8,128)(2,1)} %collective-permute-done.6.refs_6_), channel_id=1, source_target_pairs={{0,2},{2,0},{4,6},{6,4},{8,10},{10,8},{12,14},{14,12},{16,18},{18,... | collective-permute-start | bytes 3145736 | tf_op jit(solution)/shard_map/ppermute | solution.py:316
  260.8 37.2 %collective-permute-start.19 = (bf16[2,4,64,1024]{3,2,1,0:T(8,128)(2,1)}, bf16[2,4,64,1024]{3,2,1,0:T(8,128)(2,1)}, u32[]{:S(2)}, u32[]{:S(2)}) collective-permute-start(bf16[2,4,64,1024]{3,2,1,0:T(8,128)(2,1)} %collective-permute-done.18.refs_2_), channel_id=1, source_target_pairs={{0,2},{2,0},{4,6},{6,4},{8,10},{10,8},{12,14},{14,12},{16,18},{18,... | collective-permute-start | bytes 3145736 | tf_op jit(solution)/shard_map/ppermute | solution.py:316
  274.3 57.0 %collective-permute-start.23 = (bf16[2,4,64,1024]{3,2,1,0:T(8,128)(2,1)}, bf16[2,4,64,1024]{3,2,1,0:T(8,128)(2,1)}, u32[]{:S(2)}, u32[]{:S(2)}) collective-permute-start(bf16[2,4,64,1024]{3,2,1,0:T(8,128)(2,1)} %copy-done.30), channel_id=1, source_target_pairs={{0,2},{2,0},{4,6},{6,4},{8,10},{10,8},{12,14},{14,12},{16,18},{18,... | collective-permute-start | bytes 3145736 | tf_op jit(solution)/shard_map/ppermute | solution.py:316
  281.9 49.5 %collective-permute-start.35 = (bf16[2,4,256,256]{3,2,1,0:T(8,128)(2,1)}, bf16[2,4,256,256]{3,2,1,0:T(8,128)(2,1)}, u32[]{:S(2)}, u32[]{:S(2)}) collective-permute-start(bf16[2,4,256,256]{3,2,1,0:T(8,128)(2,1)} %copy-done.34), channel_id=1, source_target_pairs={{0,2},{2,0},{4,6},{6,4},{8,10},{10,8},{12,14},{14,12},{16,18},{18,... | collective-permute-start | bytes 3145736 | tf_op jit(solution)/shard_map/ppermute | solution.py:316
  281.9 50.0 %collective-permute-start.39 = (bf16[2,4,256,256]{3,2,1,0:T(8,128)(2,1)}, bf16[2,4,256,256]{3,2,1,0:T(8,128)(2,1)}, u32[]{:S(2)}, u32[]{:S(2)}) collective-permute-start(bf16[2,4,256,256]{3,2,1,0:T(8,128)(2,1)} %copy-done.40), channel_id=1, source_target_pairs={{0,2},{2,0},{4,6},{6,4},{8,10},{10,8},{12,14},{14,12},{16,18},{18,... | collective-permute-start | bytes 3145736 | tf_op jit(solution)/shard_map/ppermute | solution.py:316
  296.5 64.1 %collective-permute-start.10 = (bf16[2,4,352,256]{3,2,1,0:T(8,128)(2,1)S(1)}, bf16[2,4,352,256]{3,2,1,0:T(8,128)(2,1)S(1)}, u32[]{:S(2)}, u32[]{:S(2)}) collective-permute-start(bf16[2,4,352,256]{3,2,1,0:T(8,128)(2,1)S(1)} %pad_maximum_fusion.1.refs_0_), channel_id=1, source_target_pairs={{0,1},{1,0},{2,3},{3,2},{4,5},{5,4},{6,7},{7,6},{8,9},{9,8},{10,11... | collective-permute-start | bytes 4325384 | tf_op jit(solution)/shard_map/ppermute | solution.py:314
  298.1 63.0 %collective-permute-start.14 = (bf16[2,4,352,256]{3,2,1,0:T(8,128)(2,1)S(1)}, bf16[2,4,352,256]{3,2,1,0:T(8,128)(2,1)S(1)}, u32[]{:S(2)}, u32[]{:S(2)}) collective-permute-start(bf16[2,4,352,256]{3,2,1,0:T(8,128)(2,1)S(1)} %pad_maximum_fusion.2.refs_4_), channel_id=1, source_target_pairs={{0,4},{2,6},{4,0},{6,2},{8,12},{10,14},{12,8},{14,10},{16,20},{18,... | collective-permute-start | bytes 4325384 | tf_op jit(solution)/shard_map/ppermute | solution.py:316
  353.1 37.6 %collective-permute-start.9 = (bf16[2,4,352,256]{3,2,1,0:T(8,128)(2,1)S(1)}, bf16[2,4,352,256]{3,2,1,0:T(8,128)(2,1)S(1)}, u32[]{:S(2)}, u32[]{:S(2)}) collective-permute-start(bf16[2,4,352,256]{3,2,1,0:T(8,128)(2,1)S(1)} %pad_maximum_fusion.1.refs_0_), channel_id=1, source_target_pairs={{0,2},{2,0},{4,6},{6,4},{8,10},{10,8},{12,14},{14,12},{16,18},{18,... | collective-permute-start | bytes 4325384 | tf_op jit(solution)/shard_map/ppermute | solution.py:316
  353.6 37.1 %collective-permute-start.13 = (bf16[2,4,352,256]{3,2,1,0:T(8,128)(2,1)S(1)}, bf16[2,4,352,256]{3,2,1,0:T(8,128)(2,1)S(1)}, u32[]{:S(2)}, u32[]{:S(2)}) collective-permute-start(bf16[2,4,352,256]{3,2,1,0:T(8,128)(2,1)S(1)} %pad_maximum_fusion.2.refs_4_), channel_id=1, source_target_pairs={{0,2},{2,0},{4,6},{6,4},{8,10},{10,8},{12,14},{14,12},{16,18},{18,... | collective-permute-start | bytes 4325384 | tf_op jit(solution)/shard_map/ppermute | solution.py:316
  634.5 84.6 %collective-permute-start.50 = (bf16[4,2,128,1024]{3,2,1,0:T(8,128)(2,1)}, bf16[4,2,128,1024]{3,2,1,0:T(8,128)(2,1)}, u32[]{:S(2)}, u32[]{:S(2)}) collective-permute-start(bf16[4,2,128,1024]{3,2,1,0:T(8,128)(2,1)} %dynamic-slice_bitcast_fusion.5), channel_id=1, source_target_pairs={{0,2},{2,0},{4,6},{6,4},{8,10},{10,8},{12,14},{14,12},{16,18},{18,... | collective-permute-start | bytes 6291464 | tf_op jit(solution)/shard_map/ppermute | solution.py:316
  636.0 64.2 %collective-permute-start.60 = (bf16[4,2,64,1024]{3,2,1,0:T(8,128)(2,1)}, bf16[4,2,64,1024]{3,2,1,0:T(8,128)(2,1)}, u32[]{:S(2)}, u32[]{:S(2)}) collective-permute-start(bf16[4,2,64,1024]{3,2,1,0:T(8,128)(2,1)} %dynamic-slice_bitcast_fusion.6), channel_id=1, source_target_pairs={{0,2},{2,0},{4,6},{6,4},{8,10},{10,8},{12,14},{14,12},{16,18},{18,... | collective-permute-start | bytes 3145736 | tf_op jit(solution)/shard_map/ppermute | solution.py:316
  651.0 43.8 %collective-permute-start.65 = (bf16[4,2,32,1024]{3,2,1,0:T(8,128)(2,1)}, bf16[4,2,32,1024]{3,2,1,0:T(8,128)(2,1)}, u32[]{:S(2)}, u32[]{:S(2)}) collective-permute-start(bf16[4,2,32,1024]{3,2,1,0:T(8,128)(2,1)} %dynamic-slice_bitcast_fusion.7), channel_id=1, source_target_pairs={{0,2},{2,0},{4,6},{6,4},{8,10},{10,8},{12,14},{14,12},{16,18},{18,... | collective-permute-start | bytes 1572872 | tf_op jit(solution)/shard_map/ppermute | solution.py:316
  706.6 69.9 %collective-permute-start.40 = (bf16[4,2,64,4096]{3,2,1,0:T(8,128)(2,1)}, bf16[4,2,64,4096]{3,2,1,0:T(8,128)(2,1)}, u32[]{:S(2)}, u32[]{:S(2)}) collective-permute-start(bf16[4,2,64,4096]{3,2,1,0:T(8,128)(2,1)} %dynamic-slice_bitcast_fusion.3), channel_id=1, source_target_pairs={{0,2},{2,0},{4,6},{6,4},{8,10},{10,8},{12,14},{14,12},{16,18},{18,... | collective-permute-start | bytes 12582920 | tf_op jit(solution)/shard_map/ppermute | solution.py:316
  717.4 37.5 %collective-permute-start.55 = (bf16[4,2,128,1024]{3,2,1,0:T(8,128)(2,1)}, bf16[4,2,128,1024]{3,2,1,0:T(8,128)(2,1)S(1)}, u32[]{:S(2)}, u32[]{:S(2)}) collective-permute-start(bf16[4,2,128,1024]{3,2,1,0:T(8,128)(2,1)} %dynamic-slice_bitcast_fusion.4), channel_id=1, source_target_pairs={{0,2},{2,0},{4,6},{6,4},{8,10},{10,8},{12,14},{14,12},{16,18},{18,... | collective-permute-start | bytes 6291464 | tf_op jit(solution)/shard_map/ppermute | solution.py:316
  718.1 348.2 %reduce-scatter.17.cloned.1.call-start = ((), (), s32[]{:S(2)}) async-start(), calls=%async_computation.12 | async-start | bytes 327680 | tf_op jit(solution)/shard_map/reduce_scatter | solution.py:503
  743.6 324.3 %reduce-scatter.13.cloned.1.call-start = ((), (), s32[]{:S(2)}) async-start(), calls=%async_computation.10 | async-start | bytes 655360 | tf_op jit(solution)/shard_map/reduce_scatter | solution.py:503
  761.0 308.5 %reduce-scatter.15.cloned.1.call-start = ((), (), s32[]{:S(2)}) async-start(), calls=%async_computation.11 | async-start | bytes 655360 | tf_op jit(solution)/shard_map/reduce_scatter | solution.py:503
  787.7 55.2 %collective-permute-start.45 = (bf16[4,2,64,4096]{3,2,1,0:T(8,128)(2,1)}, bf16[4,2,64,4096]{3,2,1,0:T(8,128)(2,1)}, u32[]{:S(2)}, u32[]{:S(2)}) collective-permute-start(bf16[4,2,64,4096]{3,2,1,0:T(8,128)(2,1)} %dynamic-slice_bitcast_fusion.2), channel_id=1, source_target_pairs={{0,2},{2,0},{4,6},{6,4},{8,10},{10,8},{12,14},{14,12},{16,18},{18,... | collective-permute-start | bytes 12582920 | tf_op jit(solution)/shard_map/ppermute | solution.py:316
  788.6 282.5 %reduce-scatter.9.cloned.1.call-start = ((), (), s32[]{:S(2)}) async-start(), calls=%async_computation.8 | async-start | bytes 1310720 | tf_op jit(solution)/shard_map/reduce_scatter | solution.py:503
  793.4 55.1 %collective-permute-start.70 = (bf16[4,2,64,4096]{3,2,1,0:T(8,128)(2,1)}, bf16[4,2,64,4096]{3,2,1,0:T(8,128)(2,1)}, u32[]{:S(2)}, u32[]{:S(2)}) collective-permute-start(bf16[4,2,64,4096]{3,2,1,0:T(8,128)(2,1)} %dynamic-slice_bitcast_fusion.1), channel_id=1, source_target_pairs={{0,2},{2,0},{4,6},{6,4},{8,10},{10,8},{12,14},{14,12},{16,18},{18,... | collective-permute-start | bytes 12582920 | tf_op jit(solution)/shard_map/ppermute | solution.py:316
  822.6 250.3 %reduce-scatter.11.cloned.1.call-start = ((), (), s32[]{:S(2)}) async-start(), calls=%async_computation.9 | async-start | bytes 1310720 | tf_op jit(solution)/shard_map/reduce_scatter | solution.py:503
  842.9 84.4 %collective-permute-start.75 = (bf16[4,2,256,1024]{3,2,1,0:T(8,128)(2,1)}, bf16[4,2,256,1024]{3,2,1,0:T(8,128)(2,1)}, u32[]{:S(2)}, u32[]{:S(2)}) collective-permute-start(bf16[4,2,256,1024]{3,2,1,0:T(8,128)(2,1)} %dynamic-slice_bitcast_fusion), channel_id=1, source_target_pairs={{0,2},{2,0},{4,6},{6,4},{8,10},{10,8},{12,14},{14,12},{16,18},{18,... | collective-permute-start | bytes 12582920 | tf_op jit(solution)/shard_map/ppermute | solution.py:316
  854.1 42.0 %collective-permute-start.71 = (bf16[4,64,2048]{2,1,0:T(8,128)(2,1)}, bf16[4,64,2048]{2,1,0:T(8,128)(2,1)S(1)}, u32[]{:S(2)}, u32[]{:S(2)}) collective-permute-start(bf16[4,64,2048]{2,1,0:T(8,128)(2,1)} %get-tuple-element.186), channel_id=1, source_target_pairs={{0,4},{2,6},{4,0},{6,2},{8,12},{10,14},{12,8},{14,10},{16,20},{18,... | collective-permute-start | bytes 3145736 | tf_op jit(solution)/shard_map/ppermute | solution.py:316
  855.5 41.1 %collective-permute-start.72 = (bf16[4,2,64,1024]{3,2,1,0:T(8,128)(2,1)}, bf16[4,2,64,1024]{3,2,1,0:T(8,128)(2,1)}, u32[]{:S(2)}, u32[]{:S(2)}) collective-permute-start(bf16[4,2,64,1024]{3,2,1,0:T(8,128)(2,1)} %get-tuple-element.188), channel_id=1, source_target_pairs={{0,1},{1,0},{2,3},{3,2},{4,5},{5,4},{6,7},{7,6},{8,9},{9,8},{10,11... | collective-permute-start | bytes 3145736 | tf_op jit(solution)/shard_map/ppermute | solution.py:314
  899.5 35.3 %collective-permute-start.73 = (bf16[4,64,1024]{2,1,0:T(8,128)(2,1)}, bf16[4,64,1024]{2,1,0:T(8,128)(2,1)}, u32[]{:S(2)}, u32[]{:S(2)}) collective-permute-start(bf16[4,64,1024]{2,1,0:T(8,128)(2,1)} %get-tuple-element.190), channel_id=1, source_target_pairs={{0,1},{1,0},{2,3},{3,2},{4,5},{5,4},{6,7},{7,6},{8,9},{9,8},{10,11... | collective-permute-start | bytes 1572872 | tf_op jit(solution)/shard_map/ppermute | solution.py:314
  899.9 34.9 %collective-permute-start.74 = (bf16[4,64,1024]{2,1,0:T(8,128)(2,1)}, bf16[4,64,1024]{2,1,0:T(8,128)(2,1)}, u32[]{:S(2)}, u32[]{:S(2)}) collective-permute-start(bf16[4,64,1024]{2,1,0:T(8,128)(2,1)} %get-tuple-element.192), channel_id=1, source_target_pairs={{0,4},{2,6},{4,0},{6,2},{8,12},{10,14},{12,8},{14,10},{16,20},{18,... | collective-permute-start | bytes 1572872 | tf_op jit(solution)/shard_map/ppermute | solution.py:316
  910.1 164.6 %reduce-scatter.21.cloned.1.call-start = ((), (), s32[]{:S(2)}) async-start(), calls=%async_computation.14 | async-start | bytes 1310720 | tf_op jit(solution)/shard_map/reduce_scatter | solution.py:503
  937.0 139.5 %reduce-scatter.23.cloned.1.call-start = ((), (), s32[]{:S(2)}) async-start(), calls=%async_computation.15 | async-start | bytes 1310720 | tf_op jit(solution)/shard_map/reduce_scatter | solution.py:503
  (201 other events, 3842.0 us)
Sparse Core Ops, SparseCore 0:
  9.6 30.6 all-gather.12
  41.8 27.4 all-gather.16
  70.8 27.4 all-gather.20
  99.7 27.4 all-gather.18
  128.6 34.4 all-gather.14
  718.3 17.9 reduce-scatter.18
  743.7 16.7 reduce-scatter.16
  762.8 19.8 reduce-scatter.12
  788.7 19.3 reduce-scatter.14
  822.8 24.1 reduce-scatter.8
  910.2 25.0 reduce-scatter.10
  937.5 25.7 reduce-scatter.20
  973.2 25.0 reduce-scatter.22

commit v3 on v1

v3 whole, which is shorter than its diff:
```python
from functools import partial
import math

import jax
import jax.numpy as jnp
from jax import lax
from jax.experimental import pallas as pl
from jax.experimental.pallas import tpu as pltpu
from jax.sharding import PartitionSpec as P

HD = 128
WINDOW = 512
MIB = 1 << 20


norm_eps = 1e-06
masked_score = -1e30
EXP_SCALE = math.log2(math.e) / math.sqrt(HD)
RAW_SCALE = 1.0 / math.sqrt(HD)
NT = (((1,), (1,)), ((), ()))
TN = (((0,), (0,)), ((), ()))
NN = (((1,), (0,)), ((), ()))


def narrow(values):
    return values.astype(jnp.bfloat16)


def matmul_left_t(left, right):
    return lax.dot_general(left, right, TN, preferred_element_type=jnp.float32)


def launch(body, operands, *, grid, in_specs, out_specs, out_shape, name, flops, after=(), where=None, scratch=(), aliases=None, exps=0, limit=48):
    count = len(operands)
    late = len(after)
    lead = 0 if where is None else 1

    def run(*refs):
        body(*refs[: lead + count], *refs[lead + count + late :])

    specs = list(in_specs) + [pl.BlockSpec(memory_space=pl.ANY)] * late
    size = sum(math.prod(item.shape) * item.dtype.itemsize for item in (*operands, *out_shape))
    kwargs = dict(grid=grid, in_specs=specs, out_specs=list(out_specs))
    if where is None:
        kwargs["scratch_shapes"] = list(scratch)
    else:
        kwargs = dict(
            grid_spec=pltpu.PrefetchScalarGridSpec(
                num_scalar_prefetch=1, scratch_shapes=list(scratch), **kwargs
            )
        )
    return pl.pallas_call(
        run,
        out_shape=list(out_shape),
        input_output_aliases=aliases or {},
        compiler_params=pltpu.CompilerParams(vmem_limit_bytes=limit * MIB),
        cost_estimate=pl.CostEstimate(flops=int(flops), bytes_accessed=int(size), transcendentals=int(exps)),
        name=name,
        **kwargs,
    )(*(() if where is None else (where,)), *operands, *after)


def shaped(shape, dtype=jnp.bfloat16):
    return jax.ShapeDtypeStruct(shape, dtype)


def whole(shape):
    return pl.BlockSpec(shape, lambda *ids: (0,) * len(shape))


SMEM = pl.BlockSpec(memory_space=pltpu.SMEM)
F32 = jnp.float32


def norm_rows(values):
    centered = values - jnp.mean(values, axis=-1, keepdims=True)
    return centered, lax.rsqrt(jnp.mean(centered * centered, axis=-1, keepdims=True) + norm_eps)


def norm_back_rows(values, gain, grad):
    centered, inverse = norm_rows(values)
    normal = centered * inverse
    scaled = grad * gain
    mean = jnp.mean(scaled, axis=-1, keepdims=True)
    along = jnp.mean(scaled * normal, axis=-1, keepdims=True)
    return inverse * (scaled - mean - normal * along), jnp.sum(grad * normal, axis=0, keepdims=True)


ROWS = 128


def norm_project_kernel(x_ref, gain_ref, w_ref, normed_ref, out_ref):
    @pl.when(pl.program_id(0) == 0)
    def _():
        @pl.loop(0, x_ref.shape[0] // ROWS)
        def _(i):
            at = pl.ds(pl.multiple_of(i * ROWS, ROWS), ROWS)
            centered, inverse = norm_rows(x_ref[at, :].astype(F32))
            normed_ref[at, :] = narrow(centered * inverse * gain_ref[...])

    out_ref[...] = narrow(dot(normed_ref[...], w_ref[...], NN))


def norm_project(x, gain, weight, after=()):
    rows, width = x.shape
    cols = weight.shape[1]
    step = 512
    return launch(
        norm_project_kernel, [x, gain, weight], after=after, name="norm_project", grid=(cols // step,),
        in_specs=[whole((rows, width)), whole((1, width)), pl.BlockSpec((width, step), lambda i: (0, i))],
        out_specs=[whole((rows, width)), pl.BlockSpec((rows, step), lambda i: (0, i))],
        out_shape=[shaped((rows, width)), shaped((rows, cols))],
        flops=2 * rows * width * cols,
    )


def update_kernel(live_ref, self_ref, cross_ref, out_w_ref, gate_w_ref, bias_ref, state_ref, mixed_ref, gate_ref, new_ref):
    width = self_ref.shape[1]
    mixed = narrow(dot(self_ref[...], out_w_ref[:width, :], NN) + dot(cross_ref[...], out_w_ref[width:, :], NN))
    mixed_ref[...] = mixed
    gate = jax.nn.sigmoid(dot(mixed, gate_w_ref[...], NN) + bias_ref[...])
    gate_ref[...] = gate
    state = state_ref[...]
    updated = gate * state + (1.0 - gate) * jnp.tanh(mixed.astype(F32))
    new_ref[...] = state + live_ref[0] * (updated - state)


def update_state(live, inner_self, inner_cross, state_out, gate_weight, bias, state, after=()):
    rows, width = state.shape
    step = 256
    tile = pl.BlockSpec((step, width), lambda i: (i, 0))
    return launch(
        update_kernel, [live, inner_self, inner_cross, state_out, gate_weight, bias, state],
        after=after, name="update_state", grid=(rows // step,),
        in_specs=[SMEM, tile, tile, whole(state_out.shape), whole(gate_weight.shape), whole((1, width)), tile],
        out_specs=[tile, tile, tile],
        out_shape=[shaped((rows, width)), shaped((rows, width), F32), shaped((rows, width), F32)],
        flops=6 * rows * width * width, exps=2 * rows * width,
    )


def branch_kernel(self_ref, cross_ref, w_ref, x_ref, gain_ref, middle_ref, normed_ref):
    width = self_ref.shape[1]
    middle = x_ref[...].astype(F32) + (
        dot(self_ref[...], w_ref[:width, :], NN) + dot(cross_ref[...], w_ref[width:, :], NN)
    )
    middle_ref[...] = middle
    centered, inverse = norm_rows(middle)
    normed_ref[...] = narrow(centered * inverse * gain_ref[...])


def branch(self_out, cross_out, token_out, x, gain, after=()):
    rows, width = x.shape
    step = 256
    tile = pl.BlockSpec((step, width), lambda i: (i, 0))
    return launch(
        branch_kernel, [self_out, cross_out, token_out, x, gain], after=after, name="branch", grid=(rows // step,),
        in_specs=[tile, tile, whole(token_out.shape), tile, whole((1, width))],
        out_specs=[tile, tile],
        out_shape=[shaped((rows, width), F32), shaped((rows, width))],
        flops=4 * rows * width * width,
    )


GELU_A = math.sqrt(2.0 / math.pi)
GELU_B = 0.044715


def hidden_kernel(normed_ref, w_ref, active_ref, slope_ref):
    for start in range(0, normed_ref.shape[0], 256):
        at = slice(start, start + 256)
        v = dot(normed_ref[at, :], w_ref[...], NN)
        square = v * v
        t = jnp.tanh(v * (GELU_A + (GELU_A * GELU_B) * square))
        half = 0.5 + 0.5 * t
        active_ref[at, :] = narrow(v * half)
        slope = half + v * (1.0 - t * t) * (0.5 * GELU_A + (1.5 * GELU_A * GELU_B) * square)
        slope_ref[at, :] = narrow(slope)


def hidden(normed, weight, after=()):
    rows, width = normed.shape
    cols = weight.shape[1]
    step = 512
    tile = pl.BlockSpec((rows, step), lambda i: (0, i))
    return launch(
        hidden_kernel, [normed, weight], after=after, name="hidden", grid=(cols // step,),
        in_specs=[whole((rows, width)), pl.BlockSpec((width, step), lambda i: (0, i))],
        out_specs=[tile, tile], out_shape=[shaped((rows, cols))] * 2,
        flops=2 * rows * width * cols, exps=rows * cols,
    )


def result_kernel(active_ref, slope_ref, w_ref, middle_ref, grad_ref, result_ref, pre_ref, total_ref):
    first = pl.program_id(0) == 0
    for start in range(0, active_ref.shape[0], 256):
        at = slice(start, start + 256)
        pre_ref[at, :] = narrow(dot(grad_ref[at, :], w_ref[...], NT) * slope_ref[at, :].astype(F32))
        total_ref[at, :] = jnp.where(first, middle_ref[at, :], total_ref[at, :]) + dot(active_ref[at, :], w_ref[...], NN)

    @pl.when(pl.program_id(0) == pl.num_programs(0) - 1)
    def _():
        result_ref[...] = narrow(total_ref[...])


def result_and_pre(active, slope, weight, middle, grad, after=()):
    rows, hidden_units = active.shape
    width = middle.shape[1]
    step = 512
    tile = pl.BlockSpec((rows, step), lambda i: (0, i))
    return launch(
        result_kernel, [active, slope, weight, middle, grad], after=after, name="result_and_pre",
        grid=(hidden_units // step,),
        in_specs=[tile, tile, pl.BlockSpec((step, width), lambda i: (i, 0)), whole((rows, width)), whole((rows, width))],
        out_specs=[whole((rows, width)), tile],
        out_shape=[shaped((rows, width)), shaped((rows, hidden_units))],
        scratch=[pltpu.VMEM((rows, width), F32)],
        flops=4 * rows * width * hidden_units,
    )


def norm_back_kernel(parts, keep_wide, scale_ref, *refs):
    grads, (w_ref, x_ref, gain_ref, plus_ref) = refs[:parts], refs[parts : parts + 4]
    outs, total_ref = refs[parts + 4 : -1], refs[-1]
    i = pl.program_id(0)
    share = pl.num_programs(0) // parts

    @pl.when(i == 0)
    def _():
        total_ref[...] = jnp.zeros_like(total_ref)

    for part in range(parts):
        @pl.when(i // share == part)
        def _():
            total_ref[...] += dot(grads[part][...], w_ref[...], NT)

    @pl.when(i == pl.num_programs(0) - 1)
    def _():
        outs[0][...] = jnp.zeros_like(outs[0])

        @pl.loop(0, x_ref.shape[0] // ROWS)
        def _(j):
            at = pl.ds(pl.multiple_of(j * ROWS, ROWS), ROWS)
            grad, gain_grad = norm_back_rows(x_ref[at, :].astype(F32), gain_ref[...], total_ref[at, :])
            grad = grad + plus_ref[at, :].astype(F32)
            outs[0][...] += gain_grad
            outs[1][at, :] = narrow(jnp.where(scale_ref[0] > 0.0, grad, 0.0))
            if keep_wide:
                outs[2][at, :] = grad


def norm_back_project(grads, weight, x, gain, plus, name, keep_wide=False, offset=0, scale=None, after=()):
    rows, width = x.shape
    step = 512
    share = grads[0].shape[1] // step
    parts = len(grads)
    steps = parts * share
    def part_spec(part):
        return pl.BlockSpec((rows, step), lambda i: (0, jnp.clip(i - part * share, 0, share - 1)))
    out_shape = [shaped((1, width), F32), shaped((rows, width))]
    if keep_wide:
        out_shape.append(shaped((rows, width), F32))
    if scale is None:
        scale = jnp.ones((1,), F32)
    return launch(
        partial(norm_back_kernel, parts, keep_wide), [scale, *grads, weight, x, gain, plus], after=after, name=name,
        grid=(steps,),
        in_specs=[SMEM] + [part_spec(part) for part in range(parts)]
        + [pl.BlockSpec((width, step), lambda i: (0, i + offset // step)), whole((rows, width)), whole((1, width)), whole((rows, width))],
        out_specs=[whole(item.shape) for item in out_shape], out_shape=out_shape,
        scratch=[pltpu.VMEM((rows, width), F32)],
        flops=2 * rows * width * steps * step,
    )


def spread_kernel(grad_ref, w_ref, out_ref):
    out_ref[...] = narrow(dot(grad_ref[...], w_ref[...], NT))


def spread(grad, weight, after=()):
    rows, width = grad.shape
    cols = weight.shape[0]
    step = 512
    return launch(
        spread_kernel, [grad, weight], after=after, name="spread", grid=(cols // step,),
        in_specs=[whole((rows, width)), pl.BlockSpec((step, width), lambda i: (i, 0))],
        out_specs=[pl.BlockSpec((rows, step), lambda i: (0, i))],
        out_shape=[shaped((rows, cols))], flops=2 * rows * width * cols,
    )[0]


def gate_back_kernel(live_ref, grad_ref, gate_ref, state_ref, mixed_ref, gate_w_ref, out_w_ref,
                     pre_ref, grad_mixed_ref, inner_ref, direct_ref, bias_ref):
    grad, gate, live = grad_ref[...], gate_ref[...], live_ref[0]
    tanh_mixed = jnp.tanh(mixed_ref[...].astype(F32))
    updated = live * grad
    direct_ref[...] = (1.0 - live) * grad + updated * gate
    pre = gate * (1.0 - gate) * updated * (state_ref[...] - tanh_mixed)

    @pl.when(pl.program_id(0) == 0)
    def _():
        bias_ref[...] = jnp.zeros_like(bias_ref)

    bias_ref[...] += jnp.sum(pre, axis=0, keepdims=True)
    low = narrow(pre)
    pre_ref[...] = low
    grad_mixed = narrow(
        dot(low, gate_w_ref[...], NT) + updated * (1.0 - gate) * (1.0 - tanh_mixed * tanh_mixed)
    )
    grad_mixed_ref[...] = grad_mixed
    inner_ref[...] = narrow(dot(grad_mixed, out_w_ref[...], NT))


def gate_back(live, grad, gate, state, mixed, gate_weight, state_out, after=()):
    rows, width = grad.shape
    step = 256
    tile = pl.BlockSpec((step, width), lambda i: (i, 0))
    wide = pl.BlockSpec((step, 2 * width), lambda i: (i, 0))
    return launch(
        gate_back_kernel, [live, grad, gate, state, mixed, gate_weight, state_out], after=after, name="gate_back",
        grid=(rows // step,),
        in_specs=[SMEM, tile, tile, tile, tile, whole(gate_weight.shape), whole(state_out.shape)],
        out_specs=[tile, tile, wide, tile, whole((1, width))],
        out_shape=[shaped((rows, width)), shaped((rows, width)), shaped((rows, 2 * width)), shaped((rows, width), F32), shaped((1, width), F32)],
        flops=6 * rows * width * width, exps=rows * width,
    )


def weight_grad_kernel(rows, plan, split, counts, place_ref, *refs):
    lefts, rights = refs[: counts[0]], refs[counts[0] : counts[0] + counts[1]]
    keep_ref, send_ref = refs[-2], refs[-1]
    core = place_ref[1]

    def run(which):
        turned = [lefts[item][...].T for item in which]
        col = 0
        for terms in plan:
            cols = rights[terms[0][1]].shape[1]
            for start in range(0, cols, 512):
                total = sum(
                    dot(turned[left], rights[right][:, start : start + 512], NN) for left, right in terms
                )
                total = narrow(total)
                at = slice(col + start, col + start + 512)
                for x in range(2):
                    even = total[2 * x * rows : (2 * x + 1) * rows]
                    odd = total[(2 * x + 1) * rows : (2 * x + 2) * rows]
                    keep_ref[0, x, :, at] = jnp.where(core == 0, even, odd)
                    send_ref[0, x, :, at] = jnp.where(core == 0, odd, even)
            col += cols

    if split:
        @pl.when(pl.program_id(0) < 2)
        def _():
            run([0])

        @pl.when(pl.program_id(0) >= 2)
        def _():
            run([1])
    else:
        run(range(len(lefts)))


def weight_grad(lefts, rights, plan, where, name, split=False, after=()):
    tokens = lefts[0].shape[0]
    total_rows = lefts[0].shape[1] * (len(lefts) if split else 1)
    rows = total_rows // 16
    cols = sum(rights[terms[0][1]].shape[1] for terms in plan)
    if split:
        left_specs = [
            pl.BlockSpec((tokens, 4 * rows), lambda z, p: (0, jnp.minimum(z, 1))),
            pl.BlockSpec((tokens, 4 * rows), lambda z, p: (0, jnp.maximum(z, 2) - 2)),
        ]
    else:
        left_specs = [pl.BlockSpec((item.shape[0], 4 * rows), lambda z, p: (0, z)) for item in lefts]
    out = pl.BlockSpec((1, 2, rows, cols), lambda z, p: (z, 0, 0, 0))
    return launch(
        partial(weight_grad_kernel, rows, plan, split, (len(lefts), len(rights))), [*lefts, *rights],
        where=where, after=after, name=name, grid=(4,),
        in_specs=left_specs + [whole(item.shape) for item in rights],
        out_specs=[out, out], out_shape=[shaped((4, 2, rows, cols))] * 2,
        flops=2 * tokens * total_rows * cols, limit=56,
    )


def dot(a, b, dims):
    return lax.dot_general(a, b, dims, preferred_element_type=jnp.float32)


def attend_tile(q, k, v, mask):
    scores = dot(k, q, NT)
    if mask is not None:
        scores = jnp.where(mask, scores, masked_score)
    top = jnp.max(scores, axis=0, keepdims=True)
    weights = jnp.exp2((scores - top) * EXP_SCALE)
    total = jnp.sum(weights, axis=0, keepdims=True)
    mixed = dot(v, weights.astype(jnp.bfloat16), TN) / total
    return mixed.T.astype(jnp.bfloat16), top * EXP_SCALE + jnp.log2(total)


def attend_back_tile(q, k, v, mask, log_total, grad_out, delta):
    probs = jnp.exp2(dot(k, q, NT) * EXP_SCALE - log_total)
    if mask is not None:
        probs = jnp.where(mask, probs, 0.0)
    grad_probs = dot(v, grad_out, NT)
    grad_raw = (probs * (grad_probs - delta)).astype(jnp.bfloat16)
    grad_v = dot(probs.astype(jnp.bfloat16), grad_out, NN)
    grad_k = dot(grad_raw, q, NN)
    grad_q = dot(k, grad_raw, TN)
    return grad_q, grad_k, grad_v


def row_delta(out, grad_out):
    both = out.astype(jnp.float32) * grad_out.astype(jnp.float32)
    return jnp.sum(both.T, axis=0, keepdims=True)


def band_mask(rows, cols, key_start, query_start, window):
    key = lax.broadcasted_iota(jnp.int32, (rows, cols), 0) + key_start
    query = lax.broadcasted_iota(jnp.int32, (rows, cols), 1) + query_start
    return (key <= query) & (key > query - window)


TILE = 256


def self_kernel(window, q_ref, k_ref, v_ref, out_ref, log_ref):
    rows = q_ref.shape[0]
    for start in range(0, rows, TILE):
        low = max(0, start - window)
        size = start + TILE - low
        mask = band_mask(size, TILE, low, start, window)
        out, log = attend_tile(
            q_ref[start : start + TILE, :], k_ref[low : low + size, :], v_ref[low : low + size, :], mask
        )
        out_ref[start : start + TILE, :] = out
        log_ref[0, :, start : start + TILE] = log


def column(rows, offset):
    return pl.BlockSpec((rows, HD), lambda h: (0, h + offset))


def stat(rows):
    return pl.BlockSpec((1, 1, rows), lambda h: (h, 0, 0))


def self_attention(projected, window, after=()):
    rows, width = projected.shape
    heads = width // 4 // HD
    return launch(
        partial(self_kernel, window), [projected] * 3, after=after, name="self_attention", grid=(heads,),
        in_specs=[column(rows, 0), column(rows, 2 * heads), column(rows, 3 * heads)],
        out_specs=[column(rows, 0), stat(rows)],
        out_shape=[shaped((rows, width // 4)), shaped((heads, 1, rows), F32)],
        flops=heads * 4 * 2304 * 256 * HD, exps=heads * 2304 * 256,
    )


def block_column(rows, block, offset):
    return pl.BlockSpec((rows, HD), lambda h: (block, h + offset))


def cross_kernel(q_ref, k_ref, v_ref, *refs):
    out_ref, log_ref = refs[-2:]
    for start in range(0, q_ref.shape[0], TILE):
        at = slice(start, start + TILE)
        out_ref[at, :], log_ref[0, :, at] = attend_tile(q_ref[at, :], k_ref[...], v_ref[...], None)


def cross_attention(projected, state_side, block, before=None, after=()):
    rows, width = state_side.shape
    heads = width // 4 // HD
    operands = [projected, state_side, state_side]
    specs = [block_column(rows, block, heads), column(rows, 2 * heads), column(rows, 3 * heads)]
    if before is not None:
        operands.append(before)
        specs.append(pl.BlockSpec(memory_space=pl.ANY))
    return launch(
        cross_kernel, operands, after=after, name="cross_attention", grid=(heads,), in_specs=specs,
        out_specs=[block_column(rows, block, 0), stat(rows)],
        out_shape=[shaped((projected.shape[0], width // 4)), shaped((heads, 1, rows), F32)],
        aliases=None if before is None else {3: 0},
        flops=heads * 4 * rows * rows * HD, exps=heads * rows * rows,
    )


def inner_kernel(live_ref, sq_ref, scq_ref, sk_ref, sv_ref, tk_ref, tv_ref, self_ref, cross_ref, self_log, cross_log):
    rows = sq_ref.shape[0]
    for start in range(0, rows, TILE):
        at = slice(start, start + TILE)
        self_ref[at, :], self_log[0, :, at] = attend_tile(sq_ref[at, :], sk_ref[...], sv_ref[...], None)
        key = lax.broadcasted_iota(jnp.int32, (rows, TILE), 0)
        cross_ref[at, :], cross_log[0, :, at] = attend_tile(
            scq_ref[at, :], tk_ref[...], tv_ref[...], key < live_ref[0]
        )


def inner_attention(projected, state_side, live_keys, block, after=()):
    rows, width = state_side.shape
    heads = width // 4 // HD
    return launch(
        inner_kernel, [live_keys] + [state_side] * 4 + [projected] * 2, after=after, name="inner_attention", grid=(heads,),
        in_specs=[SMEM] + [column(rows, part * heads) for part in range(4)]
        + [block_column(rows, block, 2 * heads), block_column(rows, block, 3 * heads)],
        out_specs=[column(rows, 0)] * 2 + [stat(rows)] * 2,
        out_shape=[shaped((rows, width // 4))] * 2 + [shaped((heads, 1, rows), F32)] * 2,
        flops=heads * 8 * rows * rows * HD, exps=2 * heads * rows * rows,
    )


def self_back_kernel(window, q_ref, k_ref, v_ref, out_ref, log_ref, grad_ref, ek_ref, ev_ref, gq_ref, gk_ref, gv_ref, sk_ref, sv_ref):
    rows = q_ref.shape[0]
    extra = ek_ref.shape[0]
    sk_ref[...] = jnp.zeros_like(sk_ref)
    sv_ref[:extra, :] = ev_ref[...]
    sv_ref[extra:, :] = jnp.zeros((rows - extra, HD), jnp.float32)
    for start in range(0, rows, TILE):
        at = slice(start, start + TILE)
        low = max(0, start - window)
        size = start + TILE - low
        keys = slice(low, low + size)
        mask = band_mask(size, TILE, low, start, window)
        grad_out = grad_ref[at, :]
        grad_q, grad_k, grad_v = attend_back_tile(
            q_ref[at, :], k_ref[keys, :], v_ref[keys, :], mask, log_ref[0, :, at], grad_out,
            row_delta(out_ref[at, :], grad_out))
        gq_ref[at, :] = (grad_q * RAW_SCALE).T.astype(jnp.bfloat16)
        sk_ref[keys, :] += grad_k
        sv_ref[keys, :] += grad_v
    gk_ref[:extra, :] = (sk_ref[:extra, :] * RAW_SCALE + ek_ref[...]).astype(jnp.bfloat16)
    gk_ref[extra:, :] = (sk_ref[extra:, :] * RAW_SCALE).astype(jnp.bfloat16)
    gv_ref[...] = sv_ref[...].astype(jnp.bfloat16)


def cross_back_kernel(cq_ref, sk_ref, sv_ref, out_ref, log_ref, grad_ref, gq_ref, gk_ref, gv_ref):
    rows = cq_ref.shape[0]
    total_k = total_v = 0.0
    for start in range(0, rows, TILE):
        at = slice(start, start + TILE)
        grad_out = grad_ref[at, :]
        grad_q, grad_k, grad_v = attend_back_tile(
            cq_ref[at, :], sk_ref[...], sv_ref[...], None, log_ref[0, :, at], grad_out,
            row_delta(out_ref[at, :], grad_out))
        gq_ref[at, :] = (grad_q * RAW_SCALE).T.astype(jnp.bfloat16)
        total_k = total_k + grad_k
        total_v = total_v + grad_v
    gk_ref[...] = (total_k * RAW_SCALE).astype(jnp.bfloat16)
    gv_ref[...] = total_v.astype(jnp.bfloat16)


def state_back_kernel(live_ref, cq_ref, sq_ref, scq_ref, sk_ref, sv_ref, tk_ref, tv_ref,
                      co_ref, so_ref, io_ref, cl_ref, sl_ref, il_ref, cg_ref, sg_ref, ig_ref, before_ref,
                      gcq_ref, gsq_ref, gscq_ref, gsk_ref, gsv_ref, gtk_ref, gtv_ref):
    rows = cq_ref.shape[0]
    sums = [0.0] * 4
    for start in range(0, rows, TILE):
        at = slice(start, start + TILE)
        key = lax.broadcasted_iota(jnp.int32, (rows, TILE), 0)
        for q_ref, k_ref, v_ref, o_ref, l_ref, g_ref, gq_ref, mask, slot in (
            (cq_ref, sk_ref, sv_ref, co_ref, cl_ref, cg_ref, gcq_ref, None, 0),
            (sq_ref, sk_ref, sv_ref, so_ref, sl_ref, sg_ref, gsq_ref, None, 0),
            (scq_ref, tk_ref, tv_ref, io_ref, il_ref, ig_ref, gscq_ref, key < live_ref[0], 2),
        ):
            grad_out = g_ref[at, :]
            grad_q, grad_k, grad_v = attend_back_tile(
                q_ref[at, :], k_ref[...], v_ref[...], mask, l_ref[0, :, at], grad_out,
                row_delta(o_ref[at, :], grad_out))
            gq_ref[at, :] = (grad_q * RAW_SCALE).T.astype(jnp.bfloat16)
            sums[slot] = sums[slot] + grad_k
            sums[slot + 1] = sums[slot + 1] + grad_v
    gsk_ref[...] = (sums[0] * RAW_SCALE).astype(jnp.bfloat16)
    gsv_ref[...] = sums[1].astype(jnp.bfloat16)
    gtk_ref[...] = sums[2] * RAW_SCALE
    gtv_ref[...] = sums[3]


def self_attention_back(projected, out, log, grad_attended, extra_k, extra_v, window, after=()):
    rows, width = projected.shape
    heads = width // 4 // HD
    extra = extra_k.shape[0]
    return launch(
        partial(self_back_kernel, window), [projected] * 3 + [out, log, grad_attended, extra_k, extra_v],
        after=after, name="self_attention_back", grid=(heads,),
        in_specs=[column(rows, 0), column(rows, 2 * heads), column(rows, 3 * heads), column(rows, 0), stat(rows),
                  column(rows, 0), column(extra, 0), column(extra, 0)],
        out_specs=[column(rows, 0)] * 3, out_shape=[shaped((rows, width // 4))] * 3,
        scratch=[pltpu.VMEM((rows, HD), F32)] * 2,
        flops=heads * 10 * 2304 * 256 * HD, exps=heads * 2304 * 256,
    )


def cross_attention_back(projected, state_side, out, log, grad_attended, block, after=()):
    rows, width = state_side.shape
    heads = width // 4 // HD
    return launch(
        cross_back_kernel, [projected, state_side, state_side, out, log, grad_attended],
        after=after, name="cross_attention_back", grid=(heads,),
        in_specs=[block_column(rows, block, heads), column(rows, 2 * heads), column(rows, 3 * heads),
                  block_column(rows, block, 0), stat(rows), block_column(rows, block, heads)],
        out_specs=[block_column(rows, block, 0), column(rows, 0), column(rows, 0)],
        out_shape=[shaped((projected.shape[0], width // 4))] + [shaped((rows, width // 4))] * 2,
        flops=heads * 10 * rows * rows * HD, exps=heads * rows * rows,
    )


def state_attention_back(projected, state_side, live_keys, cross, inner_self, inner_cross, grad_attended, grad_inner, before, block, after=()):
    rows, width = state_side.shape
    heads = width // 4 // HD
    grad, wide = shaped((rows, width // 4)), shaped((rows, width // 4), F32)
    return launch(
        state_back_kernel,
        [live_keys, projected] + [state_side] * 4 + [projected] * 2
        + [cross[0], inner_self[0], inner_cross[0], cross[1], inner_self[1], inner_cross[1]]
        + [grad_attended, grad_inner, grad_inner, before],
        after=after, name="state_attention_back", grid=(heads,),
        in_specs=[SMEM, block_column(rows, block, heads)] + [column(rows, part * heads) for part in range(4)]
        + [block_column(rows, block, 2 * heads), block_column(rows, block, 3 * heads)]
        + [block_column(rows, block, 0), column(rows, 0), column(rows, 0)] + [stat(rows)] * 3
        + [block_column(rows, block, heads), column(rows, 0), column(rows, heads), pl.BlockSpec(memory_space=pl.ANY)],
        out_specs=[block_column(rows, block, 0)] + [column(rows, 0)] * 6,
        out_shape=[shaped((projected.shape[0], width // 4))] + [grad] * 4 + [wide] * 2,
        aliases={17: 0},
        flops=heads * 30 * rows * rows * HD, exps=3 * heads * rows * rows,
    )


def swap(values, axis):
    if axis == "y":
        return lax.ppermute(values, "fsdp", [(0, 1), (1, 0)])
    bit = {"core": 1, "x": 2, "z_low": 4, "z_high": 8}[axis]
    return lax.ppermute(values, "dp", [(d, d ^ bit) for d in range(16)])


LINES = [[line + 4 * z for z in range(4)] for line in range(4)]


def place():
    dp = lax.axis_index("dp")
    return jnp.stack([(dp // 2) % 2, dp % 2, lax.axis_index("fsdp")]).astype(jnp.int32)


def assemble_kernel(sizes, place_ref, *refs):
    x, core, y = place_ref[0], place_ref[1], place_ref[2]
    pieces, outs = refs[:10], refs[10:]
    cols = pieces[0].shape[-1]

    def put(piece, dx, dy, other):
        line = (x ^ dx) * 2 + (core ^ other)
        at = pl.ds(pl.multiple_of((y ^ dy) * cols, 128), cols)
        row = 0
        for size, out in zip(sizes, outs):
            out[0, line, :, at] = piece[0, row : row + size, :]
            row += size

    for other in range(2):
        put(pieces[5 * other], 0, 0, other)
        put(pieces[5 * other + 1], 1, 0, other)
        put(pieces[5 * other + 2], 0, 1, other)

        @pl.when(pl.program_id(0) < 2)
        def _():
            put(pieces[5 * other + 3], 1, 1, other)

        @pl.when(pl.program_id(0) >= 2)
        def _():
            put(pieces[5 * other + 4], 1, 1, other)


def assemble(pieces, sizes, where, after=()):
    _, rows, cols = pieces[0].shape
    full = pl.BlockSpec((1, rows, cols), lambda z, p: (z, 0, 0))
    low = pl.BlockSpec((1, rows, cols), lambda z, p: (jnp.minimum(z, 1), 0, 0))
    high = pl.BlockSpec((1, rows, cols), lambda z, p: (jnp.maximum(z, 2) - 2, 0, 0))
    outs = launch(
        partial(assemble_kernel, sizes), pieces, where=where, after=after, name="assemble", grid=(4,),
        in_specs=[full, full, full, low, high] * 2,
        out_specs=[pl.BlockSpec((1, 4, size, 2 * cols), lambda z, p: (z, 0, 0, 0)) for size in sizes],
        out_shape=[shaped((4, 4, size, 2 * cols)) for size in sizes],
        flops=0,
    )
    return [out.reshape(-1, 2 * cols) for out in outs]


def gather_pieces(blocks):
    packed = blocks[0] if len(blocks) == 1 else jnp.concatenate(blocks, axis=0)
    line = lax.all_gather(packed, "dp", axis=0, axis_index_groups=LINES)
    over_x, over_y = swap(line, "x"), swap(line, "y")
    near = [line, over_x, over_y, swap(over_x[:2], "y"), swap(over_y[2:], "x")]
    return near + [swap(piece, "core") for piece in near]


def add(*terms):
    return sum(term.astype(F32) for term in terms)


def fold_core_kernel(place_ref, keep_ref, come_ref, low_ref, high_ref, px_ref, py_ref, own_ref):
    x, y = place_ref[0], place_ref[2]
    cols = own_ref.shape[-1]

    def total(z, dx, dy):
        at = pl.ds(pl.multiple_of((y ^ dy) * cols, 128), cols)
        return narrow(add(keep_ref[z, x ^ dx, :, at], come_ref[z, x ^ dx, :, at]))

    for z in range(2):
        own_ref[z] = total(z, 0, 0)
        px_ref[z] = total(z, 1, 0)
        py_ref[z] = total(z, 0, 1)

    @pl.when(pl.program_id(0) == 0)
    def _():
        for z in range(2):
            low_ref[z] = total(z, 1, 1)

    @pl.when(pl.program_id(0) == 1)
    def _():
        for z in range(2):
            high_ref[z] = total(z, 1, 1)


def fold_core(keep, come, where, after=()):
    _, _, rows, cols = keep.shape
    pair = pl.BlockSpec((2, 2, rows, cols), lambda i, p: (i, 0, 0, 0))
    half = pl.BlockSpec((2, rows, cols // 2), lambda i, p: (0, 0, 0))
    full = pl.BlockSpec((2, rows, cols // 2), lambda i, p: (i, 0, 0))
    return launch(
        fold_core_kernel, [keep, come], where=where, after=after, name="fold_core", grid=(2,),
        in_specs=[pair, pair], out_specs=[half, half, full, full, full],
        out_shape=[shaped((2, rows, cols // 2))] * 2 + [shaped((4, rows, cols // 2))] * 3,
        flops=keep.size,
    )


def fold_mid_kernel(px_ref, py_ref, rx_ref, ry_ref, px_out, py_out):
    px_out[...] = narrow(add(px_ref[...], ry_ref[...]))
    py_out[...] = narrow(add(py_ref[...], rx_ref[...]))


def fold_mid(px, py, rx, ry, after=()):
    block = rx.shape
    low = pl.BlockSpec(block, lambda i: (0, 0, 0))
    high = pl.BlockSpec(block, lambda i: (1, 0, 0))
    return launch(
        fold_mid_kernel, [px, py, rx, ry], after=after, name="fold_mid", grid=(1,),
        in_specs=[high, low, low, low], out_specs=[high, low],
        out_shape=[shaped(px.shape), shaped(py.shape)], aliases={0: 0, 1: 1}, flops=px.size,
    )


def fold_last_kernel(own_ref, rx_ref, ry_ref, out_ref):
    out_ref[...] = narrow(add(own_ref[...], rx_ref[...], ry_ref[...]))


def fold_last(own, rx, ry, after=()):
    _, rows, cols = own.shape
    block = pl.BlockSpec((2, rows, cols), lambda i: (i, 0, 0))
    return launch(
        fold_last_kernel, [own, rx, ry], after=after, name="fold_last", grid=(2,),
        in_specs=[block] * 3, out_specs=[block], out_shape=[shaped(own.shape)], flops=2 * own.size,
    )[0]


class Scatter:
    def __init__(self, keep, send, where):
        self.where, self.keep = where, keep
        self.come = swap(send, "core")

    def core(self, after):
        low, high, self.px, self.py, self.own = fold_core(self.keep, self.come, self.where, after)
        self.rx, self.ry = swap(low, "x"), swap(high, "y")
        return self.own

    def mid(self, after):
        px, py = fold_mid(self.px, self.py, self.rx, self.ry, after)
        self.rx, self.ry = swap(px, "x"), swap(py, "y")
        return px

    def last(self, after):
        line = fold_last(self.own, self.rx, self.ry, after)
        rows, cols = line.shape[1:]
        self.out = lax.psum_scatter(
            line.reshape(4 * rows, cols), "dp", scatter_dimension=0, axis_index_groups=LINES, tiled=True
        )
        return line


def paired():
    return lax.axis_size("dp") == 16 and lax.axis_size("fsdp") == 2


def gather_plain(block):
    return lax.all_gather(lax.all_gather(block, "fsdp", axis=1, tiled=True), "dp", axis=0, tiled=True)


def scatter_plain(grad):
    rows = lax.psum_scatter(grad, "dp", scatter_dimension=0, tiled=True)
    return lax.psum_scatter(rows, "fsdp", scatter_dimension=1, tiled=True)


def gather_vectors(vectors):
    if not paired():
        return lax.all_gather(vectors, "fsdp", axis=1, tiled=True).astype(F32)
    other = swap(vectors, "y")
    first = lax.axis_index("fsdp") == 0
    return jnp.concatenate(
        [jnp.where(first, vectors, other), jnp.where(first, other, vectors)], axis=1
    ).astype(F32)


def scatter_vectors(vectors):
    part = vectors.shape[1] // lax.axis_size("fsdp")
    y = lax.axis_index("fsdp")
    if not paired():
        total = lax.psum(vectors, ("dp", "fsdp"))
        return lax.dynamic_slice_in_dim(total, y * part, part, axis=1)
    low, high = vectors[:, :part], vectors[:, part:]
    total = jnp.where(y == 0, low, high) + swap(jnp.where(y == 0, high, low), "y")
    for axis in ("core", "x", "z_low", "z_high"):
        total = total + swap(total, axis)
    return total


def shards(
    tokens,
    incoming,
    document_lengths,
    output_grad,
    token_proj,
    state_proj,
    token_out,
    state_out,
    gate_weight,
    init_state,
    hidden_in,
    hidden_out,
    token_gain,
    state_gain,
    hidden_gain,
    gate_bias,
):
    seg_len, width = tokens.shape
    window = WINDOW
    states = incoming.shape[1]
    where = place()
    segment_id = lax.axis_index(("dp", "fsdp"))
    counts = (document_lengths + seg_len - 1) // seg_len
    ends = jnp.cumsum(counts)
    starts = ends - counts
    inside = (segment_id >= starts) & (segment_id < ends)
    valid_len = jnp.sum(
        jnp.where(
            inside, jnp.minimum(seg_len, document_lengths - (segment_id - starts) * seg_len), 0
        )
    )
    first = jnp.any(segment_id == starts)
    lives = [jnp.where(b * window < valid_len, 1.0, 0.0).astype(F32).reshape(1) for b in range(2)]
    live_keys = [jnp.clip(valid_len - b * window, 0, window).astype(jnp.int32).reshape(1) for b in range(2)]

    gains = gather_vectors(jnp.stack([token_gain, state_gain, hidden_gain, gate_bias]))
    token_gain_f, state_gain_f, hidden_gain_f, gate_bias_f = [gains[i : i + 1] for i in range(4)]
    order = ()

    if paired():
        packed_init = jnp.pad(init_state.reshape(8, 2048), ((0, 8), (0, 0)))
        pieces = [
            gather_pieces(blocks)
            for blocks in (
                [state_proj, packed_init],
                [token_proj],
                [state_out, gate_weight, token_out],
                [hidden_in],
                [hidden_out],
            )
        ]
        full_state_proj, full_init = assemble(pieces[0], [64, 16], where)
        full_init = full_init.reshape(16, 16, 2, 4, 512)[:, :8].transpose(0, 1, 3, 2, 4).reshape(states, width)
    else:
        full_state_proj, full_token_proj, full_state_out, full_gate_weight, full_token_out, full_init = [
            gather_plain(w) for w in (state_proj, token_proj, state_out, gate_weight, token_out, init_state)
        ]
        full_hidden_in, full_hidden_out = gather_plain(hidden_in), gather_plain(hidden_out)
    state_0 = jnp.where(first, full_init, incoming[0]).astype(F32)
    normed_0, side_0 = norm_project(state_0, state_gain_f, full_state_proj, order)
    order = (side_0,)
    if paired():
        (full_token_proj,) = assemble(pieces[1], [64], where, order)
    normed, projected = norm_project(tokens, token_gain_f, full_token_proj, order)
    order = (projected,)
    inner_self_0, inner_cross_0, inner_self_log, inner_cross_log = inner_attention(
        projected, side_0, live_keys[0], 0, order
    )
    order = (inner_self_log,)
    cross_out, cross_log_0 = cross_attention(projected, side_0, 0, None, order)
    order = (cross_log_0,)
    self_out, self_log = self_attention(projected, window, order)
    order = (self_log,)
    if paired():
        full_state_out, full_gate_weight, full_token_out = assemble(pieces[2], [128, 64, 128], where, order)
        order = (full_gate_weight,)
    mixed_0, gate_0, state_1 = update_state(
        lives[0], inner_self_0, inner_cross_0, full_state_out, full_gate_weight, gate_bias_f, state_0, order
    )
    order = (mixed_0,)
    normed_1, side_1 = norm_project(state_1, state_gain_f, full_state_proj, order)
    order = (normed_1,)
    cross_out, cross_log_1 = cross_attention(projected, side_1, 1, cross_out, order)
    order = (cross_log_1,)
    middle, hidden_normed = branch(self_out, cross_out, full_token_out, tokens, hidden_gain_f, order)
    order = (hidden_normed,)
    if paired():
        (full_hidden_in,) = assemble(pieces[3], [64], where, order)
    active, slope = hidden(hidden_normed, full_hidden_in, order)
    order = (active,)

    scatters = {}

    def weight(name, lefts, rights, plan, split=False):
        nonlocal order
        if paired():
            keep, send = weight_grad(lefts, rights, plan, where, "grad_" + name, split, order)
            scatters[name] = Scatter(keep, send, where)
            order = (keep,)
            return
        if split:
            lefts = [jnp.concatenate(lefts, axis=1)]
        grad = jnp.concatenate(
            [sum(matmul_left_t(lefts[a], rights[b]) for a, b in terms) for terms in plan], axis=1
        )
        scatters[name] = scatter_plain(narrow(grad))

    def fold(name, step):
        nonlocal order
        if paired():
            order = (getattr(scatters[name], step)(order),)

    weight("hidden_out", [active], [output_grad], [[(0, 0)]])
    if paired():
        (full_hidden_out,) = assemble(pieces[4], [256], where, order)
        order = (full_hidden_out,)
    fold("hidden_out", "core")
    result, grad_pre = result_and_pre(active, slope, full_hidden_out, middle, output_grad, order)
    order = (result,)
    fold("hidden_out", "mid")
    weight("hidden_in", [hidden_normed], [grad_pre], [[(0, 0)]])
    grad_hidden_gain, grad_branch, grad_middle = norm_back_project(
        [grad_pre], full_hidden_in, middle, hidden_gain_f, output_grad, "hidden_back", True, after=order
    )
    order = (grad_hidden_gain,)
    fold("hidden_in", "core")
    fold("hidden_out", "last")
    grad_attended = spread(grad_branch, full_token_out, order)
    order = (grad_attended,)
    grad_cross, grad_keys_1, grad_values_1 = cross_attention_back(
        projected, side_1, cross_out, cross_log_1, grad_attended, 1, order
    )
    order = (grad_keys_1,)
    fold("hidden_in", "mid")
    no_term = jnp.zeros((states, width), jnp.bfloat16)
    grad_state_gain_1, _, grad_state_1 = norm_back_project(
        [grad_keys_1, grad_values_1], full_state_proj, state_1, state_gain_f, no_term, "side_back", True,
        offset=2 * width, after=order,
    )
    order = (grad_state_gain_1,)
    grad_gate_low, grad_mixed, grad_inner, grad_direct, grad_gate_bias = gate_back(
        lives[0], grad_state_1, gate_0, state_0, mixed_0, full_gate_weight, full_state_out, order
    )
    order = (grad_gate_bias,)
    weight_pairs = [[(0, 0)]]
    weight("token_out", [self_out, cross_out], [grad_branch], weight_pairs, True)
    fold("hidden_in", "last")
    parts = state_attention_back(
        projected, side_0, live_keys[0], (cross_out, cross_log_0), (inner_self_0, inner_self_log),
        (inner_cross_0, inner_cross_log), grad_attended, grad_inner, grad_cross, 0, order,
    )
    grad_cross, grads_side_0, extra_keys, extra_values = parts[0], parts[1:5], parts[5], parts[6]
    order = (extra_keys,)
    fold("token_out", "core")
    weight("state_out", [inner_self_0, inner_cross_0], [grad_mixed], weight_pairs, True)
    weight("gate_weight", [mixed_0], [grad_gate_low], weight_pairs)
    fold("token_out", "mid")
    weight(
        "state_proj", [normed_0, normed_1], [*grads_side_0, grad_keys_1, grad_values_1],
        [[(0, 0)], [(0, 1)], [(0, 2), (1, 4)], [(0, 3), (1, 5)]],
    )
    fold("state_out", "core")
    fold("gate_weight", "core")
    grad_state_gain_0, grad_init = norm_back_project(
        grads_side_0, full_state_proj, state_0, state_gain_f, grad_direct, "state_back",
        scale=jnp.where(first, 1.0, 0.0).astype(F32).reshape(1), after=order,
    )
    order = (grad_state_gain_0,)
    fold("token_out", "last")
    fold("state_proj", "core")
    grad_self, grad_keys, grad_values = self_attention_back(
        projected, self_out, self_log, grad_attended, extra_keys, extra_values, window, order
    )
    order = (grad_self,)
    fold("state_out", "mid")
    fold("gate_weight", "mid")
    fold("state_proj", "mid")
    grads_projected = [grad_self, grad_cross, grad_keys, grad_values]
    weight("token_proj", [normed], grads_projected, [[(0, i)] for i in range(4)])
    fold("state_out", "last")
    fold("gate_weight", "last")
    if paired():
        parts = grad_init.reshape(4, 2, 2, 32, width)
        keep = lax.dynamic_index_in_dim(parts, where[1], 2, keepdims=False)
        send = lax.dynamic_index_in_dim(parts, 1 - where[1], 2, keepdims=False)
        scatters["init"] = Scatter(keep, send, where)
    else:
        scatters["init"] = scatter_plain(grad_init)
    grad_token_gain, tokens_grad = norm_back_project(
        grads_projected, full_token_proj, tokens, token_gain_f, grad_middle, "tokens_back", after=order
    )
    order = (grad_token_gain,)
    fold("token_proj", "core")
    fold("init", "core")
    fold("state_proj", "last")
    inner_self_1, inner_cross_1, log, _ = inner_attention(projected, side_1, live_keys[1], 1, order)
    order = (log,)
    fold("token_proj", "mid")
    fold("init", "mid")
    _, _, state_2 = update_state(
        lives[1], inner_self_1, inner_cross_1, full_state_out, full_gate_weight, gate_bias_f, state_1, order
    )
    order = (state_2,)
    fold("init", "last")
    fold("token_proj", "last")
    vector_grads = scatter_vectors(
        jnp.concatenate(
            [grad_token_gain, grad_state_gain_0 + grad_state_gain_1, grad_hidden_gain, grad_gate_bias], axis=0
        )
    )
    matrix_grads = [
        (scatters[name].out if paired() else scatters[name]).astype(F32)
        for name in (
            "token_proj", "state_proj", "token_out", "state_out", "gate_weight", "init", "hidden_in", "hidden_out",
        )
    ]
    return (
        result,
        narrow(state_2)[None],
        tokens_grad,
        *matrix_grads,
        *[vector_grads[i] for i in range(4)],
    )


def solution(mesh):
    return jax.shard_map(
        shards,
        mesh=mesh,
        in_specs=(
            P(("dp", "fsdp"), None),
            P(("dp", "fsdp"), None, None),
            P(),
            P(("dp", "fsdp"), None),
            P("dp", "fsdp"),
            P("dp", "fsdp"),
            P("dp", "fsdp"),
            P("dp", "fsdp"),
            P("dp", "fsdp"),
            P("dp", "fsdp"),
            P("dp", "fsdp"),
            P("dp", "fsdp"),
            P("fsdp"),
            P("fsdp"),
            P("fsdp"),
            P("fsdp"),
        ),
        out_specs=(
            P(("dp", "fsdp"), None),
            P(("dp", "fsdp"), None, None),
            P(("dp", "fsdp"), None),
            P("dp", "fsdp"),
            P("dp", "fsdp"),
            P("dp", "fsdp"),
            P("dp", "fsdp"),
            P("dp", "fsdp"),
            P("dp", "fsdp"),
            P("dp", "fsdp"),
            P("dp", "fsdp"),
            P("fsdp"),
            P("fsdp"),
            P("fsdp"),
            P("fsdp"),
        ),
        check_vma=False,
    )
```

time: 1470 us -> 982 us (0.67)
  waiting for transfers between devices: 837 us -> 334 us
  Pallas kernels: 120 us -> 481 us
  matrix products: 275 us -> 0 us
  blocking collectives: 117 us -> 0 us
  starting transfers between devices: 1.98 us -> 70.5 us
  other arithmetic: 40.4 us -> 20.3 us
    reduce_scatter x16 -> x8, waiting for transfers between devices: 587 us -> 20.4 us  [last(): lax.psum_scatter(line.reshape(4 * rows, cols), 'dp', scatter_dimension=0,...]
    pallas_call x6 -> x58, Pallas kernels: 120 us -> 481 us  [launch(): pl.pallas_call(run, out_shape=list(out_shape), input_output_aliases=alias...]
    dot_general x26 -> x0, matrix products: 275 us -> none  [the longest x10 106 us: matmul(): return jnp.dot(left, right, preferred_element_type=jnp.float32)]
    ppermute x0 -> x91, waiting for transfers between devices: none -> 191 us  [the longest x63 114 us: swap(): return lax.ppermute(values, 'dp', [(d, d ^ bit) for d in range(16)])]
    all_gather x8 -> x5, waiting for transfers between devices: 248 us -> 120 us  [gather_pieces(): line = lax.all_gather(packed, 'dp', axis=0, axis_index_groups=LINES)]
    all_gather x12 -> x0, blocking collectives: 79.1 us -> none  [the longest x1 9.76 us: shards(): lax.all_gather(hidden_out, 'fsdp', axis=1, tiled=True)]
    ppermute x0 -> x91, starting transfers between devices: none -> 69.7 us  [the longest x63 39.1 us: swap(): return lax.ppermute(values, 'dp', [(d, d ^ bit) for d in range(16)])]
    psum x1 -> x0, blocking collectives: 33.1 us -> none  [shards(): lax.psum((vector_parts[0], vector_parts[1], vector_parts[2], vector_parts...]
  transfers between devices with their start and end apart: 24 -> 104, of which waited for: 20 -> 29; matrix products, arithmetic and copies ran while one was open for 17% -> 4% of each run, Pallas kernels for 6% -> 38%
where the time goes in v3:
time: 982 us; the launch traced here: 975 us
  Pallas kernels  481 us (49%)
  waiting for transfers between devices  334 us (34%)
  starting transfers between devices  70.5 us (7%)
  local copies, waits for them, and re-layouts  50.9 us (5%)
  other arithmetic  20.3 us (2%)
  between operations  18.7 us (2%)
    pallas_call x58, Pallas kernels, launch(): pl.pallas_call(run, out_shape=list(out_shape), input_output_aliases=alias...  481 us
    all_gather x5, waiting for transfers between devices, gather_pieces(): line = lax.all_gather(packed, 'dp', axis=0, axis_index_groups=LINES)  120 us
    ppermute x63, waiting for transfers between devices, swap(): return lax.ppermute(values, 'dp', [(d, d ^ bit) for d in range(16)])  114 us
    ppermute x28, waiting for transfers between devices, swap(): return lax.ppermute(values, 'fsdp', [(0, 1), (1, 0)])  77.8 us
    ppermute x63, starting transfers between devices, swap(): return lax.ppermute(values, 'dp', [(d, d ^ bit) for d in range(16)])  39.1 us
    ppermute x28, starting transfers between devices, swap(): return lax.ppermute(values, 'fsdp', [(0, 1), (1, 0)])  30.7 us
    unnamed x192, local copies, waits for them, and re-layouts  30.4 us
    reduce_scatter x8, waiting for transfers between devices, last(): lax.psum_scatter(line.reshape(4 * rows, cols), 'dp', scatter_dimension=0,...  20.4 us
  transfers between devices with their start and end apart: 104, of which 29 were waited for; matrix products, arithmetic and copies ran while one was open for 4% of the time, Pallas kernels for 38%

profile of v3, /device:TPU:0, one launch (start us, length us, event | category | flops | bytes accessed | tf_op | source)
XLA Modules:
  0.0 975.1 jit_solution(2184180274817544224)
XLA Ops:
  13.1 27.1 %all-gather.11.cloned.1.call-done = bf16[256,2048]{1,0:T(8,128)(2,1)} async-done(((bf16[64,2048]{1,0:T(8,128)(2,1)}), bf16[256,2048]{1,0:T(8,128)(2,1)}) %all-gather.11.cloned.1.call-update) | async-done | bytes 1048592 | tf_op jit(solution)/shard_map/all_gather | solution.py:687
  43.2 26.1 %all-gather.17.cloned.1.call-done = bf16[256,2048]{1,0:T(8,128)(2,1)} async-done(((bf16[64,2048]{1,0:T(8,128)(2,1)}), bf16[256,2048]{1,0:T(8,128)(2,1)}) %all-gather.17.cloned.1.call-update) | async-done | bytes 1048592 | tf_op jit(solution)/shard_map/all_gather | solution.py:687
  73.0 22.7 %collective-permute-done = bf16[4,512]{1,0:T(4,128)(2,1)S(1)} collective-permute-done((bf16[4,512]{1,0:T(4,128)(2,1)S(1)}, bf16[4,512]{1,0:T(4,128)(2,1)S(1)}, u32[]{:S(2)}, u32[]{:S(2)}) %collective-permute-start) | collective-permute-done | bytes 4128 | tf_op jit(solution)/shard_map/ppermute | solution.py:630
  95.6 8.1 all-gather.13.cloned.1.call-done
  106.6 30.8 %all-gather.15.cloned.1.call-done = bf16[1280,512]{1,0:T(8,128)(2,1)} async-done(((bf16[320,512]{1,0:T(8,128)(2,1)}), bf16[1280,512]{1,0:T(8,128)(2,1)}) %all-gather.15.cloned.1.call-update) | async-done | bytes 1310736 | tf_op jit(solution)/shard_map/all_gather | solution.py:687
  140.5 11.3 %collective-permute-done.3.refs_4_ = bf16[2,64,2048]{2,1,0:T(8,128)(2,1)S(1)} collective-permute-done((bf16[2,64,2048]{2,1,0:T(8,128)(2,1)S(1)}, bf16[2,64,2048]{2,1,0:T(8,128)(2,1)S(1)}, u32[]{:S(2)}, u32[]{:S(2)}) %collective-permute-start.3) | collective-permute-done | bytes 524320 | tf_op jit(solution)/shard_map/ppermute | solution.py:630
  155.8 11.8 %collective-permute-done.19.refs_2_ = bf16[4,320,512]{2,1,0:T(8,128)(2,1)} collective-permute-done((bf16[4,320,512]{2,1,0:T(8,128)(2,1)}, bf16[4,320,512]{2,1,0:T(8,128)(2,1)}, u32[]{:S(2)}, u32[]{:S(2)}) %collective-permute-start.19) | collective-permute-done | bytes 1310752 | tf_op jit(solution)/shard_map/ppermute | solution.py:632
  169.1 25.8 %collective-permute-done.12.refs_4_ = bf16[2,80,2048]{2,1,0:T(8,128)(2,1)} collective-permute-done((bf16[2,80,2048]{2,1,0:T(8,128)(2,1)S(1)}, bf16[2,80,2048]{2,1,0:T(8,128)(2,1)}, u32[]{:S(2)}, u32[]{:S(2)}) %collective-permute-start.12) | collective-permute-done | bytes 655392 | tf_op jit(solution)/shard_map/ppermute | solution.py:630
  209.4 8.8 assemble.5
  230.3 11.9 %norm_project.3 = (bf16[512,1024]{1,0:T(8,128)(2,1)S(1)}, bf16[512,4096]{1,0:T(8,128)(2,1)}) custom-call(f32[512,1024]{1,0:T(8,128)S(1)} %fusion.refs_0_.refs_6_.refs_3_, f32[1,1024]{1,0:T(1,128)S(1)} %get-tuple-element.281.refs_1_.refs_5_.refs_7_, bf16[1024,4096]{1,0:T(8,128)(2,1)} %bitcast.86), custom_call_target="tpu_custom_call" | custom-call | flops 4294967296 | bytes 15732736 | tf_op jit(solution)/shard_map/norm_project/pallas_call | solution.py:52
  243.2 6.7 assemble.6
  256.3 15.6 %norm_project.4 = (bf16[1024,1024]{1,0:T(8,128)(2,1)S(1)}, bf16[1024,4096]{1,0:T(8,128)(2,1)}) custom-call(bf16[1024,1024]{1,0:T(8,128)(2,1)S(1)} %copy-done.74, f32[1,1024]{1,0:T(1,128)S(1)} %get-tuple-element.282.refs_1_.refs_7_, bf16[1024,4096]{1,0:T(8,128)(2,1)} %bitcast.99, ...), custom_call_target="tpu_custom_call" | custom-call | flops 8589934592 | bytes 20975616 | tf_op jit(solution)/shard_map/norm_project/pallas_call | solution.py:52
  271.9 17.9 %inner_attention.2 = (bf16[512,1024]{1,0:T(8,128)(2,1)S(1)}, bf16[512,1024]{1,0:T(8,128)(2,1)S(1)}, f32[8,1,512]{2,1,0:T(1,128)S(1)}, f32[8,1,512]{2,1,0:T(1,128)S(1)}) custom-call(s32[1]{0:T(128)} %bitcast.11.refs_0_, bf16[512,4096]{1,0:T(8,128)(2,1)} %get-tuple-element.148.refs_11_.refs_3_.refs_1_.refs_2_.refs_4_.refs_5_, ...), custom_call_target="tpu_custom_call" | custom-call | flops 2147483648 | bytes 35684356 | tf_op jit(solution)/shard_map/inner_attention/pallas_call | solution.py:52
  289.8 10.4 %cross_attention.2 = (bf16[1024,1024]{1,0:T(8,128)(2,1)S(1)}, f32[8,1,512]{2,1,0:T(1,128)S(1)}) custom-call(bf16[1024,4096]{1,0:T(8,128)(2,1)} %get-tuple-element.149.refs_5_.refs_6_.refs_7_.refs_0_.refs_1_.refs_2_, bf16[512,4096]{1,0:T(8,128)(2,1)} %get-tuple-element.148.refs_11_.refs_3_.refs_1_.refs_2_.refs_4_.refs_5_, ...), custom_call_target="tpu_custom_call" | custom-call | flops 1073741824 | bytes 18890752 | tf_op jit(solution)/shard_map/cross_attention/pallas_call | solution.py:52
  300.2 17.1 %self_attention.1 = (bf16[1024,1024]{1,0:T(8,128)(2,1)S(1)}, f32[8,1,1024]{2,1,0:T(1,128)S(1)}) custom-call(bf16[1024,4096]{1,0:T(8,128)(2,1)} %get-tuple-element.149.refs_5_.refs_6_.refs_7_.refs_0_.refs_1_.refs_2_, bf16[1024,4096]{1,0:T(8,128)(2,1)} %get-tuple-element.149.refs_5_.refs_6_.refs_7_.refs_0_.refs_1_.refs_2_, ...), custom_call_target="tpu_custom_call" | custom-call | flops 2415919104 | bytes 27295744 | tf_op jit(solution)/shard_map/self_attention/pallas_call | solution.py:52
  318.9 7.6 assemble.7
  326.5 8.2 update_state.2
  338.1 11.1 %norm_project.5 = (bf16[512,1024]{1,0:T(8,128)(2,1)S(1)}, bf16[512,4096]{1,0:T(8,128)(2,1)}) custom-call(f32[512,1024]{1,0:T(8,128)S(1)} %copy-done.14, f32[1,1024]{1,0:T(1,128)S(1)} %get-tuple-element.281.refs_1_.refs_5_.refs_7_, bf16[1024,4096]{1,0:T(8,128)(2,1)} %bitcast.87, bf16[512,1024]{1,0:T(8,128)(2,1)S(1)} %get-tuple-element.159.refs_3_.refs_4_.refs_1_), custom_call_target="tpu_custom_call" | custom-call | flops 4294967296 | bytes 15732736 | tf_op jit(solution)/shard_map/norm_project/pallas_call | solution.py:52
  349.2 10.2 %cross_attention.3 = (bf16[1024,1024]{1,0:T(8,128)(2,1)S(1)}, f32[8,1,512]{2,1,0:T(1,128)S(1)}) custom-call(bf16[1024,4096]{1,0:T(8,128)(2,1)} %get-tuple-element.149.refs_5_.refs_6_.refs_7_.refs_0_.refs_1_.refs_2_, bf16[512,4096]{1,0:T(8,128)(2,1)} %get-tuple-element.160.refs_1_.refs_2_.refs_3_.refs_4_, ...), custom_call_target="tpu_custom_call", output_to_operand_aliasing={{0}: (3, {})} | custom-call | flops 1073741824 | bytes 20987904 | tf_op jit(solution)/shard_map/cross_attention/pallas_call | solution.py:52
  360.8 9.9 %branch.1 = (f32[1024,1024]{1,0:T(8,128)}, bf16[1024,1024]{1,0:T(8,128)(2,1)S(1)}) custom-call(bf16[1024,1024]{1,0:T(8,128)(2,1)S(1)} %get-tuple-element.152.refs_0_.refs_1_.refs_3_, bf16[1024,1024]{1,0:T(8,128)(2,1)} %copy-done.1, bf16[2048,1024]{1,0:T(8,128)(2,1)} %bitcast.109, bf16[1024,1024]{1,0:T(8,128)(2,1)} %refs_6_.1, ...), custom_call_target="tpu_custom_call" | custom-call | flops 4294967296 | bytes 16781312 | tf_op jit(solution)/shard_map/branch/pallas_call | solution.py:52
  373.0 6.8 assemble.8
  379.8 19.9 %hidden.1 = (bf16[1024,4096]{1,0:T(8,128)(2,1)}, bf16[1024,4096]{1,0:T(8,128)(2,1)}) custom-call(bf16[1024,1024]{1,0:T(8,128)(2,1)S(1)} %copy-done.27, bf16[1024,4096]{1,0:T(8,128)(2,1)} %bitcast.101, bf16[1024,1024]{1,0:T(8,128)(2,1)S(1)} %copy-done.27), custom_call_target="tpu_custom_call" | custom-call | flops 8589934592 | bytes 27262976 | tf_op jit(solution)/shard_map/hidden/pallas_call | solution.py:52
  399.7 13.8 %grad_hidden_out.1 = (bf16[4,2,256,1024]{3,2,1,0:T(8,128)(2,1)}, bf16[4,2,256,1024]{3,2,1,0:T(8,128)(2,1)}) custom-call(s32[3]{0:T(128)} %copy-done.60, bf16[1024,4096]{1,0:T(8,128)(2,1)} %get-tuple-element.167.refs_1_.refs_3_.refs_0_, bf16[1024,1024]{1,0:T(8,128)(2,1)} %refs_5_.1, bf16[1024,4096]{1,0:T(8,128)(2,1)} %get-tuple-element.167.refs_1_.refs_3_.refs_0_), custom_call_target="tpu_custom_call" | custom-call | flops 8589934592 | bytes 18874368 | tf_op jit(solution)/shard_map/grad_hidden_out/pallas_call | solution.py:52
  413.7 27.9 %all-gather.19.cloned.1.call-done = bf16[1024,512]{1,0:T(8,128)(2,1)} async-done(((bf16[256,512]{1,0:T(8,128)(2,1)}), bf16[1024,512]{1,0:T(8,128)(2,1)}) %all-gather.19.cloned.1.call-update) | async-done | bytes 1048592 | tf_op jit(solution)/shard_map/all_gather | solution.py:687
  444.6 22.0 %collective-permute-done.37.refs_2_ = bf16[4,256,512]{2,1,0:T(8,128)(2,1)S(1)} collective-permute-done((bf16[4,256,512]{2,1,0:T(8,128)(2,1)}, bf16[4,256,512]{2,1,0:T(8,128)(2,1)S(1)}, u32[]{:S(2)}, u32[]{:S(2)}) %collective-permute-start.37) | collective-permute-done | bytes 1048608 | tf_op jit(solution)/shard_map/ppermute | solution.py:632
  470.3 9.1 collective-permute-done.39.refs_4_
  498.3 24.7 %result_and_pre.1 = (bf16[1024,1024]{1,0:T(8,128)(2,1)}, bf16[1024,4096]{1,0:T(8,128)(2,1)}) custom-call(bf16[1024,4096]{1,0:T(8,128)(2,1)} %get-tuple-element.167.refs_1_.refs_3_.refs_0_, bf16[1024,4096]{1,0:T(8,128)(2,1)} %get-tuple-element.168.refs_1_, bf16[4096,1024]{1,0:T(8,128)(2,1)} %bitcast.91, f32[1024,1024]{1,0:T(8,128)} %get-tuple-element.170.refs_3_, ...), custom_call_target="tpu_custom_call" | custom-call | flops 17179869184 | bytes 41943040 | tf_op jit(solution)/shard_map/result_and_pre/pallas_call | solution.py:52
  527.6 15.3 %grad_hidden_in.1 = (bf16[4,2,64,4096]{3,2,1,0:T(8,128)(2,1)}, bf16[4,2,64,4096]{3,2,1,0:T(8,128)(2,1)}) custom-call(s32[3]{0:T(128)} %copy-done.60, bf16[1024,1024]{1,0:T(8,128)(2,1)} %copy-done.26, bf16[1024,4096]{1,0:T(8,128)(2,1)} %get-tuple-element.176.refs_2_.refs_1_, bf16[4,256,512]{2,1,0:T(8,128)(2,1)} %copy-done.46), custom_call_target="tpu_custom_call" | custom-call | flops 8589934592 | bytes 18874368 | tf_op jit(solution)/shard_map/grad_hidden_in/pallas_call | solution.py:52
  545.1 20.1 %hidden_back.1 = (f32[1,1024]{1,0:T(1,128)S(1)}, bf16[1024,1024]{1,0:T(8,128)(2,1)S(1)}, f32[1024,1024]{1,0:T(8,128)}) custom-call(f32[1]{0:T(128)} %constant.80.clone.1.refs_0_, bf16[1024,4096]{1,0:T(8,128)(2,1)} %get-tuple-element.176.refs_2_.refs_1_, bf16[1024,4096]{1,0:T(8,128)(2,1)} %bitcast.102, f32[1024,1024]{1,0:T(8,128)} %get-tuple-element.170.refs_3_, ...), custom_call_target="tpu_custom_call" | custom-call | flops 8589934592 | bytes 29368324 | tf_op jit(solution)/shard_map/hidden_back/pallas_call | solution.py:52
  573.1 7.8 spread.1.refs_5_.refs_6_.refs_14_
  580.9 9.8 %cross_attention_back.1 = (bf16[1024,1024]{1,0:T(8,128)(2,1)S(1)}, bf16[512,1024]{1,0:T(8,128)(2,1)S(1)}, bf16[512,1024]{1,0:T(8,128)(2,1)S(1)}) custom-call(bf16[1024,4096]{1,0:T(8,128)(2,1)} %get-tuple-element.149.refs_5_.refs_6_.refs_7_.refs_0_.refs_1_.refs_2_, bf16[512,4096]{1,0:T(8,128)(2,1)} %get-tuple-element.160.refs_1_.refs_2_.refs_3_.refs_4_, ...), custom_call_target="tpu_custom_call" | custom-call | flops 2684354560 | bytes 27279360 | tf_op jit(solution)/shard_map/cross_attention_back/pallas_call | solution.py:52
  592.7 9.5 side_back.1
  602.2 9.0 gate_back.1
  614.1 9.4 grad_token_out.1
  625.6 23.5 %collective-permute-done.54.refs_1_ = bf16[4,64,2048]{2,1,0:T(8,128)(2,1)S(1)} collective-permute-done((bf16[4,64,2048]{2,1,0:T(8,128)(2,1)S(1)}, bf16[4,64,2048]{2,1,0:T(8,128)(2,1)S(1)}, u32[]{:S(2)}, u32[]{:S(2)}) %collective-permute-start.54) | collective-permute-done | bytes 1048608 | tf_op jit(solution)/shard_map/ppermute | solution.py:632
  651.0 22.5 %state_attention_back.1 = (bf16[1024,1024]{1,0:T(8,128)(2,1)}, bf16[512,1024]{1,0:T(8,128)(2,1)S(1)}, bf16[512,1024]{1,0:T(8,128)(2,1)S(1)}, bf16[512,1024]{1,0:...) custom-call(s32[1]{0:T(128)} %bitcast.11.refs_0_, ...), custom_call_target="tpu_custom_call", output_to_operand_aliasing={{0}: (17, {})} | custom-call | flops 8053063680 | bytes 67158016 | tf_op jit(solution)/shard_map/state_attention_back/pallas_call | solution.py:52
  682.7 6.9 grad_state_out.1
  698.9 12.8 %grad_state_proj.1 = (bf16[4,2,64,4096]{3,2,1,0:T(8,128)(2,1)}, bf16[4,2,64,4096]{3,2,1,0:T(8,128)(2,1)}) custom-call(s32[3]{0:T(128)} %copy-done.60, bf16[512,1024]{1,0:T(8,128)(2,1)} %copy-done.78, bf16[512,1024]{1,0:T(8,128)(2,1)} %copy-done.32, bf16[512,1024]{1,0:T(8,128)(2,1)} %copy-done.33, bf16[512,1024]{1,0:T(8,128)(2,1)} %copy-done.35, ...), custom_call_target="tpu_custom_call" | custom-call | flops 4294967296 | bytes 16777216 | tf_op jit(solution)/shard_map/grad_state_proj/pallas_call | solution.py:52
  714.7 7.5 collective-permute-done.63.refs_2_
  729.9 12.8 %state_back.1 = (f32[1,1024]{1,0:T(1,128)S(1)}, bf16[512,1024]{1,0:T(8,128)(2,1)S(1)}) custom-call(f32[1]{0:T(128)} %bitcast.23.refs_0_, bf16[512,1024]{1,0:T(8,128)(2,1)S(1)} %copy-done.34, bf16[512,1024]{1,0:T(8,128)(2,1)S(1)} %copy-done.36, bf16[512,1024]{1,0:T(8,128)(2,1)S(1)} %copy-done.38, bf16[512,1024]{1,0:T(8,128)(2,1)S(1)} %copy-done.40, ...), custom_call_target="tpu_custom_call" | custom-call | flops 4294967296 | bytes 17833988 | tf_op jit(solution)/shard_map/state_back/pallas_call | solution.py:52
  753.9 17.7 %self_attention_back.1 = (bf16[1024,1024]{1,0:T(8,128)(2,1)S(1)}, bf16[1024,1024]{1,0:T(8,128)(2,1)S(1)}, bf16[1024,1024]{1,0:T(8,128)(2,1)}) custom-call(bf16[1024,4096]{1,0:T(8,128)(2,1)} %get-tuple-element.149.refs_5_.refs_6_.refs_7_.refs_0_.refs_1_.refs_2_, bf16[1024,4096]{1,0:T(8,128)(2,1)} %get-tuple-element.149.refs_5_.refs_6_.refs_7_.refs_0_.refs_1_.refs_2_, ...), custom_call_target="tpu_custom_call" | custom-call | flops 6039797760 | bytes 41975808 | tf_op jit(solution)/shard_map/self_attention_back/pallas_call | solution.py:52
  777.8 15.4 %grad_token_proj.1 = (bf16[4,2,64,4096]{3,2,1,0:T(8,128)(2,1)}, bf16[4,2,64,4096]{3,2,1,0:T(8,128)(2,1)}) custom-call(s32[3]{0:T(128)} %copy-done.60, bf16[1024,1024]{1,0:T(8,128)(2,1)} %copy-done.79, bf16[1024,1024]{1,0:T(8,128)(2,1)} %copy-done.18, bf16[1024,1024]{1,0:T(8,128)(2,1)} %get-tuple-element.249.refs_3_.refs_2_, bf16[1024,1024]{1,0:T(8,128)(2,1)} %copy-done.75, ...), custom_call_target="tpu_custom_call" | custom-call | flops 8589934592 | bytes 18874368 | tf_op jit(solution)/shard_map/grad_token_proj/pallas_call | solution.py:52
  797.4 10.7 %collective-permute-done.76.refs_1_ = bf16[4,128,512]{2,1,0:T(8,128)(2,1)S(1)} collective-permute-done((bf16[4,128,512]{2,1,0:T(8,128)(2,1)S(1)}, bf16[4,128,512]{2,1,0:T(8,128)(2,1)S(1)}, u32[]{:S(2)}, u32[]{:S(2)}) %collective-permute-start.76) | collective-permute-done | bytes 524320 | tf_op jit(solution)/shard_map/ppermute | solution.py:632
  821.3 20.6 %tokens_back.1 = (f32[1,1024]{1,0:T(1,128)S(1)}, bf16[1024,1024]{1,0:T(8,128)(2,1)}) custom-call(f32[1]{0:T(128)} %constant.80.clone.1.refs_0_, bf16[1024,1024]{1,0:T(8,128)(2,1)S(1)} %copy-done.19, bf16[1024,1024]{1,0:T(8,128)(2,1)S(1)} %copy-done.17, bf16[1024,1024]{1,0:T(8,128)(2,1)} %copy-done.75, bf16[1024,1024]{1,0:T(8,128)(2,1)} %get-tuple-element.251.refs_5_.refs_4_, ...), custom_call_target="tpu_custom_call" | custom-call | flops 8589934592 | bytes 25174020 | tf_op jit(solution)/shard_map/tokens_back/pallas_call | solution.py:52
  859.2 17.8 %inner_attention.3 = (bf16[512,1024]{1,0:T(8,128)(2,1)S(1)}, bf16[512,1024]{1,0:T(8,128)(2,1)S(1)}, f32[8,1,512]{2,1,0:T(1,128)S(1)}, f32[8,1,512]{2,1,0:T(1,128)}) custom-call(s32[1]{0:T(128)} %bitcast.22.refs_0_, bf16[512,4096]{1,0:T(8,128)(2,1)} %get-tuple-element.160.refs_1_.refs_2_.refs_3_.refs_4_, ...), custom_call_target="tpu_custom_call" | custom-call | flops 2147483648 | bytes 35684356 | tf_op jit(solution)/shard_map/inner_attention/pallas_call | solution.py:52
  881.3 8.6 update_state.3
  894.8 21.4 %collective-permute-done.82.refs_1_ = bf16[4,64,2048]{2,1,0:T(8,128)(2,1)S(1)} collective-permute-done((bf16[4,64,2048]{2,1,0:T(8,128)(2,1)S(1)}, bf16[4,64,2048]{2,1,0:T(8,128)(2,1)S(1)}, u32[]{:S(2)}, u32[]{:S(2)}) %collective-permute-start.82) | collective-permute-done | bytes 1048608 | tf_op jit(solution)/shard_map/ppermute | solution.py:632
  946.0 20.4 %reduce-scatter.9.cloned.1.call-done = bf16[64,2048]{1,0:T(8,128)(2,1)} async-done(((bf16[256,2048]{1,0:T(8,128)(2,1)}), bf16[64,2048]{1,0:T(8,128)(2,1)}) %reduce-scatter.9.cloned.1.call-update) | async-done | bytes 262160 | tf_op jit(solution)/shard_map/reduce_scatter | solution.py:781
  (473 shorter events, 233.9 us)
Async XLA Ops:
  7.2 33.1 %all-gather.11.cloned.1.call-start = ((), (), s32[]{:S(2)}) async-start(), calls=%async_computation.16 | async-start | bytes 1310720 | tf_op jit(solution)/shard_map/all_gather | solution.py:687
  8.0 61.4 %all-gather.17.cloned.1.call-start = ((), (), s32[]{:S(2)}) async-start(), calls=%async_computation.19 | async-start | bytes 1310720 | tf_op jit(solution)/shard_map/all_gather | solution.py:687
  8.7 95.0 %all-gather.13.cloned.1.call-start = ((), (), s32[]{:S(2)}) async-start(), calls=%async_computation.17 | async-start | bytes 1638400 | tf_op jit(solution)/shard_map/all_gather | solution.py:687
  11.3 126.1 %all-gather.15.cloned.1.call-start = ((), (), s32[]{:S(2)}) async-start(), calls=%async_computation.18 | async-start | bytes 1638400 | tf_op jit(solution)/shard_map/all_gather | solution.py:687
  13.1 428.5 %all-gather.19.cloned.1.call-start = ((), (), s32[]{:S(2)}) async-start(), calls=%async_computation.20 | async-start | bytes 1310720 | tf_op jit(solution)/shard_map/all_gather | solution.py:687
  40.3 64.9 %collective-permute-start.1 = (bf16[4,64,2048]{2,1,0:T(8,128)(2,1)}, bf16[4,64,2048]{2,1,0:T(8,128)(2,1)S(1)}, u32[]{:S(2)}, u32[]{:S(2)}) collective-permute-start(bf16[4,64,2048]{2,1,0:T(8,128)(2,1)} %bitcast.72), channel_id=1, source_target_pairs={{0,4},{2,6},{4,0},{6,2},{8,12},{10,14},{12,8},{14,10},{16,20},{18,... | collective-permute-start | bytes 3145736 | tf_op jit(solution)/shard_map/ppermute | solution.py:632
  41.8 64.9 %collective-permute-start.2 = (bf16[4,64,2048]{2,1,0:T(8,128)(2,1)}, bf16[4,64,2048]{2,1,0:T(8,128)(2,1)}, u32[]{:S(2)}, u32[]{:S(2)}) collective-permute-start(bf16[4,64,2048]{2,1,0:T(8,128)(2,1)} %bitcast.73), channel_id=1, source_target_pairs={{0,1},{1,0},{2,3},{3,2},{4,5},{5,4},{6,7},{7,6},{8,9},{9,8},{10,11... | collective-permute-start | bytes 3145736 | tf_op jit(solution)/shard_map/ppermute | solution.py:630
  69.3 68.1 %collective-permute-start.28 = (bf16[4,64,2048]{2,1,0:T(8,128)(2,1)}, bf16[4,64,2048]{2,1,0:T(8,128)(2,1)}, u32[]{:S(2)}, u32[]{:S(2)}) collective-permute-start(bf16[4,64,2048]{2,1,0:T(8,128)(2,1)} %bitcast.82), channel_id=1, source_target_pairs={{0,4},{2,6},{4,0},{6,2},{8,12},{10,14},{12,8},{14,10},{16,20},{18,... | collective-permute-start | bytes 3145736 | tf_op jit(solution)/shard_map/ppermute | solution.py:632
  70.8 68.1 %collective-permute-start.29 = (bf16[4,64,2048]{2,1,0:T(8,128)(2,1)}, bf16[4,64,2048]{2,1,0:T(8,128)(2,1)}, u32[]{:S(2)}, u32[]{:S(2)}) collective-permute-start(bf16[4,64,2048]{2,1,0:T(8,128)(2,1)} %bitcast.83), channel_id=1, source_target_pairs={{0,1},{1,0},{2,3},{3,2},{4,5},{5,4},{6,7},{7,6},{8,9},{9,8},{10,11... | collective-permute-start | bytes 3145736 | tf_op jit(solution)/shard_map/ppermute | solution.py:630
  103.7 49.5 %collective-permute-start.10 = (bf16[4,80,2048]{2,1,0:T(8,128)(2,1)}, bf16[4,80,2048]{2,1,0:T(8,128)(2,1)S(1)}, u32[]{:S(2)}, u32[]{:S(2)}) collective-permute-start(bf16[4,80,2048]{2,1,0:T(8,128)(2,1)} %bitcast.68), channel_id=1, source_target_pairs={{0,4},{2,6},{4,0},{6,2},{8,12},{10,14},{12,8},{14,10},{16,20},{18,... | collective-permute-start | bytes 3932168 | tf_op jit(solution)/shard_map/ppermute | solution.py:632
  105.2 48.1 %collective-permute-start.11 = (bf16[4,80,2048]{2,1,0:T(8,128)(2,1)}, bf16[4,80,2048]{2,1,0:T(8,128)(2,1)}, u32[]{:S(2)}, u32[]{:S(2)}) collective-permute-start(bf16[4,80,2048]{2,1,0:T(8,128)(2,1)} %bitcast.69), channel_id=1, source_target_pairs={{0,1},{1,0},{2,3},{3,2},{4,5},{5,4},{6,7},{7,6},{8,9},{9,8},{10,11... | collective-permute-start | bytes 3932168 | tf_op jit(solution)/shard_map/ppermute | solution.py:630
  106.6 48.3 %collective-permute-start.14 = (bf16[4,80,2048]{2,1,0:T(8,128)(2,1)}, bf16[4,80,2048]{2,1,0:T(8,128)(2,1)}, u32[]{:S(2)}, u32[]{:S(2)}) collective-permute-start(bf16[4,80,2048]{2,1,0:T(8,128)(2,1)} %bitcast.70), channel_id=1, source_target_pairs={{0,2},{2,0},{4,6},{6,4},{8,10},{10,8},{12,14},{14,12},{16,18},{18,... | collective-permute-start | bytes 3932168 | tf_op jit(solution)/shard_map/ppermute | solution.py:632
  137.4 30.2 %collective-permute-start.19 = (bf16[4,320,512]{2,1,0:T(8,128)(2,1)}, bf16[4,320,512]{2,1,0:T(8,128)(2,1)}, u32[]{:S(2)}, u32[]{:S(2)}) collective-permute-start(bf16[4,320,512]{2,1,0:T(8,128)(2,1)} %bitcast.64), channel_id=1, source_target_pairs={{0,4},{2,6},{4,0},{6,2},{8,12},{10,14},{12,8},{14,10},{16,20},{18,... | collective-permute-start | bytes 3932168 | tf_op jit(solution)/shard_map/ppermute | solution.py:632
  151.7 43.6 %collective-permute-start.20 = (bf16[4,320,512]{2,1,0:T(8,128)(2,1)}, bf16[4,320,512]{2,1,0:T(8,128)(2,1)}, u32[]{:S(2)}, u32[]{:S(2)}) collective-permute-start(bf16[4,320,512]{2,1,0:T(8,128)(2,1)} %bitcast.65), channel_id=1, source_target_pairs={{0,1},{1,0},{2,3},{3,2},{4,5},{5,4},{6,7},{7,6},{8,9},{9,8},{10,11... | collective-permute-start | bytes 3932168 | tf_op jit(solution)/shard_map/ppermute | solution.py:630
  153.2 42.2 %collective-permute-start.15 = (bf16[4,80,2048]{2,1,0:T(8,128)(2,1)S(1)}, bf16[4,80,2048]{2,1,0:T(8,128)(2,1)}, u32[]{:S(2)}, u32[]{:S(2)}) collective-permute-start(bf16[4,80,2048]{2,1,0:T(8,128)(2,1)S(1)} %collective-permute-done.10.refs_2_), channel_id=1, source_target_pairs={{0,2},{2,0},{4,6},{6,4},{8,10},{10,8},{12,14},{14,12},{16,18},{18,... | collective-permute-start | bytes 3932168 | tf_op jit(solution)/shard_map/ppermute | solution.py:632
  153.2 42.7 %collective-permute-start.16 = (bf16[4,80,2048]{2,1,0:T(8,128)(2,1)}, bf16[4,80,2048]{2,1,0:T(8,128)(2,1)}, u32[]{:S(2)}, u32[]{:S(2)}) collective-permute-start(bf16[4,80,2048]{2,1,0:T(8,128)(2,1)} %collective-permute-done.11.refs_3_), channel_id=1, source_target_pairs={{0,2},{2,0},{4,6},{6,4},{8,10},{10,8},{12,14},{14,12},{16,18},{18,... | collective-permute-start | bytes 3932168 | tf_op jit(solution)/shard_map/ppermute | solution.py:632
  154.9 39.9 %collective-permute-start.12 = (bf16[2,80,2048]{2,1,0:T(8,128)(2,1)S(1)}, bf16[2,80,2048]{2,1,0:T(8,128)(2,1)}, u32[]{:S(2)}, u32[]{:S(2)}) collective-permute-start(bf16[2,80,2048]{2,1,0:T(8,128)(2,1)S(1)} %slice.87), channel_id=1, source_target_pairs={{0,1},{1,0},{2,3},{3,2},{4,5},{5,4},{6,7},{7,6},{8,9},{9,8},{10,11... | collective-permute-start | bytes 1966088 | tf_op jit(solution)/shard_map/ppermute | solution.py:630
  195.5 32.8 %collective-permute-start.6 = (bf16[4,64,2048]{2,1,0:T(8,128)(2,1)S(1)}, bf16[4,64,2048]{2,1,0:T(8,128)(2,1)}, u32[]{:S(2)}, u32[]{:S(2)}) collective-permute-start(bf16[4,64,2048]{2,1,0:T(8,128)(2,1)S(1)} %collective-permute-done.1.refs_2_), channel_id=1, source_target_pairs={{0,2},{2,0},{4,6},{6,4},{8,10},{10,8},{12,14},{14,12},{16,18},{18,... | collective-permute-start | bytes 3145736 | tf_op jit(solution)/shard_map/ppermute | solution.py:632
  195.9 32.4 %collective-permute-start.7 = (bf16[4,64,2048]{2,1,0:T(8,128)(2,1)}, bf16[4,64,2048]{2,1,0:T(8,128)(2,1)}, u32[]{:S(2)}, u32[]{:S(2)}) collective-permute-start(bf16[4,64,2048]{2,1,0:T(8,128)(2,1)} %collective-permute-done.2.refs_3_), channel_id=1, source_target_pairs={{0,2},{2,0},{4,6},{6,4},{8,10},{10,8},{12,14},{14,12},{16,18},{18,... | collective-permute-start | bytes 3145736 | tf_op jit(solution)/shard_map/ppermute | solution.py:632
  243.2 74.1 %collective-permute-start.23 = (bf16[4,320,512]{2,1,0:T(8,128)(2,1)S(1)}, bf16[4,320,512]{2,1,0:T(8,128)(2,1)S(1)}, u32[]{:S(2)}, u32[]{:S(2)}) collective-permute-start(bf16[4,320,512]{2,1,0:T(8,128)(2,1)S(1)} %bitcast.66), channel_id=1, source_target_pairs={{0,2},{2,0},{4,6},{6,4},{8,10},{10,8},{12,14},{14,12},{16,18},{18,... | collective-permute-start | bytes 3932168 | tf_op jit(solution)/shard_map/ppermute | solution.py:632
  249.8 68.0 %collective-permute-start.24 = (bf16[4,320,512]{2,1,0:T(8,128)(2,1)}, bf16[4,320,512]{2,1,0:T(8,128)(2,1)}, u32[]{:S(2)}, u32[]{:S(2)}) collective-permute-start(bf16[4,320,512]{2,1,0:T(8,128)(2,1)} %collective-permute-done.19.refs_2_), channel_id=1, source_target_pairs={{0,2},{2,0},{4,6},{6,4},{8,10},{10,8},{12,14},{14,12},{16,18},{18,... | collective-permute-start | bytes 3932168 | tf_op jit(solution)/shard_map/ppermute | solution.py:632
  250.4 67.6 %collective-permute-start.25 = (bf16[4,320,512]{2,1,0:T(8,128)(2,1)}, bf16[4,320,512]{2,1,0:T(8,128)(2,1)}, u32[]{:S(2)}, u32[]{:S(2)}) collective-permute-start(bf16[4,320,512]{2,1,0:T(8,128)(2,1)} %collective-permute-done.20.refs_3_), channel_id=1, source_target_pairs={{0,2},{2,0},{4,6},{6,4},{8,10},{10,8},{12,14},{14,12},{16,18},{18,... | collective-permute-start | bytes 3932168 | tf_op jit(solution)/shard_map/ppermute | solution.py:632
  253.5 64.9 %collective-permute-start.26 = (bf16[2,320,512]{2,1,0:T(8,128)(2,1)S(1)}, bf16[2,320,512]{2,1,0:T(8,128)(2,1)S(1)}, u32[]{:S(2)}, u32[]{:S(2)}) collective-permute-start(bf16[2,320,512]{2,1,0:T(8,128)(2,1)S(1)} %collective-permute-done.21.refs_4_), channel_id=1, source_target_pairs={{0,2},{2,0},{4,6},{6,4},{8,10},{10,8},{12,14},{14,12},{16,18},{18,... | collective-permute-start | bytes 1966088 | tf_op jit(solution)/shard_map/ppermute | solution.py:632
  254.7 63.8 %collective-permute-start.27 = (bf16[2,320,512]{2,1,0:T(8,128)(2,1)S(1)}, bf16[2,320,512]{2,1,0:T(8,128)(2,1)S(1)}, u32[]{:S(2)}, u32[]{:S(2)}) collective-permute-start(bf16[2,320,512]{2,1,0:T(8,128)(2,1)S(1)} %collective-permute-done.22.refs_5_), channel_id=1, source_target_pairs={{0,2},{2,0},{4,6},{6,4},{8,10},{10,8},{12,14},{14,12},{16,18},{18,... | collective-permute-start | bytes 1966088 | tf_op jit(solution)/shard_map/ppermute | solution.py:632
  317.3 54.8 %collective-permute-start.32 = (bf16[4,64,2048]{2,1,0:T(8,128)(2,1)S(1)}, bf16[4,64,2048]{2,1,0:T(8,128)(2,1)S(1)}, u32[]{:S(2)}, u32[]{:S(2)}) collective-permute-start(bf16[4,64,2048]{2,1,0:T(8,128)(2,1)S(1)} %bitcast.84), channel_id=1, source_target_pairs={{0,2},{2,0},{4,6},{6,4},{8,10},{10,8},{12,14},{14,12},{16,18},{18,... | collective-permute-start | bytes 3145736 | tf_op jit(solution)/shard_map/ppermute | solution.py:632
  317.9 54.2 %collective-permute-start.33 = (bf16[4,64,2048]{2,1,0:T(8,128)(2,1)}, bf16[4,64,2048]{2,1,0:T(8,128)(2,1)}, u32[]{:S(2)}, u32[]{:S(2)}) collective-permute-start(bf16[4,64,2048]{2,1,0:T(8,128)(2,1)} %collective-permute-done.28.refs_2_), channel_id=1, source_target_pairs={{0,2},{2,0},{4,6},{6,4},{8,10},{10,8},{12,14},{14,12},{16,18},{18,... | collective-permute-start | bytes 3145736 | tf_op jit(solution)/shard_map/ppermute | solution.py:632
  318.0 54.1 %collective-permute-start.34 = (bf16[4,64,2048]{2,1,0:T(8,128)(2,1)}, bf16[4,64,2048]{2,1,0:T(8,128)(2,1)}, u32[]{:S(2)}, u32[]{:S(2)}) collective-permute-start(bf16[4,64,2048]{2,1,0:T(8,128)(2,1)} %collective-permute-done.29.refs_3_), channel_id=1, source_target_pairs={{0,2},{2,0},{4,6},{6,4},{8,10},{10,8},{12,14},{14,12},{16,18},{18,... | collective-permute-start | bytes 3145736 | tf_op jit(solution)/shard_map/ppermute | solution.py:632
  318.4 53.7 %collective-permute-start.35 = (bf16[2,64,2048]{2,1,0:T(8,128)(2,1)S(1)}, bf16[2,64,2048]{2,1,0:T(8,128)(2,1)S(1)}, u32[]{:S(2)}, u32[]{:S(2)}) collective-permute-start(bf16[2,64,2048]{2,1,0:T(8,128)(2,1)S(1)} %collective-permute-done.30.refs_4_), channel_id=1, source_target_pairs={{0,2},{2,0},{4,6},{6,4},{8,10},{10,8},{12,14},{14,12},{16,18},{18,... | collective-permute-start | bytes 1572872 | tf_op jit(solution)/shard_map/ppermute | solution.py:632
  318.5 53.6 %collective-permute-start.36 = (bf16[2,64,2048]{2,1,0:T(8,128)(2,1)S(1)}, bf16[2,64,2048]{2,1,0:T(8,128)(2,1)S(1)}, u32[]{:S(2)}, u32[]{:S(2)}) collective-permute-start(bf16[2,64,2048]{2,1,0:T(8,128)(2,1)S(1)} %collective-permute-done.31.refs_5_), channel_id=1, source_target_pairs={{0,2},{2,0},{4,6},{6,4},{8,10},{10,8},{12,14},{14,12},{16,18},{18,... | collective-permute-start | bytes 1572872 | tf_op jit(solution)/shard_map/ppermute | solution.py:632
  413.5 77.4 %collective-permute-start.46 = (bf16[4,2,256,1024]{3,2,1,0:T(8,128)(2,1)}, bf16[4,2,256,1024]{3,2,1,0:T(8,128)(2,1)}, u32[]{:S(2)}, u32[]{:S(2)}) collective-permute-start(bf16[4,2,256,1024]{3,2,1,0:T(8,128)(2,1)} %get-tuple-element.171), channel_id=1, source_target_pairs={{0,2},{2,0},{4,6},{6,4},{8,10},{10,8},{12,14},{14,12},{16,18},{18,... | collective-permute-start | bytes 12582920 | tf_op jit(solution)/shard_map/ppermute | solution.py:632
  413.6 519.1 %reduce-scatter.23.cloned.1.call-start = ((), (), s32[]{:S(2)}) async-start(), calls=%async_computation.15 | async-start | bytes 1310720 | tf_op jit(solution)/shard_map/reduce_scatter | solution.py:781
  623.5 52.9 %collective-permute-start.56 = (bf16[4,2,128,1024]{3,2,1,0:T(8,128)(2,1)}, bf16[4,2,128,1024]{3,2,1,0:T(8,128)(2,1)}, u32[]{:S(2)}, u32[]{:S(2)}) collective-permute-start(bf16[4,2,128,1024]{3,2,1,0:T(8,128)(2,1)} %get-tuple-element.207), channel_id=1, source_target_pairs={{0,2},{2,0},{4,6},{6,4},{8,10},{10,8},{12,14},{14,12},{16,18},{18,... | collective-permute-start | bytes 6291464 | tf_op jit(solution)/shard_map/ppermute | solution.py:632
  711.7 35.1 %collective-permute-start.59 = (bf16[4,2,64,4096]{3,2,1,0:T(8,128)(2,1)}, bf16[4,2,64,4096]{3,2,1,0:T(8,128)(2,1)}, u32[]{:S(2)}, u32[]{:S(2)}) collective-permute-start(bf16[4,2,64,4096]{3,2,1,0:T(8,128)(2,1)} %get-tuple-element.220), channel_id=1, source_target_pairs={{0,2},{2,0},{4,6},{6,4},{8,10},{10,8},{12,14},{14,12},{16,18},{18,... | collective-permute-start | bytes 12582920 | tf_op jit(solution)/shard_map/ppermute | solution.py:632
  711.8 222.8 %reduce-scatter.21.cloned.1.call-start = ((), (), s32[]{:S(2)}) async-start(), calls=%async_computation.14 | async-start | bytes 1310720 | tf_op jit(solution)/shard_map/reduce_scatter | solution.py:781
  712.5 30.2 %collective-permute-start.60 = (bf16[4,128,512]{2,1,0:T(8,128)(2,1)S(1)}, bf16[4,128,512]{2,1,0:T(8,128)(2,1)}, u32[]{:S(2)}, u32[]{:S(2)}) collective-permute-start(bf16[4,128,512]{2,1,0:T(8,128)(2,1)S(1)} %copy-done.55), channel_id=1, source_target_pairs={{0,4},{2,6},{4,0},{6,2},{8,12},{10,14},{12,8},{14,10},{16,20},{18,... | collective-permute-start | bytes 1572872 | tf_op jit(solution)/shard_map/ppermute | solution.py:632
  713.0 30.3 %collective-permute-start.61 = (bf16[4,128,512]{2,1,0:T(8,128)(2,1)}, bf16[4,128,512]{2,1,0:T(8,128)(2,1)}, u32[]{:S(2)}, u32[]{:S(2)}) collective-permute-start(bf16[4,128,512]{2,1,0:T(8,128)(2,1)} %get-tuple-element.221), channel_id=1, source_target_pairs={{0,1},{1,0},{2,3},{3,2},{4,5},{5,4},{6,7},{7,6},{8,9},{9,8},{10,11... | collective-permute-start | bytes 1572872 | tf_op jit(solution)/shard_map/ppermute | solution.py:630
  714.7 221.6 %reduce-scatter.13.cloned.1.call-start = ((), (), s32[]{:S(2)}) async-start(), calls=%async_computation.10 | async-start | bytes 655360 | tf_op jit(solution)/shard_map/reduce_scatter | solution.py:781
  727.8 45.6 %collective-permute-start.66 = (bf16[2,64,512]{2,1,0:T(8,128)(2,1)S(1)}, bf16[2,64,512]{2,1,0:T(8,128)(2,1)S(1)}, u32[]{:S(2)}, u32[]{:S(2)}) collective-permute-start(bf16[2,64,512]{2,1,0:T(8,128)(2,1)S(1)} %get-tuple-element.235), channel_id=1, source_target_pairs={{0,4},{2,6},{4,0},{6,2},{8,12},{10,14},{12,8},{14,10},{16,20},{18,... | collective-permute-start | bytes 393224 | tf_op jit(solution)/shard_map/ppermute | solution.py:632
  742.7 30.7 %collective-permute-start.67 = (bf16[2,64,512]{2,1,0:T(8,128)(2,1)S(1)}, bf16[2,64,512]{2,1,0:T(8,128)(2,1)S(1)}, u32[]{:S(2)}, u32[]{:S(2)}) collective-permute-start(bf16[2,64,512]{2,1,0:T(8,128)(2,1)S(1)} %get-tuple-element.236), channel_id=1, source_target_pairs={{0,1},{1,0},{2,3},{3,2},{4,5},{5,4},{6,7},{7,6},{8,9},{9,8},{10,11... | collective-permute-start | bytes 393224 | tf_op jit(solution)/shard_map/ppermute | solution.py:630
  793.2 48.7 %collective-permute-start.73 = (bf16[4,2,64,4096]{3,2,1,0:T(8,128)(2,1)}, bf16[4,2,64,4096]{3,2,1,0:T(8,128)(2,1)}, u32[]{:S(2)}, u32[]{:S(2)}) collective-permute-start(bf16[4,2,64,4096]{3,2,1,0:T(8,128)(2,1)} %get-tuple-element.253), channel_id=1, source_target_pairs={{0,2},{2,0},{4,6},{6,4},{8,10},{10,8},{12,14},{14,12},{16,18},{18,... | collective-permute-start | bytes 12582920 | tf_op jit(solution)/shard_map/ppermute | solution.py:632
  793.2 145.3 %reduce-scatter.17.cloned.1.call-start = ((), (), s32[]{:S(2)}) async-start(), calls=%async_computation.12 | async-start | bytes 327680 | tf_op jit(solution)/shard_map/reduce_scatter | solution.py:781
  815.0 125.1 %reduce-scatter.15.cloned.1.call-start = ((), (), s32[]{:S(2)}) async-start(), calls=%async_computation.11 | async-start | bytes 655360 | tf_op jit(solution)/shard_map/reduce_scatter | solution.py:781
  817.5 34.3 %collective-permute-start.72 = (bf16[4,2,32,1024]{3,2,1,0:T(8,128)(2,1)}, bf16[4,2,32,1024]{3,2,1,0:T(8,128)(2,1)}, u32[]{:S(2)}, u32[]{:S(2)}) collective-permute-start(bf16[4,2,32,1024]{3,2,1,0:T(8,128)(2,1)} %get-tuple-element.277), channel_id=1, source_target_pairs={{0,2},{2,0},{4,6},{6,4},{8,10},{10,8},{12,14},{14,12},{16,18},{18,... | collective-permute-start | bytes 1572872 | tf_op jit(solution)/shard_map/ppermute | solution.py:632
  817.5 38.0 %collective-permute-start.70 = (bf16[4,64,2048]{2,1,0:T(8,128)(2,1)}, bf16[4,64,2048]{2,1,0:T(8,128)(2,1)}, u32[]{:S(2)}, u32[]{:S(2)}) collective-permute-start(bf16[4,64,2048]{2,1,0:T(8,128)(2,1)} %get-tuple-element.245.refs_6_), channel_id=1, source_target_pairs={{0,4},{2,6},{4,0},{6,2},{8,12},{10,14},{12,8},{14,10},{16,20},{18,... | collective-permute-start | bytes 3145736 | tf_op jit(solution)/shard_map/ppermute | solution.py:632
  818.5 38.1 %collective-permute-start.71 = (bf16[4,64,2048]{2,1,0:T(8,128)(2,1)}, bf16[4,64,2048]{2,1,0:T(8,128)(2,1)}, u32[]{:S(2)}, u32[]{:S(2)}) collective-permute-start(bf16[4,64,2048]{2,1,0:T(8,128)(2,1)} %get-tuple-element.246), channel_id=1, source_target_pairs={{0,1},{1,0},{2,3},{3,2},{4,5},{5,4},{6,7},{7,6},{8,9},{9,8},{10,11... | collective-permute-start | bytes 3145736 | tf_op jit(solution)/shard_map/ppermute | solution.py:630
  819.6 123.2 %reduce-scatter.19.cloned.1.call-start = ((), (), s32[]{:S(2)}) async-start(), calls=%async_computation.13 | async-start | bytes 163840 | tf_op jit(solution)/shard_map/reduce_scatter | solution.py:781
  892.2 52.1 %reduce-scatter.11.cloned.1.call-start = ((), (), s32[]{:S(2)}) async-start(), calls=%async_computation.9 | async-start | bytes 1310720 | tf_op jit(solution)/shard_map/reduce_scatter | solution.py:781
  892.7 73.7 %reduce-scatter.9.cloned.1.call-start = ((), (), s32[]{:S(2)}) async-start(), calls=%async_computation.8 | async-start | bytes 1310720 | tf_op jit(solution)/shard_map/reduce_scatter | solution.py:781
  (152 other events, 3142.9 us)
Sparse Core Ops, SparseCore 0:
  9.6 30.6 all-gather.10
  41.9 27.4 all-gather.16
  71.5 32.1 all-gather.12
  105.7 31.6 all-gather.14
  413.8 27.7 all-gather.18
  711.9 25.6 reduce-scatter.22
  740.0 25.7 reduce-scatter.20
  793.4 21.1 reduce-scatter.12
  817.4 17.8 reduce-scatter.16
  838.1 19.8 reduce-scatter.14
  892.3 18.0 reduce-scatter.18
  912.5 25.6 reduce-scatter.10
  940.6 25.7 reduce-scatter.8

commit v4 on v3

--- a/solution.py
+++ b/solution.py
@@ -87,6 +87,36 @@
 
 
 ROWS = 128
+COLS = 512
+
+
+def group_spec(weight, group):
+    array, start, rows = weight
+    groups = 4
+
+    def place_of(*ids):
+        which = group(ids[0])
+        return 0, which // groups, start // rows + which % groups, 0
+
+    return pl.BlockSpec((16, 1, rows, COLS), place_of)
+
+
+def rows_spec(weight, count, step=lambda i: i):
+    array, start, rows = weight
+    return pl.BlockSpec((count, 2, rows, COLS), lambda *ids: (step(ids[0]), 0, start // rows, 0))
+
+
+def side(w_ref, y, blocks=slice(None)):
+    values = w_ref[blocks, y]
+    return values.reshape(-1, COLS)
+
+
+def times(left, w_ref, blocks=slice(None)):
+    return jnp.concatenate([dot(left, side(w_ref, y, blocks), NN) for y in range(2)], axis=1)
+
+
+def times_turned(left, w_ref):
+    return sum(dot(left[:, y * COLS : (y + 1) * COLS], side(w_ref, y), NT) for y in range(2))
 
 
 def norm_project_kernel(x_ref, gain_ref, w_ref, normed_ref, out_ref):
@@ -98,16 +128,16 @@
             centered, inverse = norm_rows(x_ref[at, :].astype(F32))
             normed_ref[at, :] = narrow(centered * inverse * gain_ref[...])
 
-    out_ref[...] = narrow(dot(normed_ref[...], w_ref[...], NN))
+    out_ref[...] = narrow(dot(normed_ref[...], side(w_ref, 0), NN))
 
 
 def norm_project(x, gain, weight, after=()):
     rows, width = x.shape
-    cols = weight.shape[1]
-    step = 512
-    return launch(
-        norm_project_kernel, [x, gain, weight], after=after, name="norm_project", grid=(cols // step,),
-        in_specs=[whole((rows, width)), whole((1, width)), pl.BlockSpec((width, step), lambda i: (0, i))],
+    cols = 4 * width
+    step = COLS
+    return launch(
+        norm_project_kernel, [x, gain, weight[0]], after=after, name="norm_project", grid=(cols // step,),
+        in_specs=[whole((rows, width)), whole((1, width)), group_spec(weight, lambda i: i)],
         out_specs=[whole((rows, width)), pl.BlockSpec((rows, step), lambda i: (0, i))],
         out_shape=[shaped((rows, width)), shaped((rows, cols))],
         flops=2 * rows * width * cols,
@@ -115,10 +145,10 @@
 
 
 def update_kernel(live_ref, self_ref, cross_ref, out_w_ref, gate_w_ref, bias_ref, state_ref, mixed_ref, gate_ref, new_ref):
-    width = self_ref.shape[1]
-    mixed = narrow(dot(self_ref[...], out_w_ref[:width, :], NN) + dot(cross_ref[...], out_w_ref[width:, :], NN))
+    low, high = slice(0, 8), slice(8, 16)
+    mixed = narrow(times(self_ref[...], out_w_ref, low) + times(cross_ref[...], out_w_ref, high))
     mixed_ref[...] = mixed
-    gate = jax.nn.sigmoid(dot(mixed, gate_w_ref[...], NN) + bias_ref[...])
+    gate = jax.nn.sigmoid(times(mixed, gate_w_ref) + bias_ref[...])
     gate_ref[...] = gate
     state = state_ref[...]
     updated = gate * state + (1.0 - gate) * jnp.tanh(mixed.astype(F32))
@@ -130,9 +160,9 @@
     step = 256
     tile = pl.BlockSpec((step, width), lambda i: (i, 0))
     return launch(
-        update_kernel, [live, inner_self, inner_cross, state_out, gate_weight, bias, state],
+        update_kernel, [live, inner_self, inner_cross, state_out[0], gate_weight[0], bias, state],
         after=after, name="update_state", grid=(rows // step,),
-        in_specs=[SMEM, tile, tile, whole(state_out.shape), whole(gate_weight.shape), whole((1, width)), tile],
+        in_specs=[SMEM, tile, tile, rows_spec(state_out, 16, lambda i: 0), rows_spec(gate_weight, 16, lambda i: 0), whole((1, width)), tile],
         out_specs=[tile, tile, tile],
         out_shape=[shaped((rows, width)), shaped((rows, width), F32), shaped((rows, width), F32)],
         flops=6 * rows * width * width, exps=2 * rows * width,
@@ -140,10 +170,8 @@
 
 
 def branch_kernel(self_ref, cross_ref, w_ref, x_ref, gain_ref, middle_ref, normed_ref):
-    width = self_ref.shape[1]
-    middle = x_ref[...].astype(F32) + (
-        dot(self_ref[...], w_ref[:width, :], NN) + dot(cross_ref[...], w_ref[width:, :], NN)
-    )
+    low, high = slice(0, 8), slice(8, 16)
+    middle = x_ref[...].astype(F32) + (times(self_ref[...], w_ref, low) + times(cross_ref[...], w_ref, high))
     middle_ref[...] = middle
     centered, inverse = norm_rows(middle)
     normed_ref[...] = narrow(centered * inverse * gain_ref[...])
@@ -154,8 +182,8 @@
     step = 256
     tile = pl.BlockSpec((step, width), lambda i: (i, 0))
     return launch(
-        branch_kernel, [self_out, cross_out, token_out, x, gain], after=after, name="branch", grid=(rows // step,),
-        in_specs=[tile, tile, whole(token_out.shape), tile, whole((1, width))],
+        branch_kernel, [self_out, cross_out, token_out[0], x, gain], after=after, name="branch", grid=(rows // step,),
+        in_specs=[tile, tile, rows_spec(token_out, 16, lambda i: 0), tile, whole((1, width))],
         out_specs=[tile, tile],
         out_shape=[shaped((rows, width), F32), shaped((rows, width))],
         flops=4 * rows * width * width,
@@ -169,7 +197,7 @@
 def hidden_kernel(normed_ref, w_ref, active_ref, slope_ref):
     for start in range(0, normed_ref.shape[0], 256):
         at = slice(start, start + 256)
-        v = dot(normed_ref[at, :], w_ref[...], NN)
+        v = dot(normed_ref[at, :], side(w_ref, 0), NN)
         square = v * v
         t = jnp.tanh(v * (GELU_A + (GELU_A * GELU_B) * square))
         half = 0.5 + 0.5 * t
@@ -180,12 +208,12 @@
 
 def hidden(normed, weight, after=()):
     rows, width = normed.shape
-    cols = weight.shape[1]
-    step = 512
+    cols = 4 * width
+    step = COLS
     tile = pl.BlockSpec((rows, step), lambda i: (0, i))
     return launch(
-        hidden_kernel, [normed, weight], after=after, name="hidden", grid=(cols // step,),
-        in_specs=[whole((rows, width)), pl.BlockSpec((width, step), lambda i: (0, i))],
+        hidden_kernel, [normed, weight[0]], after=after, name="hidden", grid=(cols // step,),
+        in_specs=[whole((rows, width)), group_spec(weight, lambda i: i)],
         out_specs=[tile, tile], out_shape=[shaped((rows, cols))] * 2,
         flops=2 * rows * width * cols, exps=rows * cols,
     )
@@ -195,8 +223,8 @@
     first = pl.program_id(0) == 0
     for start in range(0, active_ref.shape[0], 256):
         at = slice(start, start + 256)
-        pre_ref[at, :] = narrow(dot(grad_ref[at, :], w_ref[...], NT) * slope_ref[at, :].astype(F32))
-        total_ref[at, :] = jnp.where(first, middle_ref[at, :], total_ref[at, :]) + dot(active_ref[at, :], w_ref[...], NN)
+        pre_ref[at, :] = narrow(times_turned(grad_ref[at, :], w_ref) * slope_ref[at, :].astype(F32))
+        total_ref[at, :] = jnp.where(first, middle_ref[at, :], total_ref[at, :]) + times(active_ref[at, :], w_ref)
 
     @pl.when(pl.program_id(0) == pl.num_programs(0) - 1)
     def _():
@@ -209,9 +237,9 @@
     step = 512
     tile = pl.BlockSpec((rows, step), lambda i: (0, i))
     return launch(
-        result_kernel, [active, slope, weight, middle, grad], after=after, name="result_and_pre",
+        result_kernel, [active, slope, weight[0], middle, grad], after=after, name="result_and_pre",
         grid=(hidden_units // step,),
-        in_specs=[tile, tile, pl.BlockSpec((step, width), lambda i: (i, 0)), whole((rows, width)), whole((rows, width))],
+        in_specs=[tile, tile, rows_spec(weight, step // weight[2]), whole((rows, width)), whole((rows, width))],
         out_specs=[whole((rows, width)), tile],
         out_shape=[shaped((rows, width)), shaped((rows, hidden_units))],
         scratch=[pltpu.VMEM((rows, width), F32)],
@@ -232,7 +260,7 @@
     for part in range(parts):
         @pl.when(i // share == part)
         def _():
-            total_ref[...] += dot(grads[part][...], w_ref[...], NT)
+            total_ref[...] += dot(grads[part][...], side(w_ref, 0), NT)
 
     @pl.when(i == pl.num_programs(0) - 1)
     def _():
@@ -263,10 +291,10 @@
     if scale is None:
         scale = jnp.ones((1,), F32)
     return launch(
-        partial(norm_back_kernel, parts, keep_wide), [scale, *grads, weight, x, gain, plus], after=after, name=name,
+        partial(norm_back_kernel, parts, keep_wide), [scale, *grads, weight[0], x, gain, plus], after=after, name=name,
         grid=(steps,),
         in_specs=[SMEM] + [part_spec(part) for part in range(parts)]
-        + [pl.BlockSpec((width, step), lambda i: (0, i + offset // step)), whole((rows, width)), whole((1, width)), whole((rows, width))],
+        + [group_spec(weight, lambda i: i + offset // step), whole((rows, width)), whole((1, width)), whole((rows, width))],
         out_specs=[whole(item.shape) for item in out_shape], out_shape=out_shape,
         scratch=[pltpu.VMEM((rows, width), F32)],
         flops=2 * rows * width * steps * step,
@@ -274,16 +302,16 @@
 
 
 def spread_kernel(grad_ref, w_ref, out_ref):
-    out_ref[...] = narrow(dot(grad_ref[...], w_ref[...], NT))
+    out_ref[...] = narrow(times_turned(grad_ref[...], w_ref))
 
 
 def spread(grad, weight, after=()):
     rows, width = grad.shape
-    cols = weight.shape[0]
+    cols = 16 * weight[2]
     step = 512
     return launch(
-        spread_kernel, [grad, weight], after=after, name="spread", grid=(cols // step,),
-        in_specs=[whole((rows, width)), pl.BlockSpec((step, width), lambda i: (i, 0))],
+        spread_kernel, [grad, weight[0]], after=after, name="spread", grid=(cols // step,),
+        in_specs=[whole((rows, width)), rows_spec(weight, step // weight[2])],
         out_specs=[pl.BlockSpec((rows, step), lambda i: (0, i))],
         out_shape=[shaped((rows, cols))], flops=2 * rows * width * cols,
     )[0]
@@ -305,10 +333,10 @@
     low = narrow(pre)
     pre_ref[...] = low
     grad_mixed = narrow(
-        dot(low, gate_w_ref[...], NT) + updated * (1.0 - gate) * (1.0 - tanh_mixed * tanh_mixed)
+        times_turned(low, gate_w_ref) + updated * (1.0 - gate) * (1.0 - tanh_mixed * tanh_mixed)
     )
     grad_mixed_ref[...] = grad_mixed
-    inner_ref[...] = narrow(dot(grad_mixed, out_w_ref[...], NT))
+    inner_ref[...] = narrow(times_turned(grad_mixed, out_w_ref))
 
 
 def gate_back(live, grad, gate, state, mixed, gate_weight, state_out, after=()):
@@ -317,9 +345,9 @@
     tile = pl.BlockSpec((step, width), lambda i: (i, 0))
     wide = pl.BlockSpec((step, 2 * width), lambda i: (i, 0))
     return launch(
-        gate_back_kernel, [live, grad, gate, state, mixed, gate_weight, state_out], after=after, name="gate_back",
+        gate_back_kernel, [live, grad, gate, state, mixed, gate_weight[0], state_out[0]], after=after, name="gate_back",
         grid=(rows // step,),
-        in_specs=[SMEM, tile, tile, tile, tile, whole(gate_weight.shape), whole(state_out.shape)],
+        in_specs=[SMEM, tile, tile, tile, tile, rows_spec(gate_weight, 16, lambda i: 0), rows_spec(state_out, 16, lambda i: 0)],
         out_specs=[tile, tile, wide, tile, whole((1, width))],
         out_shape=[shaped((rows, width)), shaped((rows, width)), shaped((rows, 2 * width)), shaped((rows, width), F32), shaped((1, width), F32)],
         flops=6 * rows * width * width, exps=rows * width,
@@ -636,115 +664,75 @@
 
 
 def place():
+    if not paired():
+        return jnp.zeros((3,), jnp.int32)
     dp = lax.axis_index("dp")
     return jnp.stack([(dp // 2) % 2, dp % 2, lax.axis_index("fsdp")]).astype(jnp.int32)
 
 
-def assemble_kernel(sizes, place_ref, *refs):
-    x, core, y = place_ref[0], place_ref[1], place_ref[2]
-    pieces, outs = refs[:10], refs[10:]
-    cols = pieces[0].shape[-1]
-
-    def put(piece, dx, dy, other):
-        line = (x ^ dx) * 2 + (core ^ other)
-        at = pl.ds(pl.multiple_of((y ^ dy) * cols, 128), cols)
-        row = 0
-        for size, out in zip(sizes, outs):
-            out[0, line, :, at] = piece[0, row : row + size, :]
-            row += size
-
-    for other in range(2):
-        put(pieces[5 * other], 0, 0, other)
-        put(pieces[5 * other + 1], 1, 0, other)
-        put(pieces[5 * other + 2], 0, 1, other)
-
-        @pl.when(pl.program_id(0) < 2)
-        def _():
-            put(pieces[5 * other + 3], 1, 1, other)
-
-        @pl.when(pl.program_id(0) >= 2)
-        def _():
-            put(pieces[5 * other + 4], 1, 1, other)
-
-
-def assemble(pieces, sizes, where, after=()):
-    _, rows, cols = pieces[0].shape
-    full = pl.BlockSpec((1, rows, cols), lambda z, p: (z, 0, 0))
-    low = pl.BlockSpec((1, rows, cols), lambda z, p: (jnp.minimum(z, 1), 0, 0))
-    high = pl.BlockSpec((1, rows, cols), lambda z, p: (jnp.maximum(z, 2) - 2, 0, 0))
-    outs = launch(
-        partial(assemble_kernel, sizes), pieces, where=where, after=after, name="assemble", grid=(4,),
-        in_specs=[full, full, full, low, high] * 2,
-        out_specs=[pl.BlockSpec((1, 4, size, 2 * cols), lambda z, p: (z, 0, 0, 0)) for size in sizes],
-        out_shape=[shaped((4, 4, size, 2 * cols)) for size in sizes],
-        flops=0,
-    )
-    return [out.reshape(-1, 2 * cols) for out in outs]
-
-
-def gather_pieces(blocks):
-    packed = blocks[0] if len(blocks) == 1 else jnp.concatenate(blocks, axis=0)
-    line = lax.all_gather(packed, "dp", axis=0, axis_index_groups=LINES)
-    over_x, over_y = swap(line, "x"), swap(line, "y")
-    near = [line, over_x, over_y, swap(over_x[:2], "y"), swap(over_y[2:], "x")]
-    return near + [swap(piece, "core") for piece in near]
+def fence_kernel(*refs):
+    pass
+
+
+def fence(arrays, after):
+    return launch(
+        fence_kernel, arrays, after=after, name="fence", grid=(1,),
+        in_specs=[pl.BlockSpec(memory_space=pl.ANY)] * len(arrays),
+        out_specs=[pl.BlockSpec(memory_space=pl.ANY)] * len(arrays),
+        out_shape=[shaped(item.shape, item.dtype) for item in arrays],
+        aliases={i: i for i in range(len(arrays))}, flops=0,
+    )
+
+
+def stacked(block):
+    return [block[:, i : i + COLS] for i in range(0, block.shape[1], COLS)]
+
+
+def gather_blocks(blocks):
+    packed = jnp.concatenate([part for block in blocks for part in stacked(block)], axis=0)
+    every = lax.all_gather(packed, ("dp", "fsdp"), axis=0).reshape(16, 2, *packed.shape)
+    weights, row = [], 0
+    for block in blocks:
+        weights.append((every, row, block.shape[0]))
+        row += block.shape[0] * block.shape[1] // COLS
+    return weights
 
 
 def add(*terms):
     return sum(term.astype(F32) for term in terms)
 
 
-def fold_core_kernel(place_ref, keep_ref, come_ref, low_ref, high_ref, px_ref, py_ref, own_ref):
+def fold_core_kernel(place_ref, keep_ref, come_ref, far_ref, px_ref, py_ref, own_ref):
     x, y = place_ref[0], place_ref[2]
     cols = own_ref.shape[-1]
-
-    def total(z, dx, dy):
+    for out, dx, dy in ((own_ref, 0, 0), (px_ref, 1, 0), (py_ref, 0, 1), (far_ref, 1, 1)):
         at = pl.ds(pl.multiple_of((y ^ dy) * cols, 128), cols)
-        return narrow(add(keep_ref[z, x ^ dx, :, at], come_ref[z, x ^ dx, :, at]))
-
-    for z in range(2):
-        own_ref[z] = total(z, 0, 0)
-        px_ref[z] = total(z, 1, 0)
-        py_ref[z] = total(z, 0, 1)
-
-    @pl.when(pl.program_id(0) == 0)
-    def _():
-        for z in range(2):
-            low_ref[z] = total(z, 1, 1)
-
-    @pl.when(pl.program_id(0) == 1)
-    def _():
-        for z in range(2):
-            high_ref[z] = total(z, 1, 1)
+        for z in range(out.shape[0]):
+            out[z] = narrow(add(keep_ref[z, x ^ dx, :, at], come_ref[z, x ^ dx, :, at]))
 
 
 def fold_core(keep, come, where, after=()):
     _, _, rows, cols = keep.shape
     pair = pl.BlockSpec((2, 2, rows, cols), lambda i, p: (i, 0, 0, 0))
-    half = pl.BlockSpec((2, rows, cols // 2), lambda i, p: (0, 0, 0))
     full = pl.BlockSpec((2, rows, cols // 2), lambda i, p: (i, 0, 0))
     return launch(
         fold_core_kernel, [keep, come], where=where, after=after, name="fold_core", grid=(2,),
-        in_specs=[pair, pair], out_specs=[half, half, full, full, full],
-        out_shape=[shaped((2, rows, cols // 2))] * 2 + [shaped((4, rows, cols // 2))] * 3,
+        in_specs=[pair, pair], out_specs=[full] * 4, out_shape=[shaped((4, rows, cols // 2))] * 4,
         flops=keep.size,
     )
 
 
-def fold_mid_kernel(px_ref, py_ref, rx_ref, ry_ref, px_out, py_out):
-    px_out[...] = narrow(add(px_ref[...], ry_ref[...]))
-    py_out[...] = narrow(add(py_ref[...], rx_ref[...]))
-
-
-def fold_mid(px, py, rx, ry, after=()):
-    block = rx.shape
-    low = pl.BlockSpec(block, lambda i: (0, 0, 0))
-    high = pl.BlockSpec(block, lambda i: (1, 0, 0))
-    return launch(
-        fold_mid_kernel, [px, py, rx, ry], after=after, name="fold_mid", grid=(1,),
-        in_specs=[high, low, low, low], out_specs=[high, low],
-        out_shape=[shaped(px.shape), shaped(py.shape)], aliases={0: 0, 1: 1}, flops=px.size,
-    )
+def fold_mid_kernel(near_ref, come_ref, out_ref):
+    out_ref[...] = narrow(add(near_ref[...], come_ref[...]))
+
+
+def fold_mid(near, come, after=()):
+    _, rows, cols = near.shape
+    block = pl.BlockSpec((2, rows, cols), lambda i: (i, 0, 0))
+    return launch(
+        fold_mid_kernel, [near, come], after=after, name="fold_mid", grid=(2,),
+        in_specs=[block] * 2, out_specs=[block], out_shape=[shaped(near.shape)], flops=near.size,
+    )[0]
 
 
 def fold_last_kernel(own_ref, rx_ref, ry_ref, out_ref):
@@ -761,27 +749,31 @@
 
 
 class Scatter:
-    def __init__(self, keep, send, where):
-        self.where, self.keep = where, keep
+    def __init__(self, keep, send, way, where):
+        self.where, self.keep, self.way = where, keep, way
         self.come = swap(send, "core")
 
     def core(self, after):
-        low, high, self.px, self.py, self.own = fold_core(self.keep, self.come, self.where, after)
-        self.rx, self.ry = swap(low, "x"), swap(high, "y")
-        return self.own
+        far, px, py, self.own = fold_core(self.keep, self.come, self.where, after)
+        self.far = swap(far, self.way)
+        if self.way == "x":
+            self.near, self.one = py, swap(px, "x")
+        else:
+            self.near, self.one = px, swap(py, "y")
+        return (self.own,)
 
     def mid(self, after):
-        px, py = fold_mid(self.px, self.py, self.rx, self.ry, after)
-        self.rx, self.ry = swap(px, "x"), swap(py, "y")
-        return px
+        near = fold_mid(self.near, self.far, after)
+        self.two = swap(near, "y" if self.way == "x" else "x")
+        return (near,)
 
     def last(self, after):
-        line = fold_last(self.own, self.rx, self.ry, after)
+        line = fold_last(self.own, self.one, self.two, after)
         rows, cols = line.shape[1:]
         self.out = lax.psum_scatter(
             line.reshape(4 * rows, cols), "dp", scatter_dimension=0, axis_index_groups=LINES, tiled=True
         )
-        return line
+        return (line,)
 
 
 def paired():
@@ -789,7 +781,10 @@
 
 
 def gather_plain(block):
-    return lax.all_gather(lax.all_gather(block, "fsdp", axis=1, tiled=True), "dp", axis=0, tiled=True)
+    full = lax.all_gather(lax.all_gather(block, "fsdp", axis=1, tiled=True), "dp", axis=0, tiled=True)
+    rows, cols = full.shape[0] // 16, full.shape[1]
+    cut = full.reshape(16, rows, 2, cols // 2 // COLS, COLS).transpose(0, 2, 3, 1, 4)
+    return cut.reshape(16, 2, -1, COLS), 0, rows
 
 
 def scatter_plain(grad):
@@ -860,65 +855,46 @@
     token_gain_f, state_gain_f, hidden_gain_f, gate_bias_f = [gains[i : i + 1] for i in range(4)]
     order = ()
 
-    if paired():
-        packed_init = jnp.pad(init_state.reshape(8, 2048), ((0, 8), (0, 0)))
-        pieces = [
-            gather_pieces(blocks)
-            for blocks in (
-                [state_proj, packed_init],
-                [token_proj],
-                [state_out, gate_weight, token_out],
-                [hidden_in],
-                [hidden_out],
-            )
-        ]
-        full_state_proj, full_init = assemble(pieces[0], [64, 16], where)
-        full_init = full_init.reshape(16, 16, 2, 4, 512)[:, :8].transpose(0, 1, 3, 2, 4).reshape(states, width)
-    else:
-        full_state_proj, full_token_proj, full_state_out, full_gate_weight, full_token_out, full_init = [
-            gather_plain(w) for w in (state_proj, token_proj, state_out, gate_weight, token_out, init_state)
-        ]
-        full_hidden_in, full_hidden_out = gather_plain(hidden_in), gather_plain(hidden_out)
+    early = [token_proj, state_proj, state_out, token_out, gate_weight, init_state]
+    late = [hidden_in, hidden_out]
+    gather = gather_blocks if paired() else lambda blocks: [gather_plain(block) for block in blocks]
+    full_token_proj, full_state_proj, full_state_out, full_token_out, full_gate_weight, full_init = gather(early)
+    full_hidden_in, full_hidden_out = gather(late)
+    array, row, rows = full_init
+    full_init = array[:, :, row : row + rows].transpose(0, 2, 1, 3).reshape(states, width)
     state_0 = jnp.where(first, full_init, incoming[0]).astype(F32)
+    normed, projected = norm_project(tokens, token_gain_f, full_token_proj, order)
+    order = (projected,)
     normed_0, side_0 = norm_project(state_0, state_gain_f, full_state_proj, order)
     order = (side_0,)
-    if paired():
-        (full_token_proj,) = assemble(pieces[1], [64], where, order)
-    normed, projected = norm_project(tokens, token_gain_f, full_token_proj, order)
-    order = (projected,)
     inner_self_0, inner_cross_0, inner_self_log, inner_cross_log = inner_attention(
         projected, side_0, live_keys[0], 0, order
     )
     order = (inner_self_log,)
-    cross_out, cross_log_0 = cross_attention(projected, side_0, 0, None, order)
-    order = (cross_log_0,)
-    self_out, self_log = self_attention(projected, window, order)
-    order = (self_log,)
-    if paired():
-        full_state_out, full_gate_weight, full_token_out = assemble(pieces[2], [128, 64, 128], where, order)
-        order = (full_gate_weight,)
     mixed_0, gate_0, state_1 = update_state(
         lives[0], inner_self_0, inner_cross_0, full_state_out, full_gate_weight, gate_bias_f, state_0, order
     )
     order = (mixed_0,)
     normed_1, side_1 = norm_project(state_1, state_gain_f, full_state_proj, order)
     order = (normed_1,)
+    cross_out, cross_log_0 = cross_attention(projected, side_0, 0, None, order)
+    order = (cross_log_0,)
     cross_out, cross_log_1 = cross_attention(projected, side_1, 1, cross_out, order)
     order = (cross_log_1,)
+    self_out, self_log = self_attention(projected, window, order)
+    order = (self_log,)
     middle, hidden_normed = branch(self_out, cross_out, full_token_out, tokens, hidden_gain_f, order)
     order = (hidden_normed,)
-    if paired():
-        (full_hidden_in,) = assemble(pieces[3], [64], where, order)
     active, slope = hidden(hidden_normed, full_hidden_in, order)
     order = (active,)
 
     scatters = {}
 
-    def weight(name, lefts, rights, plan, split=False):
+    def weight(name, way, lefts, rights, plan, split=False):
         nonlocal order
         if paired():
             keep, send = weight_grad(lefts, rights, plan, where, "grad_" + name, split, order)
-            scatters[name] = Scatter(keep, send, where)
+            scatters[name] = Scatter(keep, send, way, where)
             order = (keep,)
             return
         if split:
@@ -931,17 +907,15 @@
     def fold(name, step):
         nonlocal order
         if paired():
-            order = (getattr(scatters[name], step)(order),)
-
-    weight("hidden_out", [active], [output_grad], [[(0, 0)]])
-    if paired():
-        (full_hidden_out,) = assemble(pieces[4], [256], where, order)
-        order = (full_hidden_out,)
+            order = getattr(scatters[name], step)(order)
+
+    one = [[(0, 0)]]
+    weight("hidden_out", "x", [active], [output_grad], one)
     fold("hidden_out", "core")
     result, grad_pre = result_and_pre(active, slope, full_hidden_out, middle, output_grad, order)
     order = (result,)
     fold("hidden_out", "mid")
-    weight("hidden_in", [hidden_normed], [grad_pre], [[(0, 0)]])
+    weight("hidden_in", "y", [hidden_normed], [grad_pre], one)
     grad_hidden_gain, grad_branch, grad_middle = norm_back_project(
         [grad_pre], full_hidden_in, middle, hidden_gain_f, output_grad, "hidden_back", True, after=order
     )
@@ -950,11 +924,13 @@
     fold("hidden_out", "last")
     grad_attended = spread(grad_branch, full_token_out, order)
     order = (grad_attended,)
+    weight("token_out", "x", [self_out, cross_out], [grad_branch], one, True)
     grad_cross, grad_keys_1, grad_values_1 = cross_attention_back(
         projected, side_1, cross_out, cross_log_1, grad_attended, 1, order
     )
     order = (grad_keys_1,)
     fold("hidden_in", "mid")
+    fold("token_out", "core")
     no_term = jnp.zeros((states, width), jnp.bfloat16)
     grad_state_gain_1, _, grad_state_1 = norm_back_project(
         [grad_keys_1, grad_values_1], full_state_proj, state_1, state_gain_f, no_term, "side_back", True,
@@ -965,67 +941,64 @@
         lives[0], grad_state_1, gate_0, state_0, mixed_0, full_gate_weight, full_state_out, order
     )
     order = (grad_gate_bias,)
-    weight_pairs = [[(0, 0)]]
-    weight("token_out", [self_out, cross_out], [grad_branch], weight_pairs, True)
-    fold("hidden_in", "last")
+    fold("token_out", "mid")
     parts = state_attention_back(
         projected, side_0, live_keys[0], (cross_out, cross_log_0), (inner_self_0, inner_self_log),
         (inner_cross_0, inner_cross_log), grad_attended, grad_inner, grad_cross, 0, order,
     )
     grad_cross, grads_side_0, extra_keys, extra_values = parts[0], parts[1:5], parts[5], parts[6]
     order = (extra_keys,)
-    fold("token_out", "core")
-    weight("state_out", [inner_self_0, inner_cross_0], [grad_mixed], weight_pairs, True)
-    weight("gate_weight", [mixed_0], [grad_gate_low], weight_pairs)
-    fold("token_out", "mid")
-    weight(
-        "state_proj", [normed_0, normed_1], [*grads_side_0, grad_keys_1, grad_values_1],
-        [[(0, 0)], [(0, 1)], [(0, 2), (1, 4)], [(0, 3), (1, 5)]],
-    )
+    fold("hidden_in", "last")
+    weight("state_out", "y", [inner_self_0, inner_cross_0], [grad_mixed], one, True)
+    weight("gate_weight", "y", [mixed_0], [grad_gate_low], one)
+    fold("token_out", "last")
     fold("state_out", "core")
     fold("gate_weight", "core")
+    grad_self, grad_keys, grad_values = self_attention_back(
+        projected, self_out, self_log, grad_attended, extra_keys, extra_values, window, order
+    )
+    order = (grad_self,)
+    grads_projected = [grad_self, grad_cross, grad_keys, grad_values]
+    weight("token_proj", "x", [normed], grads_projected, [[(0, i)] for i in range(4)])
+    fold("state_out", "mid")
+    fold("gate_weight", "mid")
+    weight(
+        "state_proj", "y", [normed_0, normed_1], [*grads_side_0, grad_keys_1, grad_values_1],
+        [[(0, 0)], [(0, 1)], [(0, 2), (1, 4)], [(0, 3), (1, 5)]],
+    )
+    fold("token_proj", "core")
     grad_state_gain_0, grad_init = norm_back_project(
         grads_side_0, full_state_proj, state_0, state_gain_f, grad_direct, "state_back",
         scale=jnp.where(first, 1.0, 0.0).astype(F32).reshape(1), after=order,
     )
     order = (grad_state_gain_0,)
-    fold("token_out", "last")
     fold("state_proj", "core")
-    grad_self, grad_keys, grad_values = self_attention_back(
-        projected, self_out, self_log, grad_attended, extra_keys, extra_values, window, order
-    )
-    order = (grad_self,)
-    fold("state_out", "mid")
-    fold("gate_weight", "mid")
-    fold("state_proj", "mid")
-    grads_projected = [grad_self, grad_cross, grad_keys, grad_values]
-    weight("token_proj", [normed], grads_projected, [[(0, i)] for i in range(4)])
     fold("state_out", "last")
     fold("gate_weight", "last")
     if paired():
         parts = grad_init.reshape(4, 2, 2, 32, width)
         keep = lax.dynamic_index_in_dim(parts, where[1], 2, keepdims=False)
         send = lax.dynamic_index_in_dim(parts, 1 - where[1], 2, keepdims=False)
-        scatters["init"] = Scatter(keep, send, where)
+        scatters["init"] = Scatter(keep, send, "x", where)
     else:
         scatters["init"] = scatter_plain(grad_init)
     grad_token_gain, tokens_grad = norm_back_project(
         grads_projected, full_token_proj, tokens, token_gain_f, grad_middle, "tokens_back", after=order
     )
     order = (grad_token_gain,)
-    fold("token_proj", "core")
     fold("init", "core")
-    fold("state_proj", "last")
+    fold("token_proj", "mid")
     inner_self_1, inner_cross_1, log, _ = inner_attention(projected, side_1, live_keys[1], 1, order)
     order = (log,)
-    fold("token_proj", "mid")
     fold("init", "mid")
+    fold("token_proj", "last")
+    fold("state_proj", "mid")
     _, _, state_2 = update_state(
         lives[1], inner_self_1, inner_cross_1, full_state_out, full_gate_weight, gate_bias_f, state_1, order
     )
     order = (state_2,)
     fold("init", "last")
-    fold("token_proj", "last")
+    fold("state_proj", "last")
     vector_grads = scatter_vectors(
         jnp.concatenate(
             [grad_token_gain, grad_state_gain_0 + grad_state_gain_1, grad_hidden_gain, grad_gate_bias], axis=0

time: 982 us -> 842 us (0.86)
  waiting for transfers between devices: 334 us -> 274 us
  Pallas kernels: 481 us -> 439 us
  starting transfers between devices: 70.5 us -> 33.4 us
    ppermute x63 -> x24, waiting for transfers between devices: 114 us -> 27.8 us  [swap(): return lax.ppermute(values, 'dp', [(d, d ^ bit) for d in range(16)])]
    all_gather x5 -> x2, waiting for transfers between devices: 120 us -> 165 us  [gather_blocks(): lax.all_gather(packed, ('dp', 'fsdp'), axis=0).reshape(16, 2, *packed.shape)]
    pallas_call x58 -> x53, Pallas kernels: 481 us -> 439 us  [launch(): pl.pallas_call(run, out_shape=list(out_shape), input_output_aliases=alias...]
    ppermute x63 -> x24, starting transfers between devices: 39.1 us -> 16.6 us  [swap(): return lax.ppermute(values, 'dp', [(d, d ^ bit) for d in range(16)])]
    ppermute x28 -> x14, waiting for transfers between devices: 77.8 us -> 60.1 us  [swap(): return lax.ppermute(values, 'fsdp', [(0, 1), (1, 0)])]
    unnamed x192 -> x202, local copies, waits for them, and re-layouts: 30.4 us -> 48 us
    ppermute x28 -> x14, starting transfers between devices: 30.7 us -> 16.4 us  [swap(): return lax.ppermute(values, 'fsdp', [(0, 1), (1, 0)])]
    slice x12 -> x0, local copies, waits for them, and re-layouts: 12.2 us -> none  [the longest x10 11 us: gather_pieces(): near = [line, over_x, over_y, swap(over_x[:2], 'y'), swap(over_y[2:], 'x')]]
  transfers between devices with their start and end apart: 104 -> 48, of which waited for: 29 -> 14; matrix products, arithmetic and copies ran while one was open for 4% -> 2% of each run, Pallas kernels for 38% -> 42%
where the time goes in v4:
time: 842 us; the launch traced here: 836 us
  Pallas kernels  439 us (52%)
  waiting for transfers between devices  274 us (33%)
  local copies, waits for them, and re-layouts  53 us (6%)
  starting transfers between devices  33.4 us (4%)
  between operations  18.7 us (2%)
  other arithmetic  17.6 us (2%)
    pallas_call x53, Pallas kernels, launch(): pl.pallas_call(run, out_shape=list(out_shape), input_output_aliases=alias...  439 us
    all_gather x2, waiting for transfers between devices, gather_blocks(): lax.all_gather(packed, ('dp', 'fsdp'), axis=0).reshape(16, 2, *packed.shape)  165 us
    ppermute x14, waiting for transfers between devices, swap(): return lax.ppermute(values, 'fsdp', [(0, 1), (1, 0)])  60.1 us
    unnamed x202, local copies, waits for them, and re-layouts  48 us
    ppermute x24, waiting for transfers between devices, swap(): return lax.ppermute(values, 'dp', [(d, d ^ bit) for d in range(16)])  27.8 us
    reduce_scatter x8, waiting for transfers between devices, last(): lax.psum_scatter(line.reshape(4 * rows, cols), 'dp', scatter_dimension=0,...  19.9 us
  transfers between devices with their start and end apart: 48, of which 14 were waited for; matrix products, arithmetic and copies ran while one was open for 2% of the time, Pallas kernels for 42%

profile of v4, /device:TPU:0, one launch (start us, length us, event | category | flops | bytes accessed | tf_op | source)
XLA Modules:
  0.0 835.7 jit_solution(9878818491900283865)
XLA Ops:
  19.7 3.0 collective-permute-start
  26.3 164.9 %all-gather.5.cloned.1.call-done = bf16[27648,512]{1,0:T(8,128)(2,1)} async-done(((bf16[864,512]{1,0:T(8,128)(2,1)}), bf16[27648,512]{1,0:T(8,128)(2,1)}) %all-gather.5.cloned.1.call-update) | async-done | bytes 28311568 | tf_op jit(solution)/shard_map/all_gather | solution.py:693
  195.4 15.9 %norm_project.3 = (bf16[1024,1024]{1,0:T(8,128)(2,1)S(1)}, bf16[1024,4096]{1,0:T(8,128)(2,1)}) custom-call(bf16[1024,1024]{1,0:T(8,128)(2,1)S(1)} %copy-done.12, f32[1,1024]{1,0:T(1,128)S(1)} %get-tuple-element.224.refs_1_.refs_7_, bf16[16,2,864,512]{3,2,1,0:T(8,128)(2,1)} %bitcast.56), custom_call_target="tpu_custom_call" | custom-call | flops 8589934592 | bytes 40898560 | tf_op jit(solution)/shard_map/norm_project/pallas_call | solution.py:52
  211.3 12.0 %norm_project.4 = (bf16[512,1024]{1,0:T(8,128)(2,1)S(1)}, bf16[512,4096]{1,0:T(8,128)(2,1)}) custom-call(f32[512,1024]{1,0:T(8,128)S(1)} %fusion.refs_0_.refs_6_.refs_3_, f32[1,1024]{1,0:T(1,128)S(1)} %get-tuple-element.223.refs_1_.refs_5_.refs_7_, bf16[16,2,864,512]{3,2,1,0:T(8,128)(2,1)} %bitcast.57, ...), custom_call_target="tpu_custom_call" | custom-call | flops 4294967296 | bytes 35655680 | tf_op jit(solution)/shard_map/norm_project/pallas_call | solution.py:52
  223.3 17.5 %inner_attention.2 = (bf16[512,1024]{1,0:T(8,128)(2,1)S(1)}, bf16[512,1024]{1,0:T(8,128)(2,1)S(1)}, f32[8,1,512]{2,1,0:T(1,128)S(1)}, f32[8,1,512]{2,1,0:T(1,128)S(1)}) custom-call(s32[1]{0:T(128)} %bitcast.4.refs_0_, bf16[512,4096]{1,0:T(8,128)(2,1)} %get-tuple-element.118.refs_1_.refs_2_.refs_3_.refs_4_.refs_7_.refs_5_, ...), custom_call_target="tpu_custom_call" | custom-call | flops 2147483648 | bytes 35684356 | tf_op jit(solution)/shard_map/inner_attention/pallas_call | solution.py:52
  240.9 8.9 %update_state.2 = (bf16[512,1024]{1,0:T(8,128)(2,1)S(1)}, f32[512,1024]{1,0:T(8,128)S(1)}, f32[512,1024]{1,0:T(8,128)}) custom-call(f32[1]{0:T(128)} %bitcast.3.refs_0_, bf16[512,1024]{1,0:T(8,128)(2,1)S(1)} %get-tuple-element.119.refs_1_.refs_9_, bf16[512,1024]{1,0:T(8,128)(2,1)S(1)} %get-tuple-element.120.refs_2_.refs_10_, ...), custom_call_target="tpu_custom_call" | custom-call | flops 3221225472 | bytes 66064388 | tf_op jit(solution)/shard_map/update_state/pallas_call | solution.py:52
  253.0 11.1 %norm_project.5 = (bf16[512,1024]{1,0:T(8,128)(2,1)S(1)}, bf16[512,4096]{1,0:T(8,128)(2,1)}) custom-call(f32[512,1024]{1,0:T(8,128)S(1)} %copy-done.2, f32[1,1024]{1,0:T(1,128)S(1)} %get-tuple-element.223.refs_1_.refs_5_.refs_7_, bf16[16,2,864,512]{3,2,1,0:T(8,128)(2,1)} %bitcast.60, bf16[512,1024]{1,0:T(8,128)(2,1)S(1)} %get-tuple-element.123.refs_3_.refs_4_.refs_1_), custom_call_target="tpu_custom_call" | custom-call | flops 4294967296 | bytes 35655680 | tf_op jit(solution)/shard_map/norm_project/pallas_call | solution.py:52
  264.1 10.2 %cross_attention.2 = (bf16[1024,1024]{1,0:T(8,128)(2,1)S(1)}, f32[8,1,512]{2,1,0:T(1,128)S(1)}) custom-call(bf16[1024,4096]{1,0:T(8,128)(2,1)} %get-tuple-element.117.refs_3_.refs_5_.refs_6_.refs_0_.refs_1_.refs_2_.refs_7_, bf16[512,4096]{1,0:T(8,128)(2,1)} %get-tuple-element.118.refs_1_.refs_2_.refs_3_.refs_4_.refs_7_.refs_5_, ...), custom_call_target="tpu_custom_call" | custom-call | flops 1073741824 | bytes 18890752 | tf_op jit(solution)/shard_map/cross_attention/pallas_call | solution.py:52
  274.4 9.9 %cross_attention.3 = (bf16[1024,1024]{1,0:T(8,128)(2,1)S(1)}, f32[8,1,512]{2,1,0:T(1,128)S(1)}) custom-call(bf16[1024,4096]{1,0:T(8,128)(2,1)} %get-tuple-element.117.refs_3_.refs_5_.refs_6_.refs_0_.refs_1_.refs_2_.refs_7_, bf16[512,4096]{1,0:T(8,128)(2,1)} %get-tuple-element.124.refs_1_.refs_2_.refs_3_.refs_4_, ...), custom_call_target="tpu_custom_call", output_to_operand_aliasing={{0}: (3, {})} | custom-call | flops 1073741824 | bytes 20987904 | tf_op jit(solution)/shard_map/cross_attention/pallas_call | solution.py:52
  284.2 17.6 %self_attention.1 = (bf16[1024,1024]{1,0:T(8,128)(2,1)S(1)}, f32[8,1,1024]{2,1,0:T(1,128)S(1)}) custom-call(bf16[1024,4096]{1,0:T(8,128)(2,1)} %get-tuple-element.117.refs_3_.refs_5_.refs_6_.refs_0_.refs_1_.refs_2_.refs_7_, bf16[1024,4096]{1,0:T(8,128)(2,1)} %get-tuple-element.117.refs_3_.refs_5_.refs_6_.refs_0_.refs_1_.refs_2_.refs_7_, ...), custom_call_target="tpu_custom_call" | custom-call | flops 2415919104 | bytes 27295744 | tf_op jit(solution)/shard_map/self_attention/pallas_call | solution.py:52
  301.9 9.8 %branch.1 = (f32[1024,1024]{1,0:T(8,128)}, bf16[1024,1024]{1,0:T(8,128)(2,1)S(1)}) custom-call(bf16[1024,1024]{1,0:T(8,128)(2,1)S(1)} %get-tuple-element.129.refs_0_.refs_1_.refs_3_, bf16[1024,1024]{1,0:T(8,128)(2,1)} %copy-done.1, bf16[16,2,864,512]{3,2,1,0:T(8,128)(2,1)} %bitcast.61, bf16[1024,1024]{1,0:T(8,128)(2,1)} %refs_6_.1, ...), custom_call_target="tpu_custom_call" | custom-call | flops 4294967296 | bytes 40898560 | tf_op jit(solution)/shard_map/branch/pallas_call | solution.py:52
  313.0 21.1 %hidden.1 = (bf16[1024,4096]{1,0:T(8,128)(2,1)}, bf16[1024,4096]{1,0:T(8,128)(2,1)}) custom-call(bf16[1024,1024]{1,0:T(8,128)(2,1)S(1)} %get-tuple-element.132.refs_0_.refs_2_.refs_1_, bf16[16,2,512,512]{3,2,1,0:T(8,128)(2,1)} %bitcast.70, bf16[1024,1024]{1,0:T(8,128)(2,1)S(1)} %get-tuple-element.132.refs_0_.refs_2_.refs_1_), custom_call_target="tpu_custom_call" | custom-call | flops 8589934592 | bytes 35651584 | tf_op jit(solution)/shard_map/hidden/pallas_call | solution.py:52
  334.1 14.1 %grad_hidden_out.1 = (bf16[4,2,256,1024]{3,2,1,0:T(8,128)(2,1)}, bf16[4,2,256,1024]{3,2,1,0:T(8,128)(2,1)}) custom-call(s32[3]{0:T(128)} %pad_add_fusion.refs_0_, bf16[1024,4096]{1,0:T(8,128)(2,1)} %get-tuple-element.133.refs_1_.refs_3_.refs_0_, bf16[1024,1024]{1,0:T(8,128)(2,1)} %refs_5_.1, bf16[1024,4096]{1,0:T(8,128)(2,1)} %get-tuple-element.133.refs_1_.refs_3_.refs_0_), custom_call_target="tpu_custom_call" | custom-call | flops 8589934592 | bytes 18874368 | tf_op jit(solution)/shard_map/grad_hidden_out/pallas_call | solution.py:52
  348.3 7.3 collective-permute-done.1.refs_2_
  357.7 5.3 fold_core.8
  364.4 24.4 %result_and_pre.1 = (bf16[1024,1024]{1,0:T(8,128)(2,1)}, bf16[1024,4096]{1,0:T(8,128)(2,1)}) custom-call(bf16[1024,4096]{1,0:T(8,128)(2,1)} %get-tuple-element.133.refs_1_.refs_3_.refs_0_, bf16[1024,4096]{1,0:T(8,128)(2,1)} %get-tuple-element.134.refs_1_, bf16[16,2,512,512]{3,2,1,0:T(8,128)(2,1)} %bitcast.71, f32[1024,1024]{1,0:T(8,128)} %get-tuple-element.135.refs_3_, ...), custom_call_target="tpu_custom_call" | custom-call | flops 17179869184 | bytes 50331648 | tf_op jit(solution)/shard_map/result_and_pre/pallas_call | solution.py:52
  391.7 15.3 %grad_hidden_in.1 = (bf16[4,2,64,4096]{3,2,1,0:T(8,128)(2,1)}, bf16[4,2,64,4096]{3,2,1,0:T(8,128)(2,1)}) custom-call(s32[3]{0:T(128)} %pad_add_fusion.refs_0_, bf16[1024,1024]{1,0:T(8,128)(2,1)} %copy-done.67, bf16[1024,4096]{1,0:T(8,128)(2,1)} %get-tuple-element.141.refs_2_.refs_1_, bf16[4,256,512]{2,1,0:T(8,128)(2,1)} %copy-done.40), custom_call_target="tpu_custom_call" | custom-call | flops 8589934592 | bytes 18874368 | tf_op jit(solution)/shard_map/grad_hidden_in/pallas_call | solution.py:52
  408.9 20.2 %hidden_back.1 = (f32[1,1024]{1,0:T(1,128)S(1)}, bf16[1024,1024]{1,0:T(8,128)(2,1)S(1)}, f32[1024,1024]{1,0:T(8,128)}) custom-call(f32[1]{0:T(128)} %constant.78.clone.1.refs_0_, bf16[1024,4096]{1,0:T(8,128)(2,1)} %get-tuple-element.141.refs_2_.refs_1_, bf16[16,2,512,512]{3,2,1,0:T(8,128)(2,1)} %bitcast.72, f32[1024,1024]{1,0:T(8,128)} %get-tuple-element.135.refs_3_, ...), custom_call_target="tpu_custom_call" | custom-call | flops 8589934592 | bytes 37756932 | tf_op jit(solution)/shard_map/hidden_back/pallas_call | solution.py:52
  431.1 4.5 fold_core.9
  438.0 7.8 spread.1.refs_4_.refs_5_.refs_14_
  445.8 10.0 %grad_token_out.1 = (bf16[4,2,128,1024]{3,2,1,0:T(8,128)(2,1)}, bf16[4,2,128,1024]{3,2,1,0:T(8,128)(2,1)}) custom-call(s32[3]{0:T(128)} %pad_add_fusion.refs_0_, bf16[1024,1024]{1,0:T(8,128)(2,1)} %copy-done.13, bf16[1024,1024]{1,0:T(8,128)(2,1)} %copy-done.1, bf16[1024,1024]{1,0:T(8,128)(2,1)} %copy-done.30, bf16[1024,2048]{1,0:T(8,128)(2,1)} %spread.1.refs_4_.refs_5_.refs_14_), custom_call_target="tpu_custom_call" | custom-call | flops 4294967296 | bytes 10485760 | tf_op jit(solution)/shard_map/grad_token_out/pallas_call | solution.py:52
  456.7 9.8 %cross_attention_back.1 = (bf16[1024,1024]{1,0:T(8,128)(2,1)S(1)}, bf16[512,1024]{1,0:T(8,128)(2,1)S(1)}, bf16[512,1024]{1,0:T(8,128)(2,1)S(1)}) custom-call(bf16[1024,4096]{1,0:T(8,128)(2,1)} %get-tuple-element.117.refs_3_.refs_5_.refs_6_.refs_0_.refs_1_.refs_2_.refs_7_, bf16[512,4096]{1,0:T(8,128)(2,1)} %get-tuple-element.124.refs_1_.refs_2_.refs_3_.refs_4_, ...), custom_call_target="tpu_custom_call" | custom-call | flops 2684354560 | bytes 27279360 | tf_op jit(solution)/shard_map/cross_attention_back/pallas_call | solution.py:52
  467.8 13.5 %collective-permute-done.7.refs_1_ = bf16[4,64,2048]{2,1,0:T(8,128)(2,1)S(1)} collective-permute-done((bf16[4,64,2048]{2,1,0:T(8,128)(2,1)S(1)}, bf16[4,64,2048]{2,1,0:T(8,128)(2,1)S(1)}, u32[]{:S(2)}, u32[]{:S(2)}) %collective-permute-start.7) | collective-permute-done | bytes 1048608 | tf_op jit(solution)/shard_map/ppermute | solution.py:658
  483.7 3.0 fold_core.10
  489.7 9.4 %side_back.1 = (f32[1,1024]{1,0:T(1,128)S(1)}, bf16[512,1024]{1,0:T(8,128)(2,1)}, f32[512,1024]{1,0:T(8,128)}) custom-call(f32[1]{0:T(128)} %constant.78.clone.1.refs_0_, bf16[512,1024]{1,0:T(8,128)(2,1)S(1)} %get-tuple-element.152.refs_2_.refs_1_.refs_7_, bf16[512,1024]{1,0:T(8,128)(2,1)S(1)} %get-tuple-element.153.refs_2_.refs_8_, ...), custom_call_target="tpu_custom_call" | custom-call | flops 2147483648 | bytes 36708356 | tf_op jit(solution)/shard_map/side_back/pallas_call | solution.py:52
  499.1 8.8 %gate_back.1 = (bf16[512,1024]{1,0:T(8,128)(2,1)S(1)}, bf16[512,1024]{1,0:T(8,128)(2,1)S(1)}, bf16[512,2048]{1,0:T(8,128)(2,1)S(1)}, f32[512,1024]{1,0:T(8,128)}, f32[1,1024]{1,0:T(1,128)S(1)}) custom-call(f32[1]{0:T(128)} %bitcast.3.refs_0_, f32[512,1024]{1,0:T(8,128)} %get-tuple-element.158.refs_1_, f32[512,1024]{1,0:T(8,128)} %copy-done.29, ...), custom_call_target="tpu_custom_call" | custom-call | flops 3221225472 | bytes 70258688 | tf_op jit(solution)/shard_map/gate_back/pallas_call | solution.py:52
  511.8 22.4 %state_attention_back.1 = (bf16[1024,1024]{1,0:T(8,128)(2,1)}, bf16[512,1024]{1,0:T(8,128)(2,1)S(1)}, bf16[512,1024]{1,0:T(8,128)(2,1)S(1)}, bf16[512,1024]{1,0:...) custom-call(s32[1]{0:T(128)} %bitcast.4.refs_0_, ...), custom_call_target="tpu_custom_call", output_to_operand_aliasing={{0}: (17, {})} | custom-call | flops 8053063680 | bytes 67158016 | tf_op jit(solution)/shard_map/state_attention_back/pallas_call | solution.py:52
  536.6 7.0 grad_state_out.1
  543.6 5.8 grad_gate_weight.1
  552.1 12.0 %collective-permute-done.13.refs_1_ = bf16[4,128,512]{2,1,0:T(8,128)(2,1)} collective-permute-done((bf16[4,128,512]{2,1,0:T(8,128)(2,1)}, bf16[4,128,512]{2,1,0:T(8,128)(2,1)}, u32[]{:S(2)}, u32[]{:S(2)}) %collective-permute-start.13) | collective-permute-done | bytes 524320 | tf_op jit(solution)/shard_map/ppermute | solution.py:660
  568.1 2.4 fold_core.11
  572.2 2.5 fold_core.12
  575.8 17.8 %self_attention_back.1 = (bf16[1024,1024]{1,0:T(8,128)(2,1)S(1)}, bf16[1024,1024]{1,0:T(8,128)(2,1)S(1)}, bf16[1024,1024]{1,0:T(8,128)(2,1)}) custom-call(bf16[1024,4096]{1,0:T(8,128)(2,1)} %get-tuple-element.117.refs_3_.refs_5_.refs_6_.refs_0_.refs_1_.refs_2_.refs_7_, ...), custom_call_target="tpu_custom_call" | custom-call | flops 6039797760 | bytes 41975808 | tf_op jit(solution)/shard_map/self_attention_back/pallas_call | solution.py:52
  596.2 15.3 %grad_token_proj.1 = (bf16[4,2,64,4096]{3,2,1,0:T(8,128)(2,1)}, bf16[4,2,64,4096]{3,2,1,0:T(8,128)(2,1)}) custom-call(s32[3]{0:T(128)} %pad_add_fusion.refs_0_, bf16[1024,1024]{1,0:T(8,128)(2,1)} %copy-done.79, bf16[1024,1024]{1,0:T(8,128)(2,1)} %copy-done.26, bf16[1024,1024]{1,0:T(8,128)(2,1)} %get-tuple-element.179.refs_3_.refs_2_, ...), custom_call_target="tpu_custom_call" | custom-call | flops 8589934592 | bytes 18874368 | tf_op jit(solution)/shard_map/grad_token_proj/pallas_call | solution.py:52
  614.6 12.6 %grad_state_proj.1 = (bf16[4,2,64,4096]{3,2,1,0:T(8,128)(2,1)}, bf16[4,2,64,4096]{3,2,1,0:T(8,128)(2,1)}) custom-call(s32[3]{0:T(128)} %pad_add_fusion.refs_0_, bf16[512,1024]{1,0:T(8,128)(2,1)} %copy-done.68, bf16[512,1024]{1,0:T(8,128)(2,1)} %copy-done.35, bf16[512,1024]{1,0:T(8,128)(2,1)} %copy-done.46, bf16[512,1024]{1,0:T(8,128)(2,1)} %copy-done.48, ...), custom_call_target="tpu_custom_call" | custom-call | flops 4294967296 | bytes 16777216 | tf_op jit(solution)/shard_map/grad_state_proj/pallas_call | solution.py:52
  633.2 5.7 fold_core.13
  641.7 12.9 %state_back.1 = (f32[1,1024]{1,0:T(1,128)S(1)}, bf16[512,1024]{1,0:T(8,128)(2,1)S(1)}) custom-call(f32[1]{0:T(128)} %bitcast.13.refs_0_, bf16[512,1024]{1,0:T(8,128)(2,1)S(1)} %copy-done.47, bf16[512,1024]{1,0:T(8,128)(2,1)S(1)} %copy-done.49, bf16[512,1024]{1,0:T(8,128)(2,1)S(1)} %copy-done.51, bf16[512,1024]{1,0:T(8,128)(2,1)S(1)} %copy-done.53, ...), custom_call_target="tpu_custom_call" | custom-call | flops 4294967296 | bytes 37756932 | tf_op jit(solution)/shard_map/state_back/pallas_call | solution.py:52
  655.7 4.5 fold_core.14
  666.9 21.0 %tokens_back.1 = (f32[1,1024]{1,0:T(1,128)S(1)}, bf16[1024,1024]{1,0:T(8,128)(2,1)}) custom-call(f32[1]{0:T(128)} %constant.78.clone.1.refs_0_, bf16[1024,1024]{1,0:T(8,128)(2,1)S(1)} %copy-done.27, bf16[1024,1024]{1,0:T(8,128)(2,1)S(1)} %copy-done.6, bf16[1024,1024]{1,0:T(8,128)(2,1)} %copy-done.28, bf16[1024,1024]{1,0:T(8,128)(2,1)} %get-tuple-element.181.refs_5_.refs_4_, ...), custom_call_target="tpu_custom_call" | custom-call | flops 8589934592 | bytes 45096964 | tf_op jit(solution)/shard_map/tokens_back/pallas_call | solution.py:52
  697.2 17.8 %inner_attention.3 = (bf16[512,1024]{1,0:T(8,128)(2,1)S(1)}, bf16[512,1024]{1,0:T(8,128)(2,1)S(1)}, f32[8,1,512]{2,1,0:T(1,128)S(1)}, f32[8,1,512]{2,1,0:T(1,128)}) custom-call(s32[1]{0:T(128)} %bitcast.12.refs_0_, bf16[512,4096]{1,0:T(8,128)(2,1)} %get-tuple-element.124.refs_1_.refs_2_.refs_3_.refs_4_, ...), custom_call_target="tpu_custom_call" | custom-call | flops 2147483648 | bytes 35684356 | tf_op jit(solution)/shard_map/inner_attention/pallas_call | solution.py:52
  717.8 2.5 fold_last.13.refs_2_
  720.3 19.9 %collective-permute-done.25.refs_1_ = bf16[4,64,2048]{2,1,0:T(8,128)(2,1)} collective-permute-done((bf16[4,64,2048]{2,1,0:T(8,128)(2,1)S(1)}, bf16[4,64,2048]{2,1,0:T(8,128)(2,1)}, u32[]{:S(2)}, u32[]{:S(2)}) %collective-permute-start.25) | collective-permute-done | bytes 1048608 | tf_op jit(solution)/shard_map/ppermute | solution.py:658
  741.7 8.7 %update_state.3 = (bf16[512,1024]{1,0:T(8,128)(2,1)}, f32[512,1024]{1,0:T(8,128)}, f32[512,1024]{1,0:T(8,128)}) custom-call(f32[1]{0:T(128)} %bitcast.11.refs_0_, bf16[512,1024]{1,0:T(8,128)(2,1)S(1)} %get-tuple-element.207.refs_1_, bf16[512,1024]{1,0:T(8,128)(2,1)S(1)} %get-tuple-element.208.refs_2_, bf16[16,2,864,512]{3,2,1,0:T(8,128)(2,1)} %bitcast.68, ...), custom_call_target="tpu_custom_call" | custom-call | flops 3221225472 | bytes 66064388 | tf_op jit(solution)/shard_map/update_state/pallas_call | solution.py:52
  755.5 21.6 %collective-permute-done.29.refs_1_ = bf16[4,64,2048]{2,1,0:T(8,128)(2,1)S(1)} collective-permute-done((bf16[4,64,2048]{2,1,0:T(8,128)(2,1)S(1)}, bf16[4,64,2048]{2,1,0:T(8,128)(2,1)S(1)}, u32[]{:S(2)}, u32[]{:S(2)}) %collective-permute-start.29) | collective-permute-done | bytes 1048608 | tf_op jit(solution)/shard_map/ppermute | solution.py:658
  780.4 2.6 collective-permute-done.33
  785.3 2.6 collective-permute-done.35
  788.2 3.9 collective-permute-done.36
  807.0 19.9 %reduce-scatter.11.cloned.1.call-done = bf16[64,2048]{1,0:T(8,128)(2,1)} async-done(((bf16[256,2048]{1,0:T(8,128)(2,1)}), bf16[64,2048]{1,0:T(8,128)(2,1)}) %reduce-scatter.11.cloned.1.call-update) | async-done | bytes 262160 | tf_op jit(solution)/shard_map/reduce_scatter | solution.py:773
  (351 shorter events, 120.6 us)
Async XLA Ops:
  7.2 183.9 %all-gather.5.cloned.1.call-start = ((), (), s32[]{:S(2)}) async-start(), calls=%async_computation.16 | async-start | bytes 29196288 | tf_op jit(solution)/shard_map/all_gather | solution.py:693
  18.6 294.5 %all-gather.7.cloned.1.call-start = ((), (), s32[]{:S(2)}) async-start(), calls=%async_computation.17 | async-start | bytes 17301504 | tf_op jit(solution)/shard_map/all_gather | solution.py:693
  19.5 774.1 %reduce-scatter.23.cloned.1.call-start = ((), (), s32[]{:S(2)}) async-start(), calls=%async_computation.15 | async-start | bytes 1310720 | tf_op jit(solution)/shard_map/reduce_scatter | solution.py:773
  19.7 6.5 collective-permute-start
  348.3 7.4 collective-permute-start.1
  363.0 25.8 %collective-permute-start.2 = (bf16[4,256,512]{2,1,0:T(8,128)(2,1)S(1)}, bf16[4,256,512]{2,1,0:T(8,128)(2,1)S(1)}, u32[]{:S(2)}, u32[]{:S(2)}) collective-permute-start(bf16[4,256,512]{2,1,0:T(8,128)(2,1)S(1)} %get-tuple-element.143), channel_id=1, source_target_pairs={{0,4},{2,6},{4,0},{6,2},{8,12},{10,14},{12,8},{14,10},{16,20},{18,... | collective-permute-start | bytes 3145736 | tf_op jit(solution)/shard_map/ppermute | solution.py:660
  406.9 22.2 %collective-permute-start.5 = (bf16[4,2,64,4096]{3,2,1,0:T(8,128)(2,1)}, bf16[4,2,64,4096]{3,2,1,0:T(8,128)(2,1)S(1)}, u32[]{:S(2)}, u32[]{:S(2)}) collective-permute-start(bf16[4,2,64,4096]{3,2,1,0:T(8,128)(2,1)} %get-tuple-element.147), channel_id=1, source_target_pairs={{0,2},{2,0},{4,6},{6,4},{8,10},{10,8},{12,14},{14,12},{16,18},{18,... | collective-permute-start | bytes 12582920 | tf_op jit(solution)/shard_map/ppermute | solution.py:660
  406.9 29.7 %collective-permute-start.3 = (bf16[4,256,512]{2,1,0:T(8,128)(2,1)}, bf16[4,256,512]{2,1,0:T(8,128)(2,1)S(1)}, u32[]{:S(2)}, u32[]{:S(2)}) collective-permute-start(bf16[4,256,512]{2,1,0:T(8,128)(2,1)} %get-tuple-element.146), channel_id=1, source_target_pairs={{0,4},{2,6},{4,0},{6,2},{8,12},{10,14},{12,8},{14,10},{16,20},{18,... | collective-permute-start | bytes 3145736 | tf_op jit(solution)/shard_map/ppermute | solution.py:660
  407.8 28.9 %collective-permute-start.4 = (bf16[4,256,512]{2,1,0:T(8,128)(2,1)S(1)}, bf16[4,256,512]{2,1,0:T(8,128)(2,1)S(1)}, u32[]{:S(2)}, u32[]{:S(2)}) collective-permute-start(bf16[4,256,512]{2,1,0:T(8,128)(2,1)S(1)} %copy-done.41), channel_id=1, source_target_pairs={{0,1},{1,0},{2,3},{3,2},{4,5},{5,4},{6,7},{7,6},{8,9},{9,8},{10,11... | collective-permute-start | bytes 3145736 | tf_op jit(solution)/shard_map/ppermute | solution.py:658
  455.8 25.9 %collective-permute-start.6 = (bf16[4,2,128,1024]{3,2,1,0:T(8,128)(2,1)}, bf16[4,2,128,1024]{3,2,1,0:T(8,128)(2,1)S(1)}, u32[]{:S(2)}, u32[]{:S(2)}) collective-permute-start(bf16[4,2,128,1024]{3,2,1,0:T(8,128)(2,1)} %get-tuple-element.154), channel_id=1, source_target_pairs={{0,2},{2,0},{4,6},{6,4},{8,10},{10,8},{12,14},{14,12},{16,18},{18,... | collective-permute-start | bytes 6291464 | tf_op jit(solution)/shard_map/ppermute | solution.py:660
  455.8 25.6 %collective-permute-start.7 = (bf16[4,64,2048]{2,1,0:T(8,128)(2,1)S(1)}, bf16[4,64,2048]{2,1,0:T(8,128)(2,1)S(1)}, u32[]{:S(2)}, u32[]{:S(2)}) collective-permute-start(bf16[4,64,2048]{2,1,0:T(8,128)(2,1)S(1)} %copy-done.75), channel_id=1, source_target_pairs={{0,1},{1,0},{2,3},{3,2},{4,5},{5,4},{6,7},{7,6},{8,9},{9,8},{10,11... | collective-permute-start | bytes 3145736 | tf_op jit(solution)/shard_map/ppermute | solution.py:658
  486.7 23.6 %collective-permute-start.8 = (bf16[4,128,512]{2,1,0:T(8,128)(2,1)S(1)}, bf16[4,128,512]{2,1,0:T(8,128)(2,1)S(1)}, u32[]{:S(2)}, u32[]{:S(2)}) collective-permute-start(bf16[4,128,512]{2,1,0:T(8,128)(2,1)S(1)} %get-tuple-element.164), channel_id=1, source_target_pairs={{0,4},{2,6},{4,0},{6,2},{8,12},{10,14},{12,8},{14,10},{16,20},{18,... | collective-permute-start | bytes 1572872 | tf_op jit(solution)/shard_map/ppermute | solution.py:660
  487.6 46.6 %collective-permute-start.9 = (bf16[4,64,2048]{2,1,0:T(8,128)(2,1)S(1)}, bf16[4,64,2048]{2,1,0:T(8,128)(2,1)S(1)}, u32[]{:S(2)}, u32[]{:S(2)}) collective-permute-start(bf16[4,64,2048]{2,1,0:T(8,128)(2,1)S(1)} %get-tuple-element.170), channel_id=1, source_target_pairs={{0,1},{1,0},{2,3},{3,2},{4,5},{5,4},{6,7},{7,6},{8,9},{9,8},{10,11... | collective-permute-start | bytes 3145736 | tf_op jit(solution)/shard_map/ppermute | solution.py:658
  488.7 45.5 %collective-permute-start.10 = (bf16[4,64,2048]{2,1,0:T(8,128)(2,1)S(1)}, bf16[4,64,2048]{2,1,0:T(8,128)(2,1)S(1)}, u32[]{:S(2)}, u32[]{:S(2)}) collective-permute-start(bf16[4,64,2048]{2,1,0:T(8,128)(2,1)S(1)} %fold_mid.9.refs_3_), channel_id=1, source_target_pairs={{0,4},{2,6},{4,0},{6,2},{8,12},{10,14},{12,8},{14,10},{16,20},{18,... | collective-permute-start | bytes 3145736 | tf_op jit(solution)/shard_map/ppermute | solution.py:660
  543.5 24.5 %collective-permute-start.12 = (bf16[4,2,128,1024]{3,2,1,0:T(8,128)(2,1)}, bf16[4,2,128,1024]{3,2,1,0:T(8,128)(2,1)}, u32[]{:S(2)}, u32[]{:S(2)}) collective-permute-start(bf16[4,2,128,1024]{3,2,1,0:T(8,128)(2,1)} %get-tuple-element.174), channel_id=1, source_target_pairs={{0,2},{2,0},{4,6},{6,4},{8,10},{10,8},{12,14},{14,12},{16,18},{18,... | collective-permute-start | bytes 6291464 | tf_op jit(solution)/shard_map/ppermute | solution.py:660
  549.3 22.9 %collective-permute-start.11 = (bf16[4,2,64,1024]{3,2,1,0:T(8,128)(2,1)}, bf16[4,2,64,1024]{3,2,1,0:T(8,128)(2,1)}, u32[]{:S(2)}, u32[]{:S(2)}) collective-permute-start(bf16[4,2,64,1024]{3,2,1,0:T(8,128)(2,1)} %get-tuple-element.173), channel_id=1, source_target_pairs={{0,2},{2,0},{4,6},{6,4},{8,10},{10,8},{12,14},{14,12},{16,18},{18,... | collective-permute-start | bytes 3145736 | tf_op jit(solution)/shard_map/ppermute | solution.py:660
  549.9 14.2 %collective-permute-start.13 = (bf16[4,128,512]{2,1,0:T(8,128)(2,1)}, bf16[4,128,512]{2,1,0:T(8,128)(2,1)}, u32[]{:S(2)}, u32[]{:S(2)}) collective-permute-start(bf16[4,128,512]{2,1,0:T(8,128)(2,1)} %get-tuple-element.175), channel_id=1, source_target_pairs={{0,4},{2,6},{4,0},{6,2},{8,12},{10,14},{12,8},{14,10},{16,20},{18,... | collective-permute-start | bytes 1572872 | tf_op jit(solution)/shard_map/ppermute | solution.py:660
  551.1 13.7 %collective-permute-start.14 = (bf16[4,128,512]{2,1,0:T(8,128)(2,1)S(1)}, bf16[4,128,512]{2,1,0:T(8,128)(2,1)}, u32[]{:S(2)}, u32[]{:S(2)}) collective-permute-start(bf16[4,128,512]{2,1,0:T(8,128)(2,1)S(1)} %fold_mid.10.refs_18_), channel_id=1, source_target_pairs={{0,1},{1,0},{2,3},{3,2},{4,5},{5,4},{6,7},{7,6},{8,9},{9,8},{10,11... | collective-permute-start | bytes 1572872 | tf_op jit(solution)/shard_map/ppermute | solution.py:658
  552.0 243.5 %reduce-scatter.13.cloned.1.call-start = ((), (), s32[]{:S(2)}) async-start(), calls=%async_computation.10 | async-start | bytes 655360 | tf_op jit(solution)/shard_map/reduce_scatter | solution.py:773
  571.3 40.2 %collective-permute-start.17 = (bf16[4,128,512]{2,1,0:T(8,128)(2,1)S(1)}, bf16[4,128,512]{2,1,0:T(8,128)(2,1)S(1)}, u32[]{:S(2)}, u32[]{:S(2)}) collective-permute-start(bf16[4,128,512]{2,1,0:T(8,128)(2,1)S(1)} %get-tuple-element.192), channel_id=1, source_target_pairs={{0,1},{1,0},{2,3},{3,2},{4,5},{5,4},{6,7},{7,6},{8,9},{9,8},{10,11... | collective-permute-start | bytes 1572872 | tf_op jit(solution)/shard_map/ppermute | solution.py:658
  574.7 39.2 %collective-permute-start.16 = (bf16[4,64,512]{2,1,0:T(8,128)(2,1)S(1)}, bf16[4,64,512]{2,1,0:T(8,128)(2,1)S(1)}, u32[]{:S(2)}, u32[]{:S(2)}) collective-permute-start(bf16[4,64,512]{2,1,0:T(8,128)(2,1)S(1)} %get-tuple-element.190), channel_id=1, source_target_pairs={{0,1},{1,0},{2,3},{3,2},{4,5},{5,4},{6,7},{7,6},{8,9},{9,8},{10,11... | collective-permute-start | bytes 786440 | tf_op jit(solution)/shard_map/ppermute | solution.py:658
  611.5 20.4 %collective-permute-start.15 = (bf16[4,2,64,4096]{3,2,1,0:T(8,128)(2,1)}, bf16[4,2,64,4096]{3,2,1,0:T(8,128)(2,1)}, u32[]{:S(2)}, u32[]{:S(2)}) collective-permute-start(bf16[4,2,64,4096]{3,2,1,0:T(8,128)(2,1)} %get-tuple-element.183), channel_id=1, source_target_pairs={{0,2},{2,0},{4,6},{6,4},{8,10},{10,8},{12,14},{14,12},{16,18},{18,... | collective-permute-start | bytes 12582920 | tf_op jit(solution)/shard_map/ppermute | solution.py:660
  627.2 13.7 %collective-permute-start.24 = (bf16[4,2,64,4096]{3,2,1,0:T(8,128)(2,1)}, bf16[4,2,64,4096]{3,2,1,0:T(8,128)(2,1)}, u32[]{:S(2)}, u32[]{:S(2)}) collective-permute-start(bf16[4,2,64,4096]{3,2,1,0:T(8,128)(2,1)} %get-tuple-element.202), channel_id=1, source_target_pairs={{0,2},{2,0},{4,6},{6,4},{8,10},{10,8},{12,14},{14,12},{16,18},{18,... | collective-permute-start | bytes 12582920 | tf_op jit(solution)/shard_map/ppermute | solution.py:660
  627.7 169.4 %reduce-scatter.21.cloned.1.call-start = ((), (), s32[]{:S(2)}) async-start(), calls=%async_computation.14 | async-start | bytes 1310720 | tf_op jit(solution)/shard_map/reduce_scatter | solution.py:773
  628.3 171.2 %reduce-scatter.17.cloned.1.call-start = ((), (), s32[]{:S(2)}) async-start(), calls=%async_computation.12 | async-start | bytes 327680 | tf_op jit(solution)/shard_map/reduce_scatter | solution.py:773
  629.0 33.1 %collective-permute-start.22 = (bf16[4,128,512]{2,1,0:T(8,128)(2,1)S(1)}, bf16[4,128,512]{2,1,0:T(8,128)(2,1)S(1)}, u32[]{:S(2)}, u32[]{:S(2)}) collective-permute-start(bf16[4,128,512]{2,1,0:T(8,128)(2,1)S(1)} %copy-done.77), channel_id=1, source_target_pairs={{0,1},{1,0},{2,3},{3,2},{4,5},{5,4},{6,7},{7,6},{8,9},{9,8},{10,11... | collective-permute-start | bytes 1572872 | tf_op jit(solution)/shard_map/ppermute | solution.py:658
  630.0 34.4 %collective-permute-start.20 = (bf16[4,64,512]{2,1,0:T(8,128)(2,1)}, bf16[4,64,512]{2,1,0:T(8,128)(2,1)S(1)}, u32[]{:S(2)}, u32[]{:S(2)}) collective-permute-start(bf16[4,64,512]{2,1,0:T(8,128)(2,1)} %get-tuple-element.200), channel_id=1, source_target_pairs={{0,1},{1,0},{2,3},{3,2},{4,5},{5,4},{6,7},{7,6},{8,9},{9,8},{10,11... | collective-permute-start | bytes 786440 | tf_op jit(solution)/shard_map/ppermute | solution.py:658
  631.1 31.0 %collective-permute-start.23 = (bf16[4,128,512]{2,1,0:T(8,128)(2,1)S(1)}, bf16[4,128,512]{2,1,0:T(8,128)(2,1)S(1)}, u32[]{:S(2)}, u32[]{:S(2)}) collective-permute-start(bf16[4,128,512]{2,1,0:T(8,128)(2,1)S(1)} %fold_mid.11.refs_2_), channel_id=1, source_target_pairs={{0,4},{2,6},{4,0},{6,2},{8,12},{10,14},{12,8},{14,10},{16,20},{18,... | collective-permute-start | bytes 1572872 | tf_op jit(solution)/shard_map/ppermute | solution.py:660
  631.9 32.5 %collective-permute-start.21 = (bf16[4,64,512]{2,1,0:T(8,128)(2,1)}, bf16[4,64,512]{2,1,0:T(8,128)(2,1)S(1)}, u32[]{:S(2)}, u32[]{:S(2)}) collective-permute-start(bf16[4,64,512]{2,1,0:T(8,128)(2,1)} %fold_mid.12.refs_9_), channel_id=1, source_target_pairs={{0,4},{2,6},{4,0},{6,2},{8,12},{10,14},{12,8},{14,10},{16,20},{18,... | collective-permute-start | bytes 786440 | tf_op jit(solution)/shard_map/ppermute | solution.py:660
  640.9 48.8 %collective-permute-start.18 = (bf16[4,64,2048]{2,1,0:T(8,128)(2,1)}, bf16[4,64,2048]{2,1,0:T(8,128)(2,1)}, u32[]{:S(2)}, u32[]{:S(2)}) collective-permute-start(bf16[4,64,2048]{2,1,0:T(8,128)(2,1)} %get-tuple-element.195), channel_id=1, source_target_pairs={{0,4},{2,6},{4,0},{6,2},{8,12},{10,14},{12,8},{14,10},{16,20},{18,... | collective-permute-start | bytes 3145736 | tf_op jit(solution)/shard_map/ppermute | solution.py:660
  662.2 25.8 %collective-permute-start.19 = (bf16[4,2,32,1024]{3,2,1,0:T(8,128)(2,1)}, bf16[4,2,32,1024]{3,2,1,0:T(8,128)(2,1)}, u32[]{:S(2)}, u32[]{:S(2)}) collective-permute-start(bf16[4,2,32,1024]{3,2,1,0:T(8,128)(2,1)} %get-tuple-element.219), channel_id=1, source_target_pairs={{0,2},{2,0},{4,6},{6,4},{8,10},{10,8},{12,14},{14,12},{16,18},{18,... | collective-permute-start | bytes 1572872 | tf_op jit(solution)/shard_map/ppermute | solution.py:660
  662.2 53.9 %collective-permute-start.26 = (bf16[4,64,2048]{2,1,0:T(8,128)(2,1)}, bf16[4,64,2048]{2,1,0:T(8,128)(2,1)}, u32[]{:S(2)}, u32[]{:S(2)}) collective-permute-start(bf16[4,64,2048]{2,1,0:T(8,128)(2,1)} %get-tuple-element.211), channel_id=1, source_target_pairs={{0,4},{2,6},{4,0},{6,2},{8,12},{10,14},{12,8},{14,10},{16,20},{18,... | collective-permute-start | bytes 3145736 | tf_op jit(solution)/shard_map/ppermute | solution.py:660
  665.2 135.8 %reduce-scatter.15.cloned.1.call-start = ((), (), s32[]{:S(2)}) async-start(), calls=%async_computation.11 | async-start | bytes 655360 | tf_op jit(solution)/shard_map/reduce_scatter | solution.py:773
  691.6 26.2 %collective-permute-start.27 = (bf16[4,64,2048]{2,1,0:T(8,128)(2,1)S(1)}, bf16[4,64,2048]{2,1,0:T(8,128)(2,1)}, u32[]{:S(2)}, u32[]{:S(2)}) collective-permute-start(bf16[4,64,2048]{2,1,0:T(8,128)(2,1)S(1)} %fold_mid.13.refs_7_), channel_id=1, source_target_pairs={{0,1},{1,0},{2,3},{3,2},{4,5},{5,4},{6,7},{7,6},{8,9},{9,8},{10,11... | collective-permute-start | bytes 3145736 | tf_op jit(solution)/shard_map/ppermute | solution.py:658
  692.6 47.7 %collective-permute-start.25 = (bf16[4,64,2048]{2,1,0:T(8,128)(2,1)S(1)}, bf16[4,64,2048]{2,1,0:T(8,128)(2,1)}, u32[]{:S(2)}, u32[]{:S(2)}) collective-permute-start(bf16[4,64,2048]{2,1,0:T(8,128)(2,1)S(1)} %copy-done.72), channel_id=1, source_target_pairs={{0,1},{1,0},{2,3},{3,2},{4,5},{5,4},{6,7},{7,6},{8,9},{9,8},{10,11... | collective-permute-start | bytes 3145736 | tf_op jit(solution)/shard_map/ppermute | solution.py:658
  693.8 110.0 %reduce-scatter.19.cloned.1.call-start = ((), (), s32[]{:S(2)}) async-start(), calls=%async_computation.13 | async-start | bytes 163840 | tf_op jit(solution)/shard_map/reduce_scatter | solution.py:773
  695.1 19.9 %collective-permute-start.28 = (bf16[4,32,512]{2,1,0:T(8,128)(2,1)}, bf16[4,32,512]{2,1,0:T(8,128)(2,1)S(1)}, u32[]{:S(2)}, u32[]{:S(2)}) collective-permute-start(bf16[4,32,512]{2,1,0:T(8,128)(2,1)} %copy-done.78), channel_id=1, source_target_pairs={{0,4},{2,6},{4,0},{6,2},{8,12},{10,14},{12,8},{14,10},{16,20},{18,... | collective-permute-start | bytes 393224 | tf_op jit(solution)/shard_map/ppermute | solution.py:660
  696.0 54.3 %collective-permute-start.31 = (bf16[4,32,512]{2,1,0:T(8,128)(2,1)S(1)}, bf16[4,32,512]{2,1,0:T(8,128)(2,1)S(1)}, u32[]{:S(2)}, u32[]{:S(2)}) collective-permute-start(bf16[4,32,512]{2,1,0:T(8,128)(2,1)S(1)} %get-tuple-element.218), channel_id=1, source_target_pairs={{0,4},{2,6},{4,0},{6,2},{8,12},{10,14},{12,8},{14,10},{16,20},{18,... | collective-permute-start | bytes 393224 | tf_op jit(solution)/shard_map/ppermute | solution.py:660
  715.1 35.2 %collective-permute-start.32 = (bf16[4,32,512]{2,1,0:T(8,128)(2,1)S(1)}, bf16[4,32,512]{2,1,0:T(8,128)(2,1)S(1)}, u32[]{:S(2)}, u32[]{:S(2)}) collective-permute-start(bf16[4,32,512]{2,1,0:T(8,128)(2,1)S(1)} %fold_mid.14.refs_3_), channel_id=1, source_target_pairs={{0,1},{1,0},{2,3},{3,2},{4,5},{5,4},{6,7},{7,6},{8,9},{9,8},{10,11... | collective-permute-start | bytes 393224 | tf_op jit(solution)/shard_map/ppermute | solution.py:658
  752.6 52.5 %reduce-scatter.9.cloned.1.call-start = ((), (), s32[]{:S(2)}) async-start(), calls=%async_computation.8 | async-start | bytes 1310720 | tf_op jit(solution)/shard_map/reduce_scatter | solution.py:773
  753.4 73.4 %reduce-scatter.11.cloned.1.call-start = ((), (), s32[]{:S(2)}) async-start(), calls=%async_computation.9 | async-start | bytes 1310720 | tf_op jit(solution)/shard_map/reduce_scatter | solution.py:773
  753.4 23.6 %collective-permute-start.29 = (bf16[4,64,2048]{2,1,0:T(8,128)(2,1)S(1)}, bf16[4,64,2048]{2,1,0:T(8,128)(2,1)S(1)}, u32[]{:S(2)}, u32[]{:S(2)}) collective-permute-start(bf16[4,64,2048]{2,1,0:T(8,128)(2,1)S(1)} %copy-done.70), channel_id=1, source_target_pairs={{0,1},{1,0},{2,3},{3,2},{4,5},{5,4},{6,7},{7,6},{8,9},{9,8},{10,11... | collective-permute-start | bytes 3145736 | tf_op jit(solution)/shard_map/ppermute | solution.py:658
  754.4 23.4 %collective-permute-start.30 = (bf16[4,64,2048]{2,1,0:T(8,128)(2,1)S(1)}, bf16[4,64,2048]{2,1,0:T(8,128)(2,1)S(1)}, u32[]{:S(2)}, u32[]{:S(2)}) collective-permute-start(bf16[4,64,2048]{2,1,0:T(8,128)(2,1)S(1)} %fold_mid.15.refs_7_), channel_id=1, source_target_pairs={{0,4},{2,6},{4,0},{6,2},{8,12},{10,14},{12,8},{14,10},{16,20},{18,... | collective-permute-start | bytes 3145736 | tf_op jit(solution)/shard_map/ppermute | solution.py:660
  779.3 3.7 collective-permute-start.33
  783.0 1.2 collective-permute-start.34
  784.2 3.7 collective-permute-start.35
  787.9 4.2 collective-permute-start.36
  792.1 6.8 collective-permute-start.37
  (93 other events, 1381.6 us)
Sparse Core Ops, SparseCore 0:
  18.7 172.3 all-gather.4
  194.6 113.0 all-gather.6
  552.1 25.5 reduce-scatter.22
  627.8 20.2 reduce-scatter.12
  650.4 25.3 reduce-scatter.20
  678.5 18.3 reduce-scatter.16
  699.8 19.8 reduce-scatter.14
  752.8 17.9 reduce-scatter.18
  773.0 25.6 reduce-scatter.8
  801.0 25.7 reduce-scatter.10

commit v5 on v4

--- a/solution.py
+++ b/solution.py
@@ -28,6 +28,16 @@
 
 def matmul_left_t(left, right):
     return lax.dot_general(left, right, TN, preferred_element_type=jnp.float32)
+
+
+MICROSECOND = 1.15e9
+TIMES = {
+    "norm_project": 13, "self_attention": 17, "inner_attention": 17, "cross_attention": 10, "update_state": 9, "branch": 10,
+    "hidden": 20, "grad_hidden_out": 14, "result_and_pre": 24, "grad_hidden_in": 15, "hidden_back": 20, "spread": 8,
+    "cross_attention_back": 10, "side_back": 9, "gate_back": 9, "grad_out": 16, "state_attention_back": 22, "state_back": 13,
+    "grad_state_proj": 13, "self_attention_back": 18, "grad_token_proj": 15, "tokens_back": 21, "spell": 7, "fence": 1,
+    "fold_core": 5, "fold_mid": 2, "fold_last": 2, "widen": 1,
+}
 
 
 def launch(body, operands, *, grid, in_specs, out_specs, out_shape, name, flops, after=(), where=None, scratch=(), aliases=None, exps=0, limit=48):
@@ -54,7 +64,7 @@
         out_shape=list(out_shape),
         input_output_aliases=aliases or {},
         compiler_params=pltpu.CompilerParams(vmem_limit_bytes=limit * MIB),
-        cost_estimate=pl.CostEstimate(flops=int(flops), bytes_accessed=int(size), transcendentals=int(exps)),
+        cost_estimate=pl.CostEstimate(flops=int(MICROSECOND * TIMES[name]), bytes_accessed=1024, transcendentals=0),
         name=name,
         **kwargs,
     )(*(() if where is None else (where,)), *operands, *after)
@@ -90,15 +100,26 @@
 COLS = 512
 
 
+STEP = 2 * COLS
+
+
 def group_spec(weight, group):
     array, start, rows = weight
-    groups = 4
 
     def place_of(*ids):
         which = group(ids[0])
-        return 0, which // groups, start // rows + which % groups, 0
-
-    return pl.BlockSpec((16, 1, rows, COLS), place_of)
+        return 0, which // 2, start // (2 * rows) + which % 2, 0
+
+    return pl.BlockSpec((16, 1, 2 * rows, COLS), place_of)
+
+
+def group(w_ref, which):
+    rows = w_ref.shape[2] // 2
+    return w_ref[:, 0, which * rows : (which + 1) * rows, :].reshape(-1, COLS)
+
+
+def cols(which):
+    return slice(which * COLS, (which + 1) * COLS)
 
 
 def rows_spec(weight, count, step=lambda i: i):
@@ -128,19 +149,20 @@
             centered, inverse = norm_rows(x_ref[at, :].astype(F32))
             normed_ref[at, :] = narrow(centered * inverse * gain_ref[...])
 
-    out_ref[...] = narrow(dot(normed_ref[...], side(w_ref, 0), NN))
+    for which in range(2):
+        out_ref[:, cols(which)] = narrow(dot(normed_ref[...], group(w_ref, which), NN))
 
 
 def norm_project(x, gain, weight, after=()):
     rows, width = x.shape
-    cols = 4 * width
-    step = COLS
-    return launch(
-        norm_project_kernel, [x, gain, weight[0]], after=after, name="norm_project", grid=(cols // step,),
+    total_cols = 4 * width
+    step = STEP
+    return launch(
+        norm_project_kernel, [x, gain, weight[0]], after=after, name="norm_project", grid=(total_cols // step,),
         in_specs=[whole((rows, width)), whole((1, width)), group_spec(weight, lambda i: i)],
         out_specs=[whole((rows, width)), pl.BlockSpec((rows, step), lambda i: (0, i))],
-        out_shape=[shaped((rows, width)), shaped((rows, cols))],
-        flops=2 * rows * width * cols,
+        out_shape=[shaped((rows, width)), shaped((rows, total_cols))],
+        flops=2 * rows * width * total_cols,
     )
 
 
@@ -196,26 +218,27 @@
 
 def hidden_kernel(normed_ref, w_ref, active_ref, slope_ref):
     for start in range(0, normed_ref.shape[0], 256):
-        at = slice(start, start + 256)
-        v = dot(normed_ref[at, :], side(w_ref, 0), NN)
-        square = v * v
-        t = jnp.tanh(v * (GELU_A + (GELU_A * GELU_B) * square))
-        half = 0.5 + 0.5 * t
-        active_ref[at, :] = narrow(v * half)
-        slope = half + v * (1.0 - t * t) * (0.5 * GELU_A + (1.5 * GELU_A * GELU_B) * square)
-        slope_ref[at, :] = narrow(slope)
+        for which in range(2):
+            at = slice(start, start + 256), cols(which)
+            v = dot(normed_ref[start : start + 256, :], group(w_ref, which), NN)
+            square = v * v
+            t = jnp.tanh(v * (GELU_A + (GELU_A * GELU_B) * square))
+            half = 0.5 + 0.5 * t
+            active_ref[at] = narrow(v * half)
+            slope = half + v * (1.0 - t * t) * (0.5 * GELU_A + (1.5 * GELU_A * GELU_B) * square)
+            slope_ref[at] = narrow(slope)
 
 
 def hidden(normed, weight, after=()):
     rows, width = normed.shape
-    cols = 4 * width
-    step = COLS
+    total_cols = 4 * width
+    step = STEP
     tile = pl.BlockSpec((rows, step), lambda i: (0, i))
     return launch(
-        hidden_kernel, [normed, weight[0]], after=after, name="hidden", grid=(cols // step,),
+        hidden_kernel, [normed, weight[0]], after=after, name="hidden", grid=(total_cols // step,),
         in_specs=[whole((rows, width)), group_spec(weight, lambda i: i)],
-        out_specs=[tile, tile], out_shape=[shaped((rows, cols))] * 2,
-        flops=2 * rows * width * cols, exps=rows * cols,
+        out_specs=[tile, tile], out_shape=[shaped((rows, total_cols))] * 2,
+        flops=2 * rows * width * total_cols, exps=rows * total_cols,
     )
 
 
@@ -234,7 +257,7 @@
 def result_and_pre(active, slope, weight, middle, grad, after=()):
     rows, hidden_units = active.shape
     width = middle.shape[1]
-    step = 512
+    step = STEP
     tile = pl.BlockSpec((rows, step), lambda i: (0, i))
     return launch(
         result_kernel, [active, slope, weight[0], middle, grad], after=after, name="result_and_pre",
@@ -260,7 +283,7 @@
     for part in range(parts):
         @pl.when(i // share == part)
         def _():
-            total_ref[...] += dot(grads[part][...], side(w_ref, 0), NT)
+            total_ref[...] += sum(dot(grads[part][:, cols(which)], group(w_ref, which), NT) for which in range(2))
 
     @pl.when(i == pl.num_programs(0) - 1)
     def _():
@@ -279,7 +302,7 @@
 
 def norm_back_project(grads, weight, x, gain, plus, name, keep_wide=False, offset=0, scale=None, after=()):
     rows, width = x.shape
-    step = 512
+    step = STEP
     share = grads[0].shape[1] // step
     parts = len(grads)
     steps = parts * share
@@ -307,13 +330,13 @@
 
 def spread(grad, weight, after=()):
     rows, width = grad.shape
-    cols = 16 * weight[2]
-    step = 512
-    return launch(
-        spread_kernel, [grad, weight[0]], after=after, name="spread", grid=(cols // step,),
+    total_cols = 16 * weight[2]
+    step = STEP
+    return launch(
+        spread_kernel, [grad, weight[0]], after=after, name="spread", grid=(total_cols // step,),
         in_specs=[whole((rows, width)), rows_spec(weight, step // weight[2])],
         out_specs=[pl.BlockSpec((rows, step), lambda i: (0, i))],
-        out_shape=[shaped((rows, cols))], flops=2 * rows * width * cols,
+        out_shape=[shaped((rows, total_cols))], flops=2 * rows * width * total_cols,
     )[0]
 
 
@@ -354,13 +377,14 @@
     )
 
 
-def weight_grad_kernel(rows, plan, split, counts, place_ref, *refs):
+def weight_grad_kernel(jobs, counts, extra, place_ref, *refs):
     lefts, rights = refs[: counts[0]], refs[counts[0] : counts[0] + counts[1]]
     keep_ref, send_ref = refs[-2], refs[-1]
     core = place_ref[1]
-
-    def run(which):
-        turned = [lefts[item][...].T for item in which]
+    z = pl.program_id(0)
+
+    def run(plan, row, rows, pick):
+        turned = {left: lefts[pick(left)][...].T for left in sorted({left for terms in plan for left, _ in terms})}
         col = 0
         for terms in plan:
             cols = rights[terms[0][1]].shape[1]
@@ -373,41 +397,61 @@
                 for x in range(2):
                     even = total[2 * x * rows : (2 * x + 1) * rows]
                     odd = total[(2 * x + 1) * rows : (2 * x + 2) * rows]
-                    keep_ref[0, x, :, at] = jnp.where(core == 0, even, odd)
-                    send_ref[0, x, :, at] = jnp.where(core == 0, odd, even)
+                    keep_ref[0, x, row : row + rows, at] = jnp.where(core == 0, even, odd)
+                    send_ref[0, x, row : row + rows, at] = jnp.where(core == 0, odd, even)
             col += cols
 
-    if split:
-        @pl.when(pl.program_id(0) < 2)
-        def _():
-            run([0])
-
-        @pl.when(pl.program_id(0) >= 2)
-        def _():
-            run([1])
-    else:
-        run(range(len(lefts)))
-
-
-def weight_grad(lefts, rights, plan, where, name, split=False, after=()):
-    tokens = lefts[0].shape[0]
-    total_rows = lefts[0].shape[1] * (len(lefts) if split else 1)
-    rows = total_rows // 16
-    cols = sum(rights[terms[0][1]].shape[1] for terms in plan)
-    if split:
-        left_specs = [
-            pl.BlockSpec((tokens, 4 * rows), lambda z, p: (0, jnp.minimum(z, 1))),
-            pl.BlockSpec((tokens, 4 * rows), lambda z, p: (0, jnp.maximum(z, 2) - 2)),
-        ]
-    else:
-        left_specs = [pl.BlockSpec((item.shape[0], 4 * rows), lambda z, p: (0, z)) for item in lefts]
-    out = pl.BlockSpec((1, 2, rows, cols), lambda z, p: (z, 0, 0, 0))
-    return launch(
-        partial(weight_grad_kernel, rows, plan, split, (len(lefts), len(rights))), [*lefts, *rights],
-        where=where, after=after, name=name, grid=(4,),
-        in_specs=left_specs + [whole(item.shape) for item in rights],
-        out_specs=[out, out], out_shape=[shaped((4, 2, rows, cols))] * 2,
-        flops=2 * tokens * total_rows * cols, limit=56,
+    for plan, split, row, rows in jobs:
+        if split:
+            pl.when(z < 2)(partial(run, plan, row, rows, lambda left: left))
+            pl.when(z >= 2)(partial(run, plan, row, rows, lambda left: left + 1))
+        else:
+            run(plan, row, rows, lambda left: left)
+    if extra is not None:
+        source, row = refs[counts[0] + counts[1]], extra
+        for x in range(2):
+            for part in range(2):
+                for y in range(2):
+                    at = slice(y * 2048 + part * 512, y * 2048 + (part + 1) * 512)
+                    even = source[0, x, 0, part * 16 : (part + 1) * 16, y * 512 : (y + 1) * 512]
+                    odd = source[0, x, 1, part * 16 : (part + 1) * 16, y * 512 : (y + 1) * 512]
+                    keep_ref[0, x, row : row + 16, at] = jnp.where(core == 0, even, odd)
+                    send_ref[0, x, row : row + 16, at] = jnp.where(core == 0, odd, even)
+            for y in range(2):
+                at = slice(y * 2048 + 1024, (y + 1) * 2048)
+                keep_ref[0, x, row : row + 16, at] = jnp.zeros((16, 1024), jnp.bfloat16)
+                send_ref[0, x, row : row + 16, at] = jnp.zeros((16, 1024), jnp.bfloat16)
+
+
+def weight_grad(jobs, where, name, extra=None, after=()):
+    lefts, rights, specs, table, row = [], [], [], [], 0
+    for these, those, plan, split in jobs:
+        rows = these[0].shape[1] * (2 if split else 1) // 16
+        shift = [[(left + len(lefts), right + len(rights)) for left, right in terms] for terms in plan]
+        table.append((shift, split, row, rows))
+        for index, item in enumerate(these):
+            if split:
+                block = (lambda z, p: (0, jnp.minimum(z, 1))) if index == 0 else (lambda z, p: (0, jnp.maximum(z, 2) - 2))
+            else:
+                block = lambda z, p: (0, z)
+            specs.append(pl.BlockSpec((item.shape[0], 4 * rows), block))
+        lefts += these
+        rights += those
+        row += rows
+    cols = sum(rights[terms[0][1]].shape[1] for terms in table[0][0])
+    operands = [*lefts, *rights]
+    specs += [whole(item.shape) for item in rights]
+    at = None
+    if extra is not None:
+        operands.append(extra.reshape(4, 2, 2, 32, extra.shape[1]))
+        specs.append(pl.BlockSpec((1, 2, 2, 32, extra.shape[1]), lambda z, p: (z, 0, 0, 0, 0)))
+        at, row = row, row + 16
+    out = pl.BlockSpec((1, 2, row, cols), lambda z, p: (z, 0, 0, 0))
+    return launch(
+        partial(weight_grad_kernel, table, (len(lefts), len(rights)), at), operands,
+        where=where, after=after, name=name, grid=(4,), in_specs=specs,
+        out_specs=[out, out], out_shape=[shaped((4, 2, row, cols))] * 2,
+        flops=2 * rights[0].shape[0] * 16 * row * cols, limit=56,
     )
 
 
@@ -415,27 +459,32 @@
     return lax.dot_general(a, b, dims, preferred_element_type=jnp.float32)
 
 
-def attend_tile(q, k, v, mask):
-    scores = dot(k, q, NT)
-    if mask is not None:
-        scores = jnp.where(mask, scores, masked_score)
-    top = jnp.max(scores, axis=0, keepdims=True)
-    weights = jnp.exp2((scores - top) * EXP_SCALE)
-    total = jnp.sum(weights, axis=0, keepdims=True)
-    mixed = dot(v, weights.astype(jnp.bfloat16), TN) / total
-    return mixed.T.astype(jnp.bfloat16), top * EXP_SCALE + jnp.log2(total)
-
-
-def attend_back_tile(q, k, v, mask, log_total, grad_out, delta):
-    probs = jnp.exp2(dot(k, q, NT) * EXP_SCALE - log_total)
-    if mask is not None:
-        probs = jnp.where(mask, probs, 0.0)
-    grad_probs = dot(v, grad_out, NT)
-    grad_raw = (probs * (grad_probs - delta)).astype(jnp.bfloat16)
-    grad_v = dot(probs.astype(jnp.bfloat16), grad_out, NN)
-    grad_k = dot(grad_raw, q, NN)
-    grad_q = dot(k, grad_raw, TN)
-    return grad_q, grad_k, grad_v
+HEADS = 2
+TILE = 256
+
+
+def attend_all(items):
+    scores = [dot(k, q, NT) for q, k, v, mask, put in items]
+    scores = [
+        part if item[3] is None else jnp.where(item[3], part, masked_score) for part, item in zip(scores, items)
+    ]
+    tops = [jnp.max(part, axis=0, keepdims=True) for part in scores]
+    weights = [jnp.exp2((part - top) * EXP_SCALE) for part, top in zip(scores, tops)]
+    totals = [jnp.sum(part, axis=0, keepdims=True) for part in weights]
+    for (q, k, v, mask, put), top, part, total in zip(items, tops, weights, totals):
+        mixed = dot(v, narrow(part), TN) / total
+        put(narrow(mixed.T), top * EXP_SCALE + jnp.log2(total))
+
+
+def attend_all_back(items):
+    probs = [jnp.exp2(dot(k, q, NT) * EXP_SCALE - log) for q, k, v, mask, log, out, grad, put in items]
+    probs = [part if item[3] is None else jnp.where(item[3], part, 0.0) for part, item in zip(probs, items)]
+    deltas = [row_delta(out, grad) for q, k, v, mask, log, out, grad, put in items]
+    grad_probs = [dot(v, grad, NT) for q, k, v, mask, log, out, grad, put in items]
+    grad_raws = [narrow(part * (other - delta)) for part, other, delta in zip(probs, grad_probs, deltas)]
+    for (q, k, v, mask, log, out, grad, put), part, grad_raw in zip(items, probs, grad_raws):
+        grad_q = (dot(k, grad_raw, TN) * RAW_SCALE).T
+        put(narrow(grad_q), dot(grad_raw, q, NN), dot(narrow(part), grad, NN))
 
 
 def row_delta(out, grad_out):
@@ -449,35 +498,51 @@
     return (key <= query) & (key > query - window)
 
 
-TILE = 256
-
-
-def self_kernel(window, q_ref, k_ref, v_ref, out_ref, log_ref):
-    rows = q_ref.shape[0]
+def head_cols(head):
+    return slice(head * HD, (head + 1) * HD)
+
+
+def storing(out_ref, log_ref, head, at):
+    def put(out, log):
+        out_ref[at, head_cols(head)] = out
+        log_ref[head, :, at] = log
+
+    return put
+
+
+def column(rows, offset):
+    return pl.BlockSpec((rows, HD * HEADS), lambda h: (0, h + offset // HEADS))
+
+
+def block_column(rows, block, offset):
+    return pl.BlockSpec((rows, HD * HEADS), lambda h: (block, h + offset // HEADS))
+
+
+def stat(rows):
+    return pl.BlockSpec((HEADS, 1, rows), lambda h: (h, 0, 0))
+
+
+def bands(rows, window):
     for start in range(0, rows, TILE):
         low = max(0, start - window)
-        size = start + TILE - low
-        mask = band_mask(size, TILE, low, start, window)
-        out, log = attend_tile(
-            q_ref[start : start + TILE, :], k_ref[low : low + size, :], v_ref[low : low + size, :], mask
-        )
-        out_ref[start : start + TILE, :] = out
-        log_ref[0, :, start : start + TILE] = log
-
-
-def column(rows, offset):
-    return pl.BlockSpec((rows, HD), lambda h: (0, h + offset))
-
-
-def stat(rows):
-    return pl.BlockSpec((1, 1, rows), lambda h: (h, 0, 0))
+        yield slice(start, start + TILE), slice(low, start + TILE), band_mask(start + TILE - low, TILE, low, start, window)
+
+
+def self_kernel(window, q_ref, k_ref, v_ref, out_ref, log_ref):
+    attend_all(
+        [
+            (q_ref[at, head_cols(h)], k_ref[keys, head_cols(h)], v_ref[keys, head_cols(h)], mask, storing(out_ref, log_ref, h, at))
+            for h in range(HEADS)
+            for at, keys, mask in bands(q_ref.shape[0], window)
+        ]
+    )
 
 
 def self_attention(projected, window, after=()):
     rows, width = projected.shape
     heads = width // 4 // HD
     return launch(
-        partial(self_kernel, window), [projected] * 3, after=after, name="self_attention", grid=(heads,),
+        partial(self_kernel, window), [projected] * 3, after=after, name="self_attention", grid=(heads // HEADS,),
         in_specs=[column(rows, 0), column(rows, 2 * heads), column(rows, 3 * heads)],
         out_specs=[column(rows, 0), stat(rows)],
         out_shape=[shaped((rows, width // 4)), shaped((heads, 1, rows), F32)],
@@ -485,15 +550,15 @@
     )
 
 
-def block_column(rows, block, offset):
-    return pl.BlockSpec((rows, HD), lambda h: (block, h + offset))
-
-
 def cross_kernel(q_ref, k_ref, v_ref, *refs):
     out_ref, log_ref = refs[-2:]
-    for start in range(0, q_ref.shape[0], TILE):
-        at = slice(start, start + TILE)
-        out_ref[at, :], log_ref[0, :, at] = attend_tile(q_ref[at, :], k_ref[...], v_ref[...], None)
+    attend_all(
+        [
+            (q_ref[at, head_cols(h)], k_ref[:, head_cols(h)], v_ref[:, head_cols(h)], None, storing(out_ref, log_ref, h, at))
+            for h in range(HEADS)
+            for at in (slice(start, start + TILE) for start in range(0, q_ref.shape[0], TILE))
+        ]
+    )
 
 
 def cross_attention(projected, state_side, block, before=None, after=()):
@@ -505,7 +570,7 @@
         operands.append(before)
         specs.append(pl.BlockSpec(memory_space=pl.ANY))
     return launch(
-        cross_kernel, operands, after=after, name="cross_attention", grid=(heads,), in_specs=specs,
+        cross_kernel, operands, after=after, name="cross_attention", grid=(heads // HEADS,), in_specs=specs,
         out_specs=[block_column(rows, block, 0), stat(rows)],
         out_shape=[shaped((projected.shape[0], width // 4)), shaped((heads, 1, rows), F32)],
         aliases=None if before is None else {3: 0},
@@ -515,20 +580,21 @@
 
 def inner_kernel(live_ref, sq_ref, scq_ref, sk_ref, sv_ref, tk_ref, tv_ref, self_ref, cross_ref, self_log, cross_log):
     rows = sq_ref.shape[0]
-    for start in range(0, rows, TILE):
-        at = slice(start, start + TILE)
-        self_ref[at, :], self_log[0, :, at] = attend_tile(sq_ref[at, :], sk_ref[...], sv_ref[...], None)
-        key = lax.broadcasted_iota(jnp.int32, (rows, TILE), 0)
-        cross_ref[at, :], cross_log[0, :, at] = attend_tile(
-            scq_ref[at, :], tk_ref[...], tv_ref[...], key < live_ref[0]
-        )
+    mask = lax.broadcasted_iota(jnp.int32, (rows, rows), 0) < live_ref[0]
+    at = slice(0, rows)
+    items = []
+    for h in range(HEADS):
+        cols_h = head_cols(h)
+        items.append((sq_ref[:, cols_h], sk_ref[:, cols_h], sv_ref[:, cols_h], None, storing(self_ref, self_log, h, at)))
+        items.append((scq_ref[:, cols_h], tk_ref[:, cols_h], tv_ref[:, cols_h], mask, storing(cross_ref, cross_log, h, at)))
+    attend_all(items)
 
 
 def inner_attention(projected, state_side, live_keys, block, after=()):
     rows, width = state_side.shape
     heads = width // 4 // HD
     return launch(
-        inner_kernel, [live_keys] + [state_side] * 4 + [projected] * 2, after=after, name="inner_attention", grid=(heads,),
+        inner_kernel, [live_keys] + [state_side] * 4 + [projected] * 2, after=after, name="inner_attention", grid=(heads // HEADS,),
         in_specs=[SMEM] + [column(rows, part * heads) for part in range(4)]
         + [block_column(rows, block, 2 * heads), block_column(rows, block, 3 * heads)],
         out_specs=[column(rows, 0)] * 2 + [stat(rows)] * 2,
@@ -542,65 +608,78 @@
     extra = ek_ref.shape[0]
     sk_ref[...] = jnp.zeros_like(sk_ref)
     sv_ref[:extra, :] = ev_ref[...]
-    sv_ref[extra:, :] = jnp.zeros((rows - extra, HD), jnp.float32)
-    for start in range(0, rows, TILE):
-        at = slice(start, start + TILE)
-        low = max(0, start - window)
-        size = start + TILE - low
-        keys = slice(low, low + size)
-        mask = band_mask(size, TILE, low, start, window)
-        grad_out = grad_ref[at, :]
-        grad_q, grad_k, grad_v = attend_back_tile(
-            q_ref[at, :], k_ref[keys, :], v_ref[keys, :], mask, log_ref[0, :, at], grad_out,
-            row_delta(out_ref[at, :], grad_out))
-        gq_ref[at, :] = (grad_q * RAW_SCALE).T.astype(jnp.bfloat16)
-        sk_ref[keys, :] += grad_k
-        sv_ref[keys, :] += grad_v
-    gk_ref[:extra, :] = (sk_ref[:extra, :] * RAW_SCALE + ek_ref[...]).astype(jnp.bfloat16)
-    gk_ref[extra:, :] = (sk_ref[extra:, :] * RAW_SCALE).astype(jnp.bfloat16)
-    gv_ref[...] = sv_ref[...].astype(jnp.bfloat16)
-
-
-def cross_back_kernel(cq_ref, sk_ref, sv_ref, out_ref, log_ref, grad_ref, gq_ref, gk_ref, gv_ref):
-    rows = cq_ref.shape[0]
-    total_k = total_v = 0.0
-    for start in range(0, rows, TILE):
-        at = slice(start, start + TILE)
-        grad_out = grad_ref[at, :]
-        grad_q, grad_k, grad_v = attend_back_tile(
-            cq_ref[at, :], sk_ref[...], sv_ref[...], None, log_ref[0, :, at], grad_out,
-            row_delta(out_ref[at, :], grad_out))
-        gq_ref[at, :] = (grad_q * RAW_SCALE).T.astype(jnp.bfloat16)
-        total_k = total_k + grad_k
-        total_v = total_v + grad_v
-    gk_ref[...] = (total_k * RAW_SCALE).astype(jnp.bfloat16)
-    gv_ref[...] = total_v.astype(jnp.bfloat16)
+    sv_ref[extra:, :] = jnp.zeros((rows - extra, HD * HEADS), F32)
+
+    def adding(cols_h, at, keys):
+        def put(grad_q, grad_k, grad_v):
+            gq_ref[at, cols_h] = grad_q
+            sk_ref[keys, cols_h] += grad_k
+            sv_ref[keys, cols_h] += grad_v
+
+        return put
+
+    for h in range(HEADS):
+        cols_h = head_cols(h)
+        attend_all_back(
+            [
+                (q_ref[at, cols_h], k_ref[keys, cols_h], v_ref[keys, cols_h], mask, log_ref[h, :, at], out_ref[at, cols_h],
+                 grad_ref[at, cols_h], adding(cols_h, at, keys))
+                for at, keys, mask in bands(rows, window)
+            ]
+        )
+    gk_ref[:extra, :] = narrow(sk_ref[:extra, :] * RAW_SCALE + ek_ref[...])
+    gk_ref[extra:, :] = narrow(sk_ref[extra:, :] * RAW_SCALE)
+    gv_ref[...] = narrow(sv_ref[...])
+
+
+def cross_back_kernel(q_ref, k_ref, v_ref, out_ref, log_ref, grad_ref, gq_ref, gk_ref, gv_ref):
+    def storing_back(cols_h):
+        def put(grad_q, grad_k, grad_v):
+            gq_ref[:, cols_h] = grad_q
+            gk_ref[:, cols_h] = narrow(grad_k * RAW_SCALE)
+            gv_ref[:, cols_h] = narrow(grad_v)
+
+        return put
+
+    attend_all_back(
+        [
+            (q_ref[:, head_cols(h)], k_ref[:, head_cols(h)], v_ref[:, head_cols(h)], None, log_ref[h], out_ref[:, head_cols(h)],
+             grad_ref[:, head_cols(h)], storing_back(head_cols(h)))
+            for h in range(HEADS)
+        ]
+    )
 
 
 def state_back_kernel(live_ref, cq_ref, sq_ref, scq_ref, sk_ref, sv_ref, tk_ref, tv_ref,
                       co_ref, so_ref, io_ref, cl_ref, sl_ref, il_ref, cg_ref, sg_ref, ig_ref, before_ref,
                       gcq_ref, gsq_ref, gscq_ref, gsk_ref, gsv_ref, gtk_ref, gtv_ref):
     rows = cq_ref.shape[0]
-    sums = [0.0] * 4
-    for start in range(0, rows, TILE):
-        at = slice(start, start + TILE)
-        key = lax.broadcasted_iota(jnp.int32, (rows, TILE), 0)
-        for q_ref, k_ref, v_ref, o_ref, l_ref, g_ref, gq_ref, mask, slot in (
-            (cq_ref, sk_ref, sv_ref, co_ref, cl_ref, cg_ref, gcq_ref, None, 0),
-            (sq_ref, sk_ref, sv_ref, so_ref, sl_ref, sg_ref, gsq_ref, None, 0),
-            (scq_ref, tk_ref, tv_ref, io_ref, il_ref, ig_ref, gscq_ref, key < live_ref[0], 2),
-        ):
-            grad_out = g_ref[at, :]
-            grad_q, grad_k, grad_v = attend_back_tile(
-                q_ref[at, :], k_ref[...], v_ref[...], mask, l_ref[0, :, at], grad_out,
-                row_delta(o_ref[at, :], grad_out))
-            gq_ref[at, :] = (grad_q * RAW_SCALE).T.astype(jnp.bfloat16)
-            sums[slot] = sums[slot] + grad_k
-            sums[slot + 1] = sums[slot + 1] + grad_v
-    gsk_ref[...] = (sums[0] * RAW_SCALE).astype(jnp.bfloat16)
-    gsv_ref[...] = sums[1].astype(jnp.bfloat16)
-    gtk_ref[...] = sums[2] * RAW_SCALE
-    gtv_ref[...] = sums[3]
+    mask = lax.broadcasted_iota(jnp.int32, (rows, rows), 0) < live_ref[0]
+    for h in range(HEADS):
+        cols_h = head_cols(h)
+        terms = []
+
+        def put_into(gq_ref):
+            def put(grad_q, grad_k, grad_v):
+                gq_ref[:, cols_h] = grad_q
+                terms.append((grad_k, grad_v))
+
+            return put
+
+        attend_all_back(
+            [
+                (q_ref[:, cols_h], k_ref[:, cols_h], v_ref[:, cols_h], which, l_ref[h], o_ref[:, cols_h], g_ref[:, cols_h], put_into(gq_ref))
+                for q_ref, k_ref, v_ref, o_ref, l_ref, g_ref, gq_ref, which in (
+                    (cq_ref, sk_ref, sv_ref, co_ref, cl_ref, cg_ref, gcq_ref, None),
+                    (sq_ref, sk_ref, sv_ref, so_ref, sl_ref, sg_ref, gsq_ref, None),
+                    (scq_ref, tk_ref, tv_ref, io_ref, il_ref, ig_ref, gscq_ref, mask),
+                )
+            ]
+        )
+        gsk_ref[:, cols_h] = narrow((terms[0][0] + terms[1][0]) * RAW_SCALE)
+        gsv_ref[:, cols_h] = narrow(terms[0][1] + terms[1][1])
+        gtk_ref[:, cols_h] = terms[2][0] * RAW_SCALE
+        gtv_ref[:, cols_h] = terms[2][1]
 
 
 def self_attention_back(projected, out, log, grad_attended, extra_k, extra_v, window, after=()):
@@ -609,11 +688,11 @@
     extra = extra_k.shape[0]
     return launch(
         partial(self_back_kernel, window), [projected] * 3 + [out, log, grad_attended, extra_k, extra_v],
-        after=after, name="self_attention_back", grid=(heads,),
+        after=after, name="self_attention_back", grid=(heads // HEADS,),
         in_specs=[column(rows, 0), column(rows, 2 * heads), column(rows, 3 * heads), column(rows, 0), stat(rows),
                   column(rows, 0), column(extra, 0), column(extra, 0)],
         out_specs=[column(rows, 0)] * 3, out_shape=[shaped((rows, width // 4))] * 3,
-        scratch=[pltpu.VMEM((rows, HD), F32)] * 2,
+        scratch=[pltpu.VMEM((rows, HD * HEADS), F32)] * 2,
         flops=heads * 10 * 2304 * 256 * HD, exps=heads * 2304 * 256,
     )
 
@@ -623,7 +702,7 @@
     heads = width // 4 // HD
     return launch(
         cross_back_kernel, [projected, state_side, state_side, out, log, grad_attended],
-        after=after, name="cross_attention_back", grid=(heads,),
+        after=after, name="cross_attention_back", grid=(heads // HEADS,),
         in_specs=[block_column(rows, block, heads), column(rows, 2 * heads), column(rows, 3 * heads),
                   block_column(rows, block, 0), stat(rows), block_column(rows, block, heads)],
         out_specs=[block_column(rows, block, 0), column(rows, 0), column(rows, 0)],
@@ -641,7 +720,7 @@
         [live_keys, projected] + [state_side] * 4 + [projected] * 2
         + [cross[0], inner_self[0], inner_cross[0], cross[1], inner_self[1], inner_cross[1]]
         + [grad_attended, grad_inner, grad_inner, before],
-        after=after, name="state_attention_back", grid=(heads,),
+        after=after, name="state_attention_back", grid=(heads // HEADS,),
         in_specs=[SMEM, block_column(rows, block, heads)] + [column(rows, part * heads) for part in range(4)]
         + [block_column(rows, block, 2 * heads), block_column(rows, block, 3 * heads)]
         + [block_column(rows, block, 0), column(rows, 0), column(rows, 0)] + [stat(rows)] * 3
@@ -656,7 +735,7 @@
 def swap(values, axis):
     if axis == "y":
         return lax.ppermute(values, "fsdp", [(0, 1), (1, 0)])
-    bit = {"core": 1, "x": 2, "z_low": 4, "z_high": 8}[axis]
+    bit = {"core": 1, "x": 2, "z_low": 4, "z_high": 8, "z_far": 12}[axis]
     return lax.ppermute(values, "dp", [(d, d ^ bit) for d in range(16)])
 
 
@@ -665,9 +744,9 @@
 
 def place():
     if not paired():
-        return jnp.zeros((3,), jnp.int32)
+        return jnp.zeros((4,), jnp.int32)
     dp = lax.axis_index("dp")
-    return jnp.stack([(dp // 2) % 2, dp % 2, lax.axis_index("fsdp")]).astype(jnp.int32)
+    return jnp.stack([(dp // 2) % 2, dp % 2, lax.axis_index("fsdp"), dp // 4]).astype(jnp.int32)
 
 
 def fence_kernel(*refs):
@@ -690,7 +769,10 @@
 
 def gather_blocks(blocks):
     packed = jnp.concatenate([part for block in blocks for part in stacked(block)], axis=0)
-    every = lax.all_gather(packed, ("dp", "fsdp"), axis=0).reshape(16, 2, *packed.shape)
+    return cut(lax.all_gather(packed, ("dp", "fsdp"), axis=0).reshape(16, 2, *packed.shape), blocks)
+
+
+def cut(every, blocks):
     weights, row = [], 0
     for block in blocks:
         weights.append((every, row, block.shape[0]))
@@ -698,41 +780,123 @@
     return weights
 
 
+def spell_kernel(place_ref, *refs):
+    x, core, y = place_ref[0], place_ref[1], place_ref[2]
+    pieces, out = refs[:-1], refs[-1]
+    for other in range(2):
+        line, over_x, over_y, low, high = pieces[5 * other : 5 * other + 5]
+        at = core ^ other
+        out[0, x, at, y] = line[0]
+        out[0, 1 - x, at, y] = over_x[0]
+        out[0, x, at, 1 - y] = over_y[0]
+        far = jnp.where(pl.program_id(0) < 2, low[0], high[0])
+        out[0, 1 - x, at, 1 - y] = far
+
+
+def fence_kernel(*refs):
+    pass
+
+
+def fence(arrays, after):
+    return launch(
+        fence_kernel, arrays, after=after, name="fence", grid=(1,),
+        in_specs=[pl.BlockSpec(memory_space=pl.ANY)] * len(arrays),
+        out_specs=[pl.BlockSpec(memory_space=pl.ANY)] * len(arrays),
+        out_shape=[shaped(item.shape, item.dtype) for item in arrays],
+        aliases={i: i for i in range(len(arrays))}, flops=0,
+    )
+
+
+class Gather:
+    def __init__(self, blocks, where):
+        self.where, self.blocks = where, blocks
+        self.packed = jnp.concatenate([part for block in blocks for part in stacked(block)], axis=0)
+
+    def start(self, after):
+        packed = fence([self.packed], after)[0] if after else self.packed
+        self.line = jnp.stack([packed] + [swap(packed, axis) for axis in ("z_low", "z_high", "z_far")])
+        return (packed,)
+
+    def near(self, after):
+        (line,) = fence([self.line], after)
+        self.over = swap(line, "x"), swap(line, "y")
+        self.pieces = [line]
+        return (line,)
+
+    def far(self, after):
+        over_x, over_y = fence(self.over, after)
+        self.last = swap(over_x[:2], "y"), swap(over_y[2:], "x")
+        self.pieces += [over_x, over_y]
+        return (over_x,)
+
+    def cross(self, after):
+        low, high = fence(self.last, after)
+        self.pieces += [low, high]
+        self.pieces += [swap(piece, "core") for piece in self.pieces]
+        return (low,)
+
+    def whole(self, after):
+        rows = self.packed.shape[0]
+
+        def spec(low, high):
+            return pl.BlockSpec((1, rows, COLS), lambda i, p: (jnp.clip(i, low, high - 1) - low, 0, 0))
+
+        (every,) = launch(
+            spell_kernel, self.pieces, where=self.where, after=after, name="spell", grid=(4,),
+            in_specs=[spec(0, 4), spec(0, 4), spec(0, 4), spec(0, 2), spec(2, 4)] * 2,
+            out_specs=[pl.BlockSpec((1, 2, 2, 2, rows, COLS), lambda i, p: (i ^ p[3], 0, 0, 0, 0, 0))],
+            out_shape=[shaped((4, 2, 2, 2, rows, COLS))], flops=0,
+        )
+        return cut(every.reshape(16, 2, rows, COLS), self.blocks)
+
+
 def add(*terms):
     return sum(term.astype(F32) for term in terms)
 
 
-def fold_core_kernel(place_ref, keep_ref, come_ref, far_ref, px_ref, py_ref, own_ref):
+def fold_core_kernel(place_ref, keep_ref, come_ref, low_ref, high_ref, px_ref, py_ref, own_ref):
     x, y = place_ref[0], place_ref[2]
     cols = own_ref.shape[-1]
-    for out, dx, dy in ((own_ref, 0, 0), (px_ref, 1, 0), (py_ref, 0, 1), (far_ref, 1, 1)):
+
+    def fold(out, dx, dy):
         at = pl.ds(pl.multiple_of((y ^ dy) * cols, 128), cols)
         for z in range(out.shape[0]):
             out[z] = narrow(add(keep_ref[z, x ^ dx, :, at], come_ref[z, x ^ dx, :, at]))
+
+    fold(own_ref, 0, 0)
+    fold(px_ref, 1, 0)
+    fold(py_ref, 0, 1)
+    pl.when(pl.program_id(0) == 0)(lambda: fold(low_ref, 1, 1))
+    pl.when(pl.program_id(0) == 1)(lambda: fold(high_ref, 1, 1))
 
 
 def fold_core(keep, come, where, after=()):
     _, _, rows, cols = keep.shape
     pair = pl.BlockSpec((2, 2, rows, cols), lambda i, p: (i, 0, 0, 0))
     full = pl.BlockSpec((2, rows, cols // 2), lambda i, p: (i, 0, 0))
+    half = pl.BlockSpec((2, rows, cols // 2), lambda i, p: (0, 0, 0))
     return launch(
         fold_core_kernel, [keep, come], where=where, after=after, name="fold_core", grid=(2,),
-        in_specs=[pair, pair], out_specs=[full] * 4, out_shape=[shaped((4, rows, cols // 2))] * 4,
+        in_specs=[pair, pair], out_specs=[half, half, full, full, full],
+        out_shape=[shaped((2, rows, cols // 2))] * 2 + [shaped((4, rows, cols // 2))] * 3,
         flops=keep.size,
     )
 
 
-def fold_mid_kernel(near_ref, come_ref, out_ref):
-    out_ref[...] = narrow(add(near_ref[...], come_ref[...]))
-
-
-def fold_mid(near, come, after=()):
-    _, rows, cols = near.shape
-    block = pl.BlockSpec((2, rows, cols), lambda i: (i, 0, 0))
-    return launch(
-        fold_mid_kernel, [near, come], after=after, name="fold_mid", grid=(2,),
-        in_specs=[block] * 2, out_specs=[block], out_shape=[shaped(near.shape)], flops=near.size,
-    )[0]
+def fold_mid_kernel(px_ref, py_ref, rx_ref, ry_ref, px_out, py_out):
+    px_out[...] = narrow(add(px_ref[...], ry_ref[...]))
+    py_out[...] = narrow(add(py_ref[...], rx_ref[...]))
+
+
+def fold_mid(px, py, rx, ry, after=()):
+    block = rx.shape
+    low = pl.BlockSpec(block, lambda i: (0, 0, 0))
+    high = pl.BlockSpec(block, lambda i: (1, 0, 0))
+    return launch(
+        fold_mid_kernel, [px, py, rx, ry], after=after, name="fold_mid", grid=(1,),
+        in_specs=[high, low, low, low], out_specs=[high, low],
+        out_shape=[shaped(px.shape), shaped(py.shape)], aliases={0: 0, 1: 1}, flops=px.size,
+    )
 
 
 def fold_last_kernel(own_ref, rx_ref, ry_ref, out_ref):
@@ -748,24 +912,28 @@
     )[0]
 
 
+def widen_kernel(cuts, sum_ref, *outs):
+    for out, (row, rows, parts, cols) in zip(outs, cuts):
+        for part in range(parts):
+            out[part * rows : (part + 1) * rows, :] = sum_ref[
+                row : row + rows, part * cols : (part + 1) * cols
+            ].astype(F32)
+
+
 class Scatter:
-    def __init__(self, keep, send, way, where):
-        self.where, self.keep, self.way = where, keep, way
+    def __init__(self, keep, send, where):
+        self.where, self.keep = where, keep
         self.come = swap(send, "core")
 
     def core(self, after):
-        far, px, py, self.own = fold_core(self.keep, self.come, self.where, after)
-        self.far = swap(far, self.way)
-        if self.way == "x":
-            self.near, self.one = py, swap(px, "x")
-        else:
-            self.near, self.one = px, swap(py, "y")
+        low, high, self.px, self.py, self.own = fold_core(self.keep, self.come, self.where, after)
+        self.rx, self.ry = swap(low, "x"), swap(high, "y")
         return (self.own,)
 
     def mid(self, after):
-        near = fold_mid(self.near, self.far, after)
-        self.two = swap(near, "y" if self.way == "x" else "x")
-        return (near,)
+        px, py = fold_mid(self.px, self.py, self.rx, self.ry, after)
+        self.one, self.two = swap(px, "x"), swap(py, "y")
+        return (px,)
 
     def last(self, after):
         line = fold_last(self.own, self.one, self.two, after)
@@ -774,6 +942,14 @@
             line.reshape(4 * rows, cols), "dp", scatter_dimension=0, axis_index_groups=LINES, tiled=True
         )
         return (line,)
+
+    def widen(self, cuts, after):
+        outs = launch(
+            partial(widen_kernel, cuts), [self.out], after=after, name="widen", grid=(1,),
+            in_specs=[whole(self.out.shape)], out_specs=[whole((rows * parts, cols)) for _, rows, parts, cols in cuts],
+            out_shape=[shaped((rows * parts, cols), F32) for _, rows, parts, cols in cuts], flops=0,
+        )
+        return outs
 
 
 def paired():
@@ -855,16 +1031,41 @@
     token_gain_f, state_gain_f, hidden_gain_f, gate_bias_f = [gains[i : i + 1] for i in range(4)]
     order = ()
 
-    early = [token_proj, state_proj, state_out, token_out, gate_weight, init_state]
-    late = [hidden_in, hidden_out]
-    gather = gather_blocks if paired() else lambda blocks: [gather_plain(block) for block in blocks]
-    full_token_proj, full_state_proj, full_state_out, full_token_out, full_gate_weight, full_init = gather(early)
-    full_hidden_in, full_hidden_out = gather(late)
+    if paired():
+        first_gather, second_gather = Gather([token_proj], where), Gather([state_proj, init_state], where)
+        order = first_gather.start(order)
+        order = first_gather.near(order)
+        order = second_gather.start(order)
+        order = first_gather.far(order)
+        order = second_gather.near(order)
+        order = first_gather.cross(order)
+        (full_token_proj,) = first_gather.whole(order)
+        full_hidden_in, full_state_out, full_token_out, full_gate_weight = gather_blocks(
+            [hidden_in, state_out, token_out, gate_weight]
+        )
+        (full_hidden_out,) = gather_blocks([hidden_out])
+    else:
+        (
+            full_token_proj, full_state_proj, full_state_out, full_gate_weight, full_init, full_token_out, full_hidden_in,
+            full_hidden_out,
+        ) = [
+            gather_plain(block)
+            for block in (
+                token_proj, state_proj, state_out, gate_weight, init_state, token_out, hidden_in, hidden_out,
+            )
+        ]
+    normed, projected = norm_project(tokens, token_gain_f, full_token_proj, order)
+    order = (projected,)
+    if paired():
+        order = second_gather.far(order)
+    self_out, self_log = self_attention(projected, window, order)
+    order = (self_log,)
+    if paired():
+        order = second_gather.cross(order)
+        full_state_proj, full_init = second_gather.whole(order)
     array, row, rows = full_init
     full_init = array[:, :, row : row + rows].transpose(0, 2, 1, 3).reshape(states, width)
     state_0 = jnp.where(first, full_init, incoming[0]).astype(F32)
-    normed, projected = norm_project(tokens, token_gain_f, full_token_proj, order)
-    order = (projected,)
     normed_0, side_0 = norm_project(state_0, state_gain_f, full_state_proj, order)
     order = (side_0,)
     inner_self_0, inner_cross_0, inner_self_log, inner_cross_log = inner_attention(
@@ -881,8 +1082,6 @@
     order = (cross_log_0,)
     cross_out, cross_log_1 = cross_attention(projected, side_1, 1, cross_out, order)
     order = (cross_log_1,)
-    self_out, self_log = self_attention(projected, window, order)
-    order = (self_log,)
     middle, hidden_normed = branch(self_out, cross_out, full_token_out, tokens, hidden_gain_f, order)
     order = (hidden_normed,)
     active, slope = hidden(hidden_normed, full_hidden_in, order)
@@ -890,19 +1089,31 @@
 
     scatters = {}
 
-    def weight(name, way, lefts, rights, plan, split=False):
+    def weight(name, *jobs, extra=None):
         nonlocal order
         if paired():
-            keep, send = weight_grad(lefts, rights, plan, where, "grad_" + name, split, order)
-            scatters[name] = Scatter(keep, send, way, where)
+            keep, send = weight_grad(jobs, where, "grad_" + name, extra, order)
+            scatters[name] = Scatter(keep, send, where)
             order = (keep,)
             return
-        if split:
-            lefts = [jnp.concatenate(lefts, axis=1)]
-        grad = jnp.concatenate(
-            [sum(matmul_left_t(lefts[a], rights[b]) for a, b in terms) for terms in plan], axis=1
-        )
-        scatters[name] = scatter_plain(narrow(grad))
+        scatters[name] = []
+        for lefts, rights, plan, split in jobs:
+            if split:
+                lefts = [jnp.concatenate(lefts, axis=1)]
+            grad = jnp.concatenate(
+                [sum(matmul_left_t(lefts[a], rights[b]) for a, b in terms) for terms in plan], axis=1
+            )
+            scatters[name].append(scatter_plain(narrow(grad)).astype(F32))
+        if extra is not None:
+            scatters[name].append(scatter_plain(extra).astype(F32))
+
+    def sums(name, *cuts):
+        nonlocal order
+        if not paired():
+            return scatters[name]
+        outs = scatters[name].widen(cuts, order)
+        order = (outs[0],)
+        return outs
 
     def fold(name, step):
         nonlocal order
@@ -910,12 +1121,12 @@
             order = getattr(scatters[name], step)(order)
 
     one = [[(0, 0)]]
-    weight("hidden_out", "x", [active], [output_grad], one)
-    fold("hidden_out", "core")
+    weight("hidden_out", ([active], [output_grad], one, False))
     result, grad_pre = result_and_pre(active, slope, full_hidden_out, middle, output_grad, order)
     order = (result,)
+    fold("hidden_out", "core")
+    weight("hidden_in", ([hidden_normed], [grad_pre], one, False))
     fold("hidden_out", "mid")
-    weight("hidden_in", "y", [hidden_normed], [grad_pre], one)
     grad_hidden_gain, grad_branch, grad_middle = norm_back_project(
         [grad_pre], full_hidden_in, middle, hidden_gain_f, output_grad, "hidden_back", True, after=order
     )
@@ -924,13 +1135,11 @@
     fold("hidden_out", "last")
     grad_attended = spread(grad_branch, full_token_out, order)
     order = (grad_attended,)
-    weight("token_out", "x", [self_out, cross_out], [grad_branch], one, True)
     grad_cross, grad_keys_1, grad_values_1 = cross_attention_back(
         projected, side_1, cross_out, cross_log_1, grad_attended, 1, order
     )
     order = (grad_keys_1,)
     fold("hidden_in", "mid")
-    fold("token_out", "core")
     no_term = jnp.zeros((states, width), jnp.bfloat16)
     grad_state_gain_1, _, grad_state_1 = norm_back_project(
         [grad_keys_1, grad_values_1], full_state_proj, state_1, state_gain_f, no_term, "side_back", True,
@@ -941,7 +1150,12 @@
         lives[0], grad_state_1, gate_0, state_0, mixed_0, full_gate_weight, full_state_out, order
     )
     order = (grad_gate_bias,)
-    fold("token_out", "mid")
+    weight(
+        "out",
+        ([self_out, cross_out], [grad_branch], one, True),
+        ([inner_self_0, inner_cross_0], [grad_mixed], one, True),
+        ([mixed_0], [grad_gate_low], one, False),
+    )
     parts = state_attention_back(
         projected, side_0, live_keys[0], (cross_out, cross_log_0), (inner_self_0, inner_self_log),
         (inner_cross_0, inner_cross_log), grad_attended, grad_inner, grad_cross, 0, order,
@@ -949,66 +1163,58 @@
     grad_cross, grads_side_0, extra_keys, extra_values = parts[0], parts[1:5], parts[5], parts[6]
     order = (extra_keys,)
     fold("hidden_in", "last")
-    weight("state_out", "y", [inner_self_0, inner_cross_0], [grad_mixed], one, True)
-    weight("gate_weight", "y", [mixed_0], [grad_gate_low], one)
-    fold("token_out", "last")
-    fold("state_out", "core")
-    fold("gate_weight", "core")
-    grad_self, grad_keys, grad_values = self_attention_back(
-        projected, self_out, self_log, grad_attended, extra_keys, extra_values, window, order
-    )
-    order = (grad_self,)
-    grads_projected = [grad_self, grad_cross, grad_keys, grad_values]
-    weight("token_proj", "x", [normed], grads_projected, [[(0, i)] for i in range(4)])
-    fold("state_out", "mid")
-    fold("gate_weight", "mid")
-    weight(
-        "state_proj", "y", [normed_0, normed_1], [*grads_side_0, grad_keys_1, grad_values_1],
-        [[(0, 0)], [(0, 1)], [(0, 2), (1, 4)], [(0, 3), (1, 5)]],
-    )
-    fold("token_proj", "core")
+    fold("out", "core")
+    (hidden_out_sum,) = sums("hidden_out", (0, 256, 1, 512))
     grad_state_gain_0, grad_init = norm_back_project(
         grads_side_0, full_state_proj, state_0, state_gain_f, grad_direct, "state_back",
         scale=jnp.where(first, 1.0, 0.0).astype(F32).reshape(1), after=order,
     )
     order = (grad_state_gain_0,)
+    fold("out", "mid")
+    weight(
+        "state_proj",
+        (
+            [normed_0, normed_1],
+            [*grads_side_0, grad_keys_1, grad_values_1],
+            [[(0, 0)], [(0, 1)], [(0, 2), (1, 4)], [(0, 3), (1, 5)]],
+            False,
+        ),
+        extra=grad_init,
+    )
+    grad_self, grad_keys, grad_values = self_attention_back(
+        projected, self_out, self_log, grad_attended, extra_keys, extra_values, window, order
+    )
+    order = (grad_self,)
     fold("state_proj", "core")
-    fold("state_out", "last")
-    fold("gate_weight", "last")
-    if paired():
-        parts = grad_init.reshape(4, 2, 2, 32, width)
-        keep = lax.dynamic_index_in_dim(parts, where[1], 2, keepdims=False)
-        send = lax.dynamic_index_in_dim(parts, 1 - where[1], 2, keepdims=False)
-        scatters["init"] = Scatter(keep, send, "x", where)
-    else:
-        scatters["init"] = scatter_plain(grad_init)
+    fold("out", "last")
+    (hidden_in_sum,) = sums("hidden_in", (0, 64, 1, 2048))
+    grads_projected = [grad_self, grad_cross, grad_keys, grad_values]
+    weight("token_proj", ([normed], grads_projected, [[(0, i)] for i in range(4)], False))
+    fold("state_proj", "mid")
+    fold("token_proj", "core")
     grad_token_gain, tokens_grad = norm_back_project(
         grads_projected, full_token_proj, tokens, token_gain_f, grad_middle, "tokens_back", after=order
     )
     order = (grad_token_gain,)
-    fold("init", "core")
     fold("token_proj", "mid")
+    fold("state_proj", "last")
+    token_out_sum, state_out_sum, gate_sum = sums("out", (0, 128, 1, 512), (128, 128, 1, 512), (256, 64, 1, 512))
     inner_self_1, inner_cross_1, log, _ = inner_attention(projected, side_1, live_keys[1], 1, order)
     order = (log,)
-    fold("init", "mid")
     fold("token_proj", "last")
-    fold("state_proj", "mid")
     _, _, state_2 = update_state(
         lives[1], inner_self_1, inner_cross_1, full_state_out, full_gate_weight, gate_bias_f, state_1, order
     )
     order = (state_2,)
-    fold("init", "last")
-    fold("state_proj", "last")
+    state_proj_sum, init_sum = sums("state_proj", (0, 64, 1, 2048), (64, 16, 2, 512))
+    (token_proj_sum,) = sums("token_proj", (0, 64, 1, 2048))
     vector_grads = scatter_vectors(
         jnp.concatenate(
             [grad_token_gain, grad_state_gain_0 + grad_state_gain_1, grad_hidden_gain, grad_gate_bias], axis=0
         )
     )
     matrix_grads = [
-        (scatters[name].out if paired() else scatters[name]).astype(F32)
-        for name in (
-            "token_proj", "state_proj", "token_out", "state_out", "gate_weight", "init", "hidden_in", "hidden_out",
-        )
+        token_proj_sum, state_proj_sum, token_out_sum, state_out_sum, gate_sum, init_sum, hidden_in_sum, hidden_out_sum,
     ]
     return (
         result,

time: 842 us -> 715 us (0.85)
  waiting for transfers between devices: 274 us -> 161 us
  starting transfers between devices: 33.4 us -> 69.4 us
  Pallas kernels: 439 us -> 403 us
    all_gather x2, waiting for transfers between devices: 165 us -> 0.02 us  [gather_blocks(): lax.all_gather(packed, ('dp', 'fsdp'), axis=0).reshape(16, 2, *packed.shape)]
    ppermute x24 -> x39, waiting for transfers between devices: 27.8 us -> 128 us  [swap(): return lax.ppermute(values, 'dp', [(d, d ^ bit) for d in range(16)])]
    ppermute x24 -> x39, starting transfers between devices: 16.6 us -> 53.4 us  [swap(): return lax.ppermute(values, 'dp', [(d, d ^ bit) for d in range(16)])]
    pallas_call x53 -> x56, Pallas kernels: 439 us -> 403 us  [launch(): pl.pallas_call(run, out_shape=list(out_shape), input_output_aliases=alias...]
    ppermute x14 -> x16, waiting for transfers between devices: 60.1 us -> 30.1 us  [swap(): return lax.ppermute(values, 'fsdp', [(0, 1), (1, 0)])]
    reduce_scatter x8 -> x5, waiting for transfers between devices: 19.9 us -> 2.93 us  [last(): lax.psum_scatter(line.reshape(4 * rows, cols), 'dp', scatter_dimension=0,...]
    convert_element_type x8 -> x0, other arithmetic: 13.3 us -> none  [shards(): (scatters[name].out if paired() else scatters[name]).astype(F32)]
    unnamed x202 -> x193, local copies, waits for them, and re-layouts: 48 us -> 39.7 us
  transfers between devices with their start and end apart: 48 -> 62, of which waited for: 14 -> 33; matrix products, arithmetic and copies ran while one was open for 2% -> 2% of each run, Pallas kernels for 42% -> 45%
where the time goes in v5:
time: 715 us; the launch traced here: 711 us
  Pallas kernels  403 us (56%)
  waiting for transfers between devices  161 us (23%)
  starting transfers between devices  69.4 us (10%)
  local copies, waits for them, and re-layouts  47.8 us (7%)
  between operations  18.9 us (3%)
  other arithmetic  10.4 us (1%)
    pallas_call x56, Pallas kernels, launch(): pl.pallas_call(run, out_shape=list(out_shape), input_output_aliases=alias...  403 us
    ppermute x39, waiting for transfers between devices, swap(): return lax.ppermute(values, 'dp', [(d, d ^ bit) for d in range(16)])  128 us
    ppermute x39, starting transfers between devices, swap(): return lax.ppermute(values, 'dp', [(d, d ^ bit) for d in range(16)])  53.4 us
    unnamed x193, local copies, waits for them, and re-layouts  39.7 us
    ppermute x16, waiting for transfers between devices, swap(): return lax.ppermute(values, 'fsdp', [(0, 1), (1, 0)])  30.1 us
    ppermute x16, starting transfers between devices, swap(): return lax.ppermute(values, 'fsdp', [(0, 1), (1, 0)])  14.9 us
  transfers between devices with their start and end apart: 62, of which 33 were waited for; matrix products, arithmetic and copies ran while one was open for 2% of the time, Pallas kernels for 45%

profile of v5, /device:TPU:0, one launch (start us, length us, event | category | flops | bytes accessed | tf_op | source)
XLA Modules:
  0.0 710.7 jit_solution(11661789091390694000)
XLA Ops:
  20.9 9.8 %collective-permute-done.1 = bf16[256,512]{1,0:T(8,128)(2,1)S(1)} collective-permute-done((bf16[256,512]{1,0:T(8,128)(2,1)S(1)}, bf16[256,512]{1,0:T(8,128)(2,1)S(1)}, u32[]{:S(2)}, u32[]{:S(2)}) %collective-permute-start.1) | collective-permute-done | bytes 262176 | tf_op jit(solution)/shard_map/ppermute | solution.py:739
  30.7 13.4 %collective-permute-done.2 = bf16[256,512]{1,0:T(8,128)(2,1)S(1)} collective-permute-done((bf16[256,512]{1,0:T(8,128)(2,1)S(1)}, bf16[256,512]{1,0:T(8,128)(2,1)S(1)}, u32[]{:S(2)}, u32[]{:S(2)}) %collective-permute-start.2) | collective-permute-done | bytes 262176 | tf_op jit(solution)/shard_map/ppermute | solution.py:739
  48.0 14.5 %collective-permute-start.9 = (bf16[288,512]{1,0:T(8,128)(2,1)S(1)}, bf16[288,512]{1,0:T(8,128)(2,1)S(1)}, u32[]{:S(2)}, u32[]{:S(2)}) collective-permute-start(bf16[288,512]{1,0:T(8,128)(2,1)S(1)} %fence.8.refs_2_), channel_id=1, source_target_pairs={{0,16},{2,18},{4,20},{6,22},{8,24},{10,26},{12,28},{14,30},{16,0},... | collective-permute-start | bytes 884744 | tf_op jit(solution)/shard_map/ppermute | solution.py:739
  63.1 12.5 %collective-permute-done.4.refs_0_ = bf16[4,256,512]{2,1,0:T(8,128)(2,1)} collective-permute-done((bf16[4,256,512]{2,1,0:T(8,128)(2,1)S(1)}, bf16[4,256,512]{2,1,0:T(8,128)(2,1)}, u32[]{:S(2)}, u32[]{:S(2)}) %collective-permute-start.4) | collective-permute-done | bytes 1048608 | tf_op jit(solution)/shard_map/ppermute | solution.py:739
  75.6 3.4 collective-permute-done.5.refs_1_
  84.6 8.2 %collective-permute-done.9 = bf16[288,512]{1,0:T(8,128)(2,1)S(1)} collective-permute-done((bf16[288,512]{1,0:T(8,128)(2,1)S(1)}, bf16[288,512]{1,0:T(8,128)(2,1)S(1)}, u32[]{:S(2)}, u32[]{:S(2)}) %collective-permute-start.9) | collective-permute-done | bytes 294944 | tf_op jit(solution)/shard_map/ppermute | solution.py:739
  93.3 4.1 collective-permute-done.8
  104.6 7.5 %spell.2 = bf16[4,2,2,2,256,512]{5,4,3,2,1,0:T(8,128)(2,1)} custom-call(s32[4]{0:T(128)S(1)} %pad_add_fusion.refs_0_, bf16[4,256,512]{2,1,0:T(8,128)(2,1)S(1)} %copy-done.10, bf16[4,256,512]{2,1,0:T(8,128)(2,1)} %get-tuple-element.129.refs_1_.refs_2_, bf16[4,256,512]{2,1,0:T(8,128)(2,1)} %get-tuple-element.130.refs_3_, ...), custom_call_target="tpu_custom_call" | custom-call | flops 8049999872 | bytes 1024 | tf_op jit(solution)/shard_map/spell/pallas_call | solution.py:62
  112.1 14.9 %norm_project.3 = (bf16[1024,1024]{1,0:T(8,128)(2,1)S(1)}, bf16[1024,4096]{1,0:T(8,128)(2,1)}) custom-call(bf16[1024,1024]{1,0:T(8,128)(2,1)S(1)} %copy-done.25, f32[1,1024]{1,0:T(1,128)S(1)} %get-tuple-element.252.refs_1_.refs_7_, bf16[16,2,256,512]{3,2,1,0:T(8,128)(2,1)} %bitcast.82, bf16[2,256,512]{2,1,0:T(8,128)(2,1)} %get-tuple-element.131.refs_4_.refs_11_.refs_3_), custom_call_target="tpu_custom_call" | custom-call | flops 14949999616 | bytes 1024 | tf_op jit(solution)/shard_map/norm_project/pallas_call | solution.py:62
  127.0 20.1 %collective-permute-done.16.refs_0_ = bf16[4,288,512]{2,1,0:T(8,128)(2,1)S(1)} collective-permute-done((bf16[4,288,512]{2,1,0:T(8,128)(2,1)S(1)}, bf16[4,288,512]{2,1,0:T(8,128)(2,1)S(1)}, u32[]{:S(2)}, u32[]{:S(2)}) %collective-permute-start.16) | collective-permute-done | bytes 1179680 | tf_op jit(solution)/shard_map/ppermute | solution.py:739
  150.1 8.8 %self_attention.1 = (bf16[1024,1024]{1,0:T(8,128)(2,1)S(1)}, f32[8,1,1024]{2,1,0:T(1,128)S(1)}) custom-call(bf16[1024,4096]{1,0:T(8,128)(2,1)} %get-tuple-element.133.refs_2_.refs_0_.refs_1_.refs_5_.refs_6_.refs_7_, bf16[1024,4096]{1,0:T(8,128)(2,1)} %get-tuple-element.133.refs_2_.refs_0_.refs_1_.refs_5_.refs_6_.refs_7_, ...), custom_call_target="tpu_custom_call" | custom-call | flops 19549999104 | bytes 1024 | tf_op jit(solution)/shard_map/self_attention/pallas_call | solution.py:62
  160.3 16.3 %collective-permute-done.18.refs_0_ = bf16[2,288,512]{2,1,0:T(8,128)(2,1)} collective-permute-done((bf16[2,288,512]{2,1,0:T(8,128)(2,1)S(1)}, bf16[2,288,512]{2,1,0:T(8,128)(2,1)}, u32[]{:S(2)}, u32[]{:S(2)}) %collective-permute-start.18) | collective-permute-done | bytes 589856 | tf_op jit(solution)/shard_map/ppermute | solution.py:737
  183.9 7.8 %spell.3 = bf16[4,2,2,2,288,512]{5,4,3,2,1,0:T(8,128)(2,1)} custom-call(s32[4]{0:T(128)S(1)} %pad_add_fusion.refs_0_, bf16[4,288,512]{2,1,0:T(8,128)(2,1)S(1)} %fence.10.refs_2_.refs_1_, bf16[4,288,512]{2,1,0:T(8,128)(2,1)S(1)} %get-tuple-element.134.refs_3_.refs_2_, bf16[4,288,512]{2,1,0:T(8,128)(2,1)S(1)} %get-tuple-element.136.refs_3_, ...), custom_call_target="tpu_custom_call" | custom-call | flops 8049999872 | bytes 1024 | tf_op jit(solution)/shard_map/spell/pallas_call | solution.py:62
  195.2 10.5 %norm_project.4 = (bf16[512,1024]{1,0:T(8,128)(2,1)S(1)}, bf16[512,4096]{1,0:T(8,128)(2,1)}) custom-call(f32[512,1024]{1,0:T(8,128)S(1)} %fusion.refs_0_.refs_6_.refs_3_, f32[1,1024]{1,0:T(1,128)S(1)} %get-tuple-element.251.refs_1_.refs_5_.refs_7_, bf16[16,2,288,512]{3,2,1,0:T(8,128)(2,1)} %bitcast.73, ...), custom_call_target="tpu_custom_call" | custom-call | flops 14949999616 | bytes 1024 | tf_op jit(solution)/shard_map/norm_project/pallas_call | solution.py:62
  206.7 9.2 %inner_attention.2 = (bf16[512,1024]{1,0:T(8,128)(2,1)S(1)}, bf16[512,1024]{1,0:T(8,128)(2,1)S(1)}, f32[8,1,512]{2,1,0:T(1,128)S(1)}, f32[8,1,512]{2,1,0:T(1,128)S(1)}) custom-call(s32[1]{0:T(128)} %bitcast.16.refs_0_, bf16[512,4096]{1,0:T(8,128)(2,1)} %get-tuple-element.140.refs_1_.refs_2_.refs_3_.refs_4_.refs_7_.refs_5_, ...), custom_call_target="tpu_custom_call" | custom-call | flops 19549999104 | bytes 1024 | tf_op jit(solution)/shard_map/inner_attention/pallas_call | solution.py:62
  216.0 8.9 %update_state.2 = (bf16[512,1024]{1,0:T(8,128)(2,1)S(1)}, f32[512,1024]{1,0:T(8,128)S(1)}, f32[512,1024]{1,0:T(8,128)}) custom-call(f32[1]{0:T(128)} %bitcast.15.refs_0_, bf16[512,1024]{1,0:T(8,128)(2,1)S(1)} %get-tuple-element.141.refs_1_.refs_3_.refs_9_, bf16[512,1024]{1,0:T(8,128)(2,1)S(1)} %get-tuple-element.142.refs_2_.refs_4_.refs_10_, ...), custom_call_target="tpu_custom_call" | custom-call | flops 10350000128 | bytes 1024 | tf_op jit(solution)/shard_map/update_state/pallas_call | solution.py:62
  228.2 9.6 %norm_project.5 = (bf16[512,1024]{1,0:T(8,128)(2,1)S(1)}, bf16[512,4096]{1,0:T(8,128)(2,1)}) custom-call(f32[512,1024]{1,0:T(8,128)S(1)} %copy-done.1, f32[1,1024]{1,0:T(1,128)S(1)} %get-tuple-element.251.refs_1_.refs_5_.refs_7_, bf16[16,2,288,512]{3,2,1,0:T(8,128)(2,1)} %bitcast.74, bf16[512,1024]{1,0:T(8,128)(2,1)S(1)} %get-tuple-element.145.refs_3_.refs_4_.refs_5_), custom_call_target="tpu_custom_call" | custom-call | flops 14949999616 | bytes 1024 | tf_op jit(solution)/shard_map/norm_project/pallas_call | solution.py:62
  237.8 6.0 cross_attention.2
  243.8 5.9 cross_attention.3
  251.1 9.5 %branch.1 = (f32[1024,1024]{1,0:T(8,128)}, bf16[1024,1024]{1,0:T(8,128)(2,1)S(1)}) custom-call(bf16[1024,1024]{1,0:T(8,128)(2,1)S(1)} %copy-done.63, bf16[1024,1024]{1,0:T(8,128)(2,1)} %copy-done.61, bf16[16,2,576,512]{3,2,1,0:T(8,128)(2,1)} %bitcast.58, bf16[1024,1024]{1,0:T(8,128)(2,1)} %refs_6_.1, f32[1,1024]{1,0:T(1,128)S(1)} %get-tuple-element.249.refs_4_, ...), custom_call_target="tpu_custom_call" | custom-call | flops 11500000256 | bytes 1024 | tf_op jit(solution)/shard_map/branch/pallas_call | solution.py:62
  260.6 21.2 %hidden.1 = (bf16[1024,4096]{1,0:T(8,128)(2,1)}, bf16[1024,4096]{1,0:T(8,128)(2,1)}) custom-call(bf16[1024,1024]{1,0:T(8,128)(2,1)S(1)} %get-tuple-element.152.refs_0_.refs_2_.refs_1_, bf16[16,2,576,512]{3,2,1,0:T(8,128)(2,1)} %bitcast.59, bf16[1024,1024]{1,0:T(8,128)(2,1)S(1)} %get-tuple-element.152.refs_0_.refs_2_.refs_1_), custom_call_target="tpu_custom_call" | custom-call | flops 23000000512 | bytes 1024 | tf_op jit(solution)/shard_map/hidden/pallas_call | solution.py:62
  281.8 13.8 %grad_hidden_out.1 = (bf16[4,2,256,1024]{3,2,1,0:T(8,128)(2,1)}, bf16[4,2,256,1024]{3,2,1,0:T(8,128)(2,1)}) custom-call(s32[4]{0:T(128)} %copy-done.17, bf16[1024,4096]{1,0:T(8,128)(2,1)} %get-tuple-element.153.refs_1_.refs_3_.refs_0_, bf16[1024,1024]{1,0:T(8,128)(2,1)} %refs_5_.1, bf16[1024,4096]{1,0:T(8,128)(2,1)} %get-tuple-element.153.refs_1_.refs_3_.refs_0_), custom_call_target="tpu_custom_call" | custom-call | flops 16099999744 | bytes 1024 | tf_op jit(solution)/shard_map/grad_hidden_out/pallas_call | solution.py:62
  297.2 25.3 %result_and_pre.1 = (bf16[1024,1024]{1,0:T(8,128)(2,1)}, bf16[1024,4096]{1,0:T(8,128)(2,1)}) custom-call(bf16[1024,4096]{1,0:T(8,128)(2,1)} %get-tuple-element.153.refs_1_.refs_3_.refs_0_, bf16[1024,4096]{1,0:T(8,128)(2,1)} %get-tuple-element.154.refs_1_, bf16[16,2,256,512]{3,2,1,0:T(8,128)(2,1)} %bitcast.81, f32[1024,1024]{1,0:T(8,128)} %get-tuple-element.155.refs_3_, ...), custom_call_target="tpu_custom_call" | custom-call | flops 27599998976 | bytes 1024 | tf_op jit(solution)/shard_map/result_and_pre/pallas_call | solution.py:62
  322.4 4.7 fold_core.5
  328.2 15.1 %grad_hidden_in.1 = (bf16[4,2,64,4096]{3,2,1,0:T(8,128)(2,1)}, bf16[4,2,64,4096]{3,2,1,0:T(8,128)(2,1)}) custom-call(s32[4]{0:T(128)} %copy-done.17, bf16[1024,1024]{1,0:T(8,128)(2,1)} %copy-done.64, bf16[1024,4096]{1,0:T(8,128)(2,1)} %get-tuple-element.158.refs_2_.refs_1_, bf16[4,256,512]{2,1,0:T(8,128)(2,1)} %copy-done.51), custom_call_target="tpu_custom_call" | custom-call | flops 17250000896 | bytes 1024 | tf_op jit(solution)/shard_map/grad_hidden_in/pallas_call | solution.py:62
  345.9 12.2 %collective-permute-done.26.refs_2_ = bf16[2,256,512]{2,1,0:T(8,128)(2,1)S(1)} collective-permute-done((bf16[2,256,512]{2,1,0:T(8,128)(2,1)S(1)}, bf16[2,256,512]{2,1,0:T(8,128)(2,1)S(1)}, u32[]{:S(2)}, u32[]{:S(2)}) %collective-permute-start.26) | collective-permute-done | bytes 524320 | tf_op jit(solution)/shard_map/ppermute | solution.py:739
  361.2 19.1 %hidden_back.1 = (f32[1,1024]{1,0:T(1,128)S(1)}, bf16[1024,1024]{1,0:T(8,128)(2,1)S(1)}, f32[1024,1024]{1,0:T(8,128)}) custom-call(f32[1]{0:T(128)} %constant.80.clone.1.refs_0_, bf16[1024,4096]{1,0:T(8,128)(2,1)} %get-tuple-element.158.refs_2_.refs_1_, bf16[16,2,576,512]{3,2,1,0:T(8,128)(2,1)} %bitcast.60, f32[1024,1024]{1,0:T(8,128)} %get-tuple-element.155.refs_3_, ...), custom_call_target="tpu_custom_call" | custom-call | flops 23000000512 | bytes 1024 | tf_op jit(solution)/shard_map/hidden_back/pallas_call | solution.py:62
  380.4 5.0 fold_core.6
  390.1 7.8 %spread.1.refs_5_.refs_6_.refs_14_ = bf16[1024,2048]{1,0:T(8,128)(2,1)} custom-call(bf16[1024,1024]{1,0:T(8,128)(2,1)S(1)} %get-tuple-element.167.refs_0_.refs_6_, bf16[16,2,576,512]{3,2,1,0:T(8,128)(2,1)} %bitcast.61, bf16[4,256,512]{2,1,0:T(8,128)(2,1)} %fold_last.5.refs_2_), custom_call_target="tpu_custom_call" | custom-call | flops 9200000000 | bytes 1024 | tf_op jit(solution)/shard_map/spread/pallas_call | solution.py:62
  397.8 7.7 %cross_attention_back.1 = (bf16[1024,1024]{1,0:T(8,128)(2,1)S(1)}, bf16[512,1024]{1,0:T(8,128)(2,1)S(1)}, bf16[512,1024]{1,0:T(8,128)(2,1)S(1)}) custom-call(bf16[1024,4096]{1,0:T(8,128)(2,1)} %get-tuple-element.133.refs_2_.refs_0_.refs_1_.refs_5_.refs_6_.refs_7_, bf16[512,4096]{1,0:T(8,128)(2,1)} %get-tuple-element.146.refs_1_.refs_2_.refs_3_.refs_4_, ...), custom_call_target="tpu_custom_call" | custom-call | flops 11500000256 | bytes 1024 | tf_op jit(solution)/shard_map/cross_attention_back/pallas_call | solution.py:62
  407.7 8.8 %side_back.1 = (f32[1,1024]{1,0:T(1,128)S(1)}, bf16[512,1024]{1,0:T(8,128)(2,1)}, f32[512,1024]{1,0:T(8,128)}) custom-call(f32[1]{0:T(128)} %constant.80.clone.1.refs_0_, bf16[512,1024]{1,0:T(8,128)(2,1)S(1)} %get-tuple-element.172.refs_4_.refs_1_.refs_7_, bf16[512,1024]{1,0:T(8,128)(2,1)S(1)} %get-tuple-element.173.refs_2_.refs_8_, ...), custom_call_target="tpu_custom_call" | custom-call | flops 10350000128 | bytes 1024 | tf_op jit(solution)/shard_map/side_back/pallas_call | solution.py:62
  416.5 8.7 %gate_back.1 = (bf16[512,1024]{1,0:T(8,128)(2,1)S(1)}, bf16[512,1024]{1,0:T(8,128)(2,1)S(1)}, bf16[512,2048]{1,0:T(8,128)(2,1)S(1)}, f32[512,1024]{1,0:T(8,128)}, f32[1,1024]{1,0:T(1,128)S(1)}) custom-call(f32[1]{0:T(128)} %bitcast.15.refs_0_, f32[512,1024]{1,0:T(8,128)} %get-tuple-element.179.refs_1_, f32[512,1024]{1,0:T(8,128)} %copy-done.2, ...), custom_call_target="tpu_custom_call" | custom-call | flops 10350000128 | bytes 1024 | tf_op jit(solution)/shard_map/gate_back/pallas_call | solution.py:62
  429.1 15.7 %grad_out.1 = (bf16[4,2,320,1024]{3,2,1,0:T(8,128)(2,1)}, bf16[4,2,320,1024]{3,2,1,0:T(8,128)(2,1)}) custom-call(s32[4]{0:T(128)} %copy-done.17, bf16[1024,1024]{1,0:T(8,128)(2,1)} %copy-done.62, bf16[1024,1024]{1,0:T(8,128)(2,1)} %copy-done.61, bf16[512,1024]{1,0:T(8,128)(2,1)} %copy-done.4, bf16[512,1024]{1,0:T(8,128)(2,1)} %copy-done.6, ...), custom_call_target="tpu_custom_call" | custom-call | flops 18400000000 | bytes 1024 | tf_op jit(solution)/shard_map/grad_out/pallas_call | solution.py:62
  446.4 21.5 %state_attention_back.1 = (bf16[1024,1024]{1,0:T(8,128)(2,1)}, bf16[512,1024]{1,0:T(8,128)(2,1)S(1)}, bf16[512,1024]{1,0:T(8,128)(2,1)S(1)}, bf16[512,1024]{1,0:...) custom-call(s32[1]{0:T(128)} %bitcast.16.refs_0_, ...), custom_call_target="tpu_custom_call", output_to_operand_aliasing={{0}: (17, {})} | custom-call | flops 25300000768 | bytes 1024 | tf_op jit(solution)/shard_map/state_attention_back/pallas_call | solution.py:62
  472.5 6.3 fold_core.7
  487.1 10.3 %state_back.1 = (f32[1,1024]{1,0:T(1,128)S(1)}, bf16[512,1024]{1,0:T(8,128)(2,1)S(1)}) custom-call(f32[1]{0:T(128)} %bitcast.24.refs_0_, bf16[512,1024]{1,0:T(8,128)(2,1)S(1)} %copy-done.72, bf16[512,1024]{1,0:T(8,128)(2,1)S(1)} %copy-done.74, bf16[512,1024]{1,0:T(8,128)(2,1)S(1)} %copy-done.76, bf16[512,1024]{1,0:T(8,128)(2,1)S(1)} %copy-done.78, ...), custom_call_target="tpu_custom_call" | custom-call | flops 14949999616 | bytes 1024 | tf_op jit(solution)/shard_map/state_back/pallas_call | solution.py:62
  501.1 12.9 %grad_state_proj.1 = (bf16[4,2,80,4096]{3,2,1,0:T(8,128)(2,1)}, bf16[4,2,80,4096]{3,2,1,0:T(8,128)(2,1)}) custom-call(s32[4]{0:T(128)} %copy-done.17, bf16[512,1024]{1,0:T(8,128)(2,1)} %copy-done.79, bf16[512,1024]{1,0:T(8,128)(2,1)} %copy-done.68, bf16[512,1024]{1,0:T(8,128)(2,1)} %copy-done.71, bf16[512,1024]{1,0:T(8,128)(2,1)} %copy-done.73, ...), custom_call_target="tpu_custom_call" | custom-call | flops 14949999616 | bytes 1024 | tf_op jit(solution)/shard_map/grad_state_proj/pallas_call | solution.py:62
  517.3 16.4 %self_attention_back.1 = (bf16[1024,1024]{1,0:T(8,128)(2,1)S(1)}, bf16[1024,1024]{1,0:T(8,128)(2,1)S(1)}, bf16[1024,1024]{1,0:T(8,128)(2,1)}) custom-call(bf16[1024,4096]{1,0:T(8,128)(2,1)} %get-tuple-element.133.refs_2_.refs_0_.refs_1_.refs_5_.refs_6_.refs_7_, bf16[1024,4096]{1,0:T(8,128)(2,1)} %get-tuple-element.133.refs_2_.refs_0_.refs_1_.refs_5_.refs_6_.refs_7_, ...), custom_call_target="tpu_custom_call" | custom-call | flops 20700000256 | bytes 1024 | tf_op jit(solution)/shard_map/self_attention_back/pallas_call | solution.py:62
  536.3 6.1 fold_core.8
  551.7 15.3 %grad_token_proj.1 = (bf16[4,2,64,4096]{3,2,1,0:T(8,128)(2,1)}, bf16[4,2,64,4096]{3,2,1,0:T(8,128)(2,1)}) custom-call(s32[4]{0:T(128)} %copy-done.17, bf16[1024,1024]{1,0:T(8,128)(2,1)} %copy-done.70, bf16[1024,1024]{1,0:T(8,128)(2,1)} %copy-done.57, bf16[1024,1024]{1,0:T(8,128)(2,1)} %get-tuple-element.217.refs_3_.refs_2_, bf16[1024,1024]{1,0:T(8,128)(2,1)} %copy-done.69, ...), custom_call_target="tpu_custom_call" | custom-call | flops 17250000896 | bytes 1024 | tf_op jit(solution)/shard_map/grad_token_proj/pallas_call | solution.py:62
  570.3 14.2 %collective-permute-done.41.refs_2_ = bf16[2,80,2048]{2,1,0:T(8,128)(2,1)} collective-permute-done((bf16[2,80,2048]{2,1,0:T(8,128)(2,1)}, bf16[2,80,2048]{2,1,0:T(8,128)(2,1)}, u32[]{:S(2)}, u32[]{:S(2)}) %collective-permute-start.41) | collective-permute-done | bytes 655392 | tf_op jit(solution)/shard_map/ppermute | solution.py:739
  589.9 4.6 fold_core.9
  596.7 19.4 %tokens_back.1 = (f32[1,1024]{1,0:T(1,128)S(1)}, bf16[1024,1024]{1,0:T(8,128)(2,1)}) custom-call(f32[1]{0:T(128)} %constant.80.clone.1.refs_0_, bf16[1024,1024]{1,0:T(8,128)(2,1)S(1)} %copy-done.58, bf16[1024,1024]{1,0:T(8,128)(2,1)S(1)} %copy-done.60, bf16[1024,1024]{1,0:T(8,128)(2,1)} %copy-done.69, bf16[1024,1024]{1,0:T(8,128)(2,1)} %get-tuple-element.219.refs_5_.refs_4_, ...), custom_call_target="tpu_custom_call" | custom-call | flops 24149999616 | bytes 1024 | tf_op jit(solution)/shard_map/tokens_back/pallas_call | solution.py:62
  616.2 13.0 %collective-permute-done.46.refs_2_ = bf16[2,64,2048]{2,1,0:T(8,128)(2,1)S(1)} collective-permute-done((bf16[2,64,2048]{2,1,0:T(8,128)(2,1)S(1)}, bf16[2,64,2048]{2,1,0:T(8,128)(2,1)S(1)}, u32[]{:S(2)}, u32[]{:S(2)}) %collective-permute-start.46) | collective-permute-done | bytes 524320 | tf_op jit(solution)/shard_map/ppermute | solution.py:739
  640.7 10.0 %inner_attention.3 = (bf16[512,1024]{1,0:T(8,128)(2,1)S(1)}, bf16[512,1024]{1,0:T(8,128)(2,1)S(1)}, f32[8,1,512]{2,1,0:T(1,128)S(1)}, f32[8,1,512]{2,1,0:T(1,128)}) custom-call(s32[1]{0:T(128)} %bitcast.23.refs_0_, bf16[512,4096]{1,0:T(8,128)(2,1)} %get-tuple-element.146.refs_1_.refs_2_.refs_3_.refs_4_, ...), custom_call_target="tpu_custom_call" | custom-call | flops 19549999104 | bytes 1024 | tf_op jit(solution)/shard_map/inner_attention/pallas_call | solution.py:62
  650.7 8.3 %collective-permute-done.48.refs_1_ = bf16[4,64,2048]{2,1,0:T(8,128)(2,1)S(1)} collective-permute-done((bf16[4,64,2048]{2,1,0:T(8,128)(2,1)}, bf16[4,64,2048]{2,1,0:T(8,128)(2,1)S(1)}, u32[]{:S(2)}, u32[]{:S(2)}) %collective-permute-start.48) | collective-permute-done | bytes 1048608 | tf_op jit(solution)/shard_map/ppermute | solution.py:739
  670.7 8.3 %collective-permute-start.53 = (f32[4,512]{1,0:T(4,128)S(1)}, f32[4,512]{1,0:T(4,128)S(1)}, u32[]{:S(2)}, u32[]{:S(2)}) collective-permute-start(f32[4,512]{1,0:T(4,128)S(1)} %add.52), channel_id=1, source_target_pairs={{0,8},{2,10},{4,12},{6,14},{8,0},{10,2},{12,4},{14,6},{16,24},{18,... | collective-permute-start | bytes 24584 | tf_op jit(solution)/shard_map/ppermute | solution.py:739
  686.2 8.6 %update_state.3 = (bf16[512,1024]{1,0:T(8,128)(2,1)}, f32[512,1024]{1,0:T(8,128)}, f32[512,1024]{1,0:T(8,128)}) custom-call(f32[1]{0:T(128)} %bitcast.22.refs_0_, bf16[512,1024]{1,0:T(8,128)(2,1)S(1)} %get-tuple-element.233.refs_1_, bf16[512,1024]{1,0:T(8,128)(2,1)S(1)} %get-tuple-element.234.refs_2_, bf16[16,2,576,512]{3,2,1,0:T(8,128)(2,1)} %bitcast.64, ...), custom_call_target="tpu_custom_call" | custom-call | flops 10350000128 | bytes 1024 | tf_op jit(solution)/shard_map/update_state/pallas_call | solution.py:62
  (369 shorter events, 150.7 us)
Async XLA Ops:
  7.2 208.8 %all-gather.5.cloned.1.call-start = ((), (), s32[]{:S(2)}) async-start(), calls=%async_computation.10 | async-start | bytes 19464192 | tf_op jit(solution)/shard_map/all_gather | solution.py:772
  14.1 281.4 %all-gather.7.cloned.1.call-start = ((), (), s32[]{:S(2)}) async-start(), calls=%async_computation.11 | async-start | bytes 8650752 | tf_op jit(solution)/shard_map/all_gather | solution.py:772
  15.2 15.5 %collective-permute-start.1 = (bf16[256,512]{1,0:T(8,128)(2,1)S(1)}, bf16[256,512]{1,0:T(8,128)(2,1)S(1)}, u32[]{:S(2)}, u32[]{:S(2)}) collective-permute-start(bf16[256,512]{1,0:T(8,128)(2,1)S(1)} %get-tuple-element.244.refs_1_), channel_id=1, source_target_pairs={{0,8},{2,10},{4,12},{6,14},{8,0},{10,2},{12,4},{14,6},{16,24},{18,... | collective-permute-start | bytes 786440 | tf_op jit(solution)/shard_map/ppermute | solution.py:739
  18.3 25.8 %collective-permute-start.2 = (bf16[256,512]{1,0:T(8,128)(2,1)S(1)}, bf16[256,512]{1,0:T(8,128)(2,1)S(1)}, u32[]{:S(2)}, u32[]{:S(2)}) collective-permute-start(bf16[256,512]{1,0:T(8,128)(2,1)S(1)} %get-tuple-element.244.refs_1_), channel_id=1, source_target_pairs={{0,16},{2,18},{4,20},{6,22},{8,24},{10,26},{12,28},{14,30},{16,0},... | collective-permute-start | bytes 786440 | tf_op jit(solution)/shard_map/ppermute | solution.py:739
  20.9 23.7 %collective-permute-start.3 = (bf16[256,512]{1,0:T(8,128)(2,1)S(1)}, bf16[256,512]{1,0:T(8,128)(2,1)S(1)}, u32[]{:S(2)}, u32[]{:S(2)}) collective-permute-start(bf16[256,512]{1,0:T(8,128)(2,1)S(1)} %get-tuple-element.244.refs_1_), channel_id=1, source_target_pairs={{0,24},{2,26},{4,28},{6,30},{8,16},{10,18},{12,20},{14,22},{16,8},... | collective-permute-start | bytes 786440 | tf_op jit(solution)/shard_map/ppermute | solution.py:739
  44.7 30.9 %collective-permute-start.4 = (bf16[4,256,512]{2,1,0:T(8,128)(2,1)S(1)}, bf16[4,256,512]{2,1,0:T(8,128)(2,1)}, u32[]{:S(2)}, u32[]{:S(2)}) collective-permute-start(bf16[4,256,512]{2,1,0:T(8,128)(2,1)S(1)} %fence.7.refs_1_), channel_id=1, source_target_pairs={{0,4},{2,6},{4,0},{6,2},{8,12},{10,14},{12,8},{14,10},{16,20},{18,... | collective-permute-start | bytes 3145736 | tf_op jit(solution)/shard_map/ppermute | solution.py:739
  46.3 32.7 %collective-permute-start.5 = (bf16[4,256,512]{2,1,0:T(8,128)(2,1)S(1)}, bf16[4,256,512]{2,1,0:T(8,128)(2,1)}, u32[]{:S(2)}, u32[]{:S(2)}) collective-permute-start(bf16[4,256,512]{2,1,0:T(8,128)(2,1)S(1)} %fence.7.refs_1_), channel_id=1, source_target_pairs={{0,1},{1,0},{2,3},{3,2},{4,5},{5,4},{6,7},{7,6},{8,9},{9,8},{10,11... | collective-permute-start | bytes 3145736 | tf_op jit(solution)/shard_map/ppermute | solution.py:737
  48.0 44.7 %collective-permute-start.9 = (bf16[288,512]{1,0:T(8,128)(2,1)S(1)}, bf16[288,512]{1,0:T(8,128)(2,1)S(1)}, u32[]{:S(2)}, u32[]{:S(2)}) collective-permute-start(bf16[288,512]{1,0:T(8,128)(2,1)S(1)} %fence.8.refs_2_), channel_id=1, source_target_pairs={{0,16},{2,18},{4,20},{6,22},{8,24},{10,26},{12,28},{14,30},{16,0},... | collective-permute-start | bytes 884744 | tf_op jit(solution)/shard_map/ppermute | solution.py:739
  62.5 30.3 %collective-permute-start.10 = (bf16[288,512]{1,0:T(8,128)(2,1)S(1)}, bf16[288,512]{1,0:T(8,128)(2,1)}, u32[]{:S(2)}, u32[]{:S(2)}) collective-permute-start(bf16[288,512]{1,0:T(8,128)(2,1)S(1)} %fence.8.refs_2_), channel_id=1, source_target_pairs={{0,24},{2,26},{4,28},{6,30},{8,16},{10,18},{12,20},{14,22},{16,8},... | collective-permute-start | bytes 884744 | tf_op jit(solution)/shard_map/ppermute | solution.py:739
  62.9 34.4 %collective-permute-start.8 = (bf16[288,512]{1,0:T(8,128)(2,1)S(1)}, bf16[288,512]{1,0:T(8,128)(2,1)}, u32[]{:S(2)}, u32[]{:S(2)}) collective-permute-start(bf16[288,512]{1,0:T(8,128)(2,1)S(1)} %fence.8.refs_2_), channel_id=1, source_target_pairs={{0,8},{2,10},{4,12},{6,14},{8,0},{10,2},{12,4},{14,6},{16,24},{18,... | collective-permute-start | bytes 884744 | tf_op jit(solution)/shard_map/ppermute | solution.py:739
  81.0 17.8 %collective-permute-start.6 = (bf16[2,256,512]{2,1,0:T(8,128)(2,1)}, bf16[2,256,512]{2,1,0:T(8,128)(2,1)}, u32[]{:S(2)}, u32[]{:S(2)}) collective-permute-start(bf16[2,256,512]{2,1,0:T(8,128)(2,1)} %slice.90), channel_id=1, source_target_pairs={{0,1},{1,0},{2,3},{3,2},{4,5},{5,4},{6,7},{7,6},{8,9},{9,8},{10,11... | collective-permute-start | bytes 1572872 | tf_op jit(solution)/shard_map/ppermute | solution.py:737
  84.0 14.9 %collective-permute-start.7 = (bf16[2,256,512]{2,1,0:T(8,128)(2,1)S(1)}, bf16[2,256,512]{2,1,0:T(8,128)(2,1)}, u32[]{:S(2)}, u32[]{:S(2)}) collective-permute-start(bf16[2,256,512]{2,1,0:T(8,128)(2,1)S(1)} %slice.91), channel_id=1, source_target_pairs={{0,4},{2,6},{4,0},{6,2},{8,12},{10,14},{12,8},{14,10},{16,20},{18,... | collective-permute-start | bytes 1572872 | tf_op jit(solution)/shard_map/ppermute | solution.py:739
  84.5 396.9 %reduce-scatter.6.cloned.1.call-start = ((), (), s32[]{:S(2)}) async-start(), calls=%async_computation.5 | async-start | bytes 1310720 | tf_op jit(solution)/shard_map/reduce_scatter | solution.py:941
  102.6 44.5 %collective-permute-start.16 = (bf16[4,288,512]{2,1,0:T(8,128)(2,1)S(1)}, bf16[4,288,512]{2,1,0:T(8,128)(2,1)S(1)}, u32[]{:S(2)}, u32[]{:S(2)}) collective-permute-start(bf16[4,288,512]{2,1,0:T(8,128)(2,1)S(1)} %fence.10.refs_2_.refs_1_), channel_id=1, source_target_pairs={{0,4},{2,6},{4,0},{6,2},{8,12},{10,14},{12,8},{14,10},{16,20},{18,... | collective-permute-start | bytes 3538952 | tf_op jit(solution)/shard_map/ppermute | solution.py:739
  102.7 44.6 %collective-permute-start.17 = (bf16[4,288,512]{2,1,0:T(8,128)(2,1)S(1)}, bf16[4,288,512]{2,1,0:T(8,128)(2,1)S(1)}, u32[]{:S(2)}, u32[]{:S(2)}) collective-permute-start(bf16[4,288,512]{2,1,0:T(8,128)(2,1)S(1)} %fence.10.refs_2_.refs_1_), channel_id=1, source_target_pairs={{0,1},{1,0},{2,3},{3,2},{4,5},{5,4},{6,7},{7,6},{8,9},{9,8},{10,11... | collective-permute-start | bytes 3538952 | tf_op jit(solution)/shard_map/ppermute | solution.py:737
  102.8 81.1 %collective-permute-start.20 = (bf16[4,288,512]{2,1,0:T(8,128)(2,1)S(1)}, bf16[4,288,512]{2,1,0:T(8,128)(2,1)}, u32[]{:S(2)}, u32[]{:S(2)}) collective-permute-start(bf16[4,288,512]{2,1,0:T(8,128)(2,1)S(1)} %fence.10.refs_2_.refs_1_), channel_id=1, source_target_pairs={{0,2},{2,0},{4,6},{6,4},{8,10},{10,8},{12,14},{14,12},{16,18},{18,... | collective-permute-start | bytes 3538952 | tf_op jit(solution)/shard_map/ppermute | solution.py:739
  147.3 36.6 %collective-permute-start.21 = (bf16[4,288,512]{2,1,0:T(8,128)(2,1)S(1)}, bf16[4,288,512]{2,1,0:T(8,128)(2,1)}, u32[]{:S(2)}, u32[]{:S(2)}) collective-permute-start(bf16[4,288,512]{2,1,0:T(8,128)(2,1)S(1)} %get-tuple-element.134.refs_3_.refs_2_), channel_id=1, source_target_pairs={{0,2},{2,0},{4,6},{6,4},{8,10},{10,8},{12,14},{14,12},{16,18},{18,... | collective-permute-start | bytes 3538952 | tf_op jit(solution)/shard_map/ppermute | solution.py:739
  147.4 36.4 %collective-permute-start.22 = (bf16[4,288,512]{2,1,0:T(8,128)(2,1)S(1)}, bf16[4,288,512]{2,1,0:T(8,128)(2,1)}, u32[]{:S(2)}, u32[]{:S(2)}) collective-permute-start(bf16[4,288,512]{2,1,0:T(8,128)(2,1)S(1)} %get-tuple-element.136.refs_3_), channel_id=1, source_target_pairs={{0,2},{2,0},{4,6},{6,4},{8,10},{10,8},{12,14},{14,12},{16,18},{18,... | collective-permute-start | bytes 3538952 | tf_op jit(solution)/shard_map/ppermute | solution.py:739
  147.9 28.6 %collective-permute-start.18 = (bf16[2,288,512]{2,1,0:T(8,128)(2,1)S(1)}, bf16[2,288,512]{2,1,0:T(8,128)(2,1)}, u32[]{:S(2)}, u32[]{:S(2)}) collective-permute-start(bf16[2,288,512]{2,1,0:T(8,128)(2,1)S(1)} %slice.92), channel_id=1, source_target_pairs={{0,1},{1,0},{2,3},{3,2},{4,5},{5,4},{6,7},{7,6},{8,9},{9,8},{10,11... | collective-permute-start | bytes 1769480 | tf_op jit(solution)/shard_map/ppermute | solution.py:737
  148.0 28.8 %collective-permute-start.19 = (bf16[2,288,512]{2,1,0:T(8,128)(2,1)S(1)}, bf16[2,288,512]{2,1,0:T(8,128)(2,1)}, u32[]{:S(2)}, u32[]{:S(2)}) collective-permute-start(bf16[2,288,512]{2,1,0:T(8,128)(2,1)S(1)} %slice.93), channel_id=1, source_target_pairs={{0,4},{2,6},{4,0},{6,2},{8,12},{10,14},{12,8},{14,10},{16,20},{18,... | collective-permute-start | bytes 1769480 | tf_op jit(solution)/shard_map/ppermute | solution.py:739
  295.6 26.9 %collective-permute-start.25 = (bf16[4,2,256,1024]{3,2,1,0:T(8,128)(2,1)}, bf16[4,2,256,1024]{3,2,1,0:T(8,128)(2,1)}, u32[]{:S(2)}, u32[]{:S(2)}) collective-permute-start(bf16[4,2,256,1024]{3,2,1,0:T(8,128)(2,1)} %get-tuple-element.159), channel_id=1, source_target_pairs={{0,2},{2,0},{4,6},{6,4},{8,10},{10,8},{12,14},{14,12},{16,18},{18,... | collective-permute-start | bytes 12582920 | tf_op jit(solution)/shard_map/ppermute | solution.py:739
  343.3 37.0 %collective-permute-start.30 = (bf16[4,2,64,4096]{3,2,1,0:T(8,128)(2,1)}, bf16[4,2,64,4096]{3,2,1,0:T(8,128)(2,1)}, u32[]{:S(2)}, u32[]{:S(2)}) collective-permute-start(bf16[4,2,64,4096]{3,2,1,0:T(8,128)(2,1)} %get-tuple-element.169), channel_id=1, source_target_pairs={{0,2},{2,0},{4,6},{6,4},{8,10},{10,8},{12,14},{14,12},{16,18},{18,... | collective-permute-start | bytes 12582920 | tf_op jit(solution)/shard_map/ppermute | solution.py:739
  343.8 14.3 %collective-permute-start.26 = (bf16[2,256,512]{2,1,0:T(8,128)(2,1)S(1)}, bf16[2,256,512]{2,1,0:T(8,128)(2,1)S(1)}, u32[]{:S(2)}, u32[]{:S(2)}) collective-permute-start(bf16[2,256,512]{2,1,0:T(8,128)(2,1)S(1)} %get-tuple-element.162), channel_id=1, source_target_pairs={{0,4},{2,6},{4,0},{6,2},{8,12},{10,14},{12,8},{14,10},{16,20},{18,... | collective-permute-start | bytes 1572872 | tf_op jit(solution)/shard_map/ppermute | solution.py:739
  360.4 28.4 %collective-permute-start.28 = (bf16[4,256,512]{2,1,0:T(8,128)(2,1)S(1)}, bf16[4,256,512]{2,1,0:T(8,128)(2,1)S(1)}, u32[]{:S(2)}, u32[]{:S(2)}) collective-permute-start(bf16[4,256,512]{2,1,0:T(8,128)(2,1)S(1)} %get-tuple-element.166.refs_6_), channel_id=1, source_target_pairs={{0,4},{2,6},{4,0},{6,2},{8,12},{10,14},{12,8},{14,10},{16,20},{18,... | collective-permute-start | bytes 3145736 | tf_op jit(solution)/shard_map/ppermute | solution.py:739
  360.8 28.1 %collective-permute-start.29 = (bf16[4,256,512]{2,1,0:T(8,128)(2,1)S(1)}, bf16[4,256,512]{2,1,0:T(8,128)(2,1)S(1)}, u32[]{:S(2)}, u32[]{:S(2)}) collective-permute-start(bf16[4,256,512]{2,1,0:T(8,128)(2,1)S(1)} %get-tuple-element.168), channel_id=1, source_target_pairs={{0,1},{1,0},{2,3},{3,2},{4,5},{5,4},{6,7},{7,6},{8,9},{9,8},{10,11... | collective-permute-start | bytes 3145736 | tf_op jit(solution)/shard_map/ppermute | solution.py:737
  385.4 20.2 %collective-permute-start.31 = (bf16[2,64,2048]{2,1,0:T(8,128)(2,1)S(1)}, bf16[2,64,2048]{2,1,0:T(8,128)(2,1)S(1)}, u32[]{:S(2)}, u32[]{:S(2)}) collective-permute-start(bf16[2,64,2048]{2,1,0:T(8,128)(2,1)S(1)} %get-tuple-element.176), channel_id=1, source_target_pairs={{0,4},{2,6},{4,0},{6,2},{8,12},{10,14},{12,8},{14,10},{16,20},{18,... | collective-permute-start | bytes 1572872 | tf_op jit(solution)/shard_map/ppermute | solution.py:739
  387.1 18.5 %collective-permute-start.32 = (bf16[2,64,2048]{2,1,0:T(8,128)(2,1)S(1)}, bf16[2,64,2048]{2,1,0:T(8,128)(2,1)S(1)}, u32[]{:S(2)}, u32[]{:S(2)}) collective-permute-start(bf16[2,64,2048]{2,1,0:T(8,128)(2,1)S(1)} %get-tuple-element.177), channel_id=1, source_target_pairs={{0,1},{1,0},{2,3},{3,2},{4,5},{5,4},{6,7},{7,6},{8,9},{9,8},{10,11... | collective-permute-start | bytes 1572872 | tf_op jit(solution)/shard_map/ppermute | solution.py:737
  444.9 27.7 %collective-permute-start.33 = (bf16[4,2,320,1024]{3,2,1,0:T(8,128)(2,1)}, bf16[4,2,320,1024]{3,2,1,0:T(8,128)(2,1)}, u32[]{:S(2)}, u32[]{:S(2)}) collective-permute-start(bf16[4,2,320,1024]{3,2,1,0:T(8,128)(2,1)} %get-tuple-element.186), channel_id=1, source_target_pairs={{0,2},{2,0},{4,6},{6,4},{8,10},{10,8},{12,14},{14,12},{16,18},{18,... | collective-permute-start | bytes 15728648 | tf_op jit(solution)/shard_map/ppermute | solution.py:739
  445.5 104.4 %reduce-scatter.10.cloned.1.call-start = ((), (), s32[]{:S(2)}) async-start(), calls=%async_computation.7 | async-start | bytes 1310720 | tf_op jit(solution)/shard_map/reduce_scatter | solution.py:941
  445.6 25.6 %collective-permute-start.34 = (bf16[4,64,2048]{2,1,0:T(8,128)(2,1)S(1)}, bf16[4,64,2048]{2,1,0:T(8,128)(2,1)S(1)}, u32[]{:S(2)}, u32[]{:S(2)}) collective-permute-start(bf16[4,64,2048]{2,1,0:T(8,128)(2,1)S(1)} %copy-done.29), channel_id=1, source_target_pairs={{0,4},{2,6},{4,0},{6,2},{8,12},{10,14},{12,8},{14,10},{16,20},{18,... | collective-permute-start | bytes 3145736 | tf_op jit(solution)/shard_map/ppermute | solution.py:739
  446.0 25.4 %collective-permute-start.35 = (bf16[4,64,2048]{2,1,0:T(8,128)(2,1)S(1)}, bf16[4,64,2048]{2,1,0:T(8,128)(2,1)S(1)}, u32[]{:S(2)}, u32[]{:S(2)}) collective-permute-start(bf16[4,64,2048]{2,1,0:T(8,128)(2,1)S(1)} %copy-done.31), channel_id=1, source_target_pairs={{0,1},{1,0},{2,3},{3,2},{4,5},{5,4},{6,7},{7,6},{8,9},{9,8},{10,11... | collective-permute-start | bytes 3145736 | tf_op jit(solution)/shard_map/ppermute | solution.py:737
  478.9 18.5 %collective-permute-start.36 = (bf16[2,320,512]{2,1,0:T(8,128)(2,1)S(1)}, bf16[2,320,512]{2,1,0:T(8,128)(2,1)S(1)}, u32[]{:S(2)}, u32[]{:S(2)}) collective-permute-start(bf16[2,320,512]{2,1,0:T(8,128)(2,1)S(1)} %get-tuple-element.195), channel_id=1, source_target_pairs={{0,4},{2,6},{4,0},{6,2},{8,12},{10,14},{12,8},{14,10},{16,20},{18,... | collective-permute-start | bytes 1966088 | tf_op jit(solution)/shard_map/ppermute | solution.py:739
  480.5 16.9 %collective-permute-start.37 = (bf16[2,320,512]{2,1,0:T(8,128)(2,1)S(1)}, bf16[2,320,512]{2,1,0:T(8,128)(2,1)}, u32[]{:S(2)}, u32[]{:S(2)}) collective-permute-start(bf16[2,320,512]{2,1,0:T(8,128)(2,1)S(1)} %get-tuple-element.196), channel_id=1, source_target_pairs={{0,1},{1,0},{2,3},{3,2},{4,5},{5,4},{6,7},{7,6},{8,9},{9,8},{10,11... | collective-permute-start | bytes 1966088 | tf_op jit(solution)/shard_map/ppermute | solution.py:737
  514.0 22.3 %collective-permute-start.40 = (bf16[4,2,80,4096]{3,2,1,0:T(8,128)(2,1)}, bf16[4,2,80,4096]{3,2,1,0:T(8,128)(2,1)}, u32[]{:S(2)}, u32[]{:S(2)}) collective-permute-start(bf16[4,2,80,4096]{3,2,1,0:T(8,128)(2,1)} %get-tuple-element.208), channel_id=1, source_target_pairs={{0,2},{2,0},{4,6},{6,4},{8,10},{10,8},{12,14},{14,12},{16,18},{18,... | collective-permute-start | bytes 15728648 | tf_op jit(solution)/shard_map/ppermute | solution.py:739
  514.0 123.9 %reduce-scatter.8.cloned.1.call-start = ((), (), s32[]{:S(2)}) async-start(), calls=%async_computation.6 | async-start | bytes 1638400 | tf_op jit(solution)/shard_map/reduce_scatter | solution.py:941
  514.3 31.5 %collective-permute-start.38 = (bf16[4,320,512]{2,1,0:T(8,128)(2,1)}, bf16[4,320,512]{2,1,0:T(8,128)(2,1)S(1)}, u32[]{:S(2)}, u32[]{:S(2)}) collective-permute-start(bf16[4,320,512]{2,1,0:T(8,128)(2,1)} %copy-done.27), channel_id=1, source_target_pairs={{0,4},{2,6},{4,0},{6,2},{8,12},{10,14},{12,8},{14,10},{16,20},{18,... | collective-permute-start | bytes 3932168 | tf_op jit(solution)/shard_map/ppermute | solution.py:739
  515.8 31.1 %collective-permute-start.39 = (bf16[4,320,512]{2,1,0:T(8,128)(2,1)}, bf16[4,320,512]{2,1,0:T(8,128)(2,1)S(1)}, u32[]{:S(2)}, u32[]{:S(2)}) collective-permute-start(bf16[4,320,512]{2,1,0:T(8,128)(2,1)} %get-tuple-element.204), channel_id=1, source_target_pairs={{0,1},{1,0},{2,3},{3,2},{4,5},{5,4},{6,7},{7,6},{8,9},{9,8},{10,11... | collective-permute-start | bytes 3932168 | tf_op jit(solution)/shard_map/ppermute | solution.py:737
  567.0 22.9 %collective-permute-start.45 = (bf16[4,2,64,4096]{3,2,1,0:T(8,128)(2,1)}, bf16[4,2,64,4096]{3,2,1,0:T(8,128)(2,1)}, u32[]{:S(2)}, u32[]{:S(2)}) collective-permute-start(bf16[4,2,64,4096]{3,2,1,0:T(8,128)(2,1)} %get-tuple-element.223), channel_id=1, source_target_pairs={{0,2},{2,0},{4,6},{6,4},{8,10},{10,8},{12,14},{14,12},{16,18},{18,... | collective-permute-start | bytes 12582920 | tf_op jit(solution)/shard_map/ppermute | solution.py:739
  567.0 17.5 %collective-permute-start.41 = (bf16[2,80,2048]{2,1,0:T(8,128)(2,1)}, bf16[2,80,2048]{2,1,0:T(8,128)(2,1)}, u32[]{:S(2)}, u32[]{:S(2)}) collective-permute-start(bf16[2,80,2048]{2,1,0:T(8,128)(2,1)} %get-tuple-element.214), channel_id=1, source_target_pairs={{0,4},{2,6},{4,0},{6,2},{8,12},{10,14},{12,8},{14,10},{16,20},{18,... | collective-permute-start | bytes 1966088 | tf_op jit(solution)/shard_map/ppermute | solution.py:739
  568.5 17.0 %collective-permute-start.42 = (bf16[2,80,2048]{2,1,0:T(8,128)(2,1)S(1)}, bf16[2,80,2048]{2,1,0:T(8,128)(2,1)}, u32[]{:S(2)}, u32[]{:S(2)}) collective-permute-start(bf16[2,80,2048]{2,1,0:T(8,128)(2,1)S(1)} %get-tuple-element.215), channel_id=1, source_target_pairs={{0,1},{1,0},{2,3},{3,2},{4,5},{5,4},{6,7},{7,6},{8,9},{9,8},{10,11... | collective-permute-start | bytes 1966088 | tf_op jit(solution)/shard_map/ppermute | solution.py:737
  570.0 127.7 %reduce-scatter.14.cloned.1.call-start = ((), (), s32[]{:S(2)}) async-start(), calls=%async_computation.9 | async-start | bytes 1638400 | tf_op jit(solution)/shard_map/reduce_scatter | solution.py:941
  587.8 42.8 %collective-permute-start.43 = (bf16[4,80,2048]{2,1,0:T(8,128)(2,1)S(1)}, bf16[4,80,2048]{2,1,0:T(8,128)(2,1)S(1)}, u32[]{:S(2)}, u32[]{:S(2)}) collective-permute-start(bf16[4,80,2048]{2,1,0:T(8,128)(2,1)S(1)} %get-tuple-element.221.refs_3_), channel_id=1, source_target_pairs={{0,4},{2,6},{4,0},{6,2},{8,12},{10,14},{12,8},{14,10},{16,20},{18,... | collective-permute-start | bytes 3932168 | tf_op jit(solution)/shard_map/ppermute | solution.py:739
  588.4 42.2 %collective-permute-start.44 = (bf16[4,80,2048]{2,1,0:T(8,128)(2,1)S(1)}, bf16[4,80,2048]{2,1,0:T(8,128)(2,1)S(1)}, u32[]{:S(2)}, u32[]{:S(2)}) collective-permute-start(bf16[4,80,2048]{2,1,0:T(8,128)(2,1)S(1)} %get-tuple-element.222), channel_id=1, source_target_pairs={{0,1},{1,0},{2,3},{3,2},{4,5},{5,4},{6,7},{7,6},{8,9},{9,8},{10,11... | collective-permute-start | bytes 3932168 | tf_op jit(solution)/shard_map/ppermute | solution.py:737
  594.5 34.7 %collective-permute-start.46 = (bf16[2,64,2048]{2,1,0:T(8,128)(2,1)S(1)}, bf16[2,64,2048]{2,1,0:T(8,128)(2,1)S(1)}, u32[]{:S(2)}, u32[]{:S(2)}) collective-permute-start(bf16[2,64,2048]{2,1,0:T(8,128)(2,1)S(1)} %get-tuple-element.226), channel_id=1, source_target_pairs={{0,4},{2,6},{4,0},{6,2},{8,12},{10,14},{12,8},{14,10},{16,20},{18,... | collective-permute-start | bytes 1572872 | tf_op jit(solution)/shard_map/ppermute | solution.py:739
  596.0 33.7 %collective-permute-start.47 = (bf16[2,64,2048]{2,1,0:T(8,128)(2,1)S(1)}, bf16[2,64,2048]{2,1,0:T(8,128)(2,1)S(1)}, u32[]{:S(2)}, u32[]{:S(2)}) collective-permute-start(bf16[2,64,2048]{2,1,0:T(8,128)(2,1)S(1)} %get-tuple-element.227), channel_id=1, source_target_pairs={{0,1},{1,0},{2,3},{3,2},{4,5},{5,4},{6,7},{7,6},{8,9},{9,8},{10,11... | collective-permute-start | bytes 1572872 | tf_op jit(solution)/shard_map/ppermute | solution.py:737
  634.2 66.4 %reduce-scatter.12.cloned.1.call-start = ((), (), s32[]{:S(2)}) async-start(), calls=%async_computation.8 | async-start | bytes 1310720 | tf_op jit(solution)/shard_map/reduce_scatter | solution.py:941
  635.2 23.8 %collective-permute-start.48 = (bf16[4,64,2048]{2,1,0:T(8,128)(2,1)}, bf16[4,64,2048]{2,1,0:T(8,128)(2,1)S(1)}, u32[]{:S(2)}, u32[]{:S(2)}) collective-permute-start(bf16[4,64,2048]{2,1,0:T(8,128)(2,1)} %copy-done.32), channel_id=1, source_target_pairs={{0,4},{2,6},{4,0},{6,2},{8,12},{10,14},{12,8},{14,10},{16,20},{18,... | collective-permute-start | bytes 3145736 | tf_op jit(solution)/shard_map/ppermute | solution.py:739
  636.5 23.3 %collective-permute-start.49 = (bf16[4,64,2048]{2,1,0:T(8,128)(2,1)}, bf16[4,64,2048]{2,1,0:T(8,128)(2,1)}, u32[]{:S(2)}, u32[]{:S(2)}) collective-permute-start(bf16[4,64,2048]{2,1,0:T(8,128)(2,1)} %copy-done.33), channel_id=1, source_target_pairs={{0,1},{1,0},{2,3},{3,2},{4,5},{5,4},{6,7},{7,6},{8,9},{9,8},{10,11... | collective-permute-start | bytes 3145736 | tf_op jit(solution)/shard_map/ppermute | solution.py:737
  (105 other events, 825.6 us)
Sparse Core Ops, SparseCore 0:
  14.2 184.0 all-gather.4
  201.5 76.6 all-gather.6
  445.7 35.6 reduce-scatter.5
  514.2 35.7 reduce-scatter.9
  570.1 36.7 reduce-scatter.7
  634.3 37.8 reduce-scatter.13
  674.5 26.0 reduce-scatter.11

commit v6 on v5

--- a/solution.py
+++ b/solution.py
@@ -31,16 +31,7 @@
 
 
 MICROSECOND = 1.15e9
-TIMES = {
-    "norm_project": 13, "self_attention": 17, "inner_attention": 17, "cross_attention": 10, "update_state": 9, "branch": 10,
-    "hidden": 20, "grad_hidden_out": 14, "result_and_pre": 24, "grad_hidden_in": 15, "hidden_back": 20, "spread": 8,
-    "cross_attention_back": 10, "side_back": 9, "gate_back": 9, "grad_out": 16, "state_attention_back": 22, "state_back": 13,
-    "grad_state_proj": 13, "self_attention_back": 18, "grad_token_proj": 15, "tokens_back": 21, "spell": 7, "fence": 1,
-    "fold_core": 5, "fold_mid": 2, "fold_last": 2, "widen": 1,
-}
-
-
-def launch(body, operands, *, grid, in_specs, out_specs, out_shape, name, flops, after=(), where=None, scratch=(), aliases=None, exps=0, limit=48):
+def launch(body, operands, *, grid, in_specs, out_specs, out_shape, us, flops, after=(), where=None, scratch=(), aliases=None, exps=0, limit=48):
     count = len(operands)
     late = len(after)
     lead = 0 if where is None else 1
@@ -64,8 +55,8 @@
         out_shape=list(out_shape),
         input_output_aliases=aliases or {},
         compiler_params=pltpu.CompilerParams(vmem_limit_bytes=limit * MIB),
-        cost_estimate=pl.CostEstimate(flops=int(MICROSECOND * TIMES[name]), bytes_accessed=1024, transcendentals=0),
-        name=name,
+        cost_estimate=pl.CostEstimate(flops=int(MICROSECOND * us), bytes_accessed=1024, transcendentals=0),
+        name=getattr(body, "func", body).__name__,
         **kwargs,
     )(*(() if where is None else (where,)), *operands, *after)
 
@@ -158,7 +149,7 @@
     total_cols = 4 * width
     step = STEP
     return launch(
-        norm_project_kernel, [x, gain, weight[0]], after=after, name="norm_project", grid=(total_cols // step,),
+        norm_project_kernel, [x, gain, weight[0]], after=after, us=13, grid=(total_cols // step,),
         in_specs=[whole((rows, width)), whole((1, width)), group_spec(weight, lambda i: i)],
         out_specs=[whole((rows, width)), pl.BlockSpec((rows, step), lambda i: (0, i))],
         out_shape=[shaped((rows, width)), shaped((rows, total_cols))],
@@ -183,7 +174,7 @@
     tile = pl.BlockSpec((step, width), lambda i: (i, 0))
     return launch(
         update_kernel, [live, inner_self, inner_cross, state_out[0], gate_weight[0], bias, state],
-        after=after, name="update_state", grid=(rows // step,),
+        after=after, us=9, grid=(rows // step,),
         in_specs=[SMEM, tile, tile, rows_spec(state_out, 16, lambda i: 0), rows_spec(gate_weight, 16, lambda i: 0), whole((1, width)), tile],
         out_specs=[tile, tile, tile],
         out_shape=[shaped((rows, width)), shaped((rows, width), F32), shaped((rows, width), F32)],
@@ -204,7 +195,7 @@
     step = 256
     tile = pl.BlockSpec((step, width), lambda i: (i, 0))
     return launch(
-        branch_kernel, [self_out, cross_out, token_out[0], x, gain], after=after, name="branch", grid=(rows // step,),
+        branch_kernel, [self_out, cross_out, token_out[0], x, gain], after=after, us=10, grid=(rows // step,),
         in_specs=[tile, tile, rows_spec(token_out, 16, lambda i: 0), tile, whole((1, width))],
         out_specs=[tile, tile],
         out_shape=[shaped((rows, width), F32), shaped((rows, width))],
@@ -235,7 +226,7 @@
     step = STEP
     tile = pl.BlockSpec((rows, step), lambda i: (0, i))
     return launch(
-        hidden_kernel, [normed, weight[0]], after=after, name="hidden", grid=(total_cols // step,),
+        hidden_kernel, [normed, weight[0]], after=after, us=20, grid=(total_cols // step,),
         in_specs=[whole((rows, width)), group_spec(weight, lambda i: i)],
         out_specs=[tile, tile], out_shape=[shaped((rows, total_cols))] * 2,
         flops=2 * rows * width * total_cols, exps=rows * total_cols,
@@ -260,7 +251,7 @@
     step = STEP
     tile = pl.BlockSpec((rows, step), lambda i: (0, i))
     return launch(
-        result_kernel, [active, slope, weight[0], middle, grad], after=after, name="result_and_pre",
+        result_kernel, [active, slope, weight[0], middle, grad], after=after, us=40,
         grid=(hidden_units // step,),
         in_specs=[tile, tile, rows_spec(weight, step // weight[2]), whole((rows, width)), whole((rows, width))],
         out_specs=[whole((rows, width)), tile],
@@ -300,7 +291,7 @@
                 outs[2][at, :] = grad
 
 
-def norm_back_project(grads, weight, x, gain, plus, name, keep_wide=False, offset=0, scale=None, after=()):
+def norm_back_project(grads, weight, x, gain, plus, us, keep_wide=False, offset=0, scale=None, after=()):
     rows, width = x.shape
     step = STEP
     share = grads[0].shape[1] // step
@@ -314,7 +305,7 @@
     if scale is None:
         scale = jnp.ones((1,), F32)
     return launch(
-        partial(norm_back_kernel, parts, keep_wide), [scale, *grads, weight[0], x, gain, plus], after=after, name=name,
+        partial(norm_back_kernel, parts, keep_wide), [scale, *grads, weight[0], x, gain, plus], after=after, us=us,
         grid=(steps,),
         in_specs=[SMEM] + [part_spec(part) for part in range(parts)]
         + [group_spec(weight, lambda i: i + offset // step), whole((rows, width)), whole((1, width)), whole((rows, width))],
@@ -333,7 +324,7 @@
     total_cols = 16 * weight[2]
     step = STEP
     return launch(
-        spread_kernel, [grad, weight[0]], after=after, name="spread", grid=(total_cols // step,),
+        spread_kernel, [grad, weight[0]], after=after, us=8, grid=(total_cols // step,),
         in_specs=[whole((rows, width)), rows_spec(weight, step // weight[2])],
         out_specs=[pl.BlockSpec((rows, step), lambda i: (0, i))],
         out_shape=[shaped((rows, total_cols))], flops=2 * rows * width * total_cols,
@@ -368,7 +359,7 @@
     tile = pl.BlockSpec((step, width), lambda i: (i, 0))
     wide = pl.BlockSpec((step, 2 * width), lambda i: (i, 0))
     return launch(
-        gate_back_kernel, [live, grad, gate, state, mixed, gate_weight[0], state_out[0]], after=after, name="gate_back",
+        gate_back_kernel, [live, grad, gate, state, mixed, gate_weight[0], state_out[0]], after=after, us=9,
         grid=(rows // step,),
         in_specs=[SMEM, tile, tile, tile, tile, rows_spec(gate_weight, 16, lambda i: 0), rows_spec(state_out, 16, lambda i: 0)],
         out_specs=[tile, tile, wide, tile, whole((1, width))],
@@ -423,7 +414,7 @@
                 send_ref[0, x, row : row + 16, at] = jnp.zeros((16, 1024), jnp.bfloat16)
 
 
-def weight_grad(jobs, where, name, extra=None, after=()):
+def weight_grad(jobs, where, us, extra=None, after=()):
     lefts, rights, specs, table, row = [], [], [], [], 0
     for these, those, plan, split in jobs:
         rows = these[0].shape[1] * (2 if split else 1) // 16
@@ -449,7 +440,7 @@
     out = pl.BlockSpec((1, 2, row, cols), lambda z, p: (z, 0, 0, 0))
     return launch(
         partial(weight_grad_kernel, table, (len(lefts), len(rights)), at), operands,
-        where=where, after=after, name=name, grid=(4,), in_specs=specs,
+        where=where, after=after, us=us, grid=(4,), in_specs=specs,
         out_specs=[out, out], out_shape=[shaped((4, 2, row, cols))] * 2,
         flops=2 * rights[0].shape[0] * 16 * row * cols, limit=56,
     )
@@ -542,7 +533,7 @@
     rows, width = projected.shape
     heads = width // 4 // HD
     return launch(
-        partial(self_kernel, window), [projected] * 3, after=after, name="self_attention", grid=(heads // HEADS,),
+        partial(self_kernel, window), [projected] * 3, after=after, us=17, grid=(heads // HEADS,),
         in_specs=[column(rows, 0), column(rows, 2 * heads), column(rows, 3 * heads)],
         out_specs=[column(rows, 0), stat(rows)],
         out_shape=[shaped((rows, width // 4)), shaped((heads, 1, rows), F32)],
@@ -570,7 +561,7 @@
         operands.append(before)
         specs.append(pl.BlockSpec(memory_space=pl.ANY))
     return launch(
-        cross_kernel, operands, after=after, name="cross_attention", grid=(heads // HEADS,), in_specs=specs,
+        cross_kernel, operands, after=after, us=10, grid=(heads // HEADS,), in_specs=specs,
         out_specs=[block_column(rows, block, 0), stat(rows)],
         out_shape=[shaped((projected.shape[0], width // 4)), shaped((heads, 1, rows), F32)],
         aliases=None if before is None else {3: 0},
@@ -594,7 +585,7 @@
     rows, width = state_side.shape
     heads = width // 4 // HD
     return launch(
-        inner_kernel, [live_keys] + [state_side] * 4 + [projected] * 2, after=after, name="inner_attention", grid=(heads // HEADS,),
+        inner_kernel, [live_keys] + [state_side] * 4 + [projected] * 2, after=after, us=17, grid=(heads // HEADS,),
         in_specs=[SMEM] + [column(rows, part * heads) for part in range(4)]
         + [block_column(rows, block, 2 * heads), block_column(rows, block, 3 * heads)],
         out_specs=[column(rows, 0)] * 2 + [stat(rows)] * 2,
@@ -688,7 +679,7 @@
     extra = extra_k.shape[0]
     return launch(
         partial(self_back_kernel, window), [projected] * 3 + [out, log, grad_attended, extra_k, extra_v],
-        after=after, name="self_attention_back", grid=(heads // HEADS,),
+        after=after, us=18, grid=(heads // HEADS,),
         in_specs=[column(rows, 0), column(rows, 2 * heads), column(rows, 3 * heads), column(rows, 0), stat(rows),
                   column(rows, 0), column(extra, 0), column(extra, 0)],
         out_specs=[column(rows, 0)] * 3, out_shape=[shaped((rows, width // 4))] * 3,
@@ -702,7 +693,7 @@
     heads = width // 4 // HD
     return launch(
         cross_back_kernel, [projected, state_side, state_side, out, log, grad_attended],
-        after=after, name="cross_attention_back", grid=(heads // HEADS,),
+        after=after, us=10, grid=(heads // HEADS,),
         in_specs=[block_column(rows, block, heads), column(rows, 2 * heads), column(rows, 3 * heads),
                   block_column(rows, block, 0), stat(rows), block_column(rows, block, heads)],
         out_specs=[block_column(rows, block, 0), column(rows, 0), column(rows, 0)],
@@ -720,7 +711,7 @@
         [live_keys, projected] + [state_side] * 4 + [projected] * 2
         + [cross[0], inner_self[0], inner_cross[0], cross[1], inner_self[1], inner_cross[1]]
         + [grad_attended, grad_inner, grad_inner, before],
-        after=after, name="state_attention_back", grid=(heads // HEADS,),
+        after=after, us=40, grid=(heads // HEADS,),
         in_specs=[SMEM, block_column(rows, block, heads)] + [column(rows, part * heads) for part in range(4)]
         + [block_column(rows, block, 2 * heads), block_column(rows, block, 3 * heads)]
         + [block_column(rows, block, 0), column(rows, 0), column(rows, 0)] + [stat(rows)] * 3
@@ -755,7 +746,7 @@
 
 def fence(arrays, after):
     return launch(
-        fence_kernel, arrays, after=after, name="fence", grid=(1,),
+        fence_kernel, arrays, after=after, us=1, grid=(1,),
         in_specs=[pl.BlockSpec(memory_space=pl.ANY)] * len(arrays),
         out_specs=[pl.BlockSpec(memory_space=pl.ANY)] * len(arrays),
         out_shape=[shaped(item.shape, item.dtype) for item in arrays],
@@ -799,7 +790,7 @@
 
 def fence(arrays, after):
     return launch(
-        fence_kernel, arrays, after=after, name="fence", grid=(1,),
+        fence_kernel, arrays, after=after, us=1, grid=(1,),
         in_specs=[pl.BlockSpec(memory_space=pl.ANY)] * len(arrays),
         out_specs=[pl.BlockSpec(memory_space=pl.ANY)] * len(arrays),
         out_shape=[shaped(item.shape, item.dtype) for item in arrays],
@@ -842,7 +833,7 @@
             return pl.BlockSpec((1, rows, COLS), lambda i, p: (jnp.clip(i, low, high - 1) - low, 0, 0))
 
         (every,) = launch(
-            spell_kernel, self.pieces, where=self.where, after=after, name="spell", grid=(4,),
+            spell_kernel, self.pieces, where=self.where, after=after, us=7, grid=(4,),
             in_specs=[spec(0, 4), spec(0, 4), spec(0, 4), spec(0, 2), spec(2, 4)] * 2,
             out_specs=[pl.BlockSpec((1, 2, 2, 2, rows, COLS), lambda i, p: (i ^ p[3], 0, 0, 0, 0, 0))],
             out_shape=[shaped((4, 2, 2, 2, rows, COLS))], flops=0,
@@ -876,7 +867,7 @@
     full = pl.BlockSpec((2, rows, cols // 2), lambda i, p: (i, 0, 0))
     half = pl.BlockSpec((2, rows, cols // 2), lambda i, p: (0, 0, 0))
     return launch(
-        fold_core_kernel, [keep, come], where=where, after=after, name="fold_core", grid=(2,),
+        fold_core_kernel, [keep, come], where=where, after=after, us=5, grid=(2,),
         in_specs=[pair, pair], out_specs=[half, half, full, full, full],
         out_shape=[shaped((2, rows, cols // 2))] * 2 + [shaped((4, rows, cols // 2))] * 3,
         flops=keep.size,
@@ -893,7 +884,7 @@
     low = pl.BlockSpec(block, lambda i: (0, 0, 0))
     high = pl.BlockSpec(block, lambda i: (1, 0, 0))
     return launch(
-        fold_mid_kernel, [px, py, rx, ry], after=after, name="fold_mid", grid=(1,),
+        fold_mid_kernel, [px, py, rx, ry], after=after, us=2, grid=(1,),
         in_specs=[high, low, low, low], out_specs=[high, low],
         out_shape=[shaped(px.shape), shaped(py.shape)], aliases={0: 0, 1: 1}, flops=px.size,
     )
@@ -903,11 +894,11 @@
     out_ref[...] = narrow(add(own_ref[...], rx_ref[...], ry_ref[...]))
 
 
-def fold_last(own, rx, ry, after=()):
+def fold_last(own, rx, ry, us, after=()):
     _, rows, cols = own.shape
     block = pl.BlockSpec((2, rows, cols), lambda i: (i, 0, 0))
     return launch(
-        fold_last_kernel, [own, rx, ry], after=after, name="fold_last", grid=(2,),
+        fold_last_kernel, [own, rx, ry], after=after, us=us, grid=(2,),
         in_specs=[block] * 3, out_specs=[block], out_shape=[shaped(own.shape)], flops=2 * own.size,
     )[0]
 
@@ -925,6 +916,11 @@
         self.where, self.keep = where, keep
         self.come = swap(send, "core")
 
+    def step(self, after, us):
+        self.us = us
+        self.steps = getattr(self, "steps", 0) + 1
+        return (self.core, self.mid, self.last)[self.steps - 1](after)
+
     def core(self, after):
         low, high, self.px, self.py, self.own = fold_core(self.keep, self.come, self.where, after)
         self.rx, self.ry = swap(low, "x"), swap(high, "y")
@@ -936,7 +932,7 @@
         return (px,)
 
     def last(self, after):
-        line = fold_last(self.own, self.one, self.two, after)
+        line = fold_last(self.own, self.one, self.two, self.us, after)
         rows, cols = line.shape[1:]
         self.out = lax.psum_scatter(
             line.reshape(4 * rows, cols), "dp", scatter_dimension=0, axis_index_groups=LINES, tiled=True
@@ -945,7 +941,7 @@
 
     def widen(self, cuts, after):
         outs = launch(
-            partial(widen_kernel, cuts), [self.out], after=after, name="widen", grid=(1,),
+            partial(widen_kernel, cuts), [self.out], after=after, us=1, grid=(1,),
             in_specs=[whole(self.out.shape)], out_specs=[whole((rows * parts, cols)) for _, rows, parts, cols in cuts],
             out_shape=[shaped((rows * parts, cols), F32) for _, rows, parts, cols in cuts], flops=0,
         )
@@ -1038,6 +1034,9 @@
         order = second_gather.start(order)
         order = first_gather.far(order)
         order = second_gather.near(order)
+        opening, *scalars = fence([jnp.where(first, 1.0, 0.0).astype(F32).reshape(1), *lives, *live_keys], order)
+        lives, live_keys = scalars[:2], scalars[2:]
+        order = (opening,)
         order = first_gather.cross(order)
         (full_token_proj,) = first_gather.whole(order)
         full_hidden_in, full_state_out, full_token_out, full_gate_weight = gather_blocks(
@@ -1045,6 +1044,7 @@
         )
         (full_hidden_out,) = gather_blocks([hidden_out])
     else:
+        opening = jnp.where(first, 1.0, 0.0).astype(F32).reshape(1)
         (
             full_token_proj, full_state_proj, full_state_out, full_gate_weight, full_init, full_token_out, full_hidden_in,
             full_hidden_out,
@@ -1065,7 +1065,7 @@
         full_state_proj, full_init = second_gather.whole(order)
     array, row, rows = full_init
     full_init = array[:, :, row : row + rows].transpose(0, 2, 1, 3).reshape(states, width)
-    state_0 = jnp.where(first, full_init, incoming[0]).astype(F32)
+    state_0 = jnp.where(opening[0] > 0.0, full_init, incoming[0]).astype(F32)
     normed_0, side_0 = norm_project(state_0, state_gain_f, full_state_proj, order)
     order = (side_0,)
     inner_self_0, inner_cross_0, inner_self_log, inner_cross_log = inner_attention(
@@ -1087,71 +1087,69 @@
     active, slope = hidden(hidden_normed, full_hidden_in, order)
     order = (active,)
 
-    scatters = {}
-
-    def weight(name, *jobs, extra=None):
+    def weight(us, *jobs, extra=None):
         nonlocal order
         if paired():
-            keep, send = weight_grad(jobs, where, "grad_" + name, extra, order)
-            scatters[name] = Scatter(keep, send, where)
+            keep, send = weight_grad(jobs, where, us, extra, order)
             order = (keep,)
-            return
-        scatters[name] = []
+            return Scatter(keep, send, where)
+        plain = []
         for lefts, rights, plan, split in jobs:
             if split:
                 lefts = [jnp.concatenate(lefts, axis=1)]
             grad = jnp.concatenate(
                 [sum(matmul_left_t(lefts[a], rights[b]) for a, b in terms) for terms in plan], axis=1
             )
-            scatters[name].append(scatter_plain(narrow(grad)).astype(F32))
+            plain.append(scatter_plain(narrow(grad)).astype(F32))
         if extra is not None:
-            scatters[name].append(scatter_plain(extra).astype(F32))
-
-    def sums(name, *cuts):
+            plain.append(scatter_plain(extra).astype(F32))
+        return plain
+
+    def sums(scatter, *cuts):
         nonlocal order
         if not paired():
-            return scatters[name]
-        outs = scatters[name].widen(cuts, order)
+            return scatter
+        outs = scatter.widen(cuts, order)
         order = (outs[0],)
         return outs
 
-    def fold(name, step):
+    def fold(scatter, us=3):
         nonlocal order
         if paired():
-            order = getattr(scatters[name], step)(order)
+            order = scatter.step(order, us)
 
     one = [[(0, 0)]]
-    weight("hidden_out", ([active], [output_grad], one, False))
+    scatter_hidden_out = weight(14, ([active], [output_grad], one, False))
     result, grad_pre = result_and_pre(active, slope, full_hidden_out, middle, output_grad, order)
     order = (result,)
-    fold("hidden_out", "core")
-    weight("hidden_in", ([hidden_normed], [grad_pre], one, False))
-    fold("hidden_out", "mid")
+    fold(scatter_hidden_out)
+    scatter_hidden_in = weight(15, ([hidden_normed], [grad_pre], one, False))
     grad_hidden_gain, grad_branch, grad_middle = norm_back_project(
-        [grad_pre], full_hidden_in, middle, hidden_gain_f, output_grad, "hidden_back", True, after=order
+        [grad_pre], full_hidden_in, middle, hidden_gain_f, output_grad, 40, True, after=order
     )
     order = (grad_hidden_gain,)
-    fold("hidden_in", "core")
-    fold("hidden_out", "last")
+    fold(scatter_hidden_out)
+    fold(scatter_hidden_in)
     grad_attended = spread(grad_branch, full_token_out, order)
     order = (grad_attended,)
     grad_cross, grad_keys_1, grad_values_1 = cross_attention_back(
         projected, side_1, cross_out, cross_log_1, grad_attended, 1, order
     )
     order = (grad_keys_1,)
-    fold("hidden_in", "mid")
     no_term = jnp.zeros((states, width), jnp.bfloat16)
     grad_state_gain_1, _, grad_state_1 = norm_back_project(
-        [grad_keys_1, grad_values_1], full_state_proj, state_1, state_gain_f, no_term, "side_back", True,
+        [grad_keys_1, grad_values_1], full_state_proj, state_1, state_gain_f, no_term, 9, True,
         offset=2 * width, after=order,
     )
     order = (grad_state_gain_1,)
+    fold(scatter_hidden_out)
+    fold(scatter_hidden_in)
     grad_gate_low, grad_mixed, grad_inner, grad_direct, grad_gate_bias = gate_back(
         lives[0], grad_state_1, gate_0, state_0, mixed_0, full_gate_weight, full_state_out, order
     )
     order = (grad_gate_bias,)
-    weight(
-        "out",
+    scatter_out = weight(
+        16,
         ([self_out, cross_out], [grad_branch], one, True),
         ([inner_self_0, inner_cross_0], [grad_mixed], one, True),
         ([mixed_0], [grad_gate_low], one, False),
@@ -1162,57 +1160,56 @@
     )
     grad_cross, grads_side_0, extra_keys, extra_values = parts[0], parts[1:5], parts[5], parts[6]
     order = (extra_keys,)
-    fold("hidden_in", "last")
-    fold("out", "core")
-    (hidden_out_sum,) = sums("hidden_out", (0, 256, 1, 512))
-    grad_state_gain_0, grad_init = norm_back_project(
-        grads_side_0, full_state_proj, state_0, state_gain_f, grad_direct, "state_back",
-        scale=jnp.where(first, 1.0, 0.0).astype(F32).reshape(1), after=order,
-    )
-    order = (grad_state_gain_0,)
-    fold("out", "mid")
-    weight(
-        "state_proj",
+    fold(scatter_hidden_in)
+    fold(scatter_out)
+    (hidden_out_sum,) = sums(scatter_hidden_out, (0, 256, 1, 512))
+    scatter_state_proj = weight(
+        13,
         (
             [normed_0, normed_1],
             [*grads_side_0, grad_keys_1, grad_values_1],
             [[(0, 0)], [(0, 1)], [(0, 2), (1, 4)], [(0, 3), (1, 5)]],
             False,
         ),
-        extra=grad_init,
-    )
+    )
+    grad_state_gain_0, grad_init = norm_back_project(
+        grads_side_0, full_state_proj, state_0, state_gain_f, grad_direct, 40, scale=opening, after=order,
+    )
+    order = (grad_state_gain_0,)
+    fold(scatter_out)
+    fold(scatter_state_proj)
     grad_self, grad_keys, grad_values = self_attention_back(
         projected, self_out, self_log, grad_attended, extra_keys, extra_values, window, order
     )
     order = (grad_self,)
-    fold("state_proj", "core")
-    fold("out", "last")
-    (hidden_in_sum,) = sums("hidden_in", (0, 64, 1, 2048))
+    fold(scatter_state_proj)
+    fold(scatter_out)
+    (hidden_in_sum,) = sums(scatter_hidden_in, (0, 64, 1, 2048))
     grads_projected = [grad_self, grad_cross, grad_keys, grad_values]
-    weight("token_proj", ([normed], grads_projected, [[(0, i)] for i in range(4)], False))
-    fold("state_proj", "mid")
-    fold("token_proj", "core")
-    grad_token_gain, tokens_grad = norm_back_project(
-        grads_projected, full_token_proj, tokens, token_gain_f, grad_middle, "tokens_back", after=order
-    )
-    order = (grad_token_gain,)
-    fold("token_proj", "mid")
-    fold("state_proj", "last")
-    token_out_sum, state_out_sum, gate_sum = sums("out", (0, 128, 1, 512), (128, 128, 1, 512), (256, 64, 1, 512))
+    scatter_token_proj = weight(
+        15, ([normed], grads_projected, [[(0, i)] for i in range(4)], False), extra=grad_init
+    )
+    fold(scatter_state_proj, 40)
+    fold(scatter_token_proj)
     inner_self_1, inner_cross_1, log, _ = inner_attention(projected, side_1, live_keys[1], 1, order)
     order = (log,)
-    fold("token_proj", "last")
+    fold(scatter_token_proj)
+    grad_token_gain, tokens_grad = norm_back_project(
+        grads_projected, full_token_proj, tokens, token_gain_f, grad_middle, 20, after=order
+    )
+    order = (grad_token_gain,)
+    token_out_sum, state_out_sum, gate_sum = sums(scatter_out, (0, 128, 1, 512), (128, 128, 1, 512), (256, 64, 1, 512))
+    fold(scatter_token_proj)
+    vectors = jnp.concatenate(
+        [grad_token_gain, grad_state_gain_0 + grad_state_gain_1, grad_hidden_gain, grad_gate_bias], axis=0
+    )
+    vector_grads = scatter_vectors(fence([vectors], order)[0])
     _, _, state_2 = update_state(
         lives[1], inner_self_1, inner_cross_1, full_state_out, full_gate_weight, gate_bias_f, state_1, order
     )
     order = (state_2,)
-    state_proj_sum, init_sum = sums("state_proj", (0, 64, 1, 2048), (64, 16, 2, 512))
-    (token_proj_sum,) = sums("token_proj", (0, 64, 1, 2048))
-    vector_grads = scatter_vectors(
-        jnp.concatenate(
-            [grad_token_gain, grad_state_gain_0 + grad_state_gain_1, grad_hidden_gain, grad_gate_bias], axis=0
-        )
-    )
+    (state_proj_sum,) = sums(scatter_state_proj, (0, 64, 1, 2048))
+    token_proj_sum, init_sum = sums(scatter_token_proj, (0, 64, 1, 2048), (64, 16, 2, 512))
     matrix_grads = [
         token_proj_sum, state_proj_sum, token_out_sum, state_out_sum, gate_sum, init_sum, hidden_in_sum, hidden_out_sum,
     ]

time: 715 us -> 695 us (0.972)
  waiting for transfers between devices: 161 us -> 144 us
  Pallas kernels: 403 us -> 415 us
  local copies, waits for them, and re-layouts: 47.8 us -> 40.1 us
    ppermute x39, waiting for transfers between devices: 128 us -> 109 us  [swap(): return lax.ppermute(values, 'dp', [(d, d ^ bit) for d in range(16)])]
    pallas_call x56 -> x58, Pallas kernels: 403 us -> 415 us  [launch(): pl.pallas_call(run, out_shape=list(out_shape), input_output_aliases=alias...]
    unnamed x193 -> x185, local copies, waits for them, and re-layouts: 39.7 us -> 33.4 us
  transfers between devices with their start and end apart: 62 -> 62, of which waited for: 33 -> 30; matrix products, arithmetic and copies ran while one was open for 2% -> 2% of each run, Pallas kernels for 45% -> 55%
where the time goes in v6:
time: 695 us; the launch traced here: 691 us
  Pallas kernels  415 us (60%)
  waiting for transfers between devices  144 us (21%)
  starting transfers between devices  66.2 us (10%)
  local copies, waits for them, and re-layouts  40.1 us (6%)
  between operations  19.3 us (3%)
    pallas_call x58, Pallas kernels, launch(): pl.pallas_call(run, out_shape=list(out_shape), input_output_aliases=alias...  415 us
    ppermute x39, waiting for transfers between devices, swap(): return lax.ppermute(values, 'dp', [(d, d ^ bit) for d in range(16)])  109 us
    ppermute x39, starting transfers between devices, swap(): return lax.ppermute(values, 'dp', [(d, d ^ bit) for d in range(16)])  50.8 us
    unnamed x185, local copies, waits for them, and re-layouts  33.4 us
    ppermute x16, waiting for transfers between devices, swap(): return lax.ppermute(values, 'fsdp', [(0, 1), (1, 0)])  28.4 us
    ppermute x16, starting transfers between devices, swap(): return lax.ppermute(values, 'fsdp', [(0, 1), (1, 0)])  15.2 us
  transfers between devices with their start and end apart: 62, of which 30 were waited for; matrix products, arithmetic and copies ran while one was open for 2% of the time, Pallas kernels for 55%

profile of v6, /device:TPU:0, one launch (start us, length us, event | category | flops | bytes accessed | tf_op | source)
XLA Modules:
  0.0 690.7 jit_solution(10085101243726203352)
XLA Ops:
  22.0 8.7 %collective-permute-done.1 = bf16[256,512]{1,0:T(8,128)(2,1)S(1)} collective-permute-done((bf16[256,512]{1,0:T(8,128)(2,1)S(1)}, bf16[256,512]{1,0:T(8,128)(2,1)S(1)}, u32[]{:S(2)}, u32[]{:S(2)}) %collective-permute-start.1) | collective-permute-done | bytes 262176 | tf_op jit(solution)/shard_map/ppermute | solution.py:730
  30.7 13.4 %collective-permute-done.2 = bf16[256,512]{1,0:T(8,128)(2,1)S(1)} collective-permute-done((bf16[256,512]{1,0:T(8,128)(2,1)S(1)}, bf16[256,512]{1,0:T(8,128)(2,1)S(1)}, u32[]{:S(2)}, u32[]{:S(2)}) %collective-permute-start.2) | collective-permute-done | bytes 262176 | tf_op jit(solution)/shard_map/ppermute | solution.py:730
  48.8 12.4 %collective-permute-start.8 = (bf16[288,512]{1,0:T(8,128)(2,1)S(1)}, bf16[288,512]{1,0:T(8,128)(2,1)}, u32[]{:S(2)}, u32[]{:S(2)}) collective-permute-start(bf16[288,512]{1,0:T(8,128)(2,1)S(1)} %fence_kernel.10.refs_2_), channel_id=1, source_target_pairs={{0,8},{2,10},{4,12},{6,14},{8,0},{10,2},{12,4},{14,6},{16,24},{18,... | collective-permute-start | bytes 884744 | tf_op jit(solution)/shard_map/ppermute | solution.py:730
  64.3 11.9 %collective-permute-done.4.refs_0_ = bf16[4,256,512]{2,1,0:T(8,128)(2,1)S(1)} collective-permute-done((bf16[4,256,512]{2,1,0:T(8,128)(2,1)S(1)}, bf16[4,256,512]{2,1,0:T(8,128)(2,1)S(1)}, u32[]{:S(2)}, u32[]{:S(2)}) %collective-permute-start.4) | collective-permute-done | bytes 1048608 | tf_op jit(solution)/shard_map/ppermute | solution.py:730
  83.5 14.3 %collective-permute-done.9 = bf16[288,512]{1,0:T(8,128)(2,1)} collective-permute-done((bf16[288,512]{1,0:T(8,128)(2,1)S(1)}, bf16[288,512]{1,0:T(8,128)(2,1)}, u32[]{:S(2)}, u32[]{:S(2)}) %collective-permute-start.9) | collective-permute-done | bytes 294944 | tf_op jit(solution)/shard_map/ppermute | solution.py:730
  109.7 7.0 %spell_kernel.2 = bf16[4,2,2,2,256,512]{5,4,3,2,1,0:T(8,128)(2,1)} custom-call(s32[4]{0:T(128)S(1)} %pad_add_fusion.refs_0_, bf16[4,256,512]{2,1,0:T(8,128)(2,1)S(1)} %fence_kernel.9.refs_1_, bf16[4,256,512]{2,1,0:T(8,128)(2,1)S(1)} %get-tuple-element.134.refs_1_.refs_2_, bf16[4,256,512]{2,1,0:T(8,128)(2,1)S(1)} %get-tuple-element.135.refs_3_, ...), custom_call_target="tpu_custom_call" | custom-call | flops 8049999872 | bytes 1024 | tf_op jit(solution)/shard_map/spell_kernel/pallas_call | solution.py:53
  116.6 15.1 %norm_project_kernel.3 = (bf16[1024,1024]{1,0:T(8,128)(2,1)S(1)}, bf16[1024,4096]{1,0:T(8,128)(2,1)}) custom-call(bf16[1024,1024]{1,0:T(8,128)(2,1)S(1)} %copy-done.24, f32[1,1024]{1,0:T(1,128)S(1)} %get-tuple-element.262.refs_1_.refs_7_, bf16[16,2,256,512]{3,2,1,0:T(8,128)(2,1)} %bitcast.82, bf16[2,256,512]{2,1,0:T(8,128)(2,1)} %get-tuple-element.137.refs_4_.refs_11_.refs_3_), custom_call_target="tpu_custom_call" | custom-call | flops 14949999616 | bytes 1024 | tf_op jit(solution)/shard_map/norm_project_kernel/pallas_call | solution.py:53
  131.8 22.9 %collective-permute-done.16.refs_0_ = bf16[4,288,512]{2,1,0:T(8,128)(2,1)S(1)} collective-permute-done((bf16[4,288,512]{2,1,0:T(8,128)(2,1)S(1)}, bf16[4,288,512]{2,1,0:T(8,128)(2,1)S(1)}, u32[]{:S(2)}, u32[]{:S(2)}) %collective-permute-start.16) | collective-permute-done | bytes 1179680 | tf_op jit(solution)/shard_map/ppermute | solution.py:730
  158.0 8.8 %self_kernel.1 = (bf16[1024,1024]{1,0:T(8,128)(2,1)S(1)}, f32[8,1,1024]{2,1,0:T(1,128)S(1)}) custom-call(bf16[1024,4096]{1,0:T(8,128)(2,1)} %get-tuple-element.139.refs_2_.refs_0_.refs_1_.refs_5_.refs_6_.refs_7_, bf16[1024,4096]{1,0:T(8,128)(2,1)} %get-tuple-element.139.refs_2_.refs_0_.refs_1_.refs_5_.refs_6_.refs_7_, ...), custom_call_target="tpu_custom_call" | custom-call | flops 19549999104 | bytes 1024 | tf_op jit(solution)/shard_map/self_kernel/pallas_call | solution.py:53
  166.8 15.8 %collective-permute-done.18.refs_0_ = bf16[2,288,512]{2,1,0:T(8,128)(2,1)S(1)} collective-permute-done((bf16[2,288,512]{2,1,0:T(8,128)(2,1)S(1)}, bf16[2,288,512]{2,1,0:T(8,128)(2,1)S(1)}, u32[]{:S(2)}, u32[]{:S(2)}) %collective-permute-start.18) | collective-permute-done | bytes 589856 | tf_op jit(solution)/shard_map/ppermute | solution.py:728
  187.6 6.8 spell_kernel.3
  197.4 10.3 %norm_project_kernel.4 = (bf16[512,1024]{1,0:T(8,128)(2,1)S(1)}, bf16[512,4096]{1,0:T(8,128)(2,1)}) custom-call(f32[512,1024]{1,0:T(8,128)S(1)} %fusion.refs_0_.refs_6_.refs_3_, f32[1,1024]{1,0:T(1,128)S(1)} %get-tuple-element.261.refs_1_.refs_5_.refs_7_, bf16[16,2,288,512]{3,2,1,0:T(8,128)(2,1)} %bitcast.73, ...), custom_call_target="tpu_custom_call" | custom-call | flops 14949999616 | bytes 1024 | tf_op jit(solution)/shard_map/norm_project_kernel/pallas_call | solution.py:53
  208.7 9.9 %inner_kernel.2 = (bf16[512,1024]{1,0:T(8,128)(2,1)S(1)}, bf16[512,1024]{1,0:T(8,128)(2,1)S(1)}, f32[8,1,512]{2,1,0:T(1,128)S(1)}, f32[8,1,512]{2,1,0:T(1,128)S(1)}) custom-call(s32[1]{0:T(128)} %get-tuple-element.143.refs_0_, bf16[512,4096]{1,0:T(8,128)(2,1)} %get-tuple-element.148.refs_1_.refs_2_.refs_3_.refs_4_.refs_7_.refs_5_, ...), custom_call_target="tpu_custom_call" | custom-call | flops 19549999104 | bytes 1024 | tf_op jit(solution)/shard_map/inner_kernel/pallas_call | solution.py:53
  218.6 9.0 %update_kernel.2 = (bf16[512,1024]{1,0:T(8,128)(2,1)S(1)}, f32[512,1024]{1,0:T(8,128)S(1)}, f32[512,1024]{1,0:T(8,128)}) custom-call(f32[1]{0:T(128)} %get-tuple-element.142.refs_0_, bf16[512,1024]{1,0:T(8,128)(2,1)S(1)} %get-tuple-element.149.refs_1_.refs_3_.refs_9_, bf16[512,1024]{1,0:T(8,128)(2,1)S(1)} %get-tuple-element.150.refs_2_.refs_4_.refs_10_, ...), custom_call_target="tpu_custom_call" | custom-call | flops 10350000128 | bytes 1024 | tf_op jit(solution)/shard_map/update_kernel/pallas_call | solution.py:53
  230.9 9.6 %norm_project_kernel.5 = (bf16[512,1024]{1,0:T(8,128)(2,1)S(1)}, bf16[512,4096]{1,0:T(8,128)(2,1)}) custom-call(f32[512,1024]{1,0:T(8,128)S(1)} %copy-done.1, f32[1,1024]{1,0:T(1,128)S(1)} %get-tuple-element.261.refs_1_.refs_5_.refs_7_, bf16[16,2,288,512]{3,2,1,0:T(8,128)(2,1)} %bitcast.74, bf16[512,1024]{1,0:T(8,128)(2,1)S(1)} %get-tuple-element.153.refs_3_.refs_4_.refs_5_), custom_call_target="tpu_custom_call" | custom-call | flops 14949999616 | bytes 1024 | tf_op jit(solution)/shard_map/norm_project_kernel/pallas_call | solution.py:53
  240.5 6.0 cross_kernel.2
  246.5 5.8 cross_kernel.3
  253.7 10.0 %branch_kernel.1 = (f32[1024,1024]{1,0:T(8,128)}, bf16[1024,1024]{1,0:T(8,128)(2,1)S(1)}) custom-call(bf16[1024,1024]{1,0:T(8,128)(2,1)S(1)} %copy-done.52, bf16[1024,1024]{1,0:T(8,128)(2,1)} %copy-done.48, bf16[16,2,576,512]{3,2,1,0:T(8,128)(2,1)} %bitcast.59, bf16[1024,1024]{1,0:T(8,128)(2,1)} %refs_6_.1, f32[1,1024]{1,0:T(1,128)S(1)} %get-tuple-element.259.refs_4_, ...), custom_call_target="tpu_custom_call" | custom-call | flops 11500000256 | bytes 1024 | tf_op jit(solution)/shard_map/branch_kernel/pallas_call | solution.py:53
  263.7 21.2 %hidden_kernel.1 = (bf16[1024,4096]{1,0:T(8,128)(2,1)}, bf16[1024,4096]{1,0:T(8,128)(2,1)}) custom-call(bf16[1024,1024]{1,0:T(8,128)(2,1)S(1)} %get-tuple-element.160.refs_0_.refs_2_.refs_1_, bf16[16,2,576,512]{3,2,1,0:T(8,128)(2,1)} %bitcast.60, bf16[1024,1024]{1,0:T(8,128)(2,1)S(1)} %get-tuple-element.160.refs_0_.refs_2_.refs_1_), custom_call_target="tpu_custom_call" | custom-call | flops 23000000512 | bytes 1024 | tf_op jit(solution)/shard_map/hidden_kernel/pallas_call | solution.py:53
  284.9 14.5 %weight_grad_kernel.5 = (bf16[4,2,256,1024]{3,2,1,0:T(8,128)(2,1)}, bf16[4,2,256,1024]{3,2,1,0:T(8,128)(2,1)}) custom-call(s32[4]{0:T(128)} %copy-done.17, bf16[1024,4096]{1,0:T(8,128)(2,1)} %get-tuple-element.161.refs_1_.refs_3_.refs_0_, bf16[1024,1024]{1,0:T(8,128)(2,1)} %refs_5_.1, bf16[1024,4096]{1,0:T(8,128)(2,1)} %get-tuple-element.161.refs_1_.refs_3_.refs_0_), custom_call_target="tpu_custom_call" | custom-call | flops 16099999744 | bytes 1024 | tf_op jit(solution)/shard_map/weight_grad_kernel/pallas_call | solution.py:53
  299.5 25.6 %result_kernel.1 = (bf16[1024,1024]{1,0:T(8,128)(2,1)}, bf16[1024,4096]{1,0:T(8,128)(2,1)}) custom-call(bf16[1024,4096]{1,0:T(8,128)(2,1)} %get-tuple-element.161.refs_1_.refs_3_.refs_0_, bf16[1024,4096]{1,0:T(8,128)(2,1)} %get-tuple-element.162.refs_1_, bf16[16,2,256,512]{3,2,1,0:T(8,128)(2,1)} %bitcast.81, f32[1024,1024]{1,0:T(8,128)} %get-tuple-element.163.refs_3_, ...), custom_call_target="tpu_custom_call" | custom-call | flops 46000001024 | bytes 1024 | tf_op jit(solution)/shard_map/result_kernel/pallas_call | solution.py:53
  325.1 4.9 fold_core_kernel.5
  333.6 15.1 %weight_grad_kernel.6 = (bf16[4,2,64,4096]{3,2,1,0:T(8,128)(2,1)}, bf16[4,2,64,4096]{3,2,1,0:T(8,128)(2,1)}) custom-call(s32[4]{0:T(128)} %copy-done.17, bf16[1024,1024]{1,0:T(8,128)(2,1)} %copy-done.53, bf16[1024,4096]{1,0:T(8,128)(2,1)} %get-tuple-element.169.refs_2_.refs_1_, bf16[4,256,512]{2,1,0:T(8,128)(2,1)} %copy-done.44), custom_call_target="tpu_custom_call" | custom-call | flops 17250000896 | bytes 1024 | tf_op jit(solution)/shard_map/weight_grad_kernel/pallas_call | solution.py:53
  348.8 19.2 %norm_back_kernel.4 = (f32[1,1024]{1,0:T(1,128)S(1)}, bf16[1024,1024]{1,0:T(8,128)(2,1)S(1)}, f32[1024,1024]{1,0:T(8,128)}) custom-call(f32[1]{0:T(128)} %constant.82.clone.1.refs_0_, bf16[1024,4096]{1,0:T(8,128)(2,1)} %get-tuple-element.169.refs_2_.refs_1_, bf16[16,2,576,512]{3,2,1,0:T(8,128)(2,1)} %bitcast.61, f32[1024,1024]{1,0:T(8,128)} %get-tuple-element.163.refs_3_, ...), custom_call_target="tpu_custom_call" | custom-call | flops 46000001024 | bytes 1024 | tf_op jit(solution)/shard_map/norm_back_kernel/pallas_call | solution.py:53
  370.2 4.5 fold_core_kernel.6
  374.8 8.2 %spread_kernel.1.refs_5_.refs_6_.refs_14_ = bf16[1024,2048]{1,0:T(8,128)(2,1)} custom-call(bf16[1024,1024]{1,0:T(8,128)(2,1)S(1)} %get-tuple-element.173.refs_0_.refs_6_, bf16[16,2,576,512]{3,2,1,0:T(8,128)(2,1)} %bitcast.62, bf16[4,64,2048]{2,1,0:T(8,128)(2,1)S(1)} %get-tuple-element.181.refs_2_.refs_0_), custom_call_target="tpu_custom_call" | custom-call | flops 9200000000 | bytes 1024 | tf_op jit(solution)/shard_map/spread_kernel/pallas_call | solution.py:53
  383.0 7.7 %cross_back_kernel.1 = (bf16[1024,1024]{1,0:T(8,128)(2,1)S(1)}, bf16[512,1024]{1,0:T(8,128)(2,1)S(1)}, bf16[512,1024]{1,0:T(8,128)(2,1)S(1)}) custom-call(bf16[1024,4096]{1,0:T(8,128)(2,1)} %get-tuple-element.139.refs_2_.refs_0_.refs_1_.refs_5_.refs_6_.refs_7_, bf16[512,4096]{1,0:T(8,128)(2,1)} %get-tuple-element.154.refs_1_.refs_2_.refs_3_.refs_4_, ...), custom_call_target="tpu_custom_call" | custom-call | flops 11500000256 | bytes 1024 | tf_op jit(solution)/shard_map/cross_back_kernel/pallas_call | solution.py:53
  394.9 8.6 %norm_back_kernel.5 = (f32[1,1024]{1,0:T(1,128)S(1)}, bf16[512,1024]{1,0:T(8,128)(2,1)}, f32[512,1024]{1,0:T(8,128)}) custom-call(f32[1]{0:T(128)} %constant.82.clone.1.refs_0_, bf16[512,1024]{1,0:T(8,128)(2,1)S(1)} %get-tuple-element.183.refs_1_.refs_7_, bf16[512,1024]{1,0:T(8,128)(2,1)S(1)} %get-tuple-element.184.refs_2_.refs_8_, ...), custom_call_target="tpu_custom_call" | custom-call | flops 10350000128 | bytes 1024 | tf_op jit(solution)/shard_map/norm_back_kernel/pallas_call | solution.py:53
  408.5 10.3 %gate_back_kernel.1 = (bf16[512,1024]{1,0:T(8,128)(2,1)S(1)}, bf16[512,1024]{1,0:T(8,128)(2,1)S(1)}, bf16[512,2048]{1,0:T(8,128)(2,1)}, f32[512,1024]{1,0:T(8,128)}, f32[1,1024]{1,0:T(1,128)S(1)}) custom-call(f32[1]{0:T(128)} %get-tuple-element.142.refs_0_, f32[512,1024]{1,0:T(8,128)} %get-tuple-element.185.refs_1_, f32[512,1024]{1,0:T(8,128)} %copy-done.2, ...), custom_call_target="tpu_custom_call" | custom-call | flops 10350000128 | bytes 1024 | tf_op jit(solution)/shard_map/gate_back_kernel/pallas_call | solution.py:53
  421.3 15.6 %weight_grad_kernel.7 = (bf16[4,2,320,1024]{3,2,1,0:T(8,128)(2,1)}, bf16[4,2,320,1024]{3,2,1,0:T(8,128)(2,1)}) custom-call(s32[4]{0:T(128)} %copy-done.17, bf16[1024,1024]{1,0:T(8,128)(2,1)} %copy-done.51, bf16[1024,1024]{1,0:T(8,128)(2,1)} %copy-done.48, bf16[512,1024]{1,0:T(8,128)(2,1)} %copy-done.4, bf16[512,1024]{1,0:T(8,128)(2,1)} %copy-done.6, ...), custom_call_target="tpu_custom_call" | custom-call | flops 18400000000 | bytes 1024 | tf_op jit(solution)/shard_map/weight_grad_kernel/pallas_call | solution.py:53
  438.5 21.9 %state_back_kernel.1 = (bf16[1024,1024]{1,0:T(8,128)(2,1)}, bf16[512,1024]{1,0:T(8,128)(2,1)S(1)}, bf16[512,1024]{1,0:T(8,128)(2,1)S(1)}, bf16[512,1024]{1,0:T(8...) custom-call(s32[1]{0:T(128)} %get-tuple-element.143.refs_0_, ...), custom_call_target="tpu_custom_call", output_to_operand_aliasing={{0}: (17, {})} | custom-call | flops 46000001024 | bytes 1024 | tf_op jit(solution)/shard_map/state_back_kernel/pallas_call | solution.py:53
  464.1 6.8 fold_core_kernel.7
  476.6 13.1 %weight_grad_kernel.8 = (bf16[4,2,64,4096]{3,2,1,0:T(8,128)(2,1)}, bf16[4,2,64,4096]{3,2,1,0:T(8,128)(2,1)}) custom-call(s32[4]{0:T(128)} %copy-done.17, bf16[512,1024]{1,0:T(8,128)(2,1)} %copy-done.61, bf16[512,1024]{1,0:T(8,128)(2,1)} %copy-done.58, bf16[512,1024]{1,0:T(8,128)(2,1)} %copy-done.62, bf16[512,1024]{1,0:T(8,128)(2,1)} %copy-done.64, ...), custom_call_target="tpu_custom_call" | custom-call | flops 14949999616 | bytes 1024 | tf_op jit(solution)/shard_map/weight_grad_kernel/pallas_call | solution.py:53
  489.7 11.1 %norm_back_kernel.6 = (f32[1,1024]{1,0:T(1,128)S(1)}, bf16[512,1024]{1,0:T(8,128)(2,1)S(1)}) custom-call(f32[1]{0:T(128)} %get-tuple-element.136.refs_2_.refs_0_, bf16[512,1024]{1,0:T(8,128)(2,1)S(1)} %copy-done.63, bf16[512,1024]{1,0:T(8,128)(2,1)S(1)} %copy-done.65, bf16[512,1024]{1,0:T(8,128)(2,1)S(1)} %copy-done.67, bf16[512,1024]{1,0:T(8,128)(2,1)S(1)} %copy-done.69, ...), custom_call_target="tpu_custom_call" | custom-call | flops 46000001024 | bytes 1024 | tf_op jit(solution)/shard_map/norm_back_kernel/pallas_call | solution.py:53
  504.9 5.5 fold_core_kernel.8
  513.2 16.6 %self_back_kernel.1 = (bf16[1024,1024]{1,0:T(8,128)(2,1)S(1)}, bf16[1024,1024]{1,0:T(8,128)(2,1)S(1)}, bf16[1024,1024]{1,0:T(8,128)(2,1)}) custom-call(bf16[1024,4096]{1,0:T(8,128)(2,1)} %get-tuple-element.139.refs_2_.refs_0_.refs_1_.refs_5_.refs_6_.refs_7_, bf16[1024,4096]{1,0:T(8,128)(2,1)} %get-tuple-element.139.refs_2_.refs_0_.refs_1_.refs_5_.refs_6_.refs_7_, ...), custom_call_target="tpu_custom_call" | custom-call | flops 20700000256 | bytes 1024 | tf_op jit(solution)/shard_map/self_back_kernel/pallas_call | solution.py:53
  531.1 14.9 %collective-permute-done.41.refs_2_ = bf16[2,64,2048]{2,1,0:T(8,128)(2,1)S(1)} collective-permute-done((bf16[2,64,2048]{2,1,0:T(8,128)(2,1)S(1)}, bf16[2,64,2048]{2,1,0:T(8,128)(2,1)S(1)}, u32[]{:S(2)}, u32[]{:S(2)}) %collective-permute-start.41) | collective-permute-done | bytes 524320 | tf_op jit(solution)/shard_map/ppermute | solution.py:730
  556.5 15.7 %weight_grad_kernel.9 = (bf16[4,2,80,4096]{3,2,1,0:T(8,128)(2,1)}, bf16[4,2,80,4096]{3,2,1,0:T(8,128)(2,1)}) custom-call(s32[4]{0:T(128)} %copy-done.17, bf16[1024,1024]{1,0:T(8,128)(2,1)} %copy-done.60, bf16[1024,1024]{1,0:T(8,128)(2,1)} %copy-done.37, bf16[1024,1024]{1,0:T(8,128)(2,1)} %get-tuple-element.221.refs_3_.refs_2_, ...), custom_call_target="tpu_custom_call" | custom-call | flops 17250000896 | bytes 1024 | tf_op jit(solution)/shard_map/weight_grad_kernel/pallas_call | solution.py:53
  577.2 4.0 collective-permute-done.43.refs_2_
  581.2 6.8 fold_core_kernel.9
  590.4 10.6 %inner_kernel.3 = (bf16[512,1024]{1,0:T(8,128)(2,1)S(1)}, bf16[512,1024]{1,0:T(8,128)(2,1)S(1)}, f32[8,1,512]{2,1,0:T(1,128)S(1)}, f32[8,1,512]{2,1,0:T(1,128)}) custom-call(s32[1]{0:T(128)} %get-tuple-element.167.refs_0_, bf16[512,4096]{1,0:T(8,128)(2,1)} %get-tuple-element.154.refs_1_.refs_2_.refs_3_.refs_4_, ...), custom_call_target="tpu_custom_call" | custom-call | flops 19549999104 | bytes 1024 | tf_op jit(solution)/shard_map/inner_kernel/pallas_call | solution.py:53
  601.0 3.6 collective-permute-done.46.refs_2_
  609.9 19.4 %norm_back_kernel.7 = (f32[1,1024]{1,0:T(1,128)S(1)}, bf16[1024,1024]{1,0:T(8,128)(2,1)}) custom-call(f32[1]{0:T(128)} %constant.82.clone.1.refs_0_, bf16[1024,1024]{1,0:T(8,128)(2,1)S(1)} %copy-done.38, bf16[1024,1024]{1,0:T(8,128)(2,1)S(1)} %copy-done.47, bf16[1024,1024]{1,0:T(8,128)(2,1)} %copy-done.59, ...), custom_call_target="tpu_custom_call" | custom-call | flops 23000000512 | bytes 1024 | tf_op jit(solution)/shard_map/norm_back_kernel/pallas_call | solution.py:53
  631.2 6.1 collective-permute-done.48.refs_1_
  647.6 9.2 %update_kernel.3 = (bf16[512,1024]{1,0:T(8,128)(2,1)}, f32[512,1024]{1,0:T(8,128)}, f32[512,1024]{1,0:T(8,128)}) custom-call(f32[1]{0:T(128)} %get-tuple-element.166.refs_0_, bf16[512,1024]{1,0:T(8,128)(2,1)S(1)} %get-tuple-element.235.refs_1_, bf16[512,1024]{1,0:T(8,128)(2,1)S(1)} %get-tuple-element.236.refs_2_, bf16[16,2,576,512]{3,2,1,0:T(8,128)(2,1)} %bitcast.65, ...), custom_call_target="tpu_custom_call" | custom-call | flops 10350000128 | bytes 1024 | tf_op jit(solution)/shard_map/update_kernel/pallas_call | solution.py:53
  656.8 8.6 %collective-permute-start.53 = (f32[4,512]{1,0:T(4,128)S(1)}, f32[4,512]{1,0:T(4,128)S(1)}, u32[]{:S(2)}, u32[]{:S(2)}) collective-permute-start(f32[4,512]{1,0:T(4,128)S(1)} %add.52), channel_id=1, source_target_pairs={{0,8},{2,10},{4,12},{6,14},{8,0},{10,2},{12,4},{14,6},{16,24},{18,... | collective-permute-start | bytes 24584 | tf_op jit(solution)/shard_map/ppermute | solution.py:730
  668.1 3.2 collective-permute-start.54
  674.1 6.8 reduce-scatter.12.cloned.1.call-done.refs_0_
  (363 shorter events, 134.6 us)
Async XLA Ops:
  7.2 211.4 %all-gather.5.cloned.1.call-start = ((), (), s32[]{:S(2)}) async-start(), calls=%async_computation.10 | async-start | bytes 19464192 | tf_op jit(solution)/shard_map/all_gather | solution.py:763
  14.1 285.3 %all-gather.7.cloned.1.call-start = ((), (), s32[]{:S(2)}) async-start(), calls=%async_computation.11 | async-start | bytes 8650752 | tf_op jit(solution)/shard_map/all_gather | solution.py:763
  15.2 15.5 %collective-permute-start.1 = (bf16[256,512]{1,0:T(8,128)(2,1)S(1)}, bf16[256,512]{1,0:T(8,128)(2,1)S(1)}, u32[]{:S(2)}, u32[]{:S(2)}) collective-permute-start(bf16[256,512]{1,0:T(8,128)(2,1)S(1)} %get-tuple-element.254.refs_1_), channel_id=1, source_target_pairs={{0,8},{2,10},{4,12},{6,14},{8,0},{10,2},{12,4},{14,6},{16,24},{18,... | collective-permute-start | bytes 786440 | tf_op jit(solution)/shard_map/ppermute | solution.py:730
  18.3 25.8 %collective-permute-start.2 = (bf16[256,512]{1,0:T(8,128)(2,1)S(1)}, bf16[256,512]{1,0:T(8,128)(2,1)S(1)}, u32[]{:S(2)}, u32[]{:S(2)}) collective-permute-start(bf16[256,512]{1,0:T(8,128)(2,1)S(1)} %get-tuple-element.254.refs_1_), channel_id=1, source_target_pairs={{0,16},{2,18},{4,20},{6,22},{8,24},{10,26},{12,28},{14,30},{16,0},... | collective-permute-start | bytes 786440 | tf_op jit(solution)/shard_map/ppermute | solution.py:730
  20.9 23.7 %collective-permute-start.3 = (bf16[256,512]{1,0:T(8,128)(2,1)S(1)}, bf16[256,512]{1,0:T(8,128)(2,1)S(1)}, u32[]{:S(2)}, u32[]{:S(2)}) collective-permute-start(bf16[256,512]{1,0:T(8,128)(2,1)S(1)} %get-tuple-element.254.refs_1_), channel_id=1, source_target_pairs={{0,24},{2,26},{4,28},{6,30},{8,16},{10,18},{12,20},{14,22},{16,8},... | collective-permute-start | bytes 786440 | tf_op jit(solution)/shard_map/ppermute | solution.py:730
  20.9 452.6 %reduce-scatter.6.cloned.1.call-start = ((), (), s32[]{:S(2)}) async-start(), calls=%async_computation.5 | async-start | bytes 1310720 | tf_op jit(solution)/shard_map/reduce_scatter | solution.py:937
  44.8 31.5 %collective-permute-start.4 = (bf16[4,256,512]{2,1,0:T(8,128)(2,1)S(1)}, bf16[4,256,512]{2,1,0:T(8,128)(2,1)S(1)}, u32[]{:S(2)}, u32[]{:S(2)}) collective-permute-start(bf16[4,256,512]{2,1,0:T(8,128)(2,1)S(1)} %fence_kernel.9.refs_1_), channel_id=1, source_target_pairs={{0,4},{2,6},{4,0},{6,2},{8,12},{10,14},{12,8},{14,10},{16,20},{18,... | collective-permute-start | bytes 3145736 | tf_op jit(solution)/shard_map/ppermute | solution.py:730
  46.4 33.0 %collective-permute-start.5 = (bf16[4,256,512]{2,1,0:T(8,128)(2,1)S(1)}, bf16[4,256,512]{2,1,0:T(8,128)(2,1)S(1)}, u32[]{:S(2)}, u32[]{:S(2)}) collective-permute-start(bf16[4,256,512]{2,1,0:T(8,128)(2,1)S(1)} %fence_kernel.9.refs_1_), channel_id=1, source_target_pairs={{0,1},{1,0},{2,3},{3,2},{4,5},{5,4},{6,7},{7,6},{8,9},{9,8},{10,11... | collective-permute-start | bytes 3145736 | tf_op jit(solution)/shard_map/ppermute | solution.py:728
  48.8 34.7 %collective-permute-start.8 = (bf16[288,512]{1,0:T(8,128)(2,1)S(1)}, bf16[288,512]{1,0:T(8,128)(2,1)}, u32[]{:S(2)}, u32[]{:S(2)}) collective-permute-start(bf16[288,512]{1,0:T(8,128)(2,1)S(1)} %fence_kernel.10.refs_2_), channel_id=1, source_target_pairs={{0,8},{2,10},{4,12},{6,14},{8,0},{10,2},{12,4},{14,6},{16,24},{18,... | collective-permute-start | bytes 884744 | tf_op jit(solution)/shard_map/ppermute | solution.py:730
  61.2 36.6 %collective-permute-start.9 = (bf16[288,512]{1,0:T(8,128)(2,1)S(1)}, bf16[288,512]{1,0:T(8,128)(2,1)}, u32[]{:S(2)}, u32[]{:S(2)}) collective-permute-start(bf16[288,512]{1,0:T(8,128)(2,1)S(1)} %fence_kernel.10.refs_2_), channel_id=1, source_target_pairs={{0,16},{2,18},{4,20},{6,22},{8,24},{10,26},{12,28},{14,30},{16,0},... | collective-permute-start | bytes 884744 | tf_op jit(solution)/shard_map/ppermute | solution.py:730
  62.3 36.4 %collective-permute-start.10 = (bf16[288,512]{1,0:T(8,128)(2,1)S(1)}, bf16[288,512]{1,0:T(8,128)(2,1)}, u32[]{:S(2)}, u32[]{:S(2)}) collective-permute-start(bf16[288,512]{1,0:T(8,128)(2,1)S(1)} %fence_kernel.10.refs_2_), channel_id=1, source_target_pairs={{0,24},{2,26},{4,28},{6,30},{8,16},{10,18},{12,20},{14,22},{16,8},... | collective-permute-start | bytes 884744 | tf_op jit(solution)/shard_map/ppermute | solution.py:730
  80.2 23.7 %collective-permute-start.6 = (bf16[2,256,512]{2,1,0:T(8,128)(2,1)}, bf16[2,256,512]{2,1,0:T(8,128)(2,1)}, u32[]{:S(2)}, u32[]{:S(2)}) collective-permute-start(bf16[2,256,512]{2,1,0:T(8,128)(2,1)} %slice.90), channel_id=1, source_target_pairs={{0,1},{1,0},{2,3},{3,2},{4,5},{5,4},{6,7},{7,6},{8,9},{9,8},{10,11... | collective-permute-start | bytes 1572872 | tf_op jit(solution)/shard_map/ppermute | solution.py:728
  82.9 21.4 %collective-permute-start.7 = (bf16[2,256,512]{2,1,0:T(8,128)(2,1)}, bf16[2,256,512]{2,1,0:T(8,128)(2,1)}, u32[]{:S(2)}, u32[]{:S(2)}) collective-permute-start(bf16[2,256,512]{2,1,0:T(8,128)(2,1)} %slice.91), channel_id=1, source_target_pairs={{0,4},{2,6},{4,0},{6,2},{8,12},{10,14},{12,8},{14,10},{16,20},{18,... | collective-permute-start | bytes 1572872 | tf_op jit(solution)/shard_map/ppermute | solution.py:730
  83.5 24.2 %collective-permute-start.11 = (bf16[4,256,512]{2,1,0:T(8,128)(2,1)S(1)}, bf16[4,256,512]{2,1,0:T(8,128)(2,1)}, u32[]{:S(2)}, u32[]{:S(2)}) collective-permute-start(bf16[4,256,512]{2,1,0:T(8,128)(2,1)S(1)} %fence_kernel.9.refs_1_), channel_id=1, source_target_pairs={{0,2},{2,0},{4,6},{6,4},{8,10},{10,8},{12,14},{14,12},{16,18},{18,... | collective-permute-start | bytes 3145736 | tf_op jit(solution)/shard_map/ppermute | solution.py:730
  107.6 47.0 %collective-permute-start.16 = (bf16[4,288,512]{2,1,0:T(8,128)(2,1)S(1)}, bf16[4,288,512]{2,1,0:T(8,128)(2,1)S(1)}, u32[]{:S(2)}, u32[]{:S(2)}) collective-permute-start(bf16[4,288,512]{2,1,0:T(8,128)(2,1)S(1)} %fence_kernel.12.refs_5_.refs_1_), channel_id=1, source_target_pairs={{0,4},{2,6},{4,0},{6,2},{8,12},{10,14},{12,8},{14,10},{16,20},{18,... | collective-permute-start | bytes 3538952 | tf_op jit(solution)/shard_map/ppermute | solution.py:730
  108.2 47.1 %collective-permute-start.17 = (bf16[4,288,512]{2,1,0:T(8,128)(2,1)S(1)}, bf16[4,288,512]{2,1,0:T(8,128)(2,1)S(1)}, u32[]{:S(2)}, u32[]{:S(2)}) collective-permute-start(bf16[4,288,512]{2,1,0:T(8,128)(2,1)S(1)} %fence_kernel.12.refs_5_.refs_1_), channel_id=1, source_target_pairs={{0,1},{1,0},{2,3},{3,2},{4,5},{5,4},{6,7},{7,6},{8,9},{9,8},{10,11... | collective-permute-start | bytes 3538952 | tf_op jit(solution)/shard_map/ppermute | solution.py:728
  108.2 75.7 %collective-permute-start.20 = (bf16[4,288,512]{2,1,0:T(8,128)(2,1)S(1)}, bf16[4,288,512]{2,1,0:T(8,128)(2,1)S(1)}, u32[]{:S(2)}, u32[]{:S(2)}) collective-permute-start(bf16[4,288,512]{2,1,0:T(8,128)(2,1)S(1)} %fence_kernel.12.refs_5_.refs_1_), channel_id=1, source_target_pairs={{0,2},{2,0},{4,6},{6,4},{8,10},{10,8},{12,14},{14,12},{16,18},{18,... | collective-permute-start | bytes 3538952 | tf_op jit(solution)/shard_map/ppermute | solution.py:730
  155.4 30.2 %collective-permute-start.21 = (bf16[4,288,512]{2,1,0:T(8,128)(2,1)S(1)}, bf16[4,288,512]{2,1,0:T(8,128)(2,1)S(1)}, u32[]{:S(2)}, u32[]{:S(2)}) collective-permute-start(bf16[4,288,512]{2,1,0:T(8,128)(2,1)S(1)} %get-tuple-element.140.refs_3_.refs_2_), channel_id=1, source_target_pairs={{0,2},{2,0},{4,6},{6,4},{8,10},{10,8},{12,14},{14,12},{16,18},{18,... | collective-permute-start | bytes 3538952 | tf_op jit(solution)/shard_map/ppermute | solution.py:730
  155.5 30.1 %collective-permute-start.22 = (bf16[4,288,512]{2,1,0:T(8,128)(2,1)S(1)}, bf16[4,288,512]{2,1,0:T(8,128)(2,1)S(1)}, u32[]{:S(2)}, u32[]{:S(2)}) collective-permute-start(bf16[4,288,512]{2,1,0:T(8,128)(2,1)S(1)} %get-tuple-element.144.refs_3_), channel_id=1, source_target_pairs={{0,2},{2,0},{4,6},{6,4},{8,10},{10,8},{12,14},{14,12},{16,18},{18,... | collective-permute-start | bytes 3538952 | tf_op jit(solution)/shard_map/ppermute | solution.py:730
  156.1 26.6 %collective-permute-start.18 = (bf16[2,288,512]{2,1,0:T(8,128)(2,1)S(1)}, bf16[2,288,512]{2,1,0:T(8,128)(2,1)S(1)}, u32[]{:S(2)}, u32[]{:S(2)}) collective-permute-start(bf16[2,288,512]{2,1,0:T(8,128)(2,1)S(1)} %slice.92), channel_id=1, source_target_pairs={{0,1},{1,0},{2,3},{3,2},{4,5},{5,4},{6,7},{7,6},{8,9},{9,8},{10,11... | collective-permute-start | bytes 1769480 | tf_op jit(solution)/shard_map/ppermute | solution.py:728
  156.1 26.6 %collective-permute-start.19 = (bf16[2,288,512]{2,1,0:T(8,128)(2,1)S(1)}, bf16[2,288,512]{2,1,0:T(8,128)(2,1)S(1)}, u32[]{:S(2)}, u32[]{:S(2)}) collective-permute-start(bf16[2,288,512]{2,1,0:T(8,128)(2,1)S(1)} %slice.93), channel_id=1, source_target_pairs={{0,4},{2,6},{4,0},{6,2},{8,12},{10,14},{12,8},{14,10},{16,20},{18,... | collective-permute-start | bytes 1769480 | tf_op jit(solution)/shard_map/ppermute | solution.py:730
  299.4 25.7 %collective-permute-start.25 = (bf16[4,2,256,1024]{3,2,1,0:T(8,128)(2,1)}, bf16[4,2,256,1024]{3,2,1,0:T(8,128)(2,1)}, u32[]{:S(2)}, u32[]{:S(2)}) collective-permute-start(bf16[4,2,256,1024]{3,2,1,0:T(8,128)(2,1)} %get-tuple-element.170), channel_id=1, source_target_pairs={{0,2},{2,0},{4,6},{6,4},{8,10},{10,8},{12,14},{14,12},{16,18},{18,... | collective-permute-start | bytes 12582920 | tf_op jit(solution)/shard_map/ppermute | solution.py:730
  331.0 37.0 %collective-permute-start.27 = (bf16[2,256,512]{2,1,0:T(8,128)(2,1)S(1)}, bf16[2,256,512]{2,1,0:T(8,128)(2,1)S(1)}, u32[]{:S(2)}, u32[]{:S(2)}) collective-permute-start(bf16[2,256,512]{2,1,0:T(8,128)(2,1)S(1)} %get-tuple-element.177), channel_id=1, source_target_pairs={{0,4},{2,6},{4,0},{6,2},{8,12},{10,14},{12,8},{14,10},{16,20},{18,... | collective-permute-start | bytes 1572872 | tf_op jit(solution)/shard_map/ppermute | solution.py:730
  332.7 35.3 %collective-permute-start.28 = (bf16[2,256,512]{2,1,0:T(8,128)(2,1)S(1)}, bf16[2,256,512]{2,1,0:T(8,128)(2,1)S(1)}, u32[]{:S(2)}, u32[]{:S(2)}) collective-permute-start(bf16[2,256,512]{2,1,0:T(8,128)(2,1)S(1)} %get-tuple-element.178), channel_id=1, source_target_pairs={{0,1},{1,0},{2,3},{3,2},{4,5},{5,4},{6,7},{7,6},{8,9},{9,8},{10,11... | collective-permute-start | bytes 1572872 | tf_op jit(solution)/shard_map/ppermute | solution.py:728
  348.7 21.5 %collective-permute-start.26 = (bf16[4,2,64,4096]{3,2,1,0:T(8,128)(2,1)}, bf16[4,2,64,4096]{3,2,1,0:T(8,128)(2,1)}, u32[]{:S(2)}, u32[]{:S(2)}) collective-permute-start(bf16[4,2,64,4096]{3,2,1,0:T(8,128)(2,1)} %get-tuple-element.174), channel_id=1, source_target_pairs={{0,2},{2,0},{4,6},{6,4},{8,10},{10,8},{12,14},{14,12},{16,18},{18,... | collective-permute-start | bytes 12582920 | tf_op jit(solution)/shard_map/ppermute | solution.py:730
  368.8 34.7 %collective-permute-start.31 = (bf16[4,256,512]{2,1,0:T(8,128)(2,1)S(1)}, bf16[4,256,512]{2,1,0:T(8,128)(2,1)S(1)}, u32[]{:S(2)}, u32[]{:S(2)}) collective-permute-start(bf16[4,256,512]{2,1,0:T(8,128)(2,1)S(1)} %get-tuple-element.180.refs_3_), channel_id=1, source_target_pairs={{0,4},{2,6},{4,0},{6,2},{8,12},{10,14},{12,8},{14,10},{16,20},{18,... | collective-permute-start | bytes 3145736 | tf_op jit(solution)/shard_map/ppermute | solution.py:730
  369.2 34.3 %collective-permute-start.32 = (bf16[4,256,512]{2,1,0:T(8,128)(2,1)S(1)}, bf16[4,256,512]{2,1,0:T(8,128)(2,1)S(1)}, u32[]{:S(2)}, u32[]{:S(2)}) collective-permute-start(bf16[4,256,512]{2,1,0:T(8,128)(2,1)S(1)} %get-tuple-element.191), channel_id=1, source_target_pairs={{0,1},{1,0},{2,3},{3,2},{4,5},{5,4},{6,7},{7,6},{8,9},{9,8},{10,11... | collective-permute-start | bytes 3145736 | tf_op jit(solution)/shard_map/ppermute | solution.py:728
  392.1 13.7 %collective-permute-start.29 = (bf16[2,64,2048]{2,1,0:T(8,128)(2,1)S(1)}, bf16[2,64,2048]{2,1,0:T(8,128)(2,1)S(1)}, u32[]{:S(2)}, u32[]{:S(2)}) collective-permute-start(bf16[2,64,2048]{2,1,0:T(8,128)(2,1)S(1)} %get-tuple-element.189), channel_id=1, source_target_pairs={{0,4},{2,6},{4,0},{6,2},{8,12},{10,14},{12,8},{14,10},{16,20},{18,... | collective-permute-start | bytes 1572872 | tf_op jit(solution)/shard_map/ppermute | solution.py:730
  437.0 27.1 %collective-permute-start.33 = (bf16[4,2,320,1024]{3,2,1,0:T(8,128)(2,1)}, bf16[4,2,320,1024]{3,2,1,0:T(8,128)(2,1)}, u32[]{:S(2)}, u32[]{:S(2)}) collective-permute-start(bf16[4,2,320,1024]{3,2,1,0:T(8,128)(2,1)} %get-tuple-element.207), channel_id=1, source_target_pairs={{0,2},{2,0},{4,6},{6,4},{8,10},{10,8},{12,14},{14,12},{16,18},{18,... | collective-permute-start | bytes 15728648 | tf_op jit(solution)/shard_map/ppermute | solution.py:730
  437.0 117.7 %reduce-scatter.8.cloned.1.call-start = ((), (), s32[]{:S(2)}) async-start(), calls=%async_computation.6 | async-start | bytes 1310720 | tf_op jit(solution)/shard_map/reduce_scatter | solution.py:937
  437.1 25.6 %collective-permute-start.34 = (bf16[4,64,2048]{2,1,0:T(8,128)(2,1)S(1)}, bf16[4,64,2048]{2,1,0:T(8,128)(2,1)S(1)}, u32[]{:S(2)}, u32[]{:S(2)}) collective-permute-start(bf16[4,64,2048]{2,1,0:T(8,128)(2,1)S(1)} %get-tuple-element.193.refs_7_), channel_id=1, source_target_pairs={{0,4},{2,6},{4,0},{6,2},{8,12},{10,14},{12,8},{14,10},{16,20},{18,... | collective-permute-start | bytes 3145736 | tf_op jit(solution)/shard_map/ppermute | solution.py:730
  437.5 25.3 %collective-permute-start.35 = (bf16[4,64,2048]{2,1,0:T(8,128)(2,1)S(1)}, bf16[4,64,2048]{2,1,0:T(8,128)(2,1)S(1)}, u32[]{:S(2)}, u32[]{:S(2)}) collective-permute-start(bf16[4,64,2048]{2,1,0:T(8,128)(2,1)S(1)} %get-tuple-element.208), channel_id=1, source_target_pairs={{0,1},{1,0},{2,3},{3,2},{4,5},{5,4},{6,7},{7,6},{8,9},{9,8},{10,11... | collective-permute-start | bytes 3145736 | tf_op jit(solution)/shard_map/ppermute | solution.py:728
  464.0 165.3 %reduce-scatter.10.cloned.1.call-start = ((), (), s32[]{:S(2)}) async-start(), calls=%async_computation.7 | async-start | bytes 1638400 | tf_op jit(solution)/shard_map/reduce_scatter | solution.py:937
  470.8 30.0 %collective-permute-start.37 = (bf16[2,320,512]{2,1,0:T(8,128)(2,1)}, bf16[2,320,512]{2,1,0:T(8,128)(2,1)}, u32[]{:S(2)}, u32[]{:S(2)}) collective-permute-start(bf16[2,320,512]{2,1,0:T(8,128)(2,1)} %get-tuple-element.214), channel_id=1, source_target_pairs={{0,4},{2,6},{4,0},{6,2},{8,12},{10,14},{12,8},{14,10},{16,20},{18,... | collective-permute-start | bytes 1966088 | tf_op jit(solution)/shard_map/ppermute | solution.py:730
  472.5 28.3 %collective-permute-start.38 = (bf16[2,320,512]{2,1,0:T(8,128)(2,1)S(1)}, bf16[2,320,512]{2,1,0:T(8,128)(2,1)}, u32[]{:S(2)}, u32[]{:S(2)}) collective-permute-start(bf16[2,320,512]{2,1,0:T(8,128)(2,1)S(1)} %get-tuple-element.215), channel_id=1, source_target_pairs={{0,1},{1,0},{2,3},{3,2},{4,5},{5,4},{6,7},{7,6},{8,9},{9,8},{10,11... | collective-permute-start | bytes 1966088 | tf_op jit(solution)/shard_map/ppermute | solution.py:728
  489.7 15.2 %collective-permute-start.36 = (bf16[4,2,64,4096]{3,2,1,0:T(8,128)(2,1)}, bf16[4,2,64,4096]{3,2,1,0:T(8,128)(2,1)}, u32[]{:S(2)}, u32[]{:S(2)}) collective-permute-start(bf16[4,2,64,4096]{3,2,1,0:T(8,128)(2,1)} %get-tuple-element.211), channel_id=1, source_target_pairs={{0,2},{2,0},{4,6},{6,4},{8,10},{10,8},{12,14},{14,12},{16,18},{18,... | collective-permute-start | bytes 12582920 | tf_op jit(solution)/shard_map/ppermute | solution.py:730
  503.5 47.7 %collective-permute-start.39 = (bf16[4,320,512]{2,1,0:T(8,128)(2,1)S(1)}, bf16[4,320,512]{2,1,0:T(8,128)(2,1)S(1)}, u32[]{:S(2)}, u32[]{:S(2)}) collective-permute-start(bf16[4,320,512]{2,1,0:T(8,128)(2,1)S(1)} %get-tuple-element.218.refs_3_), channel_id=1, source_target_pairs={{0,4},{2,6},{4,0},{6,2},{8,12},{10,14},{12,8},{14,10},{16,20},{18,... | collective-permute-start | bytes 3932168 | tf_op jit(solution)/shard_map/ppermute | solution.py:730
  504.0 47.2 %collective-permute-start.40 = (bf16[4,320,512]{2,1,0:T(8,128)(2,1)S(1)}, bf16[4,320,512]{2,1,0:T(8,128)(2,1)S(1)}, u32[]{:S(2)}, u32[]{:S(2)}) collective-permute-start(bf16[4,320,512]{2,1,0:T(8,128)(2,1)S(1)} %get-tuple-element.225), channel_id=1, source_target_pairs={{0,1},{1,0},{2,3},{3,2},{4,5},{5,4},{6,7},{7,6},{8,9},{9,8},{10,11... | collective-permute-start | bytes 3932168 | tf_op jit(solution)/shard_map/ppermute | solution.py:728
  510.4 35.6 %collective-permute-start.41 = (bf16[2,64,2048]{2,1,0:T(8,128)(2,1)S(1)}, bf16[2,64,2048]{2,1,0:T(8,128)(2,1)S(1)}, u32[]{:S(2)}, u32[]{:S(2)}) collective-permute-start(bf16[2,64,2048]{2,1,0:T(8,128)(2,1)S(1)} %get-tuple-element.228), channel_id=1, source_target_pairs={{0,4},{2,6},{4,0},{6,2},{8,12},{10,14},{12,8},{14,10},{16,20},{18,... | collective-permute-start | bytes 1572872 | tf_op jit(solution)/shard_map/ppermute | solution.py:730
  512.2 33.9 %collective-permute-start.42 = (bf16[2,64,2048]{2,1,0:T(8,128)(2,1)S(1)}, bf16[2,64,2048]{2,1,0:T(8,128)(2,1)S(1)}, u32[]{:S(2)}, u32[]{:S(2)}) collective-permute-start(bf16[2,64,2048]{2,1,0:T(8,128)(2,1)S(1)} %get-tuple-element.229), channel_id=1, source_target_pairs={{0,1},{1,0},{2,3},{3,2},{4,5},{5,4},{6,7},{7,6},{8,9},{9,8},{10,11... | collective-permute-start | bytes 1572872 | tf_op jit(solution)/shard_map/ppermute | solution.py:728
  548.5 25.0 %collective-permute-start.44 = (bf16[4,64,2048]{2,1,0:T(8,128)(2,1)}, bf16[4,64,2048]{2,1,0:T(8,128)(2,1)}, u32[]{:S(2)}, u32[]{:S(2)}) collective-permute-start(bf16[4,64,2048]{2,1,0:T(8,128)(2,1)} %get-tuple-element.230.refs_3_), channel_id=1, source_target_pairs={{0,4},{2,6},{4,0},{6,2},{8,12},{10,14},{12,8},{14,10},{16,20},{18,... | collective-permute-start | bytes 3145736 | tf_op jit(solution)/shard_map/ppermute | solution.py:730
  550.1 24.4 %collective-permute-start.45 = (bf16[4,64,2048]{2,1,0:T(8,128)(2,1)}, bf16[4,64,2048]{2,1,0:T(8,128)(2,1)}, u32[]{:S(2)}, u32[]{:S(2)}) collective-permute-start(bf16[4,64,2048]{2,1,0:T(8,128)(2,1)} %get-tuple-element.233), channel_id=1, source_target_pairs={{0,1},{1,0},{2,3},{3,2},{4,5},{5,4},{6,7},{7,6},{8,9},{9,8},{10,11... | collective-permute-start | bytes 3145736 | tf_op jit(solution)/shard_map/ppermute | solution.py:728
  572.2 99.1 %reduce-scatter.14.cloned.1.call-start = ((), (), s32[]{:S(2)}) async-start(), calls=%async_computation.9 | async-start | bytes 1310720 | tf_op jit(solution)/shard_map/reduce_scatter | solution.py:937
  577.2 103.7 %reduce-scatter.12.cloned.1.call-start = ((), (), s32[]{:S(2)}) async-start(), calls=%async_computation.8 | async-start | bytes 1638400 | tf_op jit(solution)/shard_map/reduce_scatter | solution.py:937
  588.0 16.6 %collective-permute-start.46 = (bf16[2,80,2048]{2,1,0:T(8,128)(2,1)S(1)}, bf16[2,80,2048]{2,1,0:T(8,128)(2,1)S(1)}, u32[]{:S(2)}, u32[]{:S(2)}) collective-permute-start(bf16[2,80,2048]{2,1,0:T(8,128)(2,1)S(1)} %get-tuple-element.239), channel_id=1, source_target_pairs={{0,4},{2,6},{4,0},{6,2},{8,12},{10,14},{12,8},{14,10},{16,20},{18,... | collective-permute-start | bytes 1966088 | tf_op jit(solution)/shard_map/ppermute | solution.py:730
  588.1 16.5 %collective-permute-start.47 = (bf16[2,80,2048]{2,1,0:T(8,128)(2,1)S(1)}, bf16[2,80,2048]{2,1,0:T(8,128)(2,1)S(1)}, u32[]{:S(2)}, u32[]{:S(2)}) collective-permute-start(bf16[2,80,2048]{2,1,0:T(8,128)(2,1)S(1)} %get-tuple-element.240), channel_id=1, source_target_pairs={{0,1},{1,0},{2,3},{3,2},{4,5},{5,4},{6,7},{7,6},{8,9},{9,8},{10,11... | collective-permute-start | bytes 1966088 | tf_op jit(solution)/shard_map/ppermute | solution.py:728
  607.3 30.0 %collective-permute-start.48 = (bf16[4,80,2048]{2,1,0:T(8,128)(2,1)}, bf16[4,80,2048]{2,1,0:T(8,128)(2,1)S(1)}, u32[]{:S(2)}, u32[]{:S(2)}) collective-permute-start(bf16[4,80,2048]{2,1,0:T(8,128)(2,1)} %get-tuple-element.242.refs_9_), channel_id=1, source_target_pairs={{0,4},{2,6},{4,0},{6,2},{8,12},{10,14},{12,8},{14,10},{16,20},{18,... | collective-permute-start | bytes 3932168 | tf_op jit(solution)/shard_map/ppermute | solution.py:730
  609.0 29.6 %collective-permute-start.49 = (bf16[4,80,2048]{2,1,0:T(8,128)(2,1)}, bf16[4,80,2048]{2,1,0:T(8,128)(2,1)}, u32[]{:S(2)}, u32[]{:S(2)}) collective-permute-start(bf16[4,80,2048]{2,1,0:T(8,128)(2,1)} %get-tuple-element.243), channel_id=1, source_target_pairs={{0,1},{1,0},{2,3},{3,2},{4,5},{5,4},{6,7},{7,6},{8,9},{9,8},{10,11... | collective-permute-start | bytes 3932168 | tf_op jit(solution)/shard_map/ppermute | solution.py:728
  (101 other events, 756.7 us)
Sparse Core Ops, SparseCore 0:
  14.3 185.1 all-gather.4
  202.6 80.7 all-gather.6
  437.1 34.4 reduce-scatter.5
  473.9 25.7 reduce-scatter.7
  572.4 38.3 reduce-scatter.9
  612.9 25.9 reduce-scatter.13
  642.1 38.7 reduce-scatter.11
